TPU v7x, 32 devices: a whole 2x2x4 slice. The times are simulated.
32 devices in a mesh: parts: 1, gx: 4 (over z), gy: 4 (over y, x), gz: 2 (over core).
Axes of the slice: x: 2, y: 2, z: 4, core: 2. Of those that a mesh axis runs over, the one named last changes fastest.
Arguments:
- state_field: bfloat16 [8, 12, 128, 128, 128], P('parts', None, 'gx', ('gy', 'gz')), may hold values from -6 to 6
- cotangent: bfloat16 [8, 12, 128, 128, 128], P('parts', None, 'gx', ('gy', 'gz')), may hold values from -6 to 6
- spectral_weight: bfloat16 [32, 32, 12, 12, 4, 32], P(('gy', 'gz'), 'gx'), may hold values from -12 to 12
- point_weight: bfloat16 [12, 12], replicated, may hold values from -1.75 to 1.75
Outputs:
- grad_field: bfloat16 [8, 12, 128, 128, 128], P('parts', None, 'gx', ('gy', 'gz'))
- grad_spectral: float32 [32, 32, 12, 12, 4, 32], P(('parts', 'gy', 'gz'), 'gx')
All inputs are finite; a program needn't handle non-finite values.
Results may differ from a plain program's by a relative error of at most 0.02.
Values may be sent and summed in bfloat16 or wider, within the bound.
No kernel may reach another device: no remote copies, remote signals or barrier semaphores. Data moves between devices by JAX's collectives and lax.ppermute only.
A program may use at most 256 MiB of HBM per device.

v0:
```python
import math

import jax
import jax.numpy as jnp
from jax import lax
from jax.sharding import PartitionSpec as P

highest = lax.Precision.HIGHEST


def build_table(row_count, col_start, col_count, extent):
    row_index = jnp.arange(row_count, dtype=jnp.int32)[:, None]
    cell_index = col_start + jnp.arange(col_count, dtype=jnp.int32)[None, :]
    frequency = (row_index + 1) // 2
    phase_turns = (frequency * cell_index % extent).astype(jnp.float32)
    radians = phase_turns * (2.0 * math.pi / extent)
    waveform = jnp.where(row_index % 2 == 0, jnp.cos(radians), jnp.sin(radians))
    row_scale = jnp.where(row_index == 0, math.sqrt(1.0 / extent), math.sqrt(2.0 / extent))
    return (waveform * row_scale).astype(jnp.bfloat16)


def exact_mix(form, left, right):
    return jnp.einsum(form, left.astype(jnp.float32), right.astype(jnp.float32), precision=highest)


def narrow_mix(form, left, right):
    return jnp.einsum(form, left, right, preferred_element_type=jnp.float32)


def shards(state_field, cotangent, spectral_weight, point_weight):
    steps_time, channels, x_local, y_local, depth = state_field.shape
    time_modes = spectral_weight.shape[4]
    modes = spectral_weight.shape[5]
    x_devices = lax.axis_size("gx")
    yz_devices = lax.axis_size(("gy", "gz"))
    x_extent = x_local * x_devices
    y_extent = y_local * yz_devices
    y_offset = lax.axis_index(("gy", "gz")) * y_local
    y_rows = modes // yz_devices
    time_table = build_table(time_modes, 0, steps_time, steps_time)
    depth_table = build_table(modes, 0, depth, depth)
    x_table = build_table(modes, 0, x_extent, x_extent)

    def head(values):
        depth_part = jnp.dot(values, depth_table.T, preferred_element_type=jnp.float32)
        return exact_mix("pt,tcxyq->cxypq", time_table, depth_part).astype(jnp.bfloat16)

    def analyze(head_modes):
        x_done = narrow_mix(
            "ix,cxypq->cyqpi",
            x_table,
            lax.all_to_all(head_modes, "gx", split_axis=4, concat_axis=1, tiled=True),
        )
        y_table = build_table(lax.axis_size(("gy", "gz")) * y_rows, y_offset, y_local, y_extent)
        return lax.psum_scatter(
            exact_mix("jy,cyqpi->jcqpi", y_table, x_done).astype(jnp.bfloat16),
            ("gy", "gz"),
            scatter_dimension=0,
            tiled=True,
        )

    def synthesize(spec_modes):
        shard_piece = lax.all_gather(spec_modes, ("gy", "gz"), axis=0, tiled=True)
        y_table = build_table(shard_piece.shape[0], y_offset, y_local, y_extent)
        y_done = narrow_mix("jy,joqpi->oyqpi", y_table, shard_piece)
        x_done = exact_mix("ix,oyqpi->oxypq", x_table, y_done).astype(jnp.bfloat16)
        middle = lax.all_to_all(x_done, "gx", split_axis=1, concat_axis=4, tiled=True)
        return middle

    def tail(middle):
        depth_syn = jnp.dot(middle, depth_table, preferred_element_type=jnp.float32)
        return exact_mix("pt,oxypz->toxyz", time_table, depth_syn)

    modes_in = analyze(head(state_field))
    modes_out = exact_mix("jcqpi,jqcopi->joqpi", modes_in, spectral_weight).astype(jnp.bfloat16)
    preact = tail(synthesize(modes_out)) + narrow_mix("tcxyz,co->toxyz", state_field, point_weight)
    gelu_slope = 0.5 * (1.0 + lax.erf(preact * (1.0 / math.sqrt(2.0)))) + preact * jnp.exp(
        -0.5 * preact * preact
    ) * (1.0 / math.sqrt(2.0 * math.pi))
    grad_pre = (cotangent.astype(jnp.float32) * gelu_slope).astype(jnp.bfloat16)
    grad_modes = analyze(head(grad_pre))
    grad_spectral = exact_mix("jcqpi,joqpi->jqcopi", modes_in, grad_modes)
    back_modes = exact_mix("joqpi,jqcopi->jcqpi", grad_modes, spectral_weight).astype(jnp.bfloat16)
    grad_field = tail(synthesize(back_modes)) + narrow_mix(
        "toxyz,co->tcxyz", grad_pre, point_weight
    )
    return (grad_field.astype(jnp.bfloat16), grad_spectral)


def solution(mesh):
    in_specs = (
        P("parts", None, "gx", ("gy", "gz"), None),
        P("parts", None, "gx", ("gy", "gz"), None),
        P(("gy", "gz"), "gx", None, None, None, None),
        P(),
    )
    out_specs = (
        P("parts", None, "gx", ("gy", "gz"), None),
        P(("parts", "gy", "gz"), "gx", None, None, None, None),
    )
    return jax.shard_map(shards, mesh=mesh, in_specs=in_specs, out_specs=out_specs, check_vma=False)
```

profile of v0, /device:TPU:0, one launch (start us, length us, event | category | flops | bytes accessed | tf_op | source)
XLA Modules:
  0.0 803.3 jit_solution(2636904817134679706)
XLA Ops:
  7.2 26.4 %fusion.17 = f32[8,12,32,16,32]{2,4,3,1,0:T(8,128)} fusion(bf16[8,12,32,16,128]{4,3,2,1,0:T(8,128)(2,1)} %param.4, f32[32]{0:T(128)S(1)} %compare_select_fusion, s32[32]{0:T(128)S(1)} %and_select_fusion, pred[32]{0:T(512)(128)(4,1)S(1)} %fusion.96), kind=kOutput, calls=%fused_computation.23 | convolution fusion | flops 402722816 | bytes 18874656 | tf_op jit(solution)/shard_map/dot_general | solution.py:45
  33.7 27.3 %copy.98 = f32[8,12,32,16,32]{4,0,3,2,1:T(8,128)} copy(f32[8,12,32,16,32]{2,4,3,1,0:T(8,128)} %fusion.17) | data formatting | bytes 12582912 | tf_op jit(solution)/shard_map/dot_general | solution.py:45
  61.0 18.1 %convert_bitcast_fusion.1 = bf16[12,32,16,4,32]{4,3,2,1,0:T(4,128)(2,1)} fusion(f32[8,12,32,16,32]{4,0,3,2,1:T(8,128)} %copy.98, f32[4]{0:T(128)S(1)} %compare_select_fusion.1, s32[4]{0:T(128)S(1)} %and_select_fusion.2, pred[4]{0:T(512)(128)(4,1)S(1)} %fusion.95), kind=kOutput, calls=%fused_computation.31 | convolution fusion | flops 76284448 | bytes 7864356 | tf_op jit(solution)/shard_map/pt,tcxyq->cxypq/dot_general | solution.py:23
  79.1 15.7 %copy.99 = bf16[12,32,16,4,32]{1,2,3,0,4:T(8,128)(2,1)} copy(bf16[12,32,16,4,32]{4,3,2,1,0:T(4,128)(2,1)} %convert_bitcast_fusion.1) | data formatting | bytes 3145728 | tf_op jit(solution)/shard_map/convert_element_type | solution.py:46
  94.8 8.3 %reshape.144 = bf16[4,2,98304]{2,1,0:T(2,128)(2,1)} reshape(bf16[32,12,4,16,32]{4,3,2,1,0:T(8,128)(2,1)} %bitcast.142) | data formatting | bytes 3145728
  103.1 6.5 all-to-all-start
  109.6 0.0 reduce-scatter.3.cloned.1.call-start
  109.7 36.9 %all-to-all-done = bf16[4,2,98304]{2,1,0:T(2,128)(2,1)S(1)} async-done(((bf16[4,2,98304]{2,1,0:T(2,128)(2,1)}), bf16[4,2,98304]{2,1,0:T(2,128)(2,1)S(1)}, u32[]{:S(2)}, u32[]{:S(2)}) %all-to-all-start) | async-done | bytes 1572896 | tf_op jit(solution)/shard_map/all_to_all | solution.py:52
  146.6 4.6 reshape.145
  151.1 18.2 %copy.156 = bf16[12,4,32,16,4,8]{2,1,3,4,5,0:T(4,128)(2,1)} copy(bf16[12,4,32,16,4,8]{2,3,4,0,5,1:T(8,128)(2,1)} %bitcast.143) | data formatting | bytes 3145728 | tf_op jit(solution)/shard_map/all_to_all | solution.py:52
  169.3 7.3 reshape.142
  176.7 0.7 fusion.79
  177.4 3.2 fusion.42
  180.6 3.7 copy.103
  184.3 0.0 reduce-scatter.3.cloned.1.call-update
  184.3 45.5 %reduce-scatter.3.cloned.1.call-done = bf16[4,12,8,4,32]{4,2,3,1,0:T(8,128)(2,1)} async-done(((bf16[32,12,8,4,32]{4,2,3,1,0:T(8,128)(2,1)}), bf16[4,12,8,4,32]{4,2,3,1,0:T(8,128)(2,1)}) %reduce-scatter.3.cloned.1.call-update) | async-done | bytes 98320 | tf_op jit(solution)/shard_map/reduce_scatter | solution.py:55
  229.8 2.2 convert_bitcast_fusion.2
  232.0 0.2 copy.164
  232.2 6.5 multiply_reduce_fusion.1
  238.8 0.1 copy.228
  238.9 18.9 %all_gather.6 = bf16[32,12,8,4,32]{4,2,3,1,0:T(8,128)(2,1)S(1)} all-gather(bf16[4,12,8,4,32]{4,2,3,1,0:T(8,128)(2,1)S(1)} %bitcast.146), channel_id=1, replica_groups=mesh['parts'=1,'gx'=4,'gy'=4,'gz'=2] {'gy','gz'}, dimensions={0}, use_global_device_ids=true | all-gather | bytes 884736 | tf_op jit(solution)/shard_map/all_gather | solution.py:63
  257.8 2.3 fusion.48
  260.1 3.5 fusion.63
  263.6 17.5 %copy.106 = bf16[12,128,16,4,8]{2,4,3,0,1:T(8,128)(2,1)} copy(bf16[12,128,16,4,8]{1,4,3,2,0:T(8,128)(2,1)S(1)} %fusion.63) | data formatting | bytes 3145728 | tf_op jit(solution)/shard_map/convert_element_type | solution.py:66
  281.1 15.6 %reshape.146 = bf16[4,2,98304]{2,1,0:T(2,128)(2,1)} reshape(bf16[128,12,4,8,16]{4,3,2,1,0:T(8,128)(2,1)} %bitcast.136) | data formatting | bytes 3145728
  296.7 4.6 all-to-all-start.1
  301.3 16.4 %fusion.9 = f32[12,8,32,16,128]{4,0,3,2,1:T(8,128)} fusion(bf16[8,12,32,16,128]{4,3,2,1,0:T(8,128)(2,1)} %param.4, bf16[12,12]{1,0:T(8,128)(2,1)S(1)} %copy-done), kind=kOutput, calls=%fused_computation.12 | convolution fusion | flops 150994944 | bytes 37749024 | tf_op jit(solution)/shard_map/tcxyz,co->toxyz/dot_general | solution.py:27
  317.7 21.1 %all-to-all-done.1 = bf16[4,2,98304]{2,1,0:T(2,128)(2,1)S(1)} async-done(((bf16[4,2,98304]{2,1,0:T(2,128)(2,1)}), bf16[4,2,98304]{2,1,0:T(2,128)(2,1)S(1)}, u32[]{:S(2)}, u32[]{:S(2)}) %all-to-all-start.1) | async-done | bytes 1572896 | tf_op jit(solution)/shard_map/all_to_all | solution.py:67
  338.8 10.9 %reshape.147 = bf16[128,12,4,8,16]{4,3,2,1,0:T(8,128)(2,1)} reshape(bf16[4,2,98304]{2,1,0:T(2,128)(2,1)S(1)} %all-to-all-done.1) | data formatting | bytes 3145728
  349.7 19.1 %copy.157 = bf16[12,4,32,16,4,8]{2,1,5,4,3,0:T(4,128)(2,1)} copy(bf16[12,4,32,16,4,8]{3,5,4,0,2,1:T(8,128)(2,1)} %bitcast.137) | data formatting | bytes 3145728 | tf_op jit(solution)/shard_map/all_to_all | solution.py:67
  368.9 4.8 fusion.24
  373.7 55.9 %fusion.5 = bf16[8,12,32,16,128]{4,0,3,2,1:T(8,128)(2,1)} fusion(f32[12,8,32,16,128]{4,0,3,2,1:T(8,128)} %fusion.9, bf16[8,12,32,16,128]{4,3,2,1,0:T(8,128)(2,1)} %param.5, f32[12,32,16,4,128]{4,1,3,2,0:T(8,128)S(1)} %fusion.24, f32[4]{0:T(128)S(1)} %compare_select_fusion.1, s32[4]{0:T(128)S(1)} %and_select_fusion.2, pred[4]{0:T(512)(128)(4,1)S(1)} %fusion.95), kind=kOutput, calls=%fused_computation.6 | convolution fusion | flops 377487904 | bytes 62914596 | tf_op jit(solution)/shard_map/pt,oxypz->toxyz/dot_general | solution.py:23
  429.5 12.9 %fusion.83 = f32[8,12,32,16,32]{4,0,3,2,1:T(8,128)} fusion(bf16[8,12,32,16,128]{4,0,3,2,1:T(8,128)(2,1)} %fusion.5, f32[32]{0:T(128)S(1)} %compare_select_fusion, s32[32]{0:T(128)S(1)} %and_select_fusion, pred[32]{0:T(512)(128)(4,1)S(1)} %fusion.96), kind=kOutput, calls=%fused_computation.84 | convolution fusion | flops 402722816 | bytes 18874656 | tf_op jit(solution)/shard_map/dot_general | solution.py:45
  442.5 18.1 %convert_bitcast_fusion = bf16[12,32,16,4,32]{4,3,2,1,0:T(4,128)(2,1)} fusion(f32[8,12,32,16,32]{4,0,3,2,1:T(8,128)} %fusion.83, f32[4]{0:T(128)S(1)} %compare_select_fusion.1, s32[4]{0:T(128)S(1)} %and_select_fusion.2, pred[4]{0:T(512)(128)(4,1)S(1)} %fusion.95), kind=kOutput, calls=%fused_computation.30 | convolution fusion | flops 76284448 | bytes 7864356 | tf_op jit(solution)/shard_map/pt,tcxyq->cxypq/dot_general | solution.py:23
  460.6 15.7 %copy.114 = bf16[12,32,16,4,32]{1,2,3,0,4:T(8,128)(2,1)} copy(bf16[12,32,16,4,32]{4,3,2,1,0:T(4,128)(2,1)} %convert_bitcast_fusion) | data formatting | bytes 3145728 | tf_op jit(solution)/shard_map/convert_element_type | solution.py:46
  476.3 7.6 reshape.148
  483.9 39.1 %all_to_all.72 = bf16[4,2,98304]{2,1,0:T(2,128)(2,1)S(1)} all-to-all(bf16[4,2,98304]{2,1,0:T(2,128)(2,1)S(1)} %reshape.148), channel_id=1, replica_groups=mesh['parts'=1,'gx'=4,'gy'=4,'gz'=2] {'gx'}, dimensions={0} | all-to-all | bytes 3145728 | tf_op jit(solution)/shard_map/all_to_all | solution.py:52
  523.0 4.7 reshape.149
  527.7 17.9 %copy.160 = bf16[12,4,32,16,4,8]{2,1,3,4,5,0:T(4,128)(2,1)} copy(bf16[12,4,32,16,4,8]{2,3,4,0,5,1:T(8,128)(2,1)} %bitcast.145) | data formatting | bytes 3145728 | tf_op jit(solution)/shard_map/all_to_all | solution.py:52
  545.6 7.3 reshape.143
  552.9 0.7 fusion.77
  553.6 3.2 fusion.45
  556.9 3.7 copy.118
  560.6 0.2 copy.129
  560.8 44.3 %reduce-scatter.5.cloned.1.call-done = bf16[4,12,8,4,32]{4,2,3,1,0:T(8,128)(2,1)} async-done(((bf16[32,12,8,4,32]{4,2,3,1,0:T(8,128)(2,1)}), bf16[4,12,8,4,32]{4,2,3,1,0:T(8,128)(2,1)}) %reduce-scatter.5.cloned.1.call-update) | async-done | bytes 98320 | tf_op jit(solution)/shard_map/reduce_scatter | solution.py:55
  605.1 1.3 convert_bitcast_fusion.3
  606.5 0.2 copy.165
  606.7 6.5 multiply_reduce_fusion
  613.1 0.1 copy.229
  613.2 19.1 %all_gather.7 = bf16[32,12,8,4,32]{4,2,3,1,0:T(8,128)(2,1)S(1)} all-gather(bf16[4,12,8,4,32]{4,2,3,1,0:T(8,128)(2,1)S(1)} %bitcast.147), channel_id=1, replica_groups=mesh['parts'=1,'gx'=4,'gy'=4,'gz'=2] {'gy','gz'}, dimensions={0}, use_global_device_ids=true | all-gather | bytes 884736 | tf_op jit(solution)/shard_map/all_gather | solution.py:63
  632.4 2.3 fusion.51
  634.7 3.5 fusion.60
  638.2 17.5 %copy.121 = bf16[12,128,16,4,8]{2,4,3,0,1:T(8,128)(2,1)} copy(bf16[12,128,16,4,8]{1,4,3,2,0:T(8,128)(2,1)S(1)} %fusion.60) | data formatting | bytes 3145728 | tf_op jit(solution)/shard_map/convert_element_type | solution.py:66
  655.7 15.7 %reshape.150 = bf16[4,2,98304]{2,1,0:T(2,128)(2,1)} reshape(bf16[128,12,4,8,16]{4,3,2,1,0:T(8,128)(2,1)} %bitcast.138) | data formatting | bytes 3145728
  671.4 4.7 all-to-all-start.3
  676.1 30.2 %fusion.7 = f32[8,32,16,128,12]{3,4,2,1,0:T(8,128)} fusion(bf16[8,12,32,16,128]{4,0,3,2,1:T(8,128)(2,1)} %fusion.5, bf16[12,12]{1,0:T(8,128)(2,1)S(1)} %copy-done), kind=kOutput, calls=%fused_computation.10 | convolution fusion | flops 150994944 | bytes 37749024 | tf_op jit(solution)/shard_map/toxyz,co->tcxyz/dot_general | solution.py:27
  706.3 0.2 copy.128
  706.5 6.2 multiply_bitcast_fusion
  712.8 0.7 all-to-all-done.3
  713.4 10.9 %reshape.151 = bf16[128,12,4,8,16]{4,3,2,1,0:T(8,128)(2,1)} reshape(bf16[4,2,98304]{2,1,0:T(2,128)(2,1)S(1)} %all-to-all-done.3) | data formatting | bytes 3145728
  724.4 19.2 %copy.161 = bf16[12,4,32,16,4,8]{2,1,5,4,3,0:T(4,128)(2,1)} copy(bf16[12,4,32,16,4,8]{3,5,4,0,2,1:T(8,128)(2,1)} %bitcast.139) | data formatting | bytes 3145728 | tf_op jit(solution)/shard_map/all_to_all | solution.py:67
  743.5 4.8 fusion.22
  748.3 41.3 %fusion.6 = bf16[8,12,32,16,128]{4,0,3,2,1:T(8,128)(2,1)S(1)} fusion(f32[8,32,16,128,12]{3,4,2,1,0:T(8,128)} %fusion.7, f32[12,32,16,4,128]{4,1,3,2,0:T(8,128)S(1)} %fusion.22, f32[4]{0:T(128)S(1)} %compare_select_fusion.1, s32[4]{0:T(128)S(1)} %and_select_fusion.2, pred[4]{0:T(512)(128)(4,1)S(1)} %fusion.95), kind=kOutput, calls=%fused_computation.8 | convolution fusion | flops 314573344 | bytes 50331684 | tf_op jit(solution)/shard_map/pt,oxypz->toxyz/dot_general | solution.py:23
  789.7 6.4 copy.130
  (13 shorter events, 0.1 us)
Async XLA Ops:
  7.2 294.2 %copy-start = (bf16[12,12]{1,0:T(8,128)(2,1)S(1)}, bf16[12,12]{1,0:T(8,128)(2,1)}, u32[]{:S(2)}) copy-start(bf16[12,12]{1,0:T(8,128)(2,1)} %param.7) | copy-start | bytes 868
  103.1 43.5 %all-to-all-start = ((bf16[4,2,98304]{2,1,0:T(2,128)(2,1)}), bf16[4,2,98304]{2,1,0:T(2,128)(2,1)S(1)}, u32[]{:S(2)}, u32[]{:S(2)}) async-start(bf16[4,2,98304]{2,1,0:T(2,128)(2,1)} %reshape.144), calls=%async_computation | async-start | bytes 3145728 | tf_op jit(solution)/shard_map/all_to_all | solution.py:52
  109.6 120.2 %reduce-scatter.3.cloned.1.call-start = ((), (), s32[]{:S(2)}) async-start(), calls=%async_computation.6 | async-start | bytes 3538944 | tf_op jit(solution)/shard_map/reduce_scatter | solution.py:55
  296.7 42.1 %all-to-all-start.1 = ((bf16[4,2,98304]{2,1,0:T(2,128)(2,1)}), bf16[4,2,98304]{2,1,0:T(2,128)(2,1)S(1)}, u32[]{:S(2)}, u32[]{:S(2)}) async-start(bf16[4,2,98304]{2,1,0:T(2,128)(2,1)} %reshape.146), calls=%async_computation.2 | async-start | bytes 3145728 | tf_op jit(solution)/shard_map/all_to_all | solution.py:67
  301.3 303.8 %reduce-scatter.5.cloned.1.call-start = ((), (), s32[]{:S(2)}) async-start(), calls=%async_computation.7 | async-start | bytes 3538944 | tf_op jit(solution)/shard_map/reduce_scatter | solution.py:55
  552.9 7.7 copy-start.1
  671.4 42.1 %all-to-all-start.3 = ((bf16[4,2,98304]{2,1,0:T(2,128)(2,1)}), bf16[4,2,98304]{2,1,0:T(2,128)(2,1)S(1)}, u32[]{:S(2)}, u32[]{:S(2)}) async-start(bf16[4,2,98304]{2,1,0:T(2,128)(2,1)} %reshape.150), calls=%async_computation.5 | async-start | bytes 3145728 | tf_op jit(solution)/shard_map/all_to_all | solution.py:67
Sparse Core Ops, SparseCore 0:
  184.4 45.3 reduce-scatter.2
  560.7 44.3 reduce-scatter.4
where the time goes:
time: 815 us; the launch traced here: 803 us
  local copies, waits for them, and re-layouts  276 us (34%)
  matrix products  248 us (30%)
  waiting for transfers between devices  149 us (18%)
  blocking collectives  77.1 us (9%)
  other arithmetic  22.8 us (3%)
  starting transfers between devices  15.9 us (2%)
  between operations  14.7 us (2%)
    dot_general x8, matrix products, exact_mix(): jnp.einsum(form, left.astype(jnp.float32), right.astype(jnp.float32), pre...  147 us
    reduce_scatter x2, waiting for transfers between devices, analyze(): lax.psum_scatter(exact_mix('jy,cyqpi->jcqpi', y_table, x_done).astype(jnp...  89.8 us
    unnamed x15, local copies, waits for them, and re-layouts  85 us
    dot_general x6, matrix products, narrow_mix(): return jnp.einsum(form, left, right, preferred_element_type=jnp.float32)  52.6 us
    all_to_all x4, local copies, waits for them, and re-layouts, analyze(): lax.all_to_all(head_modes, 'gx', split_axis=4, concat_axis=1, tiled=True)  50.7 us
    dot_general x2, matrix products, head(): jnp.dot(values, depth_table.T, preferred_element_type=jnp.float32)  39.3 us
    all_to_all x1, blocking collectives, analyze(): lax.all_to_all(head_modes, 'gx', split_axis=4, concat_axis=1, tiled=True)  39.1 us
    all_to_all x2, local copies, waits for them, and re-layouts, synthesize(): lax.all_to_all(x_done, 'gx', split_axis=1, concat_axis=4, tiled=True)  38.3 us
  transfers between devices with their start and end apart: 5, of which 5 were waited for; matrix products, arithmetic and copies ran while one was open for 7% of the time, Pallas kernels for 0%

commit v1 on v0

v1 whole, which is shorter than its diff:
```python
import functools
import math

import jax
import jax.numpy as jnp
import ml_dtypes
import numpy as np
from jax import lax
from jax.experimental import pallas as pl
from jax.experimental.pallas import tpu as pltpu
from jax.sharding import PartitionSpec as P

YZ = ("gy", "gz")
HALF_ROOT = 1.0 / math.sqrt(2.0)
DENSITY = 1.0 / math.sqrt(2.0 * math.pi)


def basis(row_count, extent):
    row = np.arange(row_count)[:, None]
    cell = np.arange(extent)[None, :]
    radians = ((row + 1) // 2 * cell % extent) * (2.0 * math.pi / extent)
    wave = np.where(row % 2 == 0, np.cos(radians), np.sin(radians))
    scale = np.where(row == 0, math.sqrt(1.0 / extent), math.sqrt(2.0 / extent))
    return (wave * scale).astype(ml_dtypes.bfloat16).astype(np.float32)


def narrow(table):
    return np.asarray(table, dtype=ml_dtypes.bfloat16)


def dot(left, right, left_dim=1, right_dim=0):
    return lax.dot_general(
        left, right, (((left_dim,), (right_dim,)), ((), ())), preferred_element_type=jnp.float32
    )


def gelu_slope(value):
    size = jnp.abs(value)
    bell = jnp.exp(value * value * -0.5)
    t = 1.0 / (1.0 + (0.3275911 * HALF_ROOT) * size)
    tail = t * (
        0.5 * 0.254829592
        + t * (0.5 * -0.284496736 + t * (0.5 * 1.421413741 + t * (0.5 * -1.453152027 + t * (0.5 * 1.061405429))))
    )
    low = bell * (tail - DENSITY * size)
    return jnp.where(value >= 0.0, 1.0 - low, low)


def call(body, grid, in_specs, out_specs, out_shape, flops, moved, args):
    return pl.pallas_call(
        body,
        grid=grid,
        in_specs=in_specs,
        out_specs=out_specs,
        out_shape=out_shape,
        compiler_params=pltpu.CompilerParams(vmem_limit_bytes=48 * 1024 * 1024),
        cost_estimate=pl.CostEstimate(flops=flops, bytes_accessed=moved, transcendentals=0),
    )(*args)


def whole(shape):
    return pl.BlockSpec(shape, lambda *_: (0,) * len(shape))


def wide(ref, cell, times):
    channels, _, y_local, depth = ref.shape[1:]
    return jnp.concatenate([ref[t, :, cell].reshape(channels * y_local, depth) for t in times], axis=1)


def head_body(field_ref, table_ref, head_ref):
    def one(cell, carry):
        values = wide(field_ref, cell, range(field_ref.shape[0]))
        head_ref[cell] = dot(values, table_ref[...]).astype(jnp.bfloat16)
        return carry

    lax.fori_loop(0, field_ref.shape[2], one, 0)


def inner_body(field_ref, cot_ref, mid_ref, mix_ref, syn_ref, table_ref, grad_ref, head_ref):
    steps, channels, cells, y_local, depth = field_ref.shape

    def one(cell, carry):
        middle = mid_ref[cell]
        total = jnp.zeros(middle.shape, jnp.float32)
        for t in range(0, steps, 2):
            lanes = slice(t * depth, (t + 2) * depth)
            preact = dot(middle, syn_ref[:, lanes]) + dot(mix_ref[...], wide(field_ref, cell, (t, t + 1)))
            cot = wide(cot_ref, cell, (t, t + 1)).astype(jnp.float32)
            grad = (cot * gelu_slope(preact)).astype(jnp.bfloat16)
            for k in range(2):
                grad_ref[t + k, :, cell] = grad[:, k * depth : (k + 1) * depth].reshape(channels, y_local, depth)
            total += dot(grad, table_ref[lanes, :])
        head_ref[cell] = total.astype(jnp.bfloat16)
        return carry

    lax.fori_loop(0, cells, one, 0)


def outer_body(grad_ref, mid_ref, mix_ref, syn_ref, out_ref):
    steps, channels, cells, y_local, depth = grad_ref.shape

    def one(cell, carry):
        middle = mid_ref[cell]
        for t in range(0, steps, 2):
            lanes = slice(t * depth, (t + 2) * depth)
            total = dot(middle, syn_ref[:, lanes]) + dot(mix_ref[...], wide(grad_ref, cell, (t, t + 1)))
            total = total.astype(jnp.bfloat16)
            for k in range(2):
                out_ref[t + k, :, cell] = total[:, k * depth : (k + 1) * depth].reshape(channels, y_local, depth)
        return carry

    lax.fori_loop(0, cells, one, 0)


def y_down_body(rows_ref, table_ref, out_ref):
    owners, cells, channels, y_local, lanes = rows_ref.shape
    for c in range(channels):
        stacked = jnp.concatenate([rows_ref[s, x, c] for x in range(cells) for s in range(owners)], axis=0)
        out_ref[:, c] = dot(table_ref[...], stacked).astype(jnp.bfloat16).reshape(owners, -1, lanes)


def x_down_body(rows_ref, table_ref, out_ref):
    owners, channels, group, lanes = rows_ref.shape
    for c in range(channels):
        stacked = jnp.concatenate([rows_ref[s, c] for s in range(owners)], axis=0)
        done = dot(stacked, table_ref[...], 0, 0).astype(jnp.bfloat16)
        out_ref[:, c] = done.reshape(out_ref.shape[0], -1, done.shape[1])


def x_up_body(modes_ref, table_ref, out_ref):
    planes, channels, group, lanes = modes_ref.shape
    for c in range(channels):
        stacked = jnp.concatenate([modes_ref[d, c] for d in range(planes)], axis=0)
        done = dot(table_ref[...], stacked, 1, 1).astype(jnp.bfloat16)
        out_ref[:, c] = done.reshape(out_ref.shape[0], -1, done.shape[1])


def y_up_body(rows_ref, table_ref, out_ref):
    owners, channels, group, lanes = rows_ref.shape
    cells, y_local = out_ref.shape[1], out_ref.shape[3]
    for c in range(channels):
        stacked = jnp.concatenate([rows_ref[s, c] for s in range(owners)], axis=0)
        done = dot(table_ref[...], stacked).astype(jnp.bfloat16)
        for x in range(cells):
            for d in range(owners):
                start = (x * owners + d) * y_local
                out_ref[d, x, c] = done[start : start + y_local]


def shards(x_devices, y_devices, state_field, cotangent, spectral_weight, point_weight):
    steps, channels, x_local, y_local, depth = state_field.shape
    j_local, q_local = spectral_weight.shape[:2]
    time_modes, modes = spectral_weight.shape[4:]
    lanes = time_modes * modes
    rows = channels * y_local
    x_extent, y_extent = x_local * x_devices, y_local * y_devices
    bf16 = jnp.bfloat16

    x_pieces = math.gcd(x_local, y_devices)
    c_pieces = y_devices // x_pieces
    x_piece, c_piece = x_local // x_pieces, channels // c_pieces
    group = x_piece * j_local

    time_table, depth_table = basis(time_modes, steps), basis(modes, depth)
    x_table, y_table = basis(modes, x_extent), basis(modes, y_extent)
    synth = np.einsum("pt,qz->qptz", time_table, depth_table).reshape(lanes, steps * depth)
    y_mat = np.einsum("xw,djy->dxjwy", np.eye(x_piece), y_table.reshape(y_devices, j_local, y_extent))
    y_mat = y_mat.reshape(y_devices * group, x_piece * y_extent)
    x_mat = np.einsum("jk,igx->gxjki", np.eye(j_local), x_table.reshape(modes, x_devices, x_local))
    x_mat = x_mat.reshape(x_devices, x_local * j_local, j_local * modes)
    syn, ana = jnp.asarray(narrow(synth)), jnp.asarray(narrow(synth.T))
    y_mat, y_mat_t = jnp.asarray(narrow(y_mat)), jnp.asarray(narrow(y_mat.T))
    x_mat = lax.dynamic_index_in_dim(jnp.asarray(narrow(x_mat)), lax.axis_index("gx"), 0, keepdims=False)
    eye = jnp.eye(y_local, dtype=bf16)
    mix_up, mix_back = jnp.kron(point_weight.T, eye), jnp.kron(point_weight, eye)

    step = math.gcd(x_local, 4)
    grid = (x_local // step,)
    field_spec = pl.BlockSpec((steps, channels, step, y_local, depth), lambda g: (0, 0, g, 0, 0))
    head_spec = pl.BlockSpec((step, rows, lanes), lambda g: (g, 0, 0))
    head_shape = jax.ShapeDtypeStruct((x_local, rows, lanes), bf16)
    field_shape = jax.ShapeDtypeStruct(state_field.shape, bf16)
    field_bytes, head_bytes = 2 * state_field.size, 2 * x_local * rows * lanes
    head_flops = 2 * x_local * rows * lanes * steps * depth
    mix_flops = 2 * state_field.size * rows

    def small(body, out, values, table):
        shape = jax.ShapeDtypeStruct(out, bf16)
        return call(
            body, (1,), [whole(values.shape), whole(table.shape)], whole(out), shape,
            2 * values.size * 512, 2 * (values.size + math.prod(out)), (values, table),
        )

    def analyze(heads):
        heads = heads.reshape(y_devices, -1, lanes)
        heads = lax.all_to_all(heads, YZ, 0, 0, tiled=True)
        heads = heads.reshape(y_devices, x_piece, c_piece, y_local, lanes)
        part = small(y_down_body, (y_devices, c_piece, group, lanes), heads, y_mat)
        part = lax.all_to_all(part, YZ, 0, 0, tiled=True)
        part = part.reshape(x_pieces, channels, group, lanes)
        part = small(x_down_body, (x_devices, channels, q_local * time_modes, j_local * modes), part, x_mat)
        part = lax.all_to_all(part, "gx", 0, 0, tiled=True)
        return jnp.sum(part.astype(jnp.float32), axis=0).astype(bf16)

    def synthesize(spec):
        spec = lax.all_gather(spec, "gx", axis=0)
        part = small(x_up_body, (x_pieces, channels, group, lanes), spec, x_mat)
        part = part.reshape(y_devices, c_piece, group, lanes)
        part = lax.all_to_all(part, YZ, 0, 0, tiled=True)
        part = small(y_up_body, (y_devices, x_piece, c_piece, y_local, lanes), part, y_mat_t)
        part = lax.all_to_all(part.reshape(y_devices, -1, lanes), YZ, 0, 0, tiled=True)
        return part.reshape(x_local, rows, lanes)

    weight = jnp.transpose(spectral_weight, (2, 3, 1, 4, 0, 5))
    weight = weight.reshape(channels, channels, q_local * time_modes, j_local * modes)

    heads = call(
        head_body, grid, [field_spec, whole(ana.shape)], head_spec, head_shape,
        head_flops, field_bytes + head_bytes, (state_field, ana),
    )
    modes_in = analyze(heads).astype(jnp.float32)
    modes_out = jnp.sum(modes_in[:, None] * weight.astype(jnp.float32), axis=0).astype(bf16)
    grad_pre, heads = call(
        inner_body, grid,
        [field_spec, field_spec, head_spec, whole(mix_up.shape), whole(syn.shape), whole(ana.shape)],
        [field_spec, head_spec], [field_shape, head_shape],
        2 * head_flops + mix_flops, 3 * field_bytes + 2 * head_bytes,
        (state_field, cotangent, synthesize(modes_out), mix_up, syn, ana),
    )
    grad_modes = analyze(heads).astype(jnp.float32)
    grad_spectral = (modes_in[:, None] * grad_modes[None]).reshape(
        channels, channels, q_local, time_modes, j_local, modes
    )
    grad_spectral = jnp.transpose(grad_spectral, (4, 2, 0, 1, 3, 5))
    back_modes = jnp.sum(grad_modes[None] * weight.astype(jnp.float32), axis=1).astype(bf16)
    grad_field = call(
        outer_body, grid, [field_spec, head_spec, whole(mix_back.shape), whole(syn.shape)],
        field_spec, field_shape, head_flops + mix_flops, 2 * field_bytes + head_bytes,
        (grad_pre, synthesize(back_modes), mix_back, syn),
    )
    return grad_field, grad_spectral


def solution(mesh):
    in_specs = (
        P("parts", None, "gx", YZ, None),
        P("parts", None, "gx", YZ, None),
        P(YZ, "gx", None, None, None, None),
        P(),
    )
    out_specs = (
        P("parts", None, "gx", YZ, None),
        P(("parts",) + YZ, "gx", None, None, None, None),
    )
    body = functools.partial(shards, mesh.shape["gx"], mesh.shape["gy"] * mesh.shape["gz"])
    return jax.shard_map(body, mesh=mesh, in_specs=in_specs, out_specs=out_specs, check_vma=False)
```

time: 815 us -> 304 us (0.37); the launches traced: 803 us -> 302 us
  local copies, waits for them, and re-layouts: 276 us -> 9.41 us
  matrix products: 248 us -> 0 us
  waiting for transfers between devices: 149 us -> 36.7 us
  Pallas kernels: 0 us -> 82.1 us
  blocking collectives: 77.1 us -> 142 us
  between operations: 14.7 us -> 0.84 us
    dot_general x18 -> x0, matrix products: 248 us -> none  [the longest x8 147 us: exact_mix(): jnp.einsum(form, left.astype(jnp.float32), right.astype(jnp.float32), pre...]
    reduce_scatter x2 -> x0, waiting for transfers between devices: 89.8 us -> none  [analyze(): lax.psum_scatter(exact_mix('jy,cyqpi->jcqpi', y_table, x_done).astype(jnp...]
    all_to_all x6 -> x0, local copies, waits for them, and re-layouts: 89 us -> none  [the longest x4 50.7 us: analyze(): lax.all_to_all(head_modes, 'gx', split_axis=4, concat_axis=1, tiled=True)]
    unnamed x15 -> x14, local copies, waits for them, and re-layouts: 85 us -> 0.98 us
    pallas_call x0 -> x11, Pallas kernels: none -> 82.1 us  [call(): pl.pallas_call(body, grid=grid, in_specs=in_specs, out_specs=out_specs, o...]
    all_to_all x1 -> x7, blocking collectives: 39.1 us -> 112 us  [the longest x2 49.3 us: analyze(): heads = lax.all_to_all(heads, YZ, 0, 0, tiled=True)]
    convert_element_type x6 -> x8, local copies, waits for them, and re-layouts: 73.9 us -> 2.6 us  [the longest x2 0.73 us: shards(): jnp.sum(modes_in[:, None] * weight.astype(jnp.float32), axis=0).astype(bf16)]
    dot_general x3 -> x0, local copies, waits for them, and re-layouts: 27.5 us -> none  [the longest x1 27.3 us: head(): jnp.dot(values, depth_table.T, preferred_element_type=jnp.float32)]
  transfers between devices with their start and end apart: 5 -> 3, of which waited for: 5 -> 3; matrix products, arithmetic and copies ran while one was open for 7% -> 4% of each run, Pallas kernels for 0% -> 0%
where the time goes in v1:
time: 304 us; the launch traced here: 302 us
  blocking collectives  142 us (47%)
  Pallas kernels  82.1 us (27%)
  waiting for transfers between devices  36.7 us (12%)
  other arithmetic  20.9 us (7%)
  starting transfers between devices  10.6 us (3%)
  local copies, waits for them, and re-layouts  9.41 us (3%)
    pallas_call x11, Pallas kernels, call(): pl.pallas_call(body, grid=grid, in_specs=in_specs, out_specs=out_specs, o...  82.1 us
    all_to_all x2, blocking collectives, analyze(): heads = lax.all_to_all(heads, YZ, 0, 0, tiled=True)  49.3 us
    all_gather x2, blocking collectives, synthesize(): spec = lax.all_gather(spec, 'gx', axis=0)  30.3 us
    all_to_all x2, waiting for transfers between devices, synthesize(): lax.all_to_all(part.reshape(y_devices, -1, lanes), YZ, 0, 0, tiled=True)  29.2 us
    all_to_all x2, blocking collectives, analyze(): part = lax.all_to_all(part, 'gx', 0, 0, tiled=True)  28.9 us
    all_to_all x2, blocking collectives, synthesize(): part = lax.all_to_all(part, YZ, 0, 0, tiled=True)  22.6 us
    all_to_all x1, blocking collectives, analyze(): part = lax.all_to_all(part, YZ, 0, 0, tiled=True)  10.7 us
    all_to_all x1, waiting for transfers between devices, analyze(): part = lax.all_to_all(part, YZ, 0, 0, tiled=True)  7.5 us
  transfers between devices with their start and end apart: 3, of which 3 were waited for; matrix products, arithmetic and copies ran while one was open for 4% of the time, Pallas kernels for 0%

profile of v1, /device:TPU:0, one launch (start us, length us, event | category | flops | bytes accessed | tf_op | source)
XLA Modules:
  0.0 302.5 jit_solution(4565238970577789969)
XLA Ops:
  0.6 0.0 copy-start.1
  0.6 0.9 copy-done.1
  1.6 0.0 copy-start.4
  1.6 11.2 %shard_map.104 = bf16[32,192,128]{2,1,0:T(8,128)(2,1)S(1)} custom-call(bf16[8,12,32,16,128]{4,3,2,1,0:T(8,128)(2,1)} %field_ref.3, bf16[1024,128]{1,0:T(8,128)(2,1)S(1)} %copy-done.1), custom_call_target="tpu_custom_call" | custom-call | flops 1610612736 | bytes 14155776 | tf_op jit(solution)/shard_map/pallas_call | solution.py:50
  12.8 25.9 %all_to_all.50 = bf16[8,768,128]{2,1,0:T(8,128)(2,1)S(1)} all-to-all(bf16[8,768,128]{2,1,0:T(8,128)(2,1)S(1)} %bitcast.21), channel_id=1, replica_groups=mesh['parts'=1,'gx'=4,'gy'=4,'gz'=2] {'gy','gz'}, dimensions={0} | all-to-all | bytes 3145728 | tf_op jit(solution)/shard_map/all_to_all | solution.py:196
  38.7 0.0 copy-start.3
  38.7 0.0 copy-done.4
  38.8 1.3 shard_map.105
  40.1 3.5 %all-to-all-start.1 = ((bf16[8,12,16,128]{3,2,1,0:T(8,128)(2,1)}), bf16[8,12,16,128]{3,2,1,0:T(8,128)(2,1)S(1)}, u32[]{:S(2)}, u32[]{:S(2)}) async-start(bf16[8,12,16,128]{3,2,1,0:T(8,128)(2,1)} %shard_map.105), calls=%async_computation.1 | async-start | bytes 786432 | tf_op jit(solution)/shard_map/all_to_all | solution.py:199
  43.5 0.8 dynamic-slice_bitcast_fusion.table_ref
  44.3 0.0 copy-start.6
  44.3 7.5 %all-to-all-done.1.rows_ref = bf16[8,12,16,128]{3,2,1,0:T(8,128)(2,1)S(1)} async-done(((bf16[8,12,16,128]{3,2,1,0:T(8,128)(2,1)}), bf16[8,12,16,128]{3,2,1,0:T(8,128)(2,1)S(1)}, u32[]{:S(2)}, u32[]{:S(2)}) %all-to-all-start.1) | async-done | bytes 393248 | tf_op jit(solution)/shard_map/all_to_all | solution.py:199
  51.8 0.3 shard_map.106
  52.1 14.7 %all_to_all.51 = bf16[4,12,32,128]{3,2,1,0:T(8,128)(2,1)S(1)} all-to-all(bf16[4,12,32,128]{3,2,1,0:T(8,128)(2,1)S(1)} %shard_map.106), channel_id=1, replica_groups=mesh['parts'=1,'gx'=4,'gy'=4,'gz'=2] {'gx'}, dimensions={0} | all-to-all | bytes 786432 | tf_op jit(solution)/shard_map/all_to_all | solution.py:202
  66.8 0.1 reduce_sum.42
  66.9 0.4 reshape.103
  67.2 0.0 copy-start
  67.2 0.0 copy-start.2
  67.3 0.2 copy.22
  67.5 6.7 %fusion = bf16[12,8,4,4,32]{4,2,0,1,3:T(4,128)(2,1)S(1)} fusion(bf16[4,8,12,12,4,32]{5,4,3,2,1,0:T(4,128)(2,1)} %param.11, f32[12,8,4,4,32]{4,2,0,1,3:T(4,128)S(1)} %copy.22), kind=kLoop, calls=%fused_computation.2 | loop fusion | flops 1720320 | bytes 1474560 | tf_op jit(solution)/shard_map/reduce_sum | solution.py:222
  74.2 0.5 copy.23
  74.7 0.2 convert_element_type.73
  74.9 15.1 %all_gather.8.modes_ref = bf16[4,12,32,128]{3,2,1,0:T(8,128)(2,1)S(1)} all-gather(bf16[1,12,32,128]{3,2,1,0:T(8,128)(2,1)S(1)} %convert_element_type.73), channel_id=1, replica_groups=mesh['parts'=1,'gx'=4,'gy'=4,'gz'=2] {'gx'}, dimensions={0}, use_global_device_ids=true | all-gather | bytes 491520 | tf_op jit(solution)/shard_map/all_gather | solution.py:206
  90.0 0.4 shard_map.107
  90.4 11.9 %all_to_all.52.rows_ref = bf16[8,12,16,128]{3,2,1,0:T(8,128)(2,1)S(1)} all-to-all(bf16[8,12,16,128]{3,2,1,0:T(8,128)(2,1)S(1)} %shard_map.107), channel_id=1, replica_groups=mesh['parts'=1,'gx'=4,'gy'=4,'gz'=2] {'gy','gz'}, dimensions={0} | all-to-all | bytes 786432 | tf_op jit(solution)/shard_map/all_to_all | solution.py:209
  102.3 0.0 copy-done.3
  102.3 1.7 shard_map.108
  104.0 3.6 %all-to-all-start.4 = ((bf16[8,768,128]{2,1,0:T(8,128)(2,1)}), bf16[8,768,128]{2,1,0:T(8,128)(2,1)S(1)}, u32[]{:S(2)}, u32[]{:S(2)}) async-start(bf16[8,768,128]{2,1,0:T(8,128)(2,1)} %bitcast.4), calls=%async_computation.4 | async-start | bytes 3145728 | tf_op jit(solution)/shard_map/all_to_all | solution.py:211
  107.6 0.0 copy-done.6
  107.6 0.1 copy.24
  107.7 1.3 broadcast_multiply_fusion.1
  109.0 1.7 mul.83.mix_ref
  110.7 17.8 %all-to-all-done.4 = bf16[8,768,128]{2,1,0:T(8,128)(2,1)S(1)} async-done(((bf16[8,768,128]{2,1,0:T(8,128)(2,1)}), bf16[8,768,128]{2,1,0:T(8,128)(2,1)S(1)}, u32[]{:S(2)}, u32[]{:S(2)}) %all-to-all-start.4) | async-done | bytes 1572896 | tf_op jit(solution)/shard_map/all_to_all | solution.py:211
  128.5 0.0 copy-done
  128.5 0.0 copy-done.2
  128.5 47.8 %shard_map.109 = (bf16[8,12,32,16,128]{4,3,2,1,0:T(8,128)(2,1)}, bf16[32,192,128]{2,1,0:T(8,128)(2,1)S(1)}) custom-call(bf16[8,12,32,16,128]{4,3,2,1,0:T(8,128)(2,1)} %field_ref.3, bf16[8,12,32,16,128]{4,3,2,1,0:T(8,128)(2,1)} %cot_ref.1, bf16[32,192,128]{2,1,0:T(8,128)(2,1)S(1)} %bitcast.22, bf16[192,192]{1,0:T(8,128)(2,1)S(1)} %mul.83.mix_ref, ...), custom_call_target="tpu_custom_call" | custom-call | flops 5637144576 | bytes 40894464 | tf_op jit(solution)/shard_map/pallas_call | solution.py:50
  176.3 23.4 %all_to_all.53 = bf16[8,768,128]{2,1,0:T(8,128)(2,1)S(1)} all-to-all(bf16[8,768,128]{2,1,0:T(8,128)(2,1)S(1)} %bitcast.23), channel_id=1, replica_groups=mesh['parts'=1,'gx'=4,'gy'=4,'gz'=2] {'gy','gz'}, dimensions={0} | all-to-all | bytes 3145728 | tf_op jit(solution)/shard_map/all_to_all | solution.py:196
  199.8 0.6 shard_map.110
  200.3 10.7 %all_to_all.54.rows_ref = bf16[8,12,16,128]{3,2,1,0:T(8,128)(2,1)S(1)} all-to-all(bf16[8,12,16,128]{3,2,1,0:T(8,128)(2,1)S(1)} %shard_map.110), channel_id=1, replica_groups=mesh['parts'=1,'gx'=4,'gy'=4,'gz'=2] {'gy','gz'}, dimensions={0} | all-to-all | bytes 786432 | tf_op jit(solution)/shard_map/all_to_all | solution.py:199
  211.0 0.3 shard_map.111
  211.4 14.2 %all_to_all.55 = bf16[4,12,32,128]{3,2,1,0:T(8,128)(2,1)S(1)} all-to-all(bf16[4,12,32,128]{3,2,1,0:T(8,128)(2,1)S(1)} %shard_map.111), channel_id=1, replica_groups=mesh['parts'=1,'gx'=4,'gy'=4,'gz'=2] {'gx'}, dimensions={0} | all-to-all | bytes 786432 | tf_op jit(solution)/shard_map/all_to_all | solution.py:202
  225.5 0.1 reduce_sum.44
  225.6 0.4 reshape.104
  225.9 0.0 copy-start.5
  226.0 0.2 copy.25
  226.2 6.6 %fusion.1 = bf16[12,8,4,4,32]{4,2,0,1,3:T(4,128)(2,1)S(1)} fusion(bf16[4,8,12,12,4,32]{5,4,3,2,1,0:T(4,128)(2,1)} %param.11, f32[12,8,4,4,32]{4,2,0,1,3:T(4,128)S(1)} %copy.25), kind=kLoop, calls=%fused_computation.3 | loop fusion | flops 1720320 | bytes 1474560 | tf_op jit(solution)/shard_map/reduce_sum | solution.py:235
  232.7 0.5 copy.26
  233.2 0.2 convert_element_type.78
  233.5 15.2 %all_gather.9.modes_ref = bf16[4,12,32,128]{3,2,1,0:T(8,128)(2,1)S(1)} all-gather(bf16[1,12,32,128]{3,2,1,0:T(8,128)(2,1)S(1)} %convert_element_type.78), channel_id=1, replica_groups=mesh['parts'=1,'gx'=4,'gy'=4,'gz'=2] {'gx'}, dimensions={0}, use_global_device_ids=true | all-gather | bytes 491520 | tf_op jit(solution)/shard_map/all_gather | solution.py:206
  248.7 0.4 shard_map.112
  249.1 10.7 %all_to_all.56.rows_ref = bf16[8,12,16,128]{3,2,1,0:T(8,128)(2,1)S(1)} all-to-all(bf16[8,12,16,128]{3,2,1,0:T(8,128)(2,1)S(1)} %shard_map.112), channel_id=1, replica_groups=mesh['parts'=1,'gx'=4,'gy'=4,'gz'=2] {'gy','gz'}, dimensions={0} | all-to-all | bytes 786432 | tf_op jit(solution)/shard_map/all_to_all | solution.py:209
  259.8 1.7 shard_map.113
  261.5 0.0 copy-done.5
  261.5 3.6 %all-to-all-start.9 = ((bf16[8,768,128]{2,1,0:T(8,128)(2,1)}), bf16[8,768,128]{2,1,0:T(8,128)(2,1)S(1)}, u32[]{:S(2)}, u32[]{:S(2)}) async-start(bf16[8,768,128]{2,1,0:T(8,128)(2,1)} %bitcast.9), calls=%async_computation.9 | async-start | bytes 3145728 | tf_op jit(solution)/shard_map/all_to_all | solution.py:211
  265.1 1.7 mul.88.mix_ref
  266.8 0.2 copy.27
  267.0 1.3 copy.28
  268.4 6.2 %broadcast_multiply_fusion = f32[4,8,12,12,4,32]{5,4,3,2,1,0:T(4,128)} fusion(f32[4,8,12,4,32]{4,3,2,1,0:T(4,128)S(1)} %copy.28, f32[4,8,12,4,32]{4,3,2,1,0:T(4,128)S(1)} %copy.27), kind=kLoop, calls=%fused_computation.4 | loop fusion | flops 589824 | bytes 2752512 | tf_op jit(solution)/shard_map/mul | solution.py:231
  274.6 11.4 %all-to-all-done.9 = bf16[8,768,128]{2,1,0:T(8,128)(2,1)S(1)} async-done(((bf16[8,768,128]{2,1,0:T(8,128)(2,1)}), bf16[8,768,128]{2,1,0:T(8,128)(2,1)S(1)}, u32[]{:S(2)}, u32[]{:S(2)}) %all-to-all-start.9) | async-done | bytes 1572896 | tf_op jit(solution)/shard_map/all_to_all | solution.py:211
  286.0 16.4 %shard_map.114 = bf16[8,12,32,16,128]{4,3,2,1,0:T(8,128)(2,1)} custom-call(bf16[8,12,32,16,128]{4,3,2,1,0:T(8,128)(2,1)} %get-tuple-element.4.grad_ref, bf16[32,192,128]{2,1,0:T(8,128)(2,1)S(1)} %bitcast.20, bf16[192,192]{1,0:T(8,128)(2,1)S(1)} %mul.88.mix_ref, bf16[128,1024]{1,0:T(8,128)(2,1)S(1)} %copy-done), custom_call_target="tpu_custom_call" | custom-call | flops 4026531840 | bytes 26738688 | tf_op jit(solution)/shard_map/pallas_call | solution.py:50
  (1 shorter events, 0.0 us)
Async XLA Ops:
  0.6 1.0 copy-start.1
  1.6 37.2 %copy-start.4 = (bf16[128,512]{1,0:T(8,128)(2,1)S(1)}, bf16[128,512]{1,0:T(8,128)(2,1)}, u32[]{:S(2)}) copy-start(bf16[128,512]{1,0:T(8,128)(2,1)} %constant.28.clone.table_ref) | copy-start | bytes 393220
  38.7 63.5 %copy-start.3 = (bf16[512,128]{1,0:T(8,128)(2,1)S(1)}, bf16[512,128]{1,0:T(8,128)(2,1)}, u32[]{:S(2)}) copy-start(bf16[512,128]{1,0:T(8,128)(2,1)} %constant.29.clone.table_ref) | copy-start | bytes 393220
  40.1 11.7 %all-to-all-start.1 = ((bf16[8,12,16,128]{3,2,1,0:T(8,128)(2,1)}), bf16[8,12,16,128]{3,2,1,0:T(8,128)(2,1)S(1)}, u32[]{:S(2)}, u32[]{:S(2)}) async-start(bf16[8,12,16,128]{3,2,1,0:T(8,128)(2,1)} %shard_map.105), calls=%async_computation.1 | async-start | bytes 786432 | tf_op jit(solution)/shard_map/all_to_all | solution.py:199
  44.3 63.3 %copy-start.6 = (bf16[12,12]{1,0:T(8,128)(2,1)S(1)}, bf16[12,12]{1,0:T(8,128)(2,1)}, u32[]{:S(2)}) copy-start(bf16[12,12]{1,0:T(8,128)(2,1)} %param.12) | copy-start | bytes 868
  67.2 61.3 %copy-start = (bf16[128,1024]{1,0:T(8,128)(2,1)S(1)}, bf16[128,1024]{1,0:T(8,128)(2,1)}, u32[]{:S(2)}) copy-start(bf16[128,1024]{1,0:T(8,128)(2,1)} %constant.26.clone.syn_ref) | copy-start | bytes 786436
  67.2 61.3 %copy-start.2 = (bf16[1024,128]{1,0:T(8,128)(2,1)S(1)}, bf16[1024,128]{1,0:T(8,128)(2,1)}, u32[]{:S(2)}) copy-start(bf16[1024,128]{1,0:T(8,128)(2,1)} %constant.27.clone.table_ref) | copy-start | bytes 786436
  104.0 24.5 %all-to-all-start.4 = ((bf16[8,768,128]{2,1,0:T(8,128)(2,1)}), bf16[8,768,128]{2,1,0:T(8,128)(2,1)S(1)}, u32[]{:S(2)}, u32[]{:S(2)}) async-start(bf16[8,768,128]{2,1,0:T(8,128)(2,1)} %bitcast.4), calls=%async_computation.4 | async-start | bytes 3145728 | tf_op jit(solution)/shard_map/all_to_all | solution.py:211
  225.9 35.6 %copy-start.5 = (f32[12,8,4,4,32]{4,3,2,1,0:T(4,128)}, f32[12,8,4,4,32]{4,3,2,1,0:T(4,128)S(1)}, u32[]{:S(2)}) copy-start(f32[12,8,4,4,32]{4,3,2,1,0:T(4,128)S(1)} %reshape.104) | copy-start | bytes 589828
  261.5 24.5 %all-to-all-start.9 = ((bf16[8,768,128]{2,1,0:T(8,128)(2,1)}), bf16[8,768,128]{2,1,0:T(8,128)(2,1)S(1)}, u32[]{:S(2)}, u32[]{:S(2)}) async-start(bf16[8,768,128]{2,1,0:T(8,128)(2,1)} %bitcast.9), calls=%async_computation.9 | async-start | bytes 3145728 | tf_op jit(solution)/shard_map/all_to_all | solution.py:211

commit v2 on v1

v2 whole, which is shorter than its diff:
```python
import functools
import math

import jax
import jax.numpy as jnp
import ml_dtypes
import numpy as np
from jax import lax
from jax.experimental import pallas as pl
from jax.experimental.pallas import tpu as pltpu
from jax.sharding import PartitionSpec as P

YZ = ("gy", "gz")
HALF_ROOT = 1.0 / math.sqrt(2.0)
DENSITY = 1.0 / math.sqrt(2.0 * math.pi)


def basis(row_count, extent):
    row = np.arange(row_count)[:, None]
    cell = np.arange(extent)[None, :]
    radians = ((row + 1) // 2 * cell % extent) * (2.0 * math.pi / extent)
    wave = np.where(row % 2 == 0, np.cos(radians), np.sin(radians))
    scale = np.where(row == 0, math.sqrt(1.0 / extent), math.sqrt(2.0 / extent))
    return (wave * scale).astype(ml_dtypes.bfloat16).astype(np.float32)


def narrow(table):
    return np.asarray(table, dtype=ml_dtypes.bfloat16)


def dot(left, right, left_dim=1, right_dim=0):
    return lax.dot_general(
        left, right, (((left_dim,), (right_dim,)), ((), ())), preferred_element_type=jnp.float32
    )


def gelu_slope(value):
    size = jnp.abs(value)
    bell = jnp.exp2(value * value * (-0.5 * math.log2(math.e)))
    span = 1.0 + (0.3275911 * HALF_ROOT) * size
    t = pl.reciprocal(span, approx=True)
    t = t * (2.0 - span * t)
    tail = t * (
        0.5 * 0.254829592
        + t * (0.5 * -0.284496736 + t * (0.5 * 1.421413741 + t * (0.5 * -1.453152027 + t * (0.5 * 1.061405429))))
    )
    low = bell * (tail - DENSITY * size)
    return jnp.where(value >= 0.0, 1.0 - low, low)


def call(body, grid, in_specs, out_specs, out_shape, flops, moved, args):
    return pl.pallas_call(
        body,
        grid=grid,
        in_specs=in_specs,
        out_specs=out_specs,
        out_shape=out_shape,
        compiler_params=pltpu.CompilerParams(vmem_limit_bytes=48 * 1024 * 1024),
        cost_estimate=pl.CostEstimate(flops=flops, bytes_accessed=moved, transcendentals=0),
    )(*args)


def whole(shape):
    return pl.BlockSpec(shape, lambda *_: (0,) * len(shape))


def wide(ref, cell, times):
    channels, _, y_local, depth = ref.shape[1:]
    return jnp.concatenate([ref[t, :, cell].reshape(channels * y_local, depth) for t in times], axis=1)


def head_body(field_ref, table_ref, head_ref):
    steps, _, cells, _, depth = field_ref.shape
    for cell in range(cells):
        total = 0.0
        for t in range(0, steps, 2):
            total += dot(wide(field_ref, cell, (t, t + 1)), table_ref[t * depth : (t + 2) * depth, :])
        head_ref[cell] = total.astype(jnp.bfloat16)


def inner_body(field_ref, cot_ref, mid_ref, mix_ref, syn_ref, table_ref, grad_ref, head_ref):
    steps, channels, cells, y_local, depth = field_ref.shape
    rows = channels * y_local
    band = math.gcd(rows, 32)
    for cell in range(cells):
        middle = mid_ref[cell]
        total = 0.0
        for t in range(0, steps, 2):
            lanes = slice(t * depth, (t + 2) * depth)
            preact = dot(middle, syn_ref[:, lanes]) + dot(mix_ref[...], wide(field_ref, cell, (t, t + 1)))
            cot = wide(cot_ref, cell, (t, t + 1))
            bands = []
            for r in range(0, rows, band):
                slope = gelu_slope(preact[r : r + band])
                bands.append((cot[r : r + band].astype(jnp.float32) * slope).astype(jnp.bfloat16))
            grad = jnp.concatenate(bands, axis=0)
            for k in range(2):
                grad_ref[t + k, :, cell] = grad[:, k * depth : (k + 1) * depth].reshape(channels, y_local, depth)
            total += dot(grad, table_ref[lanes, :])
        head_ref[cell] = total.astype(jnp.bfloat16)


def outer_body(grad_ref, mid_ref, mix_ref, syn_ref, out_ref):
    steps, channels, cells, y_local, depth = grad_ref.shape
    for cell in range(cells):
        middle = mid_ref[cell]
        for t in range(0, steps, 2):
            lanes = slice(t * depth, (t + 2) * depth)
            total = dot(middle, syn_ref[:, lanes]) + dot(mix_ref[...], wide(grad_ref, cell, (t, t + 1)))
            total = total.astype(jnp.bfloat16)
            for k in range(2):
                out_ref[t + k, :, cell] = total[:, k * depth : (k + 1) * depth].reshape(channels, y_local, depth)


def y_down_body(rows_ref, table_ref, out_ref):
    owners, cells = rows_ref.shape[:2]
    planes, _, groups, height, width = out_ref.shape
    members = rows_ref.shape[2] // groups
    span = width // members
    for k in range(groups):
        done = []
        for c in range(k * members, (k + 1) * members):
            stacked = jnp.concatenate([rows_ref[s, x, c] for x in range(cells) for s in range(owners)], axis=0)
            done.append(dot(table_ref[...], stacked).astype(jnp.bfloat16))
        for g in range(planes):
            piece = jnp.concatenate([part[:, g * span : (g + 1) * span] for part in done], axis=1)
            out_ref[g, :, k] = piece.reshape(owners, height, width)


def y_up_body(rows_ref, table_ref, out_ref):
    planes, owners, groups, _, width = rows_ref.shape
    _, cells, channels, y_local, _ = out_ref.shape
    members = channels // groups
    span = width // members
    for c in range(channels):
        lanes = slice(c % members * span, (c % members + 1) * span)
        stacked = jnp.concatenate(
            [
                jnp.concatenate([rows_ref[g, s, c // members][:, lanes] for g in range(planes)], axis=1)
                for s in range(owners)
            ],
            axis=0,
        )
        done = dot(table_ref[...], stacked).astype(jnp.bfloat16)
        for x in range(cells):
            for d in range(owners):
                start = (x * owners + d) * y_local
                out_ref[d, x, c] = done[start : start + y_local]


def spectral_body(back, rows_ref, table_ref, weight_ref, modes_ref, out_ref):
    planes, x_pieces, c_pieces, groups, height, width = rows_ref.shape
    channels, span, lanes = modes_ref.shape
    members = width // span
    for h in range(c_pieces):
        for k in range(groups):
            stacked = jnp.concatenate(
                [rows_ref[g, x, h, k] for g in range(planes) for x in range(x_pieces)], axis=0
            )
            first = (h * groups + k) * members
            done = dot(stacked, table_ref[...], 0, 0).astype(jnp.bfloat16)
            modes_ref[first : first + members] = done.reshape(members, span, lanes)
    for h in range(c_pieces):
        for k in range(groups):
            mixed = []
            for m in range(members):
                to = (h * groups + k) * members + m
                total = 0.0
                for of in range(channels):
                    weight = weight_ref[to, of] if back else weight_ref[of, to]
                    total += weight.astype(jnp.float32) * modes_ref[of].astype(jnp.float32)
                mixed.append(total.astype(jnp.bfloat16))
            done = dot(table_ref[...], jnp.concatenate(mixed, axis=0), 1, 1).astype(jnp.bfloat16)
            for g in range(planes):
                for x in range(x_pieces):
                    start = (g * x_pieces + x) * height
                    out_ref[g, x, h, k] = done[start : start + height]


def shards(x_devices, y_devices, state_field, cotangent, spectral_weight, point_weight):
    steps, channels, x_local, y_local, depth = state_field.shape
    j_local, q_local = spectral_weight.shape[:2]
    time_modes, modes = spectral_weight.shape[4:]
    lanes = time_modes * modes
    rows = channels * y_local
    x_extent, y_extent = x_local * x_devices, y_local * y_devices
    bf16 = jnp.bfloat16

    x_pieces = math.gcd(x_local, y_devices)
    c_pieces = y_devices // x_pieces
    x_piece, c_piece = x_local // x_pieces, channels // c_pieces
    group = x_piece * j_local

    time_table, depth_table = basis(time_modes, steps), basis(modes, depth)
    x_table, y_table = basis(modes, x_extent), basis(modes, y_extent)
    synth = np.einsum("pt,qz->qptz", time_table, depth_table).reshape(lanes, steps * depth)
    y_mat = np.einsum("xw,djy->dxjwy", np.eye(x_piece), y_table.reshape(y_devices, j_local, y_extent))
    y_mat = y_mat.reshape(y_devices * group, x_piece * y_extent)
    x_mat = np.einsum("jk,ix->xjki", np.eye(j_local), x_table).reshape(x_extent * j_local, j_local * modes)
    syn, ana, x_mat = jnp.asarray(narrow(synth)), jnp.asarray(narrow(synth.T)), jnp.asarray(narrow(x_mat))
    y_mat, y_mat_t = jnp.asarray(narrow(y_mat)), jnp.asarray(narrow(y_mat.T))
    eye = jnp.eye(y_local, dtype=bf16)
    mix_up, mix_back = jnp.kron(point_weight.T, eye), jnp.kron(point_weight, eye)

    step = math.gcd(x_local, 4)
    grid = (x_local // step,)
    field_spec = pl.BlockSpec((steps, channels, step, y_local, depth), lambda g: (0, 0, g, 0, 0))
    head_spec = pl.BlockSpec((step, rows, lanes), lambda g: (g, 0, 0))
    head_shape = jax.ShapeDtypeStruct((x_local, rows, lanes), bf16)
    field_shape = jax.ShapeDtypeStruct(state_field.shape, bf16)
    field_bytes, head_bytes = 2 * state_field.size, 2 * x_local * rows * lanes
    head_flops = 2 * x_local * rows * lanes * steps * depth
    mix_flops = 2 * state_field.size * rows

    def small(body, outs, values, *tables):
        shapes = [jax.ShapeDtypeStruct(out, bf16) for out in outs]
        return call(
            body, (1,), [whole(arg.shape) for arg in (values, *tables)], [whole(out) for out in outs], shapes,
            2 * values.size * 512, 4 * values.size, (values, *tables),
        )

    span = q_local * time_modes
    members = max(m for m in range(1, c_piece + 1) if c_piece % m == 0 and (m == 1 or m * span <= 128))
    packed = (x_devices, y_devices, c_piece // members, group, members * span)

    def exchange(pieces):
        shape = pieces.shape
        pieces = pieces.reshape((x_devices * y_devices,) + packed[2:])
        return lax.all_to_all(pieces, ("gx",) + YZ, 0, 0, tiled=True).reshape(shape)

    def spectral(back, heads, weight):
        heads = lax.all_to_all(heads.reshape(y_devices, -1, lanes), YZ, 0, 0, tiled=True)
        heads = heads.reshape(y_devices, x_piece, c_piece, y_local, lanes)
        (part,) = small(y_down_body, [packed], heads, y_mat)
        part = exchange(part).reshape((x_devices, x_pieces, c_pieces) + packed[2:])
        kept, part = small(
            functools.partial(spectral_body, back), [(channels, span, j_local * modes), part.shape], part, x_mat, weight
        )
        part = exchange(part).reshape(packed)
        (part,) = small(y_up_body, [(y_devices, x_piece, c_piece, y_local, lanes)], part, y_mat_t)
        part = lax.all_to_all(part.reshape(y_devices, -1, lanes), YZ, 0, 0, tiled=True)
        return part.reshape(x_local, rows, lanes), kept.astype(jnp.float32)

    weight = jnp.transpose(spectral_weight, (2, 3, 1, 4, 0, 5)).reshape(channels, channels, span, j_local * modes)

    heads = call(
        head_body, grid, [field_spec, whole(ana.shape)], head_spec, head_shape,
        head_flops, field_bytes + head_bytes, (state_field, ana),
    )
    middle, modes_in = spectral(False, heads, weight)
    grad_pre, heads = call(
        inner_body, grid,
        [field_spec, field_spec, head_spec, whole(mix_up.shape), whole(syn.shape), whole(ana.shape)],
        [field_spec, head_spec], [field_shape, head_shape],
        2 * head_flops + mix_flops, 3 * field_bytes + 2 * head_bytes,
        (state_field, cotangent, middle, mix_up, syn, ana),
    )
    middle, grad_modes = spectral(True, heads, weight)
    grad_spectral = (modes_in[:, None] * grad_modes[None]).reshape(
        channels, channels, q_local, time_modes, j_local, modes
    )
    grad_spectral = jnp.transpose(grad_spectral, (4, 2, 0, 1, 3, 5))
    grad_field = call(
        outer_body, grid, [field_spec, head_spec, whole(mix_back.shape), whole(syn.shape)],
        field_spec, field_shape, head_flops + mix_flops, 2 * field_bytes + head_bytes,
        (grad_pre, middle, mix_back, syn),
    )
    return grad_field, grad_spectral


def solution(mesh):
    in_specs = (
        P("parts", None, "gx", YZ, None),
        P("parts", None, "gx", YZ, None),
        P(YZ, "gx", None, None, None, None),
        P(),
    )
    out_specs = (
        P("parts", None, "gx", YZ, None),
        P(("parts",) + YZ, "gx", None, None, None, None),
    )
    body = functools.partial(shards, mesh.shape["gx"], mesh.shape["gy"] * mesh.shape["gz"])
    return jax.shard_map(body, mesh=mesh, in_specs=in_specs, out_specs=out_specs, check_vma=False)
```

time: 304 us -> 240 us (0.79)
  blocking collectives: 142 us -> 98.7 us
  local copies, waits for them, and re-layouts: 9.41 us -> 24.4 us
  Pallas kernels: 82.1 us -> 68.3 us
  other arithmetic: 20.9 us -> 8.81 us
  waiting for transfers between devices: 36.7 us -> 26.6 us
    all_gather x2 -> x0, blocking collectives: 30.3 us -> none  [synthesize(): spec = lax.all_gather(spec, 'gx', axis=0)]
    pallas_call x11 -> x9, Pallas kernels: 82.1 us -> 68.3 us  [call(): pl.pallas_call(body, grid=grid, in_specs=in_specs, out_specs=out_specs, o...]
    reduce_sum x4 -> x0, other arithmetic: 13.4 us -> none  [the longest x1 6.69 us: shards(): jnp.sum(modes_in[:, None] * weight.astype(jnp.float32), axis=0).astype(bf16)]
    all_to_all x7 -> x5, blocking collectives: 112 us -> 98.7 us  [the longest x3 49.4 us: exchange(): return lax.all_to_all(pieces, ('gx',) + YZ, 0, 0, tiled=True).reshape(shape)]
    transpose x0 -> x1, local copies, waits for them, and re-layouts: none -> 10.6 us  [shards(): jnp.transpose(spectral_weight, (2, 3, 1, 4, 0, 5))]
    all_to_all x3, waiting for transfers between devices: 36.7 us -> 26.6 us  [the longest x2 26.6 us: spectral(): lax.all_to_all(part.reshape(y_devices, -1, lanes), YZ, 0, 0, tiled=True)]
    reshape x0 -> x1, local copies, waits for them, and re-layouts: none -> 5.66 us  [shards(): jnp.transpose(spectral_weight, (2, 3, 1, 4, 0, 5))]
  transfers between devices with their start and end apart: 3 -> 3, of which waited for: 3 -> 2; matrix products, arithmetic and copies ran while one was open for 4% -> 13% of each run, Pallas kernels for 0% -> 0%
where the time goes in v2:
time: 240 us; the launch traced here: 239 us
  blocking collectives  98.7 us (41%)
  Pallas kernels  68.3 us (28%)
  waiting for transfers between devices  26.6 us (11%)
  local copies, waits for them, and re-layouts  24.4 us (10%)
  starting transfers between devices  11.3 us (5%)
  other arithmetic  8.81 us (4%)
    pallas_call x9, Pallas kernels, call(): pl.pallas_call(body, grid=grid, in_specs=in_specs, out_specs=out_specs, o...  68.3 us
    all_to_all x3, blocking collectives, exchange(): return lax.all_to_all(pieces, ('gx',) + YZ, 0, 0, tiled=True).reshape(shape)  49.4 us
    all_to_all x2, blocking collectives, spectral(): lax.all_to_all(heads.reshape(y_devices, -1, lanes), YZ, 0, 0, tiled=True)  49.3 us
    all_to_all x2, waiting for transfers between devices, spectral(): lax.all_to_all(part.reshape(y_devices, -1, lanes), YZ, 0, 0, tiled=True)  26.6 us
    transpose x1, local copies, waits for them, and re-layouts, shards(): jnp.transpose(spectral_weight, (2, 3, 1, 4, 0, 5))  10.6 us
    mul x1, other arithmetic, shards(): modes_in[:, None] * grad_modes[None]  7.48 us
    all_to_all x2, starting transfers between devices, spectral(): lax.all_to_all(part.reshape(y_devices, -1, lanes), YZ, 0, 0, tiled=True)  7.34 us
    reshape x1, local copies, waits for them, and re-layouts, shards(): jnp.transpose(spectral_weight, (2, 3, 1, 4, 0, 5))  5.66 us
  transfers between devices with their start and end apart: 3, of which 2 were waited for; matrix products, arithmetic and copies ran while one was open for 13% of the time, Pallas kernels for 0%

profile of v2, /device:TPU:0, one launch (start us, length us, event | category | flops | bytes accessed | tf_op | source)
XLA Modules:
  0.0 239.0 jit_solution(10741217999456968913)
XLA Ops:
  0.6 0.0 copy-start.1
  0.6 0.9 copy-done.1
  1.6 0.0 copy-start.8
  1.6 8.9 %shard_map.104 = bf16[32,192,128]{2,1,0:T(8,128)(2,1)S(1)} custom-call(bf16[8,12,32,16,128]{4,3,2,1,0:T(8,128)(2,1)} %field_ref.3, bf16[1024,128]{1,0:T(8,128)(2,1)S(1)} %copy-done.1), custom_call_target="tpu_custom_call" | custom-call | flops 1610612736 | bytes 14155776 | tf_op jit(solution)/shard_map/pallas_call | solution.py:52
  10.5 25.9 %all_to_all.40 = bf16[8,768,128]{2,1,0:T(8,128)(2,1)S(1)} all-to-all(bf16[8,768,128]{2,1,0:T(8,128)(2,1)S(1)} %bitcast.21), channel_id=1, replica_groups=mesh['parts'=1,'gx'=4,'gy'=4,'gz'=2] {'gy','gz'}, dimensions={0} | all-to-all | bytes 3145728 | tf_op jit(solution)/shard_map/all_to_all | solution.py:232
  36.5 0.0 copy-done.8
  36.5 1.4 shard_map.105
  37.9 4.0 %all-to-all-start.1 = ((bf16[32,3,16,128]{3,2,1,0:T(8,128)(2,1)}), bf16[32,3,16,128]{3,2,1,0:T(8,128)(2,1)S(1)}, u32[]{:S(2)}, u32[]{:S(2)}) async-start(bf16[32,3,16,128]{3,2,1,0:T(8,128)(2,1)} %bitcast.2), calls=%async_computation.1 | async-start | bytes 786432 | tf_op jit(solution)/shard_map/all_to_all | solution.py:229
  41.8 10.6 %copy.15 = bf16[12,12,8,4,4,32]{5,4,3,2,1,0:T(4,128)(2,1)} copy(bf16[12,12,8,4,4,32]{5,3,1,0,2,4:T(4,128)(2,1)} %bitcast.33) | data formatting | bytes 2359296 | tf_op jit(solution)/shard_map/transpose | solution.py:244
  52.4 0.0 copy-start.4
  52.4 0.0 copy-start.3
  52.4 5.7 %reshape.74.weight_ref = bf16[12,12,32,128]{3,2,1,0:T(8,128)(2,1)S(1)} reshape(bf16[12,12,8,4,4,32]{5,4,3,2,1,0:T(4,128)(2,1)} %copy.15) | data formatting | bytes 2359296 | tf_op jit(solution)/shard_map/reshape | solution.py:244
  58.1 0.0 copy-start.10
  58.1 0.0 all-to-all-done.1
  58.1 0.0 copy-done.4
  58.1 0.0 copy-start
  58.2 0.0 copy-start.2
  58.2 0.6 shard_map.106
  58.8 0.0 copy-start.6
  58.8 18.8 %all_to_all.41 = bf16[32,3,16,128]{3,2,1,0:T(8,128)(2,1)S(1)} all-to-all(bf16[32,3,16,128]{3,2,1,0:T(8,128)(2,1)S(1)} %bitcast.31), channel_id=1, replica_groups=mesh['parts'=1,'gx'=4,'gy'=4,'gz'=2] {'gx','gy','gz'}, dimensions={0} | all-to-all | bytes 786432 | tf_op jit(solution)/shard_map/all_to_all | solution.py:229
  77.6 0.0 copy-done.3
  77.6 1.8 shard_map.107
  79.4 0.0 copy-done.6
  79.4 3.8 %all-to-all-start.3 = ((bf16[8,768,128]{2,1,0:T(8,128)(2,1)}), bf16[8,768,128]{2,1,0:T(8,128)(2,1)S(1)}, u32[]{:S(2)}, u32[]{:S(2)}) async-start(bf16[8,768,128]{2,1,0:T(8,128)(2,1)} %bitcast.7), calls=%async_computation.3 | async-start | bytes 3145728 | tf_op jit(solution)/shard_map/all_to_all | solution.py:241
  83.2 0.0 copy-done.10
  83.2 0.1 copy.16
  83.3 1.3 broadcast_multiply_fusion.1
  84.6 2.4 mul.71.mix_ref
  87.0 17.0 %all-to-all-done.3 = bf16[8,768,128]{2,1,0:T(8,128)(2,1)S(1)} async-done(((bf16[8,768,128]{2,1,0:T(8,128)(2,1)}), bf16[8,768,128]{2,1,0:T(8,128)(2,1)S(1)}, u32[]{:S(2)}, u32[]{:S(2)}) %all-to-all-start.3) | async-done | bytes 1572896 | tf_op jit(solution)/shard_map/all_to_all | solution.py:241
  104.0 0.0 copy-done
  104.0 0.0 copy-done.2
  104.0 0.0 copy-start.5
  104.0 0.9 copy-done.5
  104.9 0.0 copy-start.9
  104.9 38.6 %shard_map.108 = (bf16[8,12,32,16,128]{4,3,2,1,0:T(8,128)(2,1)}, bf16[32,192,128]{2,1,0:T(8,128)(2,1)S(1)}) custom-call(bf16[8,12,32,16,128]{4,3,2,1,0:T(8,128)(2,1)} %field_ref.3, bf16[8,12,32,16,128]{4,3,2,1,0:T(8,128)(2,1)} %cot_ref.1, bf16[32,192,128]{2,1,0:T(8,128)(2,1)S(1)} %bitcast.22, bf16[192,192]{1,0:T(8,128)(2,1)S(1)} %copy-done.5, ...), custom_call_target="tpu_custom_call" | custom-call | flops 5637144576 | bytes 40894464 | tf_op jit(solution)/shard_map/pallas_call | solution.py:52
  143.5 23.4 %all_to_all.42 = bf16[8,768,128]{2,1,0:T(8,128)(2,1)S(1)} all-to-all(bf16[8,768,128]{2,1,0:T(8,128)(2,1)S(1)} %bitcast.23), channel_id=1, replica_groups=mesh['parts'=1,'gx'=4,'gy'=4,'gz'=2] {'gy','gz'}, dimensions={0} | all-to-all | bytes 3145728 | tf_op jit(solution)/shard_map/all_to_all | solution.py:232
  166.9 0.0 copy-done.9
  166.9 0.6 shard_map.109
  167.5 0.0 copy-start.7
  167.5 15.0 %all_to_all.43 = bf16[32,3,16,128]{3,2,1,0:T(8,128)(2,1)S(1)} all-to-all(bf16[32,3,16,128]{3,2,1,0:T(8,128)(2,1)S(1)} %bitcast.32), channel_id=1, replica_groups=mesh['parts'=1,'gx'=4,'gy'=4,'gz'=2] {'gx','gy','gz'}, dimensions={0} | all-to-all | bytes 786432 | tf_op jit(solution)/shard_map/all_to_all | solution.py:229
  182.6 0.6 shard_map.110
  183.2 15.5 %all_to_all.44 = bf16[32,3,16,128]{3,2,1,0:T(8,128)(2,1)S(1)} all-to-all(bf16[32,3,16,128]{3,2,1,0:T(8,128)(2,1)S(1)} %bitcast.30), channel_id=1, replica_groups=mesh['parts'=1,'gx'=4,'gy'=4,'gz'=2] {'gx','gy','gz'}, dimensions={0} | all-to-all | bytes 786432 | tf_op jit(solution)/shard_map/all_to_all | solution.py:229
  198.7 1.8 shard_map.111
  200.5 3.6 %all-to-all-start.7 = ((bf16[8,768,128]{2,1,0:T(8,128)(2,1)}), bf16[8,768,128]{2,1,0:T(8,128)(2,1)S(1)}, u32[]{:S(2)}, u32[]{:S(2)}) async-start(bf16[8,768,128]{2,1,0:T(8,128)(2,1)} %bitcast.16), calls=%async_computation.7 | async-start | bytes 3145728 | tf_op jit(solution)/shard_map/all_to_all | solution.py:241
  204.1 1.7 mul.74.mix_ref
  205.8 0.0 copy-done.7
  205.8 0.4 reshape.84
  206.2 1.1 copy.17
  207.3 0.4 reshape.85
  207.7 0.2 copy.18
  207.9 7.5 %broadcast_multiply_fusion = f32[4,8,12,12,4,32]{5,4,3,2,1,0:T(4,128)} fusion(f32[4,8,12,4,32]{4,3,2,1,0:T(4,128)S(1)} %copy.18, f32[4,8,12,4,32]{4,3,2,1,0:T(4,128)} %copy.17), kind=kLoop, calls=%fused_computation | loop fusion | flops 589824 | bytes 2752512 | tf_op jit(solution)/shard_map/mul | solution.py:259
  215.4 9.6 %all-to-all-done.7 = bf16[8,768,128]{2,1,0:T(8,128)(2,1)S(1)} async-done(((bf16[8,768,128]{2,1,0:T(8,128)(2,1)}), bf16[8,768,128]{2,1,0:T(8,128)(2,1)S(1)}, u32[]{:S(2)}, u32[]{:S(2)}) %all-to-all-start.7) | async-done | bytes 1572896 | tf_op jit(solution)/shard_map/all_to_all | solution.py:241
  225.0 13.9 %shard_map.112 = bf16[8,12,32,16,128]{4,3,2,1,0:T(8,128)(2,1)} custom-call(bf16[8,12,32,16,128]{4,3,2,1,0:T(8,128)(2,1)} %get-tuple-element.9.grad_ref, bf16[32,192,128]{2,1,0:T(8,128)(2,1)S(1)} %bitcast.20, bf16[192,192]{1,0:T(8,128)(2,1)S(1)} %mul.74.mix_ref, bf16[128,1024]{1,0:T(8,128)(2,1)S(1)} %copy-done), custom_call_target="tpu_custom_call" | custom-call | flops 4026531840 | bytes 26738688 | tf_op jit(solution)/shard_map/pallas_call | solution.py:52
  (1 shorter events, 0.0 us)
Async XLA Ops:
  0.6 1.0 copy-start.1
  1.6 34.9 %copy-start.8 = (bf16[128,512]{1,0:T(8,128)(2,1)S(1)}, bf16[128,512]{1,0:T(8,128)(2,1)}, u32[]{:S(2)}) copy-start(bf16[128,512]{1,0:T(8,128)(2,1)} %constant.13.clone.table_ref) | copy-start | bytes 393220
  37.9 20.3 %all-to-all-start.1 = ((bf16[32,3,16,128]{3,2,1,0:T(8,128)(2,1)}), bf16[32,3,16,128]{3,2,1,0:T(8,128)(2,1)S(1)}, u32[]{:S(2)}, u32[]{:S(2)}) async-start(bf16[32,3,16,128]{3,2,1,0:T(8,128)(2,1)} %bitcast.2), calls=%async_computation.1 | async-start | bytes 786432 | tf_op jit(solution)/shard_map/all_to_all | solution.py:229
  52.4 5.7 %copy-start.4 = (bf16[512,128]{1,0:T(8,128)(2,1)S(1)}, bf16[512,128]{1,0:T(8,128)(2,1)}, u32[]{:S(2)}) copy-start(bf16[512,128]{1,0:T(8,128)(2,1)} %constant.12.clone.table_ref) | copy-start | bytes 393220
  52.4 25.2 %copy-start.3 = (bf16[512,128]{1,0:T(8,128)(2,1)S(1)}, bf16[512,128]{1,0:T(8,128)(2,1)}, u32[]{:S(2)}) copy-start(bf16[512,128]{1,0:T(8,128)(2,1)} %constant.14.clone.table_ref) | copy-start | bytes 393220
  58.1 25.1 %copy-start.10 = (bf16[12,12]{1,0:T(8,128)(2,1)S(1)}, bf16[12,12]{1,0:T(8,128)(2,1)}, u32[]{:S(2)}) copy-start(bf16[12,12]{1,0:T(8,128)(2,1)} %param.12) | copy-start | bytes 868
  58.1 45.8 %copy-start = (bf16[128,1024]{1,0:T(8,128)(2,1)S(1)}, bf16[128,1024]{1,0:T(8,128)(2,1)}, u32[]{:S(2)}) copy-start(bf16[128,1024]{1,0:T(8,128)(2,1)} %constant.10.clone.syn_ref) | copy-start | bytes 786436
  58.2 45.8 %copy-start.2 = (bf16[1024,128]{1,0:T(8,128)(2,1)S(1)}, bf16[1024,128]{1,0:T(8,128)(2,1)}, u32[]{:S(2)}) copy-start(bf16[1024,128]{1,0:T(8,128)(2,1)} %constant.11.clone.table_ref) | copy-start | bytes 786436
  58.8 20.6 %copy-start.6 = (bf16[12,32,128]{2,1,0:T(8,128)(2,1)}, bf16[12,32,128]{2,1,0:T(8,128)(2,1)S(1)}, u32[]{:S(2)}) copy-start(bf16[12,32,128]{2,1,0:T(8,128)(2,1)S(1)} %get-tuple-element.12) | copy-start | bytes 294916
  79.4 24.5 %all-to-all-start.3 = ((bf16[8,768,128]{2,1,0:T(8,128)(2,1)}), bf16[8,768,128]{2,1,0:T(8,128)(2,1)S(1)}, u32[]{:S(2)}, u32[]{:S(2)}) async-start(bf16[8,768,128]{2,1,0:T(8,128)(2,1)} %bitcast.7), calls=%async_computation.3 | async-start | bytes 3145728 | tf_op jit(solution)/shard_map/all_to_all | solution.py:241
  104.0 0.9 copy-start.5
  104.9 62.0 %copy-start.9 = (bf16[128,512]{1,0:T(8,128)(2,1)S(1)}, bf16[128,512]{1,0:T(8,128)(2,1)}, u32[]{:S(2)}) copy-start(bf16[128,512]{1,0:T(8,128)(2,1)} %constant.13.clone.table_ref) | copy-start | bytes 393220
  167.5 38.3 %copy-start.7 = (bf16[12,32,128]{2,1,0:T(8,128)(2,1)S(1)}, bf16[12,32,128]{2,1,0:T(8,128)(2,1)}, u32[]{:S(2)}) copy-start(bf16[12,32,128]{2,1,0:T(8,128)(2,1)} %copy-done.6) | copy-start | bytes 294916
  200.5 24.5 %all-to-all-start.7 = ((bf16[8,768,128]{2,1,0:T(8,128)(2,1)}), bf16[8,768,128]{2,1,0:T(8,128)(2,1)S(1)}, u32[]{:S(2)}, u32[]{:S(2)}) async-start(bf16[8,768,128]{2,1,0:T(8,128)(2,1)} %bitcast.16), calls=%async_computation.7 | async-start | bytes 3145728 | tf_op jit(solution)/shard_map/all_to_all | solution.py:241

commit v3 on v2

v3 whole, which is shorter than its diff:
```python
import functools
import math

import jax
import jax.numpy as jnp
import ml_dtypes
import numpy as np
from jax import lax
from jax.experimental import pallas as pl
from jax.experimental.pallas import tpu as pltpu
from jax.sharding import PartitionSpec as P

YZ = ("gy", "gz")
HALF_ROOT = 1.0 / math.sqrt(2.0)
DENSITY = 1.0 / math.sqrt(2.0 * math.pi)


def basis(row_count, extent):
    row = np.arange(row_count)[:, None]
    cell = np.arange(extent)[None, :]
    radians = ((row + 1) // 2 * cell % extent) * (2.0 * math.pi / extent)
    wave = np.where(row % 2 == 0, np.cos(radians), np.sin(radians))
    scale = np.where(row == 0, math.sqrt(1.0 / extent), math.sqrt(2.0 / extent))
    return (wave * scale).astype(ml_dtypes.bfloat16).astype(np.float32)


def narrow(table):
    return np.asarray(table, dtype=ml_dtypes.bfloat16)


def dot(left, right, left_dim=1, right_dim=0):
    return lax.dot_general(
        left, right, (((left_dim,), (right_dim,)), ((), ())), preferred_element_type=jnp.float32
    )


def gelu_slope(value):
    size = jnp.abs(value)
    bell = jnp.exp2(value * value * (-0.5 * math.log2(math.e)))
    span = 1.0 + (0.3275911 * HALF_ROOT) * size
    t = pl.reciprocal(span, approx=True)
    t = t * (2.0 - span * t)
    tail = t * (
        0.5 * 0.254829592
        + t * (0.5 * -0.284496736 + t * (0.5 * 1.421413741 + t * (0.5 * -1.453152027 + t * (0.5 * 1.061405429))))
    )
    low = bell * (tail - DENSITY * size)
    return jnp.where(value >= 0.0, 1.0 - low, low)


def call(body, grid, in_specs, out_specs, out_shape, flops, moved, args, order=None, scratch=(), aliases={}):
    spec = pltpu.PrefetchScalarGridSpec(
        num_scalar_prefetch=0 if order is None else 1,
        grid=grid,
        in_specs=in_specs,
        out_specs=out_specs,
        scratch_shapes=scratch,
    )
    return pl.pallas_call(
        body,
        grid_spec=spec,
        out_shape=out_shape,
        input_output_aliases=aliases,
        compiler_params=pltpu.CompilerParams(vmem_limit_bytes=48 * 1024 * 1024),
        cost_estimate=pl.CostEstimate(flops=int(flops), bytes_accessed=int(moved), transcendentals=0),
    )(*(() if order is None else (order,)), *args)


def whole(shape):
    return pl.BlockSpec(shape, lambda *_: (0,) * len(shape))


def wide(ref, cell, times):
    channels, _, y_local, depth = ref.shape[1:]
    return jnp.concatenate([ref[t, :, cell].reshape(channels * y_local, depth) for t in times], axis=1)


def admit(held, pieces, sub):
    for e, piece in enumerate(pieces):

        @pl.when(pl.program_id(0) == e * sub)
        def _(piece=piece):
            held[...] = piece[...]


def release(held, pieces, sub):
    for e, piece in enumerate(pieces):

        @pl.when(pl.program_id(0) == e * sub + sub - 1)
        def _(piece=piece):
            piece[...] = held[...]


def own_cells(sub, cells):
    return pl.ds(lax.rem(pl.program_id(0), sub) * cells, cells)


def head_body(sub, order_ref, field_ref, table_ref, *refs):
    heads, held = refs[:-1], refs[-1]
    steps, _, cells, _, depth = field_ref.shape
    total = 0.0
    for t in range(0, steps, 2):
        values = jnp.concatenate([wide(field_ref, cell, (t, t + 1)) for cell in range(cells)], axis=0)
        total += dot(values, table_ref[t * depth : (t + 2) * depth, :])
    held[own_cells(sub, cells)] = total.astype(jnp.bfloat16).reshape((cells,) + held.shape[1:])
    release(held, heads, sub)


def inner_body(sub, count, order_ref, field_ref, cot_ref, mix_ref, syn_ref, table_ref, *refs):
    mids, grad_ref, heads, (mid_held, head_held) = refs[:count], refs[count], refs[count + 1 : -2], refs[-2:]
    steps, channels, cells, y_local, depth = field_ref.shape
    rows = channels * y_local
    band = math.gcd(rows, 32)
    admit(mid_held, mids, sub)
    middle = mid_held[own_cells(sub, cells)].reshape(cells * rows, -1)
    total = 0.0
    for t in range(0, steps, 2):
        lanes = slice(t * depth, (t + 2) * depth)
        spread = dot(middle, syn_ref[:, lanes])
        bands = []
        for cell in range(cells):
            preact = spread[cell * rows : (cell + 1) * rows] + dot(mix_ref[...], wide(field_ref, cell, (t, t + 1)))
            cot = wide(cot_ref, cell, (t, t + 1))
            for r in range(0, rows, band):
                slope = gelu_slope(preact[r : r + band])
                bands.append((cot[r : r + band].astype(jnp.float32) * slope).astype(jnp.bfloat16))
        grad = jnp.concatenate(bands, axis=0)
        for cell in range(cells):
            for k in range(2):
                part = grad[cell * rows : (cell + 1) * rows, k * depth : (k + 1) * depth]
                grad_ref[t + k, :, cell] = part.reshape(channels, y_local, depth)
        total += dot(grad, table_ref[lanes, :])
    head_held[own_cells(sub, cells)] = total.astype(jnp.bfloat16).reshape((cells,) + head_held.shape[1:])
    release(head_held, heads, sub)


def outer_body(sub, count, order_ref, grad_ref, mix_ref, syn_ref, *refs):
    mids, out_ref, mid_held = refs[:count], refs[-2], refs[-1]
    steps, channels, cells, y_local, depth = grad_ref.shape
    rows = channels * y_local
    admit(mid_held, mids, sub)
    middle = mid_held[own_cells(sub, cells)].reshape(cells * rows, -1)
    for t in range(0, steps, 2):
        spread = dot(middle, syn_ref[:, t * depth : (t + 2) * depth])
        for cell in range(cells):
            total = spread[cell * rows : (cell + 1) * rows] + dot(mix_ref[...], wide(grad_ref, cell, (t, t + 1)))
            total = total.astype(jnp.bfloat16)
            for k in range(2):
                out_ref[t + k, :, cell] = total[:, k * depth : (k + 1) * depth].reshape(channels, y_local, depth)


def y_down_body(table_ref, *refs):
    pieces, out_ref = refs[:-1], refs[-1]
    cells, channels = pieces[0].shape[:2]
    planes, owners, groups, height, width = out_ref.shape
    members = channels // groups
    span = width // members
    for k in range(groups):
        done = []
        for c in range(k * members, (k + 1) * members):
            stacked = jnp.concatenate([piece[x, c] for piece in pieces for x in range(cells)], axis=0)
            done.append(dot(table_ref[...], stacked).astype(jnp.bfloat16))
        for g in range(planes):
            piece = jnp.concatenate([part[:, g * span : (g + 1) * span] for part in done], axis=1)
            out_ref[g, :, k] = piece.reshape(owners, height, width)


def y_up_body(rows_ref, table_ref, *pieces):
    planes, owners, groups, _, width = rows_ref.shape
    cells, channels, y_local, _ = pieces[0].shape
    members = channels // groups
    span = width // members
    for c in range(channels):
        lanes = slice(c % members * span, (c % members + 1) * span)
        stacked = jnp.concatenate(
            [
                jnp.concatenate([rows_ref[g, s, c // members][:, lanes] for g in range(planes)], axis=1)
                for s in range(owners)
            ],
            axis=0,
        )
        done = dot(table_ref[...], stacked).astype(jnp.bfloat16)
        for k, piece in enumerate(pieces):
            for x in range(cells):
                start = (k * cells + x) * y_local
                piece[x, c] = done[start : start + y_local]


def spectral_body(back, rows_ref, table_ref, weight_ref, modes_ref, out_ref):
    planes, x_pieces, c_pieces, groups, height, width = rows_ref.shape
    channels, span, lanes = modes_ref.shape
    members = width // span
    for h in range(c_pieces):
        for k in range(groups):
            stacked = jnp.concatenate(
                [rows_ref[g, x, h, k] for g in range(planes) for x in range(x_pieces)], axis=0
            )
            first = (h * groups + k) * members
            done = dot(stacked, table_ref[...], 0, 0).astype(jnp.bfloat16)
            modes_ref[first : first + members] = done.reshape(members, span, lanes)
    for h in range(c_pieces):
        for k in range(groups):
            mixed = []
            for m in range(members):
                to = (h * groups + k) * members + m
                total = 0.0
                for of in range(channels):
                    weight = weight_ref[to, of] if back else weight_ref[of, to]
                    total += weight.astype(jnp.float32) * modes_ref[of].astype(jnp.float32)
                mixed.append(total.astype(jnp.bfloat16))
            done = dot(table_ref[...], jnp.concatenate(mixed, axis=0), 1, 1).astype(jnp.bfloat16)
            for g in range(planes):
                for x in range(x_pieces):
                    start = (g * x_pieces + x) * height
                    out_ref[g, x, h, k] = done[start : start + height]


def shards(x_devices, y_devices, state_field, cotangent, spectral_weight, point_weight):
    steps, channels, x_local, y_local, depth = state_field.shape
    j_local, q_local = spectral_weight.shape[:2]
    time_modes, modes = spectral_weight.shape[4:]
    lanes = time_modes * modes
    rows = channels * y_local
    x_extent, y_extent = x_local * x_devices, y_local * y_devices
    bf16 = jnp.bfloat16

    x_pieces = math.gcd(x_local, y_devices)
    c_pieces = y_devices // x_pieces
    x_piece, c_piece = x_local // x_pieces, channels // c_pieces
    group = x_piece * j_local

    paired = c_pieces == 1 and y_devices & (y_devices - 1) == 0
    blocks = x_pieces
    me = lax.axis_index(YZ)
    order = jnp.arange(blocks, dtype=jnp.int32) ^ (me.astype(jnp.int32) if paired else 0)

    time_table, depth_table = basis(time_modes, steps), basis(modes, depth)
    x_table, y_table = basis(modes, x_extent), basis(modes, y_extent)
    synth = np.einsum("pt,qz->qptz", time_table, depth_table).reshape(lanes, steps * depth)
    y_mat = np.einsum("xw,djsy->dxjswy", np.eye(x_piece), y_table.reshape(y_devices, j_local, y_devices, y_local))
    y_mat = y_mat.reshape(y_devices * group, y_devices, x_piece * y_local)
    seen = [[d ^ k if paired else k for k in range(y_devices)] for d in range(y_devices if paired else 1)]
    y_mats = np.stack([y_mat[:, owners].reshape(y_devices * group, -1) for owners in seen])
    mine = me if paired else 0
    x_mat = np.einsum("jk,ix->xjki", np.eye(j_local), x_table).reshape(x_extent * j_local, j_local * modes)
    syn, ana, x_mat = jnp.asarray(narrow(synth)), jnp.asarray(narrow(synth.T)), jnp.asarray(narrow(x_mat))
    y_mat = lax.dynamic_index_in_dim(jnp.asarray(narrow(y_mats)), mine, 0, keepdims=False)
    y_mat_t = lax.dynamic_index_in_dim(jnp.asarray(narrow(y_mats.swapaxes(1, 2))), mine, 0, keepdims=False)
    eye = jnp.eye(y_local, dtype=bf16)
    mix_up, mix_back = jnp.kron(point_weight.T, eye), jnp.kron(point_weight, eye)

    step = math.gcd(x_piece, 2)
    sub = x_piece // step
    block_field = jax.ShapeDtypeStruct((steps, channels, x_piece, y_local, depth), bf16)
    block_head = jax.ShapeDtypeStruct((x_piece, rows, lanes), bf16)
    field_bytes, head_bytes = 2 * math.prod(block_field.shape), 2 * math.prod(block_head.shape)
    head_flops, mix_flops = head_bytes * steps * depth, field_bytes * rows
    held = pltpu.VMEM(block_head.shape, bf16)

    def grouped(first):
        where = lambda g, order: (0, 0, order[first + g // sub] * sub + g % sub, 0, 0)
        return pl.BlockSpec((steps, channels, step, y_local, depth), where)

    in_group = pl.BlockSpec((steps, channels, step, y_local, depth), lambda g, order: (0, 0, g, 0, 0))
    pairs = [(k, min(2, blocks - k)) for k in range(0, blocks, 2)]
    groups = [(0, 1)] + pairs[1:] + [(1, 1)] if blocks > 1 else pairs

    def head_call(first, count):
        return call(
            functools.partial(head_body, sub), (count * sub,), [grouped(first), whole(ana.shape)],
            [whole(block_head.shape)] * count, [block_head] * count,
            count * head_flops, count * (field_bytes + head_bytes), (state_field, ana), order, [held],
        )

    def inner_call(first, count, middle):
        grads = (steps, channels, count * x_piece, y_local, depth)
        tables = (mix_up, syn, ana)
        done = call(
            functools.partial(inner_body, sub, count), (count * sub,),
            [grouped(first)] * 2 + [whole(arg.shape) for arg in tables] + [whole(block_head.shape)] * count,
            [in_group] + [whole(block_head.shape)] * count,
            [jax.ShapeDtypeStruct(grads, bf16)] + [block_head] * count,
            2 * count * (2 * head_flops + mix_flops), count * (3 * field_bytes + 2 * head_bytes),
            (state_field, cotangent, *tables, *middle[first : first + count]), order, [held, held],
        )
        return done[0], done[1:]

    def outer_call(first, count, grads, middle, field):
        tables = (mix_back, syn)
        return call(
            functools.partial(outer_body, sub, count), (count * sub,),
            [in_group] + [whole(arg.shape) for arg in tables] + [whole(block_head.shape)] * count
            + [pl.BlockSpec(memory_space=pl.ANY)] * len(field),
            grouped(first), jax.ShapeDtypeStruct(state_field.shape, bf16),
            count * (head_flops + mix_flops), count * (2 * field_bytes + head_bytes),
            (grads, *tables, *middle[first : first + count], *field), order, [held],
            {4 + count: 0} if field else {},
        )

    def small(body, outs, *args):
        shapes = [jax.ShapeDtypeStruct(out, bf16) for out in outs]
        size = sum(arg.size for arg in args)
        return call(
            body, (1,), [whole(arg.shape) for arg in args], [whole(out) for out in outs], shapes, 1024 * size, 4 * size, args
        )

    span = q_local * time_modes
    members = max(m for m in range(1, c_piece + 1) if c_piece % m == 0 and (m == 1 or m * span <= 128))
    packed = (x_devices, y_devices, c_piece // members, group, members * span)

    def exchange(pieces):
        shape = pieces.shape
        pieces = pieces.reshape((x_devices * y_devices,) + packed[2:])
        return lax.all_to_all(pieces, ("gx",) + YZ, 0, 0, tiled=True).reshape(shape)

    def swap(pieces, count, shape):
        if paired:
            pairs = [[(d, d ^ k) for d in range(y_devices)] for k in range(y_devices)]
            pieces = [lax.ppermute(piece, YZ, pairs[k]) if k else piece for k, piece in enumerate(pieces)]
        else:
            pieces = jnp.stack(pieces).reshape(y_devices, -1, lanes)
            pieces = lax.all_to_all(pieces, YZ, 0, 0, tiled=True).reshape((count,) + shape)
        return [pieces[k].reshape(shape) for k in range(count)]

    def spectral(back, heads, weight):
        cells = (x_piece, c_piece, y_local, lanes)
        (part,) = small(y_down_body, [packed], y_mat, *swap(heads, y_devices, cells))
        part = exchange(part).reshape((x_devices, x_pieces, c_pieces) + packed[2:])
        kept, part = small(
            functools.partial(spectral_body, back), [(channels, span, j_local * modes), part.shape], part, x_mat, weight
        )
        part = exchange(part).reshape(packed)
        pieces = small(y_up_body, [cells] * y_devices, part, y_mat_t)
        return swap(pieces, blocks, block_head.shape), kept.astype(jnp.float32)

    weight = jnp.transpose(spectral_weight, (2, 3, 1, 4, 0, 5)).reshape(channels, channels, span, j_local * modes)

    heads = [None] * blocks
    for first, count in reversed(pairs):
        heads[first : first + count] = head_call(first, count)
    middle, modes_in = spectral(False, heads, weight)
    grads = {}
    for first, count in groups:
        grads[first], heads[first : first + count] = inner_call(first, count, middle)
    middle, grad_modes = spectral(True, heads, weight)
    grad_spectral = (modes_in[:, None] * grad_modes[None]).reshape(
        channels, channels, q_local, time_modes, j_local, modes
    )
    grad_spectral = jnp.transpose(grad_spectral, (4, 2, 0, 1, 3, 5))
    field = ()
    for first, count in sorted(groups):
        field = (outer_call(first, count, grads[first], middle, field),)
    return field[0], grad_spectral


def solution(mesh):
    in_specs = (
        P("parts", None, "gx", YZ, None),
        P("parts", None, "gx", YZ, None),
        P(YZ, "gx", None, None, None, None),
        P(),
    )
    out_specs = (
        P("parts", None, "gx", YZ, None),
        P(("parts",) + YZ, "gx", None, None, None, None),
    )
    body = functools.partial(shards, mesh.shape["gx"], mesh.shape["gy"] * mesh.shape["gz"])
    return jax.shard_map(body, mesh=mesh, in_specs=in_specs, out_specs=out_specs, check_vma=False)
```

time: 240 us -> 221 us (0.921)
  blocking collectives: 98.7 us -> 15.8 us
  starting transfers between devices: 11.3 us -> 41.7 us
  local copies, waits for them, and re-layouts: 24.4 us -> 42.8 us
  Pallas kernels: 68.3 us -> 84 us
    all_to_all x2 -> x0, blocking collectives: 49.3 us -> none  [spectral(): lax.all_to_all(heads.reshape(y_devices, -1, lanes), YZ, 0, 0, tiled=True)]
    all_to_all x3 -> x1, blocking collectives: 49.4 us -> 15.8 us  [exchange(): return lax.all_to_all(pieces, ('gx',) + YZ, 0, 0, tiled=True).reshape(shape)]
    ppermute x0 -> x28, starting transfers between devices: none -> 26.9 us  [swap(): lax.ppermute(piece, YZ, pairs[k])]
    all_to_all x2 -> x0, waiting for transfers between devices: 26.6 us -> none  [spectral(): lax.all_to_all(part.reshape(y_devices, -1, lanes), YZ, 0, 0, tiled=True)]
    pallas_call x9 -> x20, Pallas kernels: 68.3 us -> 84 us  [call(): pl.pallas_call(body, grid_spec=spec, out_shape=out_shape, input_output_al...]
    all_to_all x1 -> x3, waiting for transfers between devices: 0.01 us -> 15 us  [exchange(): return lax.all_to_all(pieces, ('gx',) + YZ, 0, 0, tiled=True).reshape(shape)]
    ppermute x0 -> x28, waiting for transfers between devices: none -> 10.9 us  [swap(): lax.ppermute(piece, YZ, pairs[k])]
    all_to_all x1 -> x3, starting transfers between devices: 3.97 us -> 14.8 us  [exchange(): return lax.all_to_all(pieces, ('gx',) + YZ, 0, 0, tiled=True).reshape(shape)]
  transfers between devices with their start and end apart: 3 -> 31, of which waited for: 2 -> 4; matrix products, arithmetic and copies ran while one was open for 13% -> 18% of each run, Pallas kernels for 0% -> 32%
where the time goes in v3:
time: 221 us; the launch traced here: 220 us
  Pallas kernels  84 us (38%)
  local copies, waits for them, and re-layouts  42.8 us (19%)
  starting transfers between devices  41.7 us (19%)
  waiting for transfers between devices  25.8 us (12%)
  blocking collectives  15.8 us (7%)
  other arithmetic  9.04 us (4%)
    pallas_call x20, Pallas kernels, call(): pl.pallas_call(body, grid_spec=spec, out_shape=out_shape, input_output_al...  84 us
    ppermute x28, starting transfers between devices, swap(): lax.ppermute(piece, YZ, pairs[k])  26.9 us
    all_to_all x1, blocking collectives, exchange(): return lax.all_to_all(pieces, ('gx',) + YZ, 0, 0, tiled=True).reshape(shape)  15.8 us
    all_to_all x3, waiting for transfers between devices, exchange(): return lax.all_to_all(pieces, ('gx',) + YZ, 0, 0, tiled=True).reshape(shape)  15 us
    all_to_all x3, starting transfers between devices, exchange(): return lax.all_to_all(pieces, ('gx',) + YZ, 0, 0, tiled=True).reshape(shape)  14.8 us
    unnamed x52, local copies, waits for them, and re-layouts  12.7 us
    ppermute x28, waiting for transfers between devices, swap(): lax.ppermute(piece, YZ, pairs[k])  10.9 us
    transpose x1, local copies, waits for them, and re-layouts, shards(): jnp.transpose(spectral_weight, (2, 3, 1, 4, 0, 5))  10.6 us
  transfers between devices with their start and end apart: 31, of which 4 were waited for; matrix products, arithmetic and copies ran while one was open for 18% of the time, Pallas kernels for 32%

profile of v3, /device:TPU:0, one launch (start us, length us, event | category | flops | bytes accessed | tf_op | source)
XLA Modules:
  0.0 220.3 jit_solution(8701360590339518383)
XLA Ops:
  0.7 0.9 copy-done.1
  1.6 4.2 %shard_map.104 = (bf16[4,192,128]{2,1,0:T(8,128)(2,1)S(1)}, bf16[4,192,128]{2,1,0:T(8,128)(2,1)S(1)}) custom-call(s32[8]{0:T(128)S(1)} %iota_xor_fusion.order_ref, bf16[8,12,32,16,128]{4,3,2,1,0:T(8,128)(2,1)} %field_ref.17, bf16[1024,128]{1,0:T(8,128)(2,1)S(1)} %copy-done.1), custom_call_target="tpu_custom_call" | custom-call | flops 402653184 | bytes 3538944 | tf_op jit(solution)/shard_map/pallas_call | solution.py:59
  6.3 4.2 %shard_map.105 = (bf16[4,192,128]{2,1,0:T(8,128)(2,1)S(1)}, bf16[4,192,128]{2,1,0:T(8,128)(2,1)S(1)}) custom-call(s32[8]{0:T(128)S(1)} %iota_xor_fusion.order_ref, bf16[8,12,32,16,128]{4,3,2,1,0:T(8,128)(2,1)} %field_ref.17, bf16[1024,128]{1,0:T(8,128)(2,1)S(1)} %copy-done.1), custom_call_target="tpu_custom_call" | custom-call | flops 402653184 | bytes 3538944 | tf_op jit(solution)/shard_map/pallas_call | solution.py:59
  10.5 2.6 %collective-permute-start.1 = (bf16[4,192,128]{2,1,0:T(8,128)(2,1)S(1)}, bf16[4,192,128]{2,1,0:T(8,128)(2,1)S(1)}, u32[]{:S(2)}, u32[]{:S(2)}) collective-permute-start(bf16[4,192,128]{2,1,0:T(8,128)(2,1)S(1)} %get-tuple-element.45), channel_id=1, source_target_pairs={{0,2},{1,3},{2,0},{3,1},{4,6},{5,7},{6,4},{7,5},{8,10},{9,11},{10,... | collective-permute-start | bytes 589832 | tf_op jit(solution)/shard_map/ppermute | solution.py:319
  13.2 4.2 %shard_map.106 = (bf16[4,192,128]{2,1,0:T(8,128)(2,1)S(1)}, bf16[4,192,128]{2,1,0:T(8,128)(2,1)S(1)}) custom-call(s32[8]{0:T(128)S(1)} %iota_xor_fusion.order_ref, bf16[8,12,32,16,128]{4,3,2,1,0:T(8,128)(2,1)} %field_ref.17, bf16[1024,128]{1,0:T(8,128)(2,1)S(1)} %copy-done.1), custom_call_target="tpu_custom_call" | custom-call | flops 402653184 | bytes 3538944 | tf_op jit(solution)/shard_map/pallas_call | solution.py:59
  17.4 1.8 collective-permute-start.3
  19.2 4.2 %shard_map.107 = (bf16[4,192,128]{2,1,0:T(8,128)(2,1)S(1)}, bf16[4,192,128]{2,1,0:T(8,128)(2,1)S(1)}) custom-call(s32[8]{0:T(128)S(1)} %iota_xor_fusion.order_ref, bf16[8,12,32,16,128]{4,3,2,1,0:T(8,128)(2,1)} %field_ref.17, bf16[1024,128]{1,0:T(8,128)(2,1)S(1)} %copy-done.1), custom_call_target="tpu_custom_call" | custom-call | flops 402653184 | bytes 3538944 | tf_op jit(solution)/shard_map/pallas_call | solution.py:59
  23.3 2.6 %collective-permute-start.5 = (bf16[4,192,128]{2,1,0:T(8,128)(2,1)S(1)}, bf16[4,192,128]{2,1,0:T(8,128)(2,1)S(1)}, u32[]{:S(2)}, u32[]{:S(2)}) collective-permute-start(bf16[4,192,128]{2,1,0:T(8,128)(2,1)S(1)} %get-tuple-element.49), channel_id=1, source_target_pairs={{0,6},{1,7},{2,4},{3,5},{4,2},{5,3},{6,0},{7,1},{8,14},{9,15},{10,... | collective-permute-start | bytes 589832 | tf_op jit(solution)/shard_map/ppermute | solution.py:319
  26.2 0.9 dynamic-slice_bitcast_fusion.1.table_ref
  27.1 9.4 %collective-permute-done.4 = bf16[4,192,128]{2,1,0:T(8,128)(2,1)S(1)} collective-permute-done((bf16[4,192,128]{2,1,0:T(8,128)(2,1)S(1)}, bf16[4,192,128]{2,1,0:T(8,128)(2,1)S(1)}, u32[]{:S(2)}, u32[]{:S(2)}) %collective-permute-start.4) | collective-permute-done | bytes 196640 | tf_op jit(solution)/shard_map/ppermute | solution.py:319
  36.5 1.4 shard_map.108
  37.9 6.2 %all-to-all-start = ((bf16[32,3,16,128]{3,2,1,0:T(8,128)(2,1)}), bf16[32,3,16,128]{3,2,1,0:T(8,128)(2,1)S(1)}, u32[]{:S(2)}, u32[]{:S(2)}) async-start(bf16[32,3,16,128]{3,2,1,0:T(8,128)(2,1)} %bitcast.10), calls=%async_computation | async-start | bytes 786432 | tf_op jit(solution)/shard_map/all_to_all | solution.py:314
  44.1 10.6 %copy.20 = bf16[12,12,8,4,4,32]{5,4,3,2,1,0:T(4,128)(2,1)} copy(bf16[12,12,8,4,4,32]{5,3,1,0,2,4:T(4,128)(2,1)} %bitcast.84) | data formatting | bytes 2359296 | tf_op jit(solution)/shard_map/transpose | solution.py:336
  54.7 5.6 %reshape.152.weight_ref = bf16[12,12,32,128]{3,2,1,0:T(8,128)(2,1)S(1)} reshape(bf16[12,12,8,4,4,32]{5,4,3,2,1,0:T(4,128)(2,1)} %copy.20) | data formatting | bytes 2359296 | tf_op jit(solution)/shard_map/reshape | solution.py:336
  60.4 1.3 shard_map.109
  61.7 6.0 %all-to-all-start.1 = ((bf16[32,3,16,128]{3,2,1,0:T(8,128)(2,1)}), bf16[32,3,16,128]{3,2,1,0:T(8,128)(2,1)S(1)}, u32[]{:S(2)}, u32[]{:S(2)}) async-start(bf16[32,3,16,128]{3,2,1,0:T(8,128)(2,1)} %bitcast.13), calls=%async_computation.1 | async-start | bytes 786432 | tf_op jit(solution)/shard_map/all_to_all | solution.py:314
  67.9 1.6 dynamic-slice_bitcast_fusion.table_ref
  69.4 11.3 %all-to-all-done.1 = bf16[32,3,16,128]{3,2,1,0:T(8,128)(2,1)S(1)} async-done(((bf16[32,3,16,128]{3,2,1,0:T(8,128)(2,1)}), bf16[32,3,16,128]{3,2,1,0:T(8,128)(2,1)S(1)}, u32[]{:S(2)}, u32[]{:S(2)}) %all-to-all-start.1) | async-done | bytes 393248 | tf_op jit(solution)/shard_map/all_to_all | solution.py:314
  80.8 0.9 copy-done.16
  81.7 1.5 shard_map.110
  83.2 1.0 collective-permute-start.11
  84.2 0.9 collective-permute-start.12
  85.1 1.3 broadcast_multiply_fusion.1
  86.4 1.7 mul.75.mix_ref
  88.1 1.5 collective-permute-start.7
  89.6 1.2 collective-permute-start.8
  91.5 1.0 collective-permute-start.15
  92.5 0.9 copy-done.15
  93.4 6.0 %shard_map.113 = (bf16[8,12,4,16,128]{4,3,2,1,0:T(8,128)(2,1)S(1)}, bf16[4,192,128]{2,1,0:T(8,128)(2,1)S(1)}) custom-call(s32[8]{0:T(128)S(1)} %iota_xor_fusion.order_ref, bf16[8,12,32,16,128]{4,3,2,1,0:T(8,128)(2,1)} %field_ref.17, bf16[8,12,32,16,128]{4,3,2,1,0:T(8,128)(2,1)} %cot_ref.9, bf16[192,192]{1,0:T(8,128)(2,1)S(1)} %mul.75.mix_ref, ...), custom_call_target="tpu_custom_call" | custom-call | flops 1409286144 | bytes 5111808 | tf_op jit(solution)/shard_map/pallas_call | solution.py:59
  100.7 10.3 %shard_map.114 = (bf16[8,12,8,16,128]{4,3,2,1,0:T(8,128)(2,1)S(1)}, bf16[4,192,128]{2,1,0:T(8,128)(2,1)S(1)}, bf16[4,192,128]{2,1,0:T(8,128)(2,1)S(1)}) custom-call(s32[8]{0:T(128)S(1)} %iota_xor_fusion.order_ref, bf16[8,12,32,16,128]{4,3,2,1,0:T(8,128)(2,1)} %field_ref.17, bf16[8,12,32,16,128]{4,3,2,1,0:T(8,128)(2,1)} %cot_ref.9, ...), custom_call_target="tpu_custom_call" | custom-call | flops 2818572288 | bytes 10223616 | tf_op jit(solution)/shard_map/pallas_call | solution.py:59
  111.0 1.6 copy-done.3
  112.6 0.9 collective-permute-start.13
  114.1 10.2 %shard_map.115 = (bf16[8,12,8,16,128]{4,3,2,1,0:T(8,128)(2,1)S(1)}, bf16[4,192,128]{2,1,0:T(8,128)(2,1)S(1)}, bf16[4,192,128]{2,1,0:T(8,128)(2,1)S(1)}) custom-call(s32[8]{0:T(128)S(1)} %iota_xor_fusion.order_ref, bf16[8,12,32,16,128]{4,3,2,1,0:T(8,128)(2,1)} %field_ref.17, bf16[8,12,32,16,128]{4,3,2,1,0:T(8,128)(2,1)} %cot_ref.9, ...), custom_call_target="tpu_custom_call" | custom-call | flops 2818572288 | bytes 10223616 | tf_op jit(solution)/shard_map/pallas_call | solution.py:59
  124.3 1.7 copy-done.5
  125.9 1.0 collective-permute-start.17
  126.9 1.0 collective-permute-start.18
  127.9 10.2 %shard_map.111 = (bf16[8,12,8,16,128]{4,3,2,1,0:T(8,128)(2,1)S(1)}, bf16[4,192,128]{2,1,0:T(8,128)(2,1)S(1)}, bf16[4,192,128]{2,1,0:T(8,128)(2,1)S(1)}) custom-call(s32[8]{0:T(128)S(1)} %iota_xor_fusion.order_ref, bf16[8,12,32,16,128]{4,3,2,1,0:T(8,128)(2,1)} %field_ref.17, bf16[8,12,32,16,128]{4,3,2,1,0:T(8,128)(2,1)} %cot_ref.9, ...), custom_call_target="tpu_custom_call" | custom-call | flops 2818572288 | bytes 10223616 | tf_op jit(solution)/shard_map/pallas_call | solution.py:59
  138.1 1.7 copy-done.7
  139.8 1.4 collective-permute-start.19
  141.2 1.0 collective-permute-start.20
  142.2 6.2 %shard_map.112 = (bf16[8,12,4,16,128]{4,3,2,1,0:T(8,128)(2,1)S(1)}, bf16[4,192,128]{2,1,0:T(8,128)(2,1)S(1)}) custom-call(s32[8]{0:T(128)S(1)} %iota_xor_fusion.order_ref, bf16[8,12,32,16,128]{4,3,2,1,0:T(8,128)(2,1)} %field_ref.17, bf16[8,12,32,16,128]{4,3,2,1,0:T(8,128)(2,1)} %cot_ref.9, bf16[192,192]{1,0:T(8,128)(2,1)S(1)} %mul.75.mix_ref, ...), custom_call_target="tpu_custom_call" | custom-call | flops 1409286144 | bytes 5111808 | tf_op jit(solution)/shard_map/pallas_call | solution.py:59
  148.5 1.1 copy-done.9
  149.7 1.5 collective-permute-done.20
  151.7 15.8 %all_to_all.20 = bf16[32,3,16,128]{3,2,1,0:T(8,128)(2,1)S(1)} all-to-all(bf16[32,3,16,128]{3,2,1,0:T(8,128)(2,1)S(1)} %bitcast.52), channel_id=1, replica_groups=mesh['parts'=1,'gx'=4,'gy'=4,'gz'=2] {'gx','gy','gz'}, dimensions={0} | all-to-all | bytes 786432 | tf_op jit(solution)/shard_map/all_to_all | solution.py:314
  169.0 2.6 %all-to-all-start.3 = ((bf16[32,3,16,128]{3,2,1,0:T(8,128)(2,1)}), bf16[32,3,16,128]{3,2,1,0:T(8,128)(2,1)S(1)}, u32[]{:S(2)}, u32[]{:S(2)}) async-start(bf16[32,3,16,128]{3,2,1,0:T(8,128)(2,1)} %bitcast.50), calls=%async_computation.3 | async-start | bytes 786432 | tf_op jit(solution)/shard_map/all_to_all | solution.py:314
  171.6 1.7 mul.78.mix_ref
  173.3 2.1 reshape.180
  175.5 2.2 %copy.21 = f32[4,8,12,4,32]{4,3,2,1,0:T(4,128)} copy(f32[4,8,12,4,32]{4,0,3,1,2:T(4,128)} %bitcast.85) | data formatting | bytes 393216 | tf_op jit(solution)/shard_map/mul | solution.py:346
  177.7 1.3 reshape.181
  178.9 2.2 %copy.22 = f32[4,8,12,4,32]{4,3,2,1,0:T(4,128)} copy(f32[4,8,12,4,32]{4,0,3,1,2:T(4,128)} %bitcast.86) | data formatting | bytes 393216 | tf_op jit(solution)/shard_map/mul | solution.py:346
  181.1 3.6 %all-to-all-done.3 = bf16[32,3,16,128]{3,2,1,0:T(8,128)(2,1)S(1)} async-done(((bf16[32,3,16,128]{3,2,1,0:T(8,128)(2,1)}), bf16[32,3,16,128]{3,2,1,0:T(8,128)(2,1)S(1)}, u32[]{:S(2)}, u32[]{:S(2)}) %all-to-all-start.3) | async-done | bytes 393248 | tf_op jit(solution)/shard_map/all_to_all | solution.py:314
  184.8 0.9 copy-done.17
  186.3 1.1 collective-permute-start.23
  187.4 1.3 collective-permute-start.25
  188.7 1.2 collective-permute-start.26
  189.9 7.7 %broadcast_multiply_fusion = f32[4,8,12,12,4,32]{5,4,3,2,1,0:T(4,128)} fusion(f32[4,8,12,4,32]{4,3,2,1,0:T(4,128)} %copy.22, f32[4,8,12,4,32]{4,3,2,1,0:T(4,128)} %copy.21), kind=kLoop, calls=%fused_computation | loop fusion | flops 589824 | bytes 2752512 | tf_op jit(solution)/shard_map/mul | solution.py:346
  197.6 1.4 copy-done.10
  199.0 2.8 %shard_map.119.refs_1_ = bf16[8,12,32,16,128]{4,3,2,1,0:T(8,128)(2,1)} custom-call(s32[8]{0:T(128)S(1)} %iota_xor_fusion.order_ref, bf16[8,12,4,16,128]{4,3,2,1,0:T(8,128)(2,1)S(1)} %copy-done.10, bf16[192,192]{1,0:T(8,128)(2,1)S(1)} %mul.78.mix_ref, bf16[128,1024]{1,0:T(8,128)(2,1)S(1)} %copy-done, bf16[4,192,128]{2,1,0:T(8,128)(2,1)S(1)} %bitcast.64), custom_call_target="tpu_custom_call" | custom-call | flops 503316480 | bytes 3342336 | tf_op jit(solution)/shard_map/pallas_call | solution.py:59
  201.8 1.4 collective-permute-start.21
  203.2 1.4 collective-permute-start.22
  204.6 2.8 %shard_map.120.refs_2_ = bf16[8,12,32,16,128]{4,3,2,1,0:T(8,128)(2,1)} custom-call(s32[8]{0:T(128)S(1)} %iota_xor_fusion.order_ref, bf16[8,12,4,16,128]{4,3,2,1,0:T(8,128)(2,1)S(1)} %get-tuple-element.78.grad_ref, bf16[192,192]{1,0:T(8,128)(2,1)S(1)} %mul.78.mix_ref, bf16[128,1024]{1,0:T(8,128)(2,1)S(1)} %copy-done, ...), custom_call_target="tpu_custom_call", output_to_operand_aliasing={{}: (5, {})} | custom-call | flops 503316480 | bytes 3342336 | tf_op jit(solution)/shard_map/pallas_call | solution.py:59
  207.3 4.3 %shard_map.121.refs_2_ = bf16[8,12,32,16,128]{4,3,2,1,0:T(8,128)(2,1)} custom-call(s32[8]{0:T(128)S(1)} %iota_xor_fusion.order_ref, bf16[8,12,8,16,128]{4,3,2,1,0:T(8,128)(2,1)S(1)} %copy-done.4, bf16[192,192]{1,0:T(8,128)(2,1)S(1)} %mul.78.mix_ref, bf16[128,1024]{1,0:T(8,128)(2,1)S(1)} %copy-done, ...), custom_call_target="tpu_custom_call", output_to_operand_aliasing={{}: (6, {})} | custom-call | flops 1006632960 | bytes 6684672 | tf_op jit(solution)/shard_map/pallas_call | solution.py:59
  211.7 4.3 %shard_map.122.refs_2_ = bf16[8,12,32,16,128]{4,3,2,1,0:T(8,128)(2,1)} custom-call(s32[8]{0:T(128)S(1)} %iota_xor_fusion.order_ref, bf16[8,12,8,16,128]{4,3,2,1,0:T(8,128)(2,1)S(1)} %copy-done.6, bf16[192,192]{1,0:T(8,128)(2,1)S(1)} %mul.78.mix_ref, bf16[128,1024]{1,0:T(8,128)(2,1)S(1)} %copy-done, ...), custom_call_target="tpu_custom_call", output_to_operand_aliasing={{}: (6, {})} | custom-call | flops 1006632960 | bytes 6684672 | tf_op jit(solution)/shard_map/pallas_call | solution.py:59
  216.0 4.3 %shard_map.123 = bf16[8,12,32,16,128]{4,3,2,1,0:T(8,128)(2,1)} custom-call(s32[8]{0:T(128)S(1)} %iota_xor_fusion.order_ref, bf16[8,12,8,16,128]{4,3,2,1,0:T(8,128)(2,1)S(1)} %copy-done.8, bf16[192,192]{1,0:T(8,128)(2,1)S(1)} %mul.78.mix_ref, bf16[128,1024]{1,0:T(8,128)(2,1)S(1)} %copy-done, ...), custom_call_target="tpu_custom_call", output_to_operand_aliasing={{}: (6, {})} | custom-call | flops 1006632960 | bytes 6684672 | tf_op jit(solution)/shard_map/pallas_call | solution.py:59
  (86 shorter events, 6.4 us)
Async XLA Ops:
  0.6 1.0 copy-start.1
  5.8 17.6 %collective-permute-start = (bf16[4,192,128]{2,1,0:T(8,128)(2,1)S(1)}, bf16[4,192,128]{2,1,0:T(8,128)(2,1)S(1)}, u32[]{:S(2)}, u32[]{:S(2)}) collective-permute-start(bf16[4,192,128]{2,1,0:T(8,128)(2,1)S(1)} %get-tuple-element.44), channel_id=1, source_target_pairs={{0,1},{1,0},{2,3},{3,2},{4,5},{5,4},{6,7},{7,6},{8,9},{9,8},{10,11... | collective-permute-start | bytes 589832 | tf_op jit(solution)/shard_map/ppermute | solution.py:319
  10.5 15.5 %collective-permute-start.1 = (bf16[4,192,128]{2,1,0:T(8,128)(2,1)S(1)}, bf16[4,192,128]{2,1,0:T(8,128)(2,1)S(1)}, u32[]{:S(2)}, u32[]{:S(2)}) collective-permute-start(bf16[4,192,128]{2,1,0:T(8,128)(2,1)S(1)} %get-tuple-element.45), channel_id=1, source_target_pairs={{0,2},{1,3},{2,0},{3,1},{4,6},{5,7},{6,4},{7,5},{8,10},{9,11},{10,... | collective-permute-start | bytes 589832 | tf_op jit(solution)/shard_map/ppermute | solution.py:319
  13.0 14.0 %collective-permute-start.2 = (bf16[4,192,128]{2,1,0:T(8,128)(2,1)S(1)}, bf16[4,192,128]{2,1,0:T(8,128)(2,1)S(1)}, u32[]{:S(2)}, u32[]{:S(2)}) collective-permute-start(bf16[4,192,128]{2,1,0:T(8,128)(2,1)S(1)} %get-tuple-element.46), channel_id=1, source_target_pairs={{0,3},{1,2},{2,1},{3,0},{4,7},{5,6},{6,5},{7,4},{8,11},{9,10},{10,... | collective-permute-start | bytes 589832 | tf_op jit(solution)/shard_map/ppermute | solution.py:319
  17.4 9.7 %collective-permute-start.3 = (bf16[4,192,128]{2,1,0:T(8,128)(2,1)S(1)}, bf16[4,192,128]{2,1,0:T(8,128)(2,1)S(1)}, u32[]{:S(2)}, u32[]{:S(2)}) collective-permute-start(bf16[4,192,128]{2,1,0:T(8,128)(2,1)S(1)} %get-tuple-element.47), channel_id=1, source_target_pairs={{0,4},{1,5},{2,6},{3,7},{4,0},{5,1},{6,2},{7,3},{8,12},{9,13},{10,... | collective-permute-start | bytes 589832 | tf_op jit(solution)/shard_map/ppermute | solution.py:319
  19.2 17.3 %collective-permute-start.4 = (bf16[4,192,128]{2,1,0:T(8,128)(2,1)S(1)}, bf16[4,192,128]{2,1,0:T(8,128)(2,1)S(1)}, u32[]{:S(2)}, u32[]{:S(2)}) collective-permute-start(bf16[4,192,128]{2,1,0:T(8,128)(2,1)S(1)} %get-tuple-element.48), channel_id=1, source_target_pairs={{0,5},{1,4},{2,7},{3,6},{4,1},{5,0},{6,3},{7,2},{8,13},{9,12},{10,... | collective-permute-start | bytes 589832 | tf_op jit(solution)/shard_map/ppermute | solution.py:319
  23.3 13.1 %collective-permute-start.5 = (bf16[4,192,128]{2,1,0:T(8,128)(2,1)S(1)}, bf16[4,192,128]{2,1,0:T(8,128)(2,1)S(1)}, u32[]{:S(2)}, u32[]{:S(2)}) collective-permute-start(bf16[4,192,128]{2,1,0:T(8,128)(2,1)S(1)} %get-tuple-element.49), channel_id=1, source_target_pairs={{0,6},{1,7},{2,4},{3,5},{4,2},{5,3},{6,0},{7,1},{8,14},{9,15},{10,... | collective-permute-start | bytes 589832 | tf_op jit(solution)/shard_map/ppermute | solution.py:319
  26.0 10.5 %collective-permute-start.6 = (bf16[4,192,128]{2,1,0:T(8,128)(2,1)S(1)}, bf16[4,192,128]{2,1,0:T(8,128)(2,1)S(1)}, u32[]{:S(2)}, u32[]{:S(2)}) collective-permute-start(bf16[4,192,128]{2,1,0:T(8,128)(2,1)S(1)} %get-tuple-element.50), channel_id=1, source_target_pairs={{0,7},{1,6},{2,5},{3,4},{4,3},{5,2},{6,1},{7,0},{8,15},{9,14},{10,... | collective-permute-start | bytes 589832 | tf_op jit(solution)/shard_map/ppermute | solution.py:319
  36.5 23.9 %copy-start.23 = (bf16[512,128]{1,0:T(8,128)(2,1)S(1)}, bf16[512,128]{1,0:T(8,128)(2,1)}, u32[]{:S(2)}) copy-start(bf16[512,128]{1,0:T(8,128)(2,1)} %constant.32.clone.table_ref) | copy-start | bytes 393220
  37.9 22.5 %all-to-all-start = ((bf16[32,3,16,128]{3,2,1,0:T(8,128)(2,1)}), bf16[32,3,16,128]{3,2,1,0:T(8,128)(2,1)S(1)}, u32[]{:S(2)}, u32[]{:S(2)}) async-start(bf16[32,3,16,128]{3,2,1,0:T(8,128)(2,1)} %bitcast.10), calls=%async_computation | async-start | bytes 786432 | tf_op jit(solution)/shard_map/all_to_all | solution.py:314
  44.0 23.7 %copy-start.25 = (bf16[12,12]{1,0:T(8,128)(2,1)S(1)}, bf16[12,12]{1,0:T(8,128)(2,1)}, u32[]{:S(2)}) copy-start(bf16[12,12]{1,0:T(8,128)(2,1)} %param.12) | copy-start | bytes 868
  44.1 48.4 %copy-start = (bf16[128,1024]{1,0:T(8,128)(2,1)S(1)}, bf16[128,1024]{1,0:T(8,128)(2,1)}, u32[]{:S(2)}) copy-start(bf16[128,1024]{1,0:T(8,128)(2,1)} %constant.30.clone.syn_ref) | copy-start | bytes 786436
  44.1 48.4 %copy-start.2 = (bf16[1024,128]{1,0:T(8,128)(2,1)S(1)}, bf16[1024,128]{1,0:T(8,128)(2,1)}, u32[]{:S(2)}) copy-start(bf16[1024,128]{1,0:T(8,128)(2,1)} %constant.31.clone.table_ref) | copy-start | bytes 786436
  61.7 19.0 %copy-start.18 = (bf16[12,32,128]{2,1,0:T(8,128)(2,1)}, bf16[12,32,128]{2,1,0:T(8,128)(2,1)S(1)}, u32[]{:S(2)}) copy-start(bf16[12,32,128]{2,1,0:T(8,128)(2,1)S(1)} %get-tuple-element.82) | copy-start | bytes 294916
  61.7 19.0 %all-to-all-start.1 = ((bf16[32,3,16,128]{3,2,1,0:T(8,128)(2,1)}), bf16[32,3,16,128]{3,2,1,0:T(8,128)(2,1)S(1)}, u32[]{:S(2)}, u32[]{:S(2)}) async-start(bf16[32,3,16,128]{3,2,1,0:T(8,128)(2,1)} %bitcast.13), calls=%async_computation.1 | async-start | bytes 786432 | tf_op jit(solution)/shard_map/all_to_all | solution.py:314
  80.7 0.9 copy-start.16
  83.1 3.3 %copy-start.19 = (bf16[4,12,16,128]{3,2,1,0:T(8,128)(2,1)}, bf16[4,12,16,128]{3,2,1,0:T(8,128)(2,1)S(1)}, u32[]{:S(2)}) copy-start(bf16[4,12,16,128]{3,2,1,0:T(8,128)(2,1)S(1)} %get-tuple-element.53) | copy-start | bytes 589828
  83.1 3.3 %copy-start.20 = (bf16[4,12,16,128]{3,2,1,0:T(8,128)(2,1)}, bf16[4,12,16,128]{3,2,1,0:T(8,128)(2,1)S(1)}, u32[]{:S(2)}) copy-start(bf16[4,12,16,128]{3,2,1,0:T(8,128)(2,1)S(1)} %get-tuple-element.52) | copy-start | bytes 589828
  83.1 9.3 %copy-start.12 = (bf16[4,12,16,128]{3,2,1,0:T(8,128)(2,1)}, bf16[4,12,16,128]{3,2,1,0:T(8,128)(2,1)S(1)}, u32[]{:S(2)}) copy-start(bf16[4,12,16,128]{3,2,1,0:T(8,128)(2,1)S(1)} %get-tuple-element.55) | copy-start | bytes 589828
  83.1 9.3 %copy-start.21 = (bf16[4,12,16,128]{3,2,1,0:T(8,128)(2,1)}, bf16[4,12,16,128]{3,2,1,0:T(8,128)(2,1)S(1)}, u32[]{:S(2)}) copy-start(bf16[4,12,16,128]{3,2,1,0:T(8,128)(2,1)S(1)} %get-tuple-element.64) | copy-start | bytes 589828
  83.1 7.6 %collective-permute-start.9 = (bf16[4,12,16,128]{3,2,1,0:T(8,128)(2,1)S(1)}, bf16[4,12,16,128]{3,2,1,0:T(8,128)(2,1)S(1)}, u32[]{:S(2)}, u32[]{:S(2)}) collective-permute-start(bf16[4,12,16,128]{3,2,1,0:T(8,128)(2,1)S(1)} %get-tuple-element.57), channel_id=1, source_target_pairs={{0,1},{1,0},{2,3},{3,2},{4,5},{5,4},{6,7},{7,6},{8,9},{9,8},{10,11... | collective-permute-start | bytes 589832 | tf_op jit(solution)/shard_map/ppermute | solution.py:319
  83.2 16.2 %collective-permute-start.11 = (bf16[4,12,16,128]{3,2,1,0:T(8,128)(2,1)}, bf16[4,12,16,128]{3,2,1,0:T(8,128)(2,1)}, u32[]{:S(2)}, u32[]{:S(2)}) collective-permute-start(bf16[4,12,16,128]{3,2,1,0:T(8,128)(2,1)} %get-tuple-element.59), channel_id=1, source_target_pairs={{0,2},{1,3},{2,0},{3,1},{4,6},{5,7},{6,4},{7,5},{8,10},{9,11},{10,... | collective-permute-start | bytes 589832 | tf_op jit(solution)/shard_map/ppermute | solution.py:319
  84.2 16.2 %collective-permute-start.12 = (bf16[4,12,16,128]{3,2,1,0:T(8,128)(2,1)}, bf16[4,12,16,128]{3,2,1,0:T(8,128)(2,1)}, u32[]{:S(2)}, u32[]{:S(2)}) collective-permute-start(bf16[4,12,16,128]{3,2,1,0:T(8,128)(2,1)} %get-tuple-element.60), channel_id=1, source_target_pairs={{0,3},{1,2},{2,1},{3,0},{4,7},{5,6},{6,5},{7,4},{8,11},{9,10},{10,... | collective-permute-start | bytes 589832 | tf_op jit(solution)/shard_map/ppermute | solution.py:319
  88.1 37.8 %collective-permute-start.7 = (bf16[4,12,16,128]{3,2,1,0:T(8,128)(2,1)}, bf16[4,12,16,128]{3,2,1,0:T(8,128)(2,1)S(1)}, u32[]{:S(2)}, u32[]{:S(2)}) collective-permute-start(bf16[4,12,16,128]{3,2,1,0:T(8,128)(2,1)} %copy-done.20), channel_id=1, source_target_pairs={{0,6},{1,7},{2,4},{3,5},{4,2},{5,3},{6,0},{7,1},{8,14},{9,15},{10,... | collective-permute-start | bytes 589832 | tf_op jit(solution)/shard_map/ppermute | solution.py:319
  89.6 37.3 %collective-permute-start.8 = (bf16[4,12,16,128]{3,2,1,0:T(8,128)(2,1)}, bf16[4,12,16,128]{3,2,1,0:T(8,128)(2,1)S(1)}, u32[]{:S(2)}, u32[]{:S(2)}) collective-permute-start(bf16[4,12,16,128]{3,2,1,0:T(8,128)(2,1)} %copy-done.19), channel_id=1, source_target_pairs={{0,7},{1,6},{2,5},{3,4},{4,3},{5,2},{6,1},{7,0},{8,15},{9,14},{10,... | collective-permute-start | bytes 589832 | tf_op jit(solution)/shard_map/ppermute | solution.py:319
  90.8 0.7 copy-start.14
  91.5 21.1 %collective-permute-start.15 = (bf16[4,12,16,128]{3,2,1,0:T(8,128)(2,1)}, bf16[4,12,16,128]{3,2,1,0:T(8,128)(2,1)S(1)}, u32[]{:S(2)}, u32[]{:S(2)}) collective-permute-start(bf16[4,12,16,128]{3,2,1,0:T(8,128)(2,1)} %get-tuple-element.63), channel_id=1, source_target_pairs={{0,4},{1,5},{2,6},{3,7},{4,0},{5,1},{6,2},{7,3},{8,12},{9,13},{10,... | collective-permute-start | bytes 589832 | tf_op jit(solution)/shard_map/ppermute | solution.py:319
  92.5 0.9 copy-start.15
  93.4 6.1 %copy-start.22 = (bf16[4,12,16,128]{3,2,1,0:T(8,128)(2,1)S(1)}, bf16[4,12,16,128]{3,2,1,0:T(8,128)(2,1)}, u32[]{:S(2)}) copy-start(bf16[4,12,16,128]{3,2,1,0:T(8,128)(2,1)} %copy-done.21) | copy-start | bytes 589828
  99.5 14.0 %collective-permute-start.16 = (bf16[4,12,16,128]{3,2,1,0:T(8,128)(2,1)S(1)}, bf16[4,12,16,128]{3,2,1,0:T(8,128)(2,1)S(1)}, u32[]{:S(2)}, u32[]{:S(2)}) collective-permute-start(bf16[4,12,16,128]{3,2,1,0:T(8,128)(2,1)S(1)} %copy-done.22), channel_id=1, source_target_pairs={{0,5},{1,4},{2,7},{3,6},{4,1},{5,0},{6,3},{7,2},{8,13},{9,12},{10,... | collective-permute-start | bytes 589832 | tf_op jit(solution)/shard_map/ppermute | solution.py:319
  100.3 39.5 %collective-permute-start.10 = (bf16[4,192,128]{2,1,0:T(8,128)(2,1)S(1)}, bf16[4,192,128]{2,1,0:T(8,128)(2,1)S(1)}, u32[]{:S(2)}, u32[]{:S(2)}) collective-permute-start(bf16[4,192,128]{2,1,0:T(8,128)(2,1)S(1)} %get-tuple-element.58), channel_id=1, source_target_pairs={{0,1},{1,0},{2,3},{3,2},{4,5},{5,4},{6,7},{7,6},{8,9},{9,8},{10,11... | collective-permute-start | bytes 589832 | tf_op jit(solution)/shard_map/ppermute | solution.py:319
  110.9 1.6 copy-start.3
  112.6 28.6 %collective-permute-start.13 = (bf16[4,192,128]{2,1,0:T(8,128)(2,1)S(1)}, bf16[4,192,128]{2,1,0:T(8,128)(2,1)S(1)}, u32[]{:S(2)}, u32[]{:S(2)}) collective-permute-start(bf16[4,192,128]{2,1,0:T(8,128)(2,1)S(1)} %get-tuple-element.61), channel_id=1, source_target_pairs={{0,2},{1,3},{2,0},{3,1},{4,6},{5,7},{6,4},{7,5},{8,10},{9,11},{10,... | collective-permute-start | bytes 589832 | tf_op jit(solution)/shard_map/ppermute | solution.py:319
  113.5 36.1 %collective-permute-start.14 = (bf16[4,192,128]{2,1,0:T(8,128)(2,1)S(1)}, bf16[4,192,128]{2,1,0:T(8,128)(2,1)S(1)}, u32[]{:S(2)}, u32[]{:S(2)}) collective-permute-start(bf16[4,192,128]{2,1,0:T(8,128)(2,1)S(1)} %get-tuple-element.62), channel_id=1, source_target_pairs={{0,3},{1,2},{2,1},{3,0},{4,7},{5,6},{6,5},{7,4},{8,11},{9,10},{10,... | collective-permute-start | bytes 589832 | tf_op jit(solution)/shard_map/ppermute | solution.py:319
  124.3 1.7 copy-start.5
  125.9 23.7 %collective-permute-start.17 = (bf16[4,192,128]{2,1,0:T(8,128)(2,1)S(1)}, bf16[4,192,128]{2,1,0:T(8,128)(2,1)S(1)}, u32[]{:S(2)}, u32[]{:S(2)}) collective-permute-start(bf16[4,192,128]{2,1,0:T(8,128)(2,1)S(1)} %get-tuple-element.65), channel_id=1, source_target_pairs={{0,4},{1,5},{2,6},{3,7},{4,0},{5,1},{6,2},{7,3},{8,12},{9,13},{10,... | collective-permute-start | bytes 589832 | tf_op jit(solution)/shard_map/ppermute | solution.py:319
  126.9 22.7 %collective-permute-start.18 = (bf16[4,192,128]{2,1,0:T(8,128)(2,1)S(1)}, bf16[4,192,128]{2,1,0:T(8,128)(2,1)S(1)}, u32[]{:S(2)}, u32[]{:S(2)}) collective-permute-start(bf16[4,192,128]{2,1,0:T(8,128)(2,1)S(1)} %get-tuple-element.66), channel_id=1, source_target_pairs={{0,5},{1,4},{2,7},{3,6},{4,1},{5,0},{6,3},{7,2},{8,13},{9,12},{10,... | collective-permute-start | bytes 589832 | tf_op jit(solution)/shard_map/ppermute | solution.py:319
  127.9 14.3 %copy-start.13 = (bf16[4,12,16,128]{3,2,1,0:T(8,128)(2,1)S(1)}, bf16[4,12,16,128]{3,2,1,0:T(8,128)(2,1)}, u32[]{:S(2)}) copy-start(bf16[4,12,16,128]{3,2,1,0:T(8,128)(2,1)} %copy-done.12) | copy-start | bytes 589828
  138.1 1.7 copy-start.7
  139.8 9.8 %collective-permute-start.19 = (bf16[4,192,128]{2,1,0:T(8,128)(2,1)S(1)}, bf16[4,192,128]{2,1,0:T(8,128)(2,1)S(1)}, u32[]{:S(2)}, u32[]{:S(2)}) collective-permute-start(bf16[4,192,128]{2,1,0:T(8,128)(2,1)S(1)} %get-tuple-element.67), channel_id=1, source_target_pairs={{0,6},{1,7},{2,4},{3,5},{4,2},{5,3},{6,0},{7,1},{8,14},{9,15},{10,... | collective-permute-start | bytes 589832 | tf_op jit(solution)/shard_map/ppermute | solution.py:319
  141.2 9.9 %collective-permute-start.20 = (bf16[4,192,128]{2,1,0:T(8,128)(2,1)S(1)}, bf16[4,192,128]{2,1,0:T(8,128)(2,1)S(1)}, u32[]{:S(2)}, u32[]{:S(2)}) collective-permute-start(bf16[4,192,128]{2,1,0:T(8,128)(2,1)S(1)} %get-tuple-element.68), channel_id=1, source_target_pairs={{0,7},{1,6},{2,5},{3,4},{4,3},{5,2},{6,1},{7,0},{8,15},{9,14},{10,... | collective-permute-start | bytes 589832 | tf_op jit(solution)/shard_map/ppermute | solution.py:319
  142.2 25.4 %copy-start.24 = (bf16[512,128]{1,0:T(8,128)(2,1)S(1)}, bf16[512,128]{1,0:T(8,128)(2,1)}, u32[]{:S(2)}) copy-start(bf16[512,128]{1,0:T(8,128)(2,1)} %constant.32.clone.table_ref) | copy-start | bytes 393220
  148.5 1.1 copy-start.9
  168.2 0.8 copy-start.11
  169.0 15.8 %all-to-all-start.3 = ((bf16[32,3,16,128]{3,2,1,0:T(8,128)(2,1)}), bf16[32,3,16,128]{3,2,1,0:T(8,128)(2,1)S(1)}, u32[]{:S(2)}, u32[]{:S(2)}) async-start(bf16[32,3,16,128]{3,2,1,0:T(8,128)(2,1)} %bitcast.50), calls=%async_computation.3 | async-start | bytes 786432 | tf_op jit(solution)/shard_map/all_to_all | solution.py:314
  184.8 0.9 copy-start.17
  186.3 25.3 %collective-permute-start.23 = (bf16[4,12,16,128]{3,2,1,0:T(8,128)(2,1)S(1)}, bf16[4,12,16,128]{3,2,1,0:T(8,128)(2,1)S(1)}, u32[]{:S(2)}, u32[]{:S(2)}) collective-permute-start(bf16[4,12,16,128]{3,2,1,0:T(8,128)(2,1)S(1)} %get-tuple-element.73), channel_id=1, source_target_pairs={{0,4},{1,5},{2,6},{3,7},{4,0},{5,1},{6,2},{7,3},{8,12},{9,13},{10,... | collective-permute-start | bytes 589832 | tf_op jit(solution)/shard_map/ppermute | solution.py:319
  187.4 24.2 %collective-permute-start.24 = (bf16[4,12,16,128]{3,2,1,0:T(8,128)(2,1)S(1)}, bf16[4,12,16,128]{3,2,1,0:T(8,128)(2,1)S(1)}, u32[]{:S(2)}, u32[]{:S(2)}) collective-permute-start(bf16[4,12,16,128]{3,2,1,0:T(8,128)(2,1)S(1)} %get-tuple-element.74), channel_id=1, source_target_pairs={{0,5},{1,4},{2,7},{3,6},{4,1},{5,0},{6,3},{7,2},{8,13},{9,12},{10,... | collective-permute-start | bytes 589832 | tf_op jit(solution)/shard_map/ppermute | solution.py:319
  187.4 14.4 %collective-permute-start.25 = (bf16[4,12,16,128]{3,2,1,0:T(8,128)(2,1)S(1)}, bf16[4,12,16,128]{3,2,1,0:T(8,128)(2,1)S(1)}, u32[]{:S(2)}, u32[]{:S(2)}) collective-permute-start(bf16[4,12,16,128]{3,2,1,0:T(8,128)(2,1)S(1)} %get-tuple-element.76), channel_id=1, source_target_pairs={{0,2},{1,3},{2,0},{3,1},{4,6},{5,7},{6,4},{7,5},{8,10},{9,11},{10,... | collective-permute-start | bytes 589832 | tf_op jit(solution)/shard_map/ppermute | solution.py:319
  188.7 18.6 %collective-permute-start.26 = (bf16[4,12,16,128]{3,2,1,0:T(8,128)(2,1)S(1)}, bf16[4,12,16,128]{3,2,1,0:T(8,128)(2,1)S(1)}, u32[]{:S(2)}, u32[]{:S(2)}) collective-permute-start(bf16[4,12,16,128]{3,2,1,0:T(8,128)(2,1)S(1)} %get-tuple-element.77), channel_id=1, source_target_pairs={{0,3},{1,2},{2,1},{3,0},{4,7},{5,6},{6,5},{7,4},{8,11},{9,10},{10,... | collective-permute-start | bytes 589832 | tf_op jit(solution)/shard_map/ppermute | solution.py:319
  189.9 13.3 %collective-permute-start.27 = (bf16[4,12,16,128]{3,2,1,0:T(8,128)(2,1)S(1)}, bf16[4,12,16,128]{3,2,1,0:T(8,128)(2,1)S(1)}, u32[]{:S(2)}, u32[]{:S(2)}) collective-permute-start(bf16[4,12,16,128]{3,2,1,0:T(8,128)(2,1)S(1)} %get-tuple-element.79), channel_id=1, source_target_pairs={{0,1},{1,0},{2,3},{3,2},{4,5},{5,4},{6,7},{7,6},{8,9},{9,8},{10,11... | collective-permute-start | bytes 589832 | tf_op jit(solution)/shard_map/ppermute | solution.py:319
  197.6 1.4 copy-start.10
  201.8 14.2 %collective-permute-start.21 = (bf16[4,12,16,128]{3,2,1,0:T(8,128)(2,1)S(1)}, bf16[4,12,16,128]{3,2,1,0:T(8,128)(2,1)S(1)}, u32[]{:S(2)}, u32[]{:S(2)}) collective-permute-start(bf16[4,12,16,128]{3,2,1,0:T(8,128)(2,1)S(1)} %get-tuple-element.70), channel_id=1, source_target_pairs={{0,6},{1,7},{2,4},{3,5},{4,2},{5,3},{6,0},{7,1},{8,14},{9,15},{10,... | collective-permute-start | bytes 589832 | tf_op jit(solution)/shard_map/ppermute | solution.py:319
  203.2 12.7 %collective-permute-start.22 = (bf16[4,12,16,128]{3,2,1,0:T(8,128)(2,1)S(1)}, bf16[4,12,16,128]{3,2,1,0:T(8,128)(2,1)S(1)}, u32[]{:S(2)}, u32[]{:S(2)}) collective-permute-start(bf16[4,12,16,128]{3,2,1,0:T(8,128)(2,1)S(1)} %get-tuple-element.71), channel_id=1, source_target_pairs={{0,7},{1,6},{2,5},{3,4},{4,3},{5,2},{6,1},{7,0},{8,15},{9,14},{10,... | collective-permute-start | bytes 589832 | tf_op jit(solution)/shard_map/ppermute | solution.py:319
  204.6 2.8 %copy-start.4 = (bf16[8,12,8,16,128]{4,3,2,1,0:T(8,128)(2,1)S(1)}, bf16[8,12,8,16,128]{4,3,2,1,0:T(8,128)(2,1)}, u32[]{:S(2)}) copy-start(bf16[8,12,8,16,128]{4,3,2,1,0:T(8,128)(2,1)} %copy-done.3) | copy-start | bytes 9437188
  207.3 4.3 %copy-start.6 = (bf16[8,12,8,16,128]{4,3,2,1,0:T(8,128)(2,1)S(1)}, bf16[8,12,8,16,128]{4,3,2,1,0:T(8,128)(2,1)}, u32[]{:S(2)}) copy-start(bf16[8,12,8,16,128]{4,3,2,1,0:T(8,128)(2,1)} %copy-done.5) | copy-start | bytes 9437188
  211.6 4.3 %copy-start.8 = (bf16[8,12,8,16,128]{4,3,2,1,0:T(8,128)(2,1)S(1)}, bf16[8,12,8,16,128]{4,3,2,1,0:T(8,128)(2,1)}, u32[]{:S(2)}) copy-start(bf16[8,12,8,16,128]{4,3,2,1,0:T(8,128)(2,1)} %copy-done.7) | copy-start | bytes 9437188

commit v4 on v3

--- a/solution.py
+++ b/solution.py
@@ -48,22 +48,31 @@
     return jnp.where(value >= 0.0, 1.0 - low, low)
 
 
-def call(body, grid, in_specs, out_specs, out_shape, flops, moved, args, order=None, scratch=(), aliases={}):
+ANY = pl.BlockSpec(memory_space=pl.ANY)
+
+
+def call(body, grid, in_specs, out_specs, out_shape, flops, moved, args, order=None, scratch=(), aliases={}, after=()):
+    lead = 0 if order is None else 1
+    count = lead + len(args)
+
+    def placed(*refs):
+        body(*refs[:count], *refs[count + len(after) :])
+
     spec = pltpu.PrefetchScalarGridSpec(
-        num_scalar_prefetch=0 if order is None else 1,
+        num_scalar_prefetch=lead,
         grid=grid,
-        in_specs=in_specs,
+        in_specs=list(in_specs) + [ANY] * len(after),
         out_specs=out_specs,
         scratch_shapes=scratch,
     )
     return pl.pallas_call(
-        body,
+        placed,
         grid_spec=spec,
         out_shape=out_shape,
-        input_output_aliases=aliases,
-        compiler_params=pltpu.CompilerParams(vmem_limit_bytes=48 * 1024 * 1024),
+        input_output_aliases={lead + operand: out for operand, out in aliases.items()},
+        compiler_params=pltpu.CompilerParams(vmem_limit_bytes=60 * 1024 * 1024),
         cost_estimate=pl.CostEstimate(flops=int(flops), bytes_accessed=int(moved), transcendentals=0),
-    )(*(() if order is None else (order,)), *args)
+    )(*(() if order is None else (order,)), *args, *after)
 
 
 def whole(shape):
@@ -98,16 +107,17 @@
 def head_body(sub, order_ref, field_ref, table_ref, *refs):
     heads, held = refs[:-1], refs[-1]
     steps, _, cells, _, depth = field_ref.shape
-    total = 0.0
-    for t in range(0, steps, 2):
-        values = jnp.concatenate([wide(field_ref, cell, (t, t + 1)) for cell in range(cells)], axis=0)
-        total += dot(values, table_ref[t * depth : (t + 2) * depth, :])
-    held[own_cells(sub, cells)] = total.astype(jnp.bfloat16).reshape((cells,) + held.shape[1:])
+    first = lax.rem(pl.program_id(0), sub) * cells
+    for cell in range(cells):
+        total = 0.0
+        for t in range(0, steps, 2):
+            total += dot(wide(field_ref, cell, (t, t + 1)), table_ref[t * depth : (t + 2) * depth, :])
+        held[first + cell] = total.astype(jnp.bfloat16)
     release(held, heads, sub)
 
 
 def inner_body(sub, count, order_ref, field_ref, cot_ref, mix_ref, syn_ref, table_ref, *refs):
-    mids, grad_ref, heads, (mid_held, head_held) = refs[:count], refs[count], refs[count + 1 : -2], refs[-2:]
+    mids, (grad_ref, *heads), (mid_held, head_held) = refs[:count], refs[-count - 3 : -2], refs[-2:]
     steps, channels, cells, y_local, depth = field_ref.shape
     rows = channels * y_local
     band = math.gcd(rows, 32)
@@ -215,6 +225,21 @@
                     out_ref[g, x, h, k] = done[start : start + height]
 
 
+def outer_product_body(left_ref, right_ref, out_ref):
+    _, q_local, channels, _, time_modes, modes = out_ref.shape
+    for j in range(left_ref.shape[2] // modes):
+
+        @pl.when(pl.program_id(0) == j)
+        def _(j=j):
+            lanes = slice(j * modes, (j + 1) * modes)
+            left = left_ref[:, :, lanes].astype(jnp.float32)
+            right = right_ref[:, :, lanes].astype(jnp.float32)
+            for q in range(q_local):
+                rows = slice(q * time_modes, (q + 1) * time_modes)
+                for c in range(channels):
+                    out_ref[0, q, c] = left[c, rows] * right[:, rows]
+
+
 def shards(x_devices, y_devices, state_field, cotangent, spectral_weight, point_weight):
     steps, channels, x_local, y_local, depth = state_field.shape
     j_local, q_local = spectral_weight.shape[:2]
@@ -249,59 +274,61 @@
     eye = jnp.eye(y_local, dtype=bf16)
     mix_up, mix_back = jnp.kron(point_weight.T, eye), jnp.kron(point_weight, eye)
 
-    step = math.gcd(x_piece, 2)
-    sub = x_piece // step
-    block_field = jax.ShapeDtypeStruct((steps, channels, x_piece, y_local, depth), bf16)
     block_head = jax.ShapeDtypeStruct((x_piece, rows, lanes), bf16)
-    field_bytes, head_bytes = 2 * math.prod(block_field.shape), 2 * math.prod(block_head.shape)
+    full_field = jax.ShapeDtypeStruct(state_field.shape, bf16)
+    field_bytes, head_bytes = 2 * state_field.size // blocks, 2 * math.prod(block_head.shape)
     head_flops, mix_flops = head_bytes * steps * depth, field_bytes * rows
     held = pltpu.VMEM(block_head.shape, bf16)
-
-    def grouped(first):
+    head_step, step = math.gcd(x_piece, 4), math.gcd(x_piece, 2)
+
+    def grouped(first, step):
+        sub = x_piece // step
         where = lambda g, order: (0, 0, order[first + g // sub] * sub + g % sub, 0, 0)
         return pl.BlockSpec((steps, channels, step, y_local, depth), where)
 
-    in_group = pl.BlockSpec((steps, channels, step, y_local, depth), lambda g, order: (0, 0, g, 0, 0))
     pairs = [(k, min(2, blocks - k)) for k in range(0, blocks, 2)]
     groups = [(0, 1)] + pairs[1:] + [(1, 1)] if blocks > 1 else pairs
 
-    def head_call(first, count):
+    def head_call(first, count, after):
+        sub = x_piece // head_step
         return call(
-            functools.partial(head_body, sub), (count * sub,), [grouped(first), whole(ana.shape)],
+            functools.partial(head_body, sub), (count * sub,), [grouped(first, head_step), whole(ana.shape)],
             [whole(block_head.shape)] * count, [block_head] * count,
-            count * head_flops, count * (field_bytes + head_bytes), (state_field, ana), order, [held],
-        )
-
-    def inner_call(first, count, middle):
-        grads = (steps, channels, count * x_piece, y_local, depth)
+            count * head_flops, count * (field_bytes + head_bytes), (state_field, ana), order, [held], after=after,
+        )
+
+    def inner_call(first, count, middle, grads):
+        sub = x_piece // step
         tables = (mix_up, syn, ana)
+        spec = grouped(first, step)
         done = call(
             functools.partial(inner_body, sub, count), (count * sub,),
-            [grouped(first)] * 2 + [whole(arg.shape) for arg in tables] + [whole(block_head.shape)] * count,
-            [in_group] + [whole(block_head.shape)] * count,
-            [jax.ShapeDtypeStruct(grads, bf16)] + [block_head] * count,
+            [spec] * 2 + [whole(arg.shape) for arg in tables] + [whole(block_head.shape)] * count + [ANY] * len(grads),
+            [spec] + [whole(block_head.shape)] * count, [full_field] + [block_head] * count,
             2 * count * (2 * head_flops + mix_flops), count * (3 * field_bytes + 2 * head_bytes),
-            (state_field, cotangent, *tables, *middle[first : first + count]), order, [held, held],
-        )
-        return done[0], done[1:]
-
-    def outer_call(first, count, grads, middle, field):
+            (state_field, cotangent, *tables, *middle[first : first + count], *grads), order, [held, held],
+            {5 + count: 0} if grads else {},
+        )
+        return done[:1], done[1:]
+
+    def outer_call(first, count, middle, grads, field):
+        sub = x_piece // step
         tables = (mix_back, syn)
+        spec = grouped(first, step)
         return call(
             functools.partial(outer_body, sub, count), (count * sub,),
-            [in_group] + [whole(arg.shape) for arg in tables] + [whole(block_head.shape)] * count
-            + [pl.BlockSpec(memory_space=pl.ANY)] * len(field),
-            grouped(first), jax.ShapeDtypeStruct(state_field.shape, bf16),
-            count * (head_flops + mix_flops), count * (2 * field_bytes + head_bytes),
-            (grads, *tables, *middle[first : first + count], *field), order, [held],
-            {4 + count: 0} if field else {},
-        )
-
-    def small(body, outs, *args):
+            [spec] + [whole(arg.shape) for arg in tables] + [whole(block_head.shape)] * count + [ANY] * len(field),
+            [spec], [full_field], count * (head_flops + mix_flops), count * (2 * field_bytes + head_bytes),
+            (*grads, *tables, *middle[first : first + count], *field), order, [held],
+            {3 + count: 0} if field else {},
+        )
+
+    def small(body, outs, *args, after=()):
         shapes = [jax.ShapeDtypeStruct(out, bf16) for out in outs]
         size = sum(arg.size for arg in args)
         return call(
-            body, (1,), [whole(arg.shape) for arg in args], [whole(out) for out in outs], shapes, 1024 * size, 4 * size, args
+            body, (1,), [whole(arg.shape) for arg in args], [whole(out) for out in outs], shapes, 1024 * size, 4 * size, args,
+            after=after,
         )
 
     span = q_local * time_modes
@@ -322,34 +349,40 @@
             pieces = lax.all_to_all(pieces, YZ, 0, 0, tiled=True).reshape((count,) + shape)
         return [pieces[k].reshape(shape) for k in range(count)]
 
-    def spectral(back, heads, weight):
+    def spectral(back, heads, weight, after=()):
         cells = (x_piece, c_piece, y_local, lanes)
-        (part,) = small(y_down_body, [packed], y_mat, *swap(heads, y_devices, cells))
+        (part,) = small(y_down_body, [packed], y_mat, *swap(heads, y_devices, cells), after=after)
         part = exchange(part).reshape((x_devices, x_pieces, c_pieces) + packed[2:])
         kept, part = small(
             functools.partial(spectral_body, back), [(channels, span, j_local * modes), part.shape], part, x_mat, weight
         )
         part = exchange(part).reshape(packed)
         pieces = small(y_up_body, [cells] * y_devices, part, y_mat_t)
-        return swap(pieces, blocks, block_head.shape), kept.astype(jnp.float32)
+        return swap(pieces, blocks, block_head.shape), kept
 
     weight = jnp.transpose(spectral_weight, (2, 3, 1, 4, 0, 5)).reshape(channels, channels, span, j_local * modes)
 
-    heads = [None] * blocks
-    for first, count in reversed(pairs):
-        heads[first : first + count] = head_call(first, count)
-    middle, modes_in = spectral(False, heads, weight)
-    grads = {}
+    heads, after = [None] * blocks, ()
+    half = -(-blocks // 2)
+    for first, count in ((half, blocks - half), (0, half)):
+        if count:
+            heads[first : first + count] = head_call(first, count, after)
+            after = (heads[first],)
+    middle, modes_in = spectral(False, heads, weight, (weight, mix_up, mix_back))
+    grads = ()
     for first, count in groups:
-        grads[first], heads[first : first + count] = inner_call(first, count, middle)
+        grads, heads[first : first + count] = inner_call(first, count, middle, grads)
     middle, grad_modes = spectral(True, heads, weight)
-    grad_spectral = (modes_in[:, None] * grad_modes[None]).reshape(
-        channels, channels, q_local, time_modes, j_local, modes
-    )
-    grad_spectral = jnp.transpose(grad_spectral, (4, 2, 0, 1, 3, 5))
+    spec = whole(modes_in.shape)
+    grad_spectral = call(
+        outer_product_body, (j_local,), [spec, spec],
+        pl.BlockSpec((1,) + spectral_weight.shape[1:], lambda j: (j, 0, 0, 0, 0, 0)),
+        jax.ShapeDtypeStruct(spectral_weight.shape, jnp.float32),
+        spectral_weight.size, 16 * spectral_weight.size, (modes_in, grad_modes),
+    )
     field = ()
     for first, count in sorted(groups):
-        field = (outer_call(first, count, grads[first], middle, field),)
+        field = outer_call(first, count, middle, grads, field)
     return field[0], grad_spectral
 
 

time: 221 us -> 257 us (1.16)
  blocking collectives: 15.8 us -> 51 us
  Pallas kernels: 84 us -> 111 us
  local copies, waits for them, and re-layouts: 42.8 us -> 29.5 us
  starting transfers between devices: 41.7 us -> 31.6 us
  other arithmetic: 9.04 us -> 0.69 us
  waiting for transfers between devices: 25.8 us -> 30.4 us
    all_to_all x1 -> x3, blocking collectives: 15.8 us -> 51 us  [exchange(): return lax.all_to_all(pieces, ('gx',) + YZ, 0, 0, tiled=True).reshape(shape)]
    pallas_call x20 -> x19, Pallas kernels: 84 us -> 111 us  [call(): pl.pallas_call(placed, grid_spec=spec, out_shape=out_shape, input_output_...]
    all_to_all x3 -> x1, starting transfers between devices: 14.8 us -> 2.64 us  [exchange(): return lax.all_to_all(pieces, ('gx',) + YZ, 0, 0, tiled=True).reshape(shape)]
    ppermute x28, waiting for transfers between devices: 10.9 us -> 18.8 us  [swap(): lax.ppermute(piece, YZ, pairs[k])]
    mul x4 -> x0, local copies, waits for them, and re-layouts: 7.82 us -> none  [shards(): modes_in[:, None] * grad_modes[None]]
    mul x1 -> x0, other arithmetic: 7.72 us -> none  [shards(): modes_in[:, None] * grad_modes[None]]
    unnamed x52 -> x86, local copies, waits for them, and re-layouts: 12.7 us -> 6.69 us
    all_to_all x3 -> x1, waiting for transfers between devices: 15 us -> 11.6 us  [exchange(): return lax.all_to_all(pieces, ('gx',) + YZ, 0, 0, tiled=True).reshape(shape)]
  transfers between devices with their start and end apart: 31 -> 29, of which waited for: 4 -> 6; matrix products, arithmetic and copies ran while one was open for 18% -> 9% of each run, Pallas kernels for 32% -> 26%
where the time goes in v4:
time: 257 us; the launch traced here: 255 us
  Pallas kernels  111 us (43%)
  blocking collectives  51 us (20%)
  starting transfers between devices  31.6 us (12%)
  waiting for transfers between devices  30.4 us (12%)
  local copies, waits for them, and re-layouts  29.5 us (11%)
    pallas_call x19, Pallas kernels, call(): pl.pallas_call(placed, grid_spec=spec, out_shape=out_shape, input_output_...  111 us
    all_to_all x3, blocking collectives, exchange(): return lax.all_to_all(pieces, ('gx',) + YZ, 0, 0, tiled=True).reshape(shape)  51 us
    ppermute x28, starting transfers between devices, swap(): lax.ppermute(piece, YZ, pairs[k])  29 us
    ppermute x28, waiting for transfers between devices, swap(): lax.ppermute(piece, YZ, pairs[k])  18.8 us
    all_to_all x1, waiting for transfers between devices, exchange(): return lax.all_to_all(pieces, ('gx',) + YZ, 0, 0, tiled=True).reshape(shape)  11.6 us
    transpose x1, local copies, waits for them, and re-layouts, shards(): jnp.transpose(spectral_weight, (2, 3, 1, 4, 0, 5))  10.6 us
    unnamed x86, local copies, waits for them, and re-layouts  6.69 us
    reshape x1, local copies, waits for them, and re-layouts, shards(): jnp.transpose(spectral_weight, (2, 3, 1, 4, 0, 5))  6.44 us
  transfers between devices with their start and end apart: 29, of which 6 were waited for; matrix products, arithmetic and copies ran while one was open for 9% of the time, Pallas kernels for 26%

profile of v4, /device:TPU:0, one launch (start us, length us, event | category | flops | bytes accessed | tf_op | source)
XLA Modules:
  0.0 255.2 jit_solution(9688989825225800481)
XLA Ops:
  0.6 0.5 iota_xor_fusion.refs_0_
  1.2 6.5 %shard_map.104 = (bf16[4,192,128]{2,1,0:T(8,128)(2,1)}, bf16[4,192,128]{2,1,0:T(8,128)(2,1)}, bf16[4,192,128]{2,1,0:T(8,128)(2,1)}, bf16[4,192,128]{2,1,0:T(8,128)(2,1)}) custom-call(s32[8]{0:T(128)} %iota_xor_fusion.refs_0_, bf16[8,12,32,16,128]{4,3,2,1,0:T(8,128)(2,1)} %refs_1_.15, bf16[1024,128]{1,0:T(8,128)(2,1)} %constant.31.clone.refs_2_.refs_5_), custom_call_target="tpu_custom_call" | custom-call | flops 805306368 | bytes 7077888 | tf_op jit(solution)/shard_map/pallas_call | solution.py:68
  7.6 6.5 %shard_map.105 = (bf16[4,192,128]{2,1,0:T(8,128)(2,1)}, bf16[4,192,128]{2,1,0:T(8,128)(2,1)}, bf16[4,192,128]{2,1,0:T(8,128)(2,1)}, bf16[4,192,128]{2,1,0:T(8,128)(2,1)}) custom-call(s32[8]{0:T(128)} %iota_xor_fusion.refs_0_, bf16[8,12,32,16,128]{4,3,2,1,0:T(8,128)(2,1)} %refs_1_.15, bf16[1024,128]{1,0:T(8,128)(2,1)} %constant.31.clone.refs_2_.refs_5_, ...), custom_call_target="tpu_custom_call" | custom-call | flops 805306368 | bytes 7077888 | tf_op jit(solution)/shard_map/pallas_call | solution.py:68
  14.5 2.5 collective-permute-start.1
  17.0 1.5 collective-permute-start.3
  19.0 3.0 %collective-permute-start.5 = (bf16[4,192,128]{2,1,0:T(8,128)(2,1)S(1)}, bf16[4,192,128]{2,1,0:T(8,128)(2,1)S(1)}, u32[]{:S(2)}, u32[]{:S(2)}) collective-permute-start(bf16[4,192,128]{2,1,0:T(8,128)(2,1)S(1)} %copy-done.26), channel_id=1, source_target_pairs={{0,6},{1,7},{2,4},{3,5},{4,2},{5,3},{6,0},{7,1},{8,14},{9,15},{10,... | collective-permute-start | bytes 589832 | tf_op jit(solution)/shard_map/ppermute | solution.py:346
  22.0 1.0 collective-permute-done.1
  23.0 1.8 collective-permute-start.6
  25.0 1.2 mul.48.refs_10_.refs_3_
  26.3 10.6 %copy.22 = bf16[12,12,8,4,4,32]{5,4,3,2,1,0:T(4,128)(2,1)} copy(bf16[12,12,8,4,4,32]{5,3,1,0,2,4:T(4,128)(2,1)} %bitcast.46) | data formatting | bytes 2359296 | tf_op jit(solution)/shard_map/transpose | solution.py:363
  36.9 6.4 %reshape.142.refs_9_.refs_2_ = bf16[12,12,32,128]{3,2,1,0:T(8,128)(2,1)} reshape(bf16[12,12,8,4,4,32]{5,4,3,2,1,0:T(4,128)(2,1)} %copy.22) | data formatting | bytes 2359296 | tf_op jit(solution)/shard_map/reshape | solution.py:363
  43.3 1.3 mul.51.refs_11_.refs_2_
  44.6 1.6 dynamic-slice_bitcast_fusion.1.refs_0_
  46.3 0.6 copy-done.19
  47.1 2.9 %shard_map.106 = bf16[4,8,3,16,128]{4,3,2,1,0:T(8,128)(2,1)} custom-call(bf16[128,512]{1,0:T(8,128)(2,1)} %dynamic-slice_bitcast_fusion.1.refs_0_, bf16[4,12,16,128]{3,2,1,0:T(8,128)(2,1)} %bitcast.71, bf16[4,12,16,128]{3,2,1,0:T(8,128)(2,1)} %bitcast.72, bf16[4,12,16,128]{3,2,1,0:T(8,128)(2,1)} %bitcast.73, bf16[4,12,16,128]{3,2,1,0:T(8,128)(2,1)} %bitcast.75, ...), custom_call_target="tpu_custom_call" | custom-call | flops 872415232 | bytes 3407872 | tf_op jit(solution)/shard_map/pallas_call | solution.py:68
  50.0 18.0 %all_to_all.20 = bf16[32,3,16,128]{3,2,1,0:T(8,128)(2,1)} all-to-all(bf16[32,3,16,128]{3,2,1,0:T(8,128)(2,1)} %bitcast.47), channel_id=1, replica_groups=mesh['parts'=1,'gx'=4,'gy'=4,'gz'=2] {'gx','gy','gz'}, dimensions={0} | all-to-all | bytes 786432 | tf_op jit(solution)/shard_map/all_to_all | solution.py:341
  68.0 2.8 %shard_map.107 = (bf16[12,32,128]{2,1,0:T(8,128)(2,1)}, bf16[4,8,1,3,16,128]{5,4,3,2,1,0:T(8,128)(2,1)}) custom-call(bf16[4,8,1,3,16,128]{5,4,3,2,1,0:T(8,128)(2,1)} %bitcast.54, bf16[512,128]{1,0:T(8,128)(2,1)} %constant.32.clone.refs_1_, bf16[12,12,32,128]{3,2,1,0:T(8,128)(2,1)} %reshape.142.refs_9_.refs_2_), custom_call_target="tpu_custom_call" | custom-call | flops 872415232 | bytes 3407872 | tf_op jit(solution)/shard_map/pallas_call | solution.py:68
  70.9 2.6 %all-to-all-start.1 = ((bf16[32,3,16,128]{3,2,1,0:T(8,128)(2,1)}), bf16[32,3,16,128]{3,2,1,0:T(8,128)(2,1)S(1)}, u32[]{:S(2)}, u32[]{:S(2)}) async-start(bf16[32,3,16,128]{3,2,1,0:T(8,128)(2,1)} %bitcast.49), calls=%async_computation.1 | async-start | bytes 786432 | tf_op jit(solution)/shard_map/all_to_all | solution.py:341
  73.5 1.6 dynamic-slice_bitcast_fusion.refs_1_
  75.1 11.6 %all-to-all-done.1 = bf16[32,3,16,128]{3,2,1,0:T(8,128)(2,1)S(1)} async-done(((bf16[32,3,16,128]{3,2,1,0:T(8,128)(2,1)}), bf16[32,3,16,128]{3,2,1,0:T(8,128)(2,1)S(1)}, u32[]{:S(2)}, u32[]{:S(2)}) %all-to-all-start.1) | async-done | bytes 393248 | tf_op jit(solution)/shard_map/all_to_all | solution.py:341
  86.7 0.7 copy-done
  87.4 2.8 %shard_map.108 = (bf16[4,12,16,128]{3,2,1,0:T(8,128)(2,1)}, bf16[4,12,16,128]{3,2,1,0:T(8,128)(2,1)}, bf16[4,12,16,128]{3,2,1,0:T(8,128)(2,1)}, bf16[4,12,16,128...) custom-call(bf16[4,8,3,16,128]{4,3,2,1,0:T(8,128)(2,1)} %bitcast.48,, ...), custom_call_target="tpu_custom_call" | custom-call | flops 268435456 | bytes 1048576 | tf_op jit(solution)/shard_map/pallas_call | solution.py:68
  91.0 1.3 collective-permute-start.7
  92.4 1.4 collective-permute-start.8
  93.8 0.9 collective-permute-start.9
  94.6 7.3 %shard_map.109 = (bf16[8,12,32,16,128]{4,3,2,1,0:T(8,128)(2,1)}, bf16[4,192,128]{2,1,0:T(8,128)(2,1)}) custom-call(s32[8]{0:T(128)} %iota_xor_fusion.refs_0_, bf16[8,12,32,16,128]{4,3,2,1,0:T(8,128)(2,1)} %refs_1_.15, bf16[8,12,32,16,128]{4,3,2,1,0:T(8,128)(2,1)} %refs_2_.11, bf16[192,192]{1,0:T(8,128)(2,1)} %mul.48.refs_10_.refs_3_, ...), custom_call_target="tpu_custom_call" | custom-call | flops 1409286144 | bytes 5111808 | tf_op jit(solution)/shard_map/pallas_call | solution.py:68
  101.9 1.1 collective-permute-start.10
  103.1 1.1 collective-permute-start.11
  104.2 11.4 %shard_map.110 = (bf16[8,12,32,16,128]{4,3,2,1,0:T(8,128)(2,1)}, bf16[4,192,128]{2,1,0:T(8,128)(2,1)}, bf16[4,192,128]{2,1,0:T(8,128)(2,1)}) custom-call(s32[8]{0:T(128)} %iota_xor_fusion.refs_0_, bf16[8,12,32,16,128]{4,3,2,1,0:T(8,128)(2,1)} %refs_1_.15, bf16[8,12,32,16,128]{4,3,2,1,0:T(8,128)(2,1)} %refs_2_.11, ...), custom_call_target="tpu_custom_call", output_to_operand_aliasing={{0}: (8, {})} | custom-call | flops 2818572288 | bytes 10223616 | tf_op jit(solution)/shard_map/pallas_call | solution.py:68
  115.7 2.5 collective-permute-done.11
  118.2 0.7 copy-done.14
  118.9 11.4 %shard_map.111 = (bf16[8,12,32,16,128]{4,3,2,1,0:T(8,128)(2,1)}, bf16[4,192,128]{2,1,0:T(8,128)(2,1)}, bf16[4,192,128]{2,1,0:T(8,128)(2,1)}) custom-call(s32[8]{0:T(128)} %iota_xor_fusion.refs_0_, bf16[8,12,32,16,128]{4,3,2,1,0:T(8,128)(2,1)} %refs_1_.15, bf16[8,12,32,16,128]{4,3,2,1,0:T(8,128)(2,1)} %refs_2_.11, ...), custom_call_target="tpu_custom_call", output_to_operand_aliasing={{0}: (8, {})} | custom-call | flops 2818572288 | bytes 10223616 | tf_op jit(solution)/shard_map/pallas_call | solution.py:68
  130.3 0.6 copy-done.2
  131.0 11.4 %shard_map.112 = (bf16[8,12,32,16,128]{4,3,2,1,0:T(8,128)(2,1)}, bf16[4,192,128]{2,1,0:T(8,128)(2,1)}, bf16[4,192,128]{2,1,0:T(8,128)(2,1)}) custom-call(s32[8]{0:T(128)} %iota_xor_fusion.refs_0_, bf16[8,12,32,16,128]{4,3,2,1,0:T(8,128)(2,1)} %refs_1_.15, bf16[8,12,32,16,128]{4,3,2,1,0:T(8,128)(2,1)} %refs_2_.11, ...), custom_call_target="tpu_custom_call", output_to_operand_aliasing={{0}: (8, {})} | custom-call | flops 2818572288 | bytes 10223616 | tf_op jit(solution)/shard_map/pallas_call | solution.py:68
  142.5 0.7 copy-done.1
  143.2 7.4 %shard_map.113 = (bf16[8,12,32,16,128]{4,3,2,1,0:T(8,128)(2,1)}, bf16[4,192,128]{2,1,0:T(8,128)(2,1)}) custom-call(s32[8]{0:T(128)} %iota_xor_fusion.refs_0_, bf16[8,12,32,16,128]{4,3,2,1,0:T(8,128)(2,1)} %refs_1_.15, bf16[8,12,32,16,128]{4,3,2,1,0:T(8,128)(2,1)} %refs_2_.11, ...), custom_call_target="tpu_custom_call", output_to_operand_aliasing={{0}: (7, {})} | custom-call | flops 1409286144 | bytes 5111808 | tf_op jit(solution)/shard_map/pallas_call | solution.py:68
  150.7 1.2 collective-permute-start.15
  151.8 0.6 collective-permute-start.16
  152.4 1.0 collective-permute-start.17
  153.4 0.8 collective-permute-start.18
  154.2 2.0 collective-permute-start.19
  156.2 2.2 collective-permute-done.15
  158.4 0.5 collective-permute-start.20
  158.9 2.6 %collective-permute-done.16 = bf16[4,192,128]{2,1,0:T(8,128)(2,1)S(1)} collective-permute-done((bf16[4,192,128]{2,1,0:T(8,128)(2,1)S(1)}, bf16[4,192,128]{2,1,0:T(8,128)(2,1)S(1)}, u32[]{:S(2)}, u32[]{:S(2)}) %collective-permute-start.16) | collective-permute-done | bytes 196640 | tf_op jit(solution)/shard_map/ppermute | solution.py:346
  161.5 10.3 %collective-permute-done.18 = bf16[4,192,128]{2,1,0:T(8,128)(2,1)S(1)} collective-permute-done((bf16[4,192,128]{2,1,0:T(8,128)(2,1)S(1)}, bf16[4,192,128]{2,1,0:T(8,128)(2,1)S(1)}, u32[]{:S(2)}, u32[]{:S(2)}) %collective-permute-start.18) | collective-permute-done | bytes 196640 | tf_op jit(solution)/shard_map/ppermute | solution.py:346
  171.9 0.6 copy-done.40
  172.6 2.9 %shard_map.114 = bf16[4,8,3,16,128]{4,3,2,1,0:T(8,128)(2,1)} custom-call(bf16[128,512]{1,0:T(8,128)(2,1)} %dynamic-slice_bitcast_fusion.1.refs_0_, bf16[4,12,16,128]{3,2,1,0:T(8,128)(2,1)} %bitcast.80, bf16[4,12,16,128]{3,2,1,0:T(8,128)(2,1)} %bitcast.81, bf16[4,12,16,128]{3,2,1,0:T(8,128)(2,1)} %bitcast.82, bf16[4,12,16,128]{3,2,1,0:T(8,128)(2,1)} %bitcast.83, ...), custom_call_target="tpu_custom_call" | custom-call | flops 872415232 | bytes 3407872 | tf_op jit(solution)/shard_map/pallas_call | solution.py:68
  175.5 16.5 %all_to_all.21 = bf16[32,3,16,128]{3,2,1,0:T(8,128)(2,1)} all-to-all(bf16[32,3,16,128]{3,2,1,0:T(8,128)(2,1)} %bitcast.51), channel_id=1, replica_groups=mesh['parts'=1,'gx'=4,'gy'=4,'gz'=2] {'gx','gy','gz'}, dimensions={0} | all-to-all | bytes 786432 | tf_op jit(solution)/shard_map/all_to_all | solution.py:341
  192.0 2.8 %shard_map.115 = (bf16[12,32,128]{2,1,0:T(8,128)(2,1)}, bf16[4,8,1,3,16,128]{5,4,3,2,1,0:T(8,128)(2,1)}) custom-call(bf16[4,8,1,3,16,128]{5,4,3,2,1,0:T(8,128)(2,1)} %bitcast.52, bf16[512,128]{1,0:T(8,128)(2,1)} %constant.32.clone.refs_1_, bf16[12,12,32,128]{3,2,1,0:T(8,128)(2,1)} %reshape.142.refs_9_.refs_2_), custom_call_target="tpu_custom_call" | custom-call | flops 872415232 | bytes 3407872 | tf_op jit(solution)/shard_map/pallas_call | solution.py:68
  194.8 16.5 %all_to_all.22 = bf16[32,3,16,128]{3,2,1,0:T(8,128)(2,1)} all-to-all(bf16[32,3,16,128]{3,2,1,0:T(8,128)(2,1)} %bitcast.53), channel_id=1, replica_groups=mesh['parts'=1,'gx'=4,'gy'=4,'gz'=2] {'gx','gy','gz'}, dimensions={0} | all-to-all | bytes 786432 | tf_op jit(solution)/shard_map/all_to_all | solution.py:341
  211.3 2.8 %shard_map.116 = (bf16[4,12,16,128]{3,2,1,0:T(8,128)(2,1)}, bf16[4,12,16,128]{3,2,1,0:T(8,128)(2,1)}, bf16[4,12,16,128]{3,2,1,0:T(8,128)(2,1)}, bf16[4,12,16,128...) custom-call(bf16[4,8,3,16,128]{4,3,2,1,0:T(8,128)(2,1)} %bitcast.50,, ...), custom_call_target="tpu_custom_call" | custom-call | flops 268435456 | bytes 1048576 | tf_op jit(solution)/shard_map/pallas_call | solution.py:68
  214.7 1.5 collective-permute-start.26
  216.2 1.0 collective-permute-start.23
  217.6 5.5 %shard_map.122 = f32[4,8,12,12,4,32]{5,4,3,2,1,0:T(4,128)} custom-call(bf16[12,32,128]{2,1,0:T(8,128)(2,1)} %get-tuple-element.82.refs_0_, bf16[12,32,128]{2,1,0:T(8,128)(2,1)} %get-tuple-element.83.refs_1_), custom_call_target="tpu_custom_call" | custom-call | flops 589824 | bytes 9437184 | tf_op jit(solution)/shard_map/pallas_call | solution.py:68
  223.1 4.2 %shard_map.117.refs_5_ = bf16[8,12,32,16,128]{4,3,2,1,0:T(8,128)(2,1)} custom-call(s32[8]{0:T(128)} %iota_xor_fusion.refs_0_, bf16[8,12,32,16,128]{4,3,2,1,0:T(8,128)(2,1)} %get-tuple-element.64.refs_1_, bf16[192,192]{1,0:T(8,128)(2,1)} %mul.51.refs_11_.refs_2_, bf16[128,1024]{1,0:T(8,128)(2,1)} %constant.30.clone.refs_4_.refs_3_, bf16[4,192,128]{2,1,0:T(8,128)(2,1)} %bitcast.66), custom_call_target="tpu_custom_call" | custom-call | flops 503316480 | bytes 3342336 | tf_op jit(solution)/shard_map/pallas_call | solution.py:68
  227.3 1.5 collective-permute-start.21
  228.7 1.7 collective-permute-start.22
  230.4 4.1 %shard_map.118.refs_6_ = bf16[8,12,32,16,128]{4,3,2,1,0:T(8,128)(2,1)} custom-call(s32[8]{0:T(128)} %iota_xor_fusion.refs_0_, bf16[8,12,32,16,128]{4,3,2,1,0:T(8,128)(2,1)} %get-tuple-element.64.refs_1_, bf16[192,192]{1,0:T(8,128)(2,1)} %mul.51.refs_11_.refs_2_, bf16[128,1024]{1,0:T(8,128)(2,1)} %constant.30.clone.refs_4_.refs_3_, ...), custom_call_target="tpu_custom_call", output_to_operand_aliasing={{}: (5, {})} | custom-call | flops 503316480 | bytes 3342336 | tf_op jit(solution)/shard_map/pallas_call | solution.py:68
  234.5 0.7 copy-done.8
  235.2 6.2 %shard_map.119.refs_6_ = bf16[8,12,32,16,128]{4,3,2,1,0:T(8,128)(2,1)} custom-call(s32[8]{0:T(128)} %iota_xor_fusion.refs_0_, bf16[8,12,32,16,128]{4,3,2,1,0:T(8,128)(2,1)} %get-tuple-element.64.refs_1_, bf16[192,192]{1,0:T(8,128)(2,1)} %mul.51.refs_11_.refs_2_, bf16[128,1024]{1,0:T(8,128)(2,1)} %constant.30.clone.refs_4_.refs_3_, ...), custom_call_target="tpu_custom_call", output_to_operand_aliasing={{}: (6, {})} | custom-call | flops 1006632960 | bytes 6684672 | tf_op jit(solution)/shard_map/pallas_call | solution.py:68
  241.4 0.6 copy-done.5
  242.1 6.2 %shard_map.120.refs_6_ = bf16[8,12,32,16,128]{4,3,2,1,0:T(8,128)(2,1)} custom-call(s32[8]{0:T(128)} %iota_xor_fusion.refs_0_, bf16[8,12,32,16,128]{4,3,2,1,0:T(8,128)(2,1)} %get-tuple-element.64.refs_1_, bf16[192,192]{1,0:T(8,128)(2,1)} %mul.51.refs_11_.refs_2_, bf16[128,1024]{1,0:T(8,128)(2,1)} %constant.30.clone.refs_4_.refs_3_, ...), custom_call_target="tpu_custom_call", output_to_operand_aliasing={{}: (6, {})} | custom-call | flops 1006632960 | bytes 6684672 | tf_op jit(solution)/shard_map/pallas_call | solution.py:68
  248.3 0.6 copy-done.7
  249.0 6.2 %shard_map.121 = bf16[8,12,32,16,128]{4,3,2,1,0:T(8,128)(2,1)} custom-call(s32[8]{0:T(128)} %iota_xor_fusion.refs_0_, bf16[8,12,32,16,128]{4,3,2,1,0:T(8,128)(2,1)} %get-tuple-element.64.refs_1_, bf16[192,192]{1,0:T(8,128)(2,1)} %mul.51.refs_11_.refs_2_, bf16[128,1024]{1,0:T(8,128)(2,1)} %constant.30.clone.refs_4_.refs_3_, ...), custom_call_target="tpu_custom_call", output_to_operand_aliasing={{}: (6, {})} | custom-call | flops 1006632960 | bytes 6684672 | tf_op jit(solution)/shard_map/pallas_call | solution.py:68
  (112 shorter events, 3.9 us)
Async XLA Ops:
  1.2 17.7 %copy-start.23 = (bf16[12,12]{1,0:T(8,128)(2,1)S(1)}, bf16[12,12]{1,0:T(8,128)(2,1)}, u32[]{:S(2)}) copy-start(bf16[12,12]{1,0:T(8,128)(2,1)} %param.12) | copy-start | bytes 868
  7.6 9.4 %copy-start.18 = (bf16[4,192,128]{2,1,0:T(8,128)(2,1)S(1)}, bf16[4,192,128]{2,1,0:T(8,128)(2,1)}, u32[]{:S(2)}) copy-start(bf16[4,192,128]{2,1,0:T(8,128)(2,1)} %get-tuple-element.43.refs_3_) | copy-start | bytes 589828
  7.6 11.4 %copy-start.26 = (bf16[4,192,128]{2,1,0:T(8,128)(2,1)S(1)}, bf16[4,192,128]{2,1,0:T(8,128)(2,1)}, u32[]{:S(2)}) copy-start(bf16[4,192,128]{2,1,0:T(8,128)(2,1)} %get-tuple-element.49) | copy-start | bytes 589828
  7.6 15.4 %copy-start.24 = (bf16[4,192,128]{2,1,0:T(8,128)(2,1)S(1)}, bf16[4,192,128]{2,1,0:T(8,128)(2,1)}, u32[]{:S(2)}) copy-start(bf16[4,192,128]{2,1,0:T(8,128)(2,1)} %get-tuple-element.50) | copy-start | bytes 589828
  14.1 4.9 %collective-permute-start = (bf16[4,192,128]{2,1,0:T(8,128)(2,1)}, bf16[4,192,128]{2,1,0:T(8,128)(2,1)S(1)}, u32[]{:S(2)}, u32[]{:S(2)}) collective-permute-start(bf16[4,192,128]{2,1,0:T(8,128)(2,1)} %get-tuple-element.45), channel_id=1, source_target_pairs={{0,1},{1,0},{2,3},{3,2},{4,5},{5,4},{6,7},{7,6},{8,9},{9,8},{10,11... | collective-permute-start | bytes 589832 | tf_op jit(solution)/shard_map/ppermute | solution.py:346
  14.5 8.5 %collective-permute-start.1 = (bf16[4,192,128]{2,1,0:T(8,128)(2,1)}, bf16[4,192,128]{2,1,0:T(8,128)(2,1)S(1)}, u32[]{:S(2)}, u32[]{:S(2)}) collective-permute-start(bf16[4,192,128]{2,1,0:T(8,128)(2,1)} %get-tuple-element.46), channel_id=1, source_target_pairs={{0,2},{1,3},{2,0},{3,1},{4,6},{5,7},{6,4},{7,5},{8,10},{9,11},{10,... | collective-permute-start | bytes 589832 | tf_op jit(solution)/shard_map/ppermute | solution.py:346
  17.0 29.1 %collective-permute-start.3 = (bf16[4,192,128]{2,1,0:T(8,128)(2,1)S(1)}, bf16[4,192,128]{2,1,0:T(8,128)(2,1)S(1)}, u32[]{:S(2)}, u32[]{:S(2)}) collective-permute-start(bf16[4,192,128]{2,1,0:T(8,128)(2,1)S(1)} %copy-done.18), channel_id=1, source_target_pairs={{0,4},{1,5},{2,6},{3,7},{4,0},{5,1},{6,2},{7,3},{8,12},{9,13},{10,... | collective-permute-start | bytes 589832 | tf_op jit(solution)/shard_map/ppermute | solution.py:346
  18.6 27.6 %collective-permute-start.2 = (bf16[4,192,128]{2,1,0:T(8,128)(2,1)}, bf16[4,192,128]{2,1,0:T(8,128)(2,1)S(1)}, u32[]{:S(2)}, u32[]{:S(2)}) collective-permute-start(bf16[4,192,128]{2,1,0:T(8,128)(2,1)} %get-tuple-element.47), channel_id=1, source_target_pairs={{0,3},{1,2},{2,1},{3,0},{4,7},{5,6},{6,5},{7,4},{8,11},{9,10},{10,... | collective-permute-start | bytes 589832 | tf_op jit(solution)/shard_map/ppermute | solution.py:346
  18.6 27.5 %collective-permute-start.4 = (bf16[4,192,128]{2,1,0:T(8,128)(2,1)}, bf16[4,192,128]{2,1,0:T(8,128)(2,1)S(1)}, u32[]{:S(2)}, u32[]{:S(2)}) collective-permute-start(bf16[4,192,128]{2,1,0:T(8,128)(2,1)} %get-tuple-element.48), channel_id=1, source_target_pairs={{0,5},{1,4},{2,7},{3,6},{4,1},{5,0},{6,3},{7,2},{8,13},{9,12},{10,... | collective-permute-start | bytes 589832 | tf_op jit(solution)/shard_map/ppermute | solution.py:346
  19.0 27.3 %copy-start.15 = (bf16[4,192,128]{2,1,0:T(8,128)(2,1)}, bf16[4,192,128]{2,1,0:T(8,128)(2,1)S(1)}, u32[]{:S(2)}) copy-start(bf16[4,192,128]{2,1,0:T(8,128)(2,1)S(1)} %collective-permute-done) | copy-start | bytes 589828
  19.0 27.2 %collective-permute-start.5 = (bf16[4,192,128]{2,1,0:T(8,128)(2,1)S(1)}, bf16[4,192,128]{2,1,0:T(8,128)(2,1)S(1)}, u32[]{:S(2)}, u32[]{:S(2)}) collective-permute-start(bf16[4,192,128]{2,1,0:T(8,128)(2,1)S(1)} %copy-done.26), channel_id=1, source_target_pairs={{0,6},{1,7},{2,4},{3,5},{4,2},{5,3},{6,0},{7,1},{8,14},{9,15},{10,... | collective-permute-start | bytes 589832 | tf_op jit(solution)/shard_map/ppermute | solution.py:346
  23.0 23.3 %copy-start.16 = (bf16[4,192,128]{2,1,0:T(8,128)(2,1)}, bf16[4,192,128]{2,1,0:T(8,128)(2,1)S(1)}, u32[]{:S(2)}) copy-start(bf16[4,192,128]{2,1,0:T(8,128)(2,1)S(1)} %collective-permute-done.1) | copy-start | bytes 589828
  23.0 23.2 %collective-permute-start.6 = (bf16[4,192,128]{2,1,0:T(8,128)(2,1)S(1)}, bf16[4,192,128]{2,1,0:T(8,128)(2,1)S(1)}, u32[]{:S(2)}, u32[]{:S(2)}) collective-permute-start(bf16[4,192,128]{2,1,0:T(8,128)(2,1)S(1)} %copy-done.24), channel_id=1, source_target_pairs={{0,7},{1,6},{2,5},{3,4},{4,3},{5,2},{6,1},{7,0},{8,15},{9,14},{10,... | collective-permute-start | bytes 589832 | tf_op jit(solution)/shard_map/ppermute | solution.py:346
  46.2 0.7 copy-start.17
  46.2 0.8 copy-start.20
  46.2 0.9 copy-start.21
  46.2 0.9 copy-start.22
  70.9 15.8 %all-to-all-start.1 = ((bf16[32,3,16,128]{3,2,1,0:T(8,128)(2,1)}), bf16[32,3,16,128]{3,2,1,0:T(8,128)(2,1)S(1)}, u32[]{:S(2)}, u32[]{:S(2)}) async-start(bf16[32,3,16,128]{3,2,1,0:T(8,128)(2,1)} %bitcast.49), calls=%async_computation.1 | async-start | bytes 786432 | tf_op jit(solution)/shard_map/all_to_all | solution.py:341
  86.7 0.7 copy-start
  90.2 11.7 %collective-permute-start.12 = (bf16[4,12,16,128]{3,2,1,0:T(8,128)(2,1)}, bf16[4,12,16,128]{3,2,1,0:T(8,128)(2,1)S(1)}, u32[]{:S(2)}, u32[]{:S(2)}) collective-permute-start(bf16[4,12,16,128]{3,2,1,0:T(8,128)(2,1)} %get-tuple-element.57), channel_id=1, source_target_pairs={{0,2},{1,3},{2,0},{3,1},{4,6},{5,7},{6,4},{7,5},{8,10},{9,11},{10,... | collective-permute-start | bytes 589832 | tf_op jit(solution)/shard_map/ppermute | solution.py:346
  90.7 12.4 %collective-permute-start.13 = (bf16[4,12,16,128]{3,2,1,0:T(8,128)(2,1)}, bf16[4,12,16,128]{3,2,1,0:T(8,128)(2,1)S(1)}, u32[]{:S(2)}, u32[]{:S(2)}) collective-permute-start(bf16[4,12,16,128]{3,2,1,0:T(8,128)(2,1)} %get-tuple-element.58), channel_id=1, source_target_pairs={{0,3},{1,2},{2,1},{3,0},{4,7},{5,6},{6,5},{7,4},{8,11},{9,10},{10,... | collective-permute-start | bytes 589832 | tf_op jit(solution)/shard_map/ppermute | solution.py:346
  91.0 51.4 %collective-permute-start.7 = (bf16[4,12,16,128]{3,2,1,0:T(8,128)(2,1)}, bf16[4,12,16,128]{3,2,1,0:T(8,128)(2,1)S(1)}, u32[]{:S(2)}, u32[]{:S(2)}) collective-permute-start(bf16[4,12,16,128]{3,2,1,0:T(8,128)(2,1)} %get-tuple-element.52), channel_id=1, source_target_pairs={{0,1},{1,0},{2,3},{3,2},{4,5},{5,4},{6,7},{7,6},{8,9},{9,8},{10,11... | collective-permute-start | bytes 589832 | tf_op jit(solution)/shard_map/ppermute | solution.py:346
  92.4 37.9 %collective-permute-start.8 = (bf16[4,12,16,128]{3,2,1,0:T(8,128)(2,1)}, bf16[4,12,16,128]{3,2,1,0:T(8,128)(2,1)S(1)}, u32[]{:S(2)}, u32[]{:S(2)}) collective-permute-start(bf16[4,12,16,128]{3,2,1,0:T(8,128)(2,1)} %get-tuple-element.53), channel_id=1, source_target_pairs={{0,6},{1,7},{2,4},{3,5},{4,2},{5,3},{6,0},{7,1},{8,14},{9,15},{10,... | collective-permute-start | bytes 589832 | tf_op jit(solution)/shard_map/ppermute | solution.py:346
  93.8 36.5 %collective-permute-start.9 = (bf16[4,12,16,128]{3,2,1,0:T(8,128)(2,1)}, bf16[4,12,16,128]{3,2,1,0:T(8,128)(2,1)S(1)}, u32[]{:S(2)}, u32[]{:S(2)}) collective-permute-start(bf16[4,12,16,128]{3,2,1,0:T(8,128)(2,1)} %get-tuple-element.54), channel_id=1, source_target_pairs={{0,7},{1,6},{2,5},{3,4},{4,3},{5,2},{6,1},{7,0},{8,15},{9,14},{10,... | collective-permute-start | bytes 589832 | tf_op jit(solution)/shard_map/ppermute | solution.py:346
  94.6 7.3 %copy-start.37 = (bf16[4,12,16,128]{3,2,1,0:T(8,128)(2,1)S(1)}, bf16[4,12,16,128]{3,2,1,0:T(8,128)(2,1)}, u32[]{:S(2)}) copy-start(bf16[4,12,16,128]{3,2,1,0:T(8,128)(2,1)} %get-tuple-element.55) | copy-start | bytes 589828
  94.6 8.5 %copy-start.35 = (bf16[4,12,16,128]{3,2,1,0:T(8,128)(2,1)S(1)}, bf16[4,12,16,128]{3,2,1,0:T(8,128)(2,1)}, u32[]{:S(2)}) copy-start(bf16[4,12,16,128]{3,2,1,0:T(8,128)(2,1)} %get-tuple-element.56) | copy-start | bytes 589828
  101.9 2.3 copy-start.9
  101.9 13.7 %collective-permute-start.10 = (bf16[4,12,16,128]{3,2,1,0:T(8,128)(2,1)S(1)}, bf16[4,12,16,128]{3,2,1,0:T(8,128)(2,1)S(1)}, u32[]{:S(2)}, u32[]{:S(2)}) collective-permute-start(bf16[4,12,16,128]{3,2,1,0:T(8,128)(2,1)S(1)} %copy-done.37), channel_id=1, source_target_pairs={{0,4},{1,5},{2,6},{3,7},{4,0},{5,1},{6,2},{7,3},{8,12},{9,13},{10,... | collective-permute-start | bytes 589832 | tf_op jit(solution)/shard_map/ppermute | solution.py:346
  103.1 1.1 copy-start.10
  103.1 15.1 %collective-permute-start.11 = (bf16[4,12,16,128]{3,2,1,0:T(8,128)(2,1)S(1)}, bf16[4,12,16,128]{3,2,1,0:T(8,128)(2,1)S(1)}, u32[]{:S(2)}, u32[]{:S(2)}) collective-permute-start(bf16[4,12,16,128]{3,2,1,0:T(8,128)(2,1)S(1)} %copy-done.35), channel_id=1, source_target_pairs={{0,5},{1,4},{2,7},{3,6},{4,1},{5,0},{6,3},{7,2},{8,13},{9,12},{10,... | collective-permute-start | bytes 589832 | tf_op jit(solution)/shard_map/ppermute | solution.py:346
  115.6 2.5 copy-start.13
  130.3 0.7 copy-start.3
  143.1 7.5 %copy-start.28 = (bf16[4,192,128]{2,1,0:T(8,128)(2,1)S(1)}, bf16[4,192,128]{2,1,0:T(8,128)(2,1)}, u32[]{:S(2)}) copy-start(bf16[4,192,128]{2,1,0:T(8,128)(2,1)} %get-tuple-element.67) | copy-start | bytes 589828
  143.1 8.7 %copy-start.25 = (bf16[4,192,128]{2,1,0:T(8,128)(2,1)S(1)}, bf16[4,192,128]{2,1,0:T(8,128)(2,1)}, u32[]{:S(2)}) copy-start(bf16[4,192,128]{2,1,0:T(8,128)(2,1)} %get-tuple-element.68) | copy-start | bytes 589828
  143.1 9.3 %copy-start.30 = (bf16[4,192,128]{2,1,0:T(8,128)(2,1)S(1)}, bf16[4,192,128]{2,1,0:T(8,128)(2,1)}, u32[]{:S(2)}) copy-start(bf16[4,192,128]{2,1,0:T(8,128)(2,1)} %get-tuple-element.69) | copy-start | bytes 589828
  143.1 10.2 %copy-start.27 = (bf16[4,192,128]{2,1,0:T(8,128)(2,1)S(1)}, bf16[4,192,128]{2,1,0:T(8,128)(2,1)}, u32[]{:S(2)}) copy-start(bf16[4,192,128]{2,1,0:T(8,128)(2,1)} %get-tuple-element.70) | copy-start | bytes 589828
  143.1 11.1 %copy-start.33 = (bf16[4,192,128]{2,1,0:T(8,128)(2,1)S(1)}, bf16[4,192,128]{2,1,0:T(8,128)(2,1)}, u32[]{:S(2)}) copy-start(bf16[4,192,128]{2,1,0:T(8,128)(2,1)} %get-tuple-element.71) | copy-start | bytes 589828
  143.2 15.2 %copy-start.32 = (bf16[4,192,128]{2,1,0:T(8,128)(2,1)S(1)}, bf16[4,192,128]{2,1,0:T(8,128)(2,1)}, u32[]{:S(2)}) copy-start(bf16[4,192,128]{2,1,0:T(8,128)(2,1)} %get-tuple-element.72) | copy-start | bytes 589828
  150.5 3.7 %collective-permute-start.14 = (bf16[4,192,128]{2,1,0:T(8,128)(2,1)}, bf16[4,192,128]{2,1,0:T(8,128)(2,1)S(1)}, u32[]{:S(2)}, u32[]{:S(2)}) collective-permute-start(bf16[4,192,128]{2,1,0:T(8,128)(2,1)} %get-tuple-element.66), channel_id=1, source_target_pairs={{0,1},{1,0},{2,3},{3,2},{4,5},{5,4},{6,7},{7,6},{8,9},{9,8},{10,11... | collective-permute-start | bytes 589832 | tf_op jit(solution)/shard_map/ppermute | solution.py:346
  150.7 7.7 %collective-permute-start.15 = (bf16[4,192,128]{2,1,0:T(8,128)(2,1)S(1)}, bf16[4,192,128]{2,1,0:T(8,128)(2,1)S(1)}, u32[]{:S(2)}, u32[]{:S(2)}) collective-permute-start(bf16[4,192,128]{2,1,0:T(8,128)(2,1)S(1)} %copy-done.28), channel_id=1, source_target_pairs={{0,2},{1,3},{2,0},{3,1},{4,6},{5,7},{6,4},{7,5},{8,10},{9,11},{10,... | collective-permute-start | bytes 589832 | tf_op jit(solution)/shard_map/ppermute | solution.py:346
  151.8 9.7 %collective-permute-start.16 = (bf16[4,192,128]{2,1,0:T(8,128)(2,1)S(1)}, bf16[4,192,128]{2,1,0:T(8,128)(2,1)S(1)}, u32[]{:S(2)}, u32[]{:S(2)}) collective-permute-start(bf16[4,192,128]{2,1,0:T(8,128)(2,1)S(1)} %copy-done.25), channel_id=1, source_target_pairs={{0,3},{1,2},{2,1},{3,0},{4,7},{5,6},{6,5},{7,4},{8,11},{9,10},{10,... | collective-permute-start | bytes 589832 | tf_op jit(solution)/shard_map/ppermute | solution.py:346
  152.4 9.1 %collective-permute-start.17 = (bf16[4,192,128]{2,1,0:T(8,128)(2,1)S(1)}, bf16[4,192,128]{2,1,0:T(8,128)(2,1)S(1)}, u32[]{:S(2)}, u32[]{:S(2)}) collective-permute-start(bf16[4,192,128]{2,1,0:T(8,128)(2,1)S(1)} %copy-done.30), channel_id=1, source_target_pairs={{0,4},{1,5},{2,6},{3,7},{4,0},{5,1},{6,2},{7,3},{8,12},{9,13},{10,... | collective-permute-start | bytes 589832 | tf_op jit(solution)/shard_map/ppermute | solution.py:346
  153.4 18.5 %collective-permute-start.18 = (bf16[4,192,128]{2,1,0:T(8,128)(2,1)S(1)}, bf16[4,192,128]{2,1,0:T(8,128)(2,1)S(1)}, u32[]{:S(2)}, u32[]{:S(2)}) collective-permute-start(bf16[4,192,128]{2,1,0:T(8,128)(2,1)S(1)} %copy-done.27), channel_id=1, source_target_pairs={{0,5},{1,4},{2,7},{3,6},{4,1},{5,0},{6,3},{7,2},{8,13},{9,12},{10,... | collective-permute-start | bytes 589832 | tf_op jit(solution)/shard_map/ppermute | solution.py:346
  154.2 17.6 %copy-start.34 = (bf16[4,192,128]{2,1,0:T(8,128)(2,1)}, bf16[4,192,128]{2,1,0:T(8,128)(2,1)S(1)}, u32[]{:S(2)}) copy-start(bf16[4,192,128]{2,1,0:T(8,128)(2,1)S(1)} %collective-permute-done.14) | copy-start | bytes 589828
  154.2 17.6 %collective-permute-start.19 = (bf16[4,192,128]{2,1,0:T(8,128)(2,1)S(1)}, bf16[4,192,128]{2,1,0:T(8,128)(2,1)S(1)}, u32[]{:S(2)}, u32[]{:S(2)}) collective-permute-start(bf16[4,192,128]{2,1,0:T(8,128)(2,1)S(1)} %copy-done.33), channel_id=1, source_target_pairs={{0,6},{1,7},{2,4},{3,5},{4,2},{5,3},{6,0},{7,1},{8,14},{9,15},{10,... | collective-permute-start | bytes 589832 | tf_op jit(solution)/shard_map/ppermute | solution.py:346
  158.4 13.5 %copy-start.36 = (bf16[4,192,128]{2,1,0:T(8,128)(2,1)}, bf16[4,192,128]{2,1,0:T(8,128)(2,1)S(1)}, u32[]{:S(2)}) copy-start(bf16[4,192,128]{2,1,0:T(8,128)(2,1)S(1)} %collective-permute-done.15) | copy-start | bytes 589828
  158.4 13.4 %collective-permute-start.20 = (bf16[4,192,128]{2,1,0:T(8,128)(2,1)S(1)}, bf16[4,192,128]{2,1,0:T(8,128)(2,1)S(1)}, u32[]{:S(2)}, u32[]{:S(2)}) collective-permute-start(bf16[4,192,128]{2,1,0:T(8,128)(2,1)S(1)} %copy-done.32), channel_id=1, source_target_pairs={{0,7},{1,6},{2,5},{3,4},{4,3},{5,2},{6,1},{7,0},{8,15},{9,14},{10,... | collective-permute-start | bytes 589832 | tf_op jit(solution)/shard_map/ppermute | solution.py:346
  161.5 10.4 %copy-start.38 = (bf16[4,192,128]{2,1,0:T(8,128)(2,1)}, bf16[4,192,128]{2,1,0:T(8,128)(2,1)S(1)}, u32[]{:S(2)}) copy-start(bf16[4,192,128]{2,1,0:T(8,128)(2,1)S(1)} %collective-permute-done.16) | copy-start | bytes 589828
  161.5 10.4 %copy-start.39 = (bf16[4,192,128]{2,1,0:T(8,128)(2,1)}, bf16[4,192,128]{2,1,0:T(8,128)(2,1)S(1)}, u32[]{:S(2)}) copy-start(bf16[4,192,128]{2,1,0:T(8,128)(2,1)S(1)} %collective-permute-done.17) | copy-start | bytes 589828
  171.8 0.7 copy-start.41
  171.8 0.8 copy-start.42
  214.1 13.2 %collective-permute-start.25 = (bf16[4,12,16,128]{3,2,1,0:T(8,128)(2,1)}, bf16[4,12,16,128]{3,2,1,0:T(8,128)(2,1)S(1)}, u32[]{:S(2)}, u32[]{:S(2)}) collective-permute-start(bf16[4,12,16,128]{3,2,1,0:T(8,128)(2,1)} %get-tuple-element.78), channel_id=1, source_target_pairs={{0,2},{1,3},{2,0},{3,1},{4,6},{5,7},{6,4},{7,5},{8,10},{9,11},{10,... | collective-permute-start | bytes 589832 | tf_op jit(solution)/shard_map/ppermute | solution.py:346
  214.5 14.2 %collective-permute-start.27 = (bf16[4,12,16,128]{3,2,1,0:T(8,128)(2,1)}, bf16[4,12,16,128]{3,2,1,0:T(8,128)(2,1)S(1)}, u32[]{:S(2)}, u32[]{:S(2)}) collective-permute-start(bf16[4,12,16,128]{3,2,1,0:T(8,128)(2,1)} %get-tuple-element.80), channel_id=1, source_target_pairs={{0,1},{1,0},{2,3},{3,2},{4,5},{5,4},{6,7},{7,6},{8,9},{9,8},{10,11... | collective-permute-start | bytes 589832 | tf_op jit(solution)/shard_map/ppermute | solution.py:346
  214.7 19.8 %collective-permute-start.26 = (bf16[4,12,16,128]{3,2,1,0:T(8,128)(2,1)}, bf16[4,12,16,128]{3,2,1,0:T(8,128)(2,1)S(1)}, u32[]{:S(2)}, u32[]{:S(2)}) collective-permute-start(bf16[4,12,16,128]{3,2,1,0:T(8,128)(2,1)} %get-tuple-element.79), channel_id=1, source_target_pairs={{0,3},{1,2},{2,1},{3,0},{4,7},{5,6},{6,5},{7,4},{8,11},{9,10},{10,... | collective-permute-start | bytes 589832 | tf_op jit(solution)/shard_map/ppermute | solution.py:346
  216.2 25.1 %collective-permute-start.23 = (bf16[4,12,16,128]{3,2,1,0:T(8,128)(2,1)}, bf16[4,12,16,128]{3,2,1,0:T(8,128)(2,1)S(1)}, u32[]{:S(2)}, u32[]{:S(2)}) collective-permute-start(bf16[4,12,16,128]{3,2,1,0:T(8,128)(2,1)} %get-tuple-element.76), channel_id=1, source_target_pairs={{0,4},{1,5},{2,6},{3,7},{4,0},{5,1},{6,2},{7,3},{8,12},{9,13},{10,... | collective-permute-start | bytes 589832 | tf_op jit(solution)/shard_map/ppermute | solution.py:346
  217.2 24.2 %collective-permute-start.24 = (bf16[4,12,16,128]{3,2,1,0:T(8,128)(2,1)}, bf16[4,12,16,128]{3,2,1,0:T(8,128)(2,1)S(1)}, u32[]{:S(2)}, u32[]{:S(2)}) collective-permute-start(bf16[4,12,16,128]{3,2,1,0:T(8,128)(2,1)} %get-tuple-element.77), channel_id=1, source_target_pairs={{0,5},{1,4},{2,7},{3,6},{4,1},{5,0},{6,3},{7,2},{8,13},{9,12},{10,... | collective-permute-start | bytes 589832 | tf_op jit(solution)/shard_map/ppermute | solution.py:346
  223.1 4.2 %copy-start.31 = (bf16[4,12,16,128]{3,2,1,0:T(8,128)(2,1)S(1)}, bf16[4,12,16,128]{3,2,1,0:T(8,128)(2,1)}, u32[]{:S(2)}) copy-start(bf16[4,12,16,128]{3,2,1,0:T(8,128)(2,1)} %get-tuple-element.74) | copy-start | bytes 589828
  223.1 5.7 %copy-start.29 = (bf16[4,12,16,128]{3,2,1,0:T(8,128)(2,1)S(1)}, bf16[4,12,16,128]{3,2,1,0:T(8,128)(2,1)}, u32[]{:S(2)}) copy-start(bf16[4,12,16,128]{3,2,1,0:T(8,128)(2,1)} %get-tuple-element.75) | copy-start | bytes 589828
  227.3 7.2 %copy-start.4 = (bf16[4,12,16,128]{3,2,1,0:T(8,128)(2,1)}, bf16[4,12,16,128]{3,2,1,0:T(8,128)(2,1)S(1)}, u32[]{:S(2)}) copy-start(bf16[4,12,16,128]{3,2,1,0:T(8,128)(2,1)S(1)} %collective-permute-done.25) | copy-start | bytes 589828
  227.3 21.0 %collective-permute-start.21 = (bf16[4,12,16,128]{3,2,1,0:T(8,128)(2,1)S(1)}, bf16[4,12,16,128]{3,2,1,0:T(8,128)(2,1)S(1)}, u32[]{:S(2)}, u32[]{:S(2)}) collective-permute-start(bf16[4,12,16,128]{3,2,1,0:T(8,128)(2,1)S(1)} %copy-done.31), channel_id=1, source_target_pairs={{0,6},{1,7},{2,4},{3,5},{4,2},{5,3},{6,0},{7,1},{8,14},{9,15},{10,... | collective-permute-start | bytes 589832 | tf_op jit(solution)/shard_map/ppermute | solution.py:346
  228.7 1.7 copy-start.11
  228.7 19.5 %collective-permute-start.22 = (bf16[4,12,16,128]{3,2,1,0:T(8,128)(2,1)S(1)}, bf16[4,12,16,128]{3,2,1,0:T(8,128)(2,1)S(1)}, u32[]{:S(2)}, u32[]{:S(2)}) collective-permute-start(bf16[4,12,16,128]{3,2,1,0:T(8,128)(2,1)S(1)} %copy-done.29), channel_id=1, source_target_pairs={{0,7},{1,6},{2,5},{3,4},{4,3},{5,2},{6,1},{7,0},{8,15},{9,14},{10,... | collective-permute-start | bytes 589832 | tf_op jit(solution)/shard_map/ppermute | solution.py:346
  241.4 0.7 copy-start.6
  248.3 0.7 copy-start.12
  (8 other events, 5.4 us)

commit v5 on v4

--- a/solution.py
+++ b/solution.py
@@ -51,7 +51,7 @@
 ANY = pl.BlockSpec(memory_space=pl.ANY)
 
 
-def call(body, grid, in_specs, out_specs, out_shape, flops, moved, args, order=None, scratch=(), aliases={}, after=()):
+def call(body, grid, in_specs, out_specs, out_shape, args, order=None, scratch=(), aliases={}, after=()):
     lead = 0 if order is None else 1
     count = lead + len(args)
 
@@ -70,8 +70,8 @@
         grid_spec=spec,
         out_shape=out_shape,
         input_output_aliases={lead + operand: out for operand, out in aliases.items()},
-        compiler_params=pltpu.CompilerParams(vmem_limit_bytes=60 * 1024 * 1024),
-        cost_estimate=pl.CostEstimate(flops=int(flops), bytes_accessed=int(moved), transcendentals=0),
+        compiler_params=pltpu.CompilerParams(vmem_limit_bytes=52 * 1024 * 1024),
+        cost_estimate=pl.CostEstimate(flops=0, bytes_accessed=0, transcendentals=0),
     )(*(() if order is None else (order,)), *args, *after)
 
 
@@ -208,6 +208,8 @@
             first = (h * groups + k) * members
             done = dot(stacked, table_ref[...], 0, 0).astype(jnp.bfloat16)
             modes_ref[first : first + members] = done.reshape(members, span, lanes)
+    held = weight_ref.shape[:1] + weight_ref.shape[3:]
+    modes = [modes_ref[c].astype(jnp.float32).reshape(held) for c in range(channels)]
     for h in range(c_pieces):
         for k in range(groups):
             mixed = []
@@ -215,14 +217,18 @@
                 to = (h * groups + k) * members + m
                 total = 0.0
                 for of in range(channels):
-                    weight = weight_ref[to, of] if back else weight_ref[of, to]
-                    total += weight.astype(jnp.float32) * modes_ref[of].astype(jnp.float32)
-                mixed.append(total.astype(jnp.bfloat16))
+                    weight = weight_ref[:, to, of] if back else weight_ref[:, of, to]
+                    total += weight.astype(jnp.float32) * modes[of]
+                mixed.append(total.reshape(span, lanes).astype(jnp.bfloat16))
             done = dot(table_ref[...], jnp.concatenate(mixed, axis=0), 1, 1).astype(jnp.bfloat16)
             for g in range(planes):
                 for x in range(x_pieces):
                     start = (g * x_pieces + x) * height
                     out_ref[g, x, h, k] = done[start : start + height]
+
+
+def weight_body(weight_ref, out_ref):
+    out_ref[0] = jnp.concatenate([weight_ref[j, 0] for j in range(weight_ref.shape[0])], axis=-1)
 
 
 def outer_product_body(left_ref, right_ref, out_ref):
@@ -276,8 +282,6 @@
 
     block_head = jax.ShapeDtypeStruct((x_piece, rows, lanes), bf16)
     full_field = jax.ShapeDtypeStruct(state_field.shape, bf16)
-    field_bytes, head_bytes = 2 * state_field.size // blocks, 2 * math.prod(block_head.shape)
-    head_flops, mix_flops = head_bytes * steps * depth, field_bytes * rows
     held = pltpu.VMEM(block_head.shape, bf16)
     head_step, step = math.gcd(x_piece, 4), math.gcd(x_piece, 2)
 
@@ -294,10 +298,10 @@
         return call(
             functools.partial(head_body, sub), (count * sub,), [grouped(first, head_step), whole(ana.shape)],
             [whole(block_head.shape)] * count, [block_head] * count,
-            count * head_flops, count * (field_bytes + head_bytes), (state_field, ana), order, [held], after=after,
-        )
-
-    def inner_call(first, count, middle, grads):
+            (state_field, ana), order, [held], after=after,
+        )
+
+    def inner_call(first, count, middle, grads, after):
         sub = x_piece // step
         tables = (mix_up, syn, ana)
         spec = grouped(first, step)
@@ -305,9 +309,8 @@
             functools.partial(inner_body, sub, count), (count * sub,),
             [spec] * 2 + [whole(arg.shape) for arg in tables] + [whole(block_head.shape)] * count + [ANY] * len(grads),
             [spec] + [whole(block_head.shape)] * count, [full_field] + [block_head] * count,
-            2 * count * (2 * head_flops + mix_flops), count * (3 * field_bytes + 2 * head_bytes),
             (state_field, cotangent, *tables, *middle[first : first + count], *grads), order, [held, held],
-            {5 + count: 0} if grads else {},
+            {5 + count: 0} if grads else {}, after,
         )
         return done[:1], done[1:]
 
@@ -318,17 +321,15 @@
         return call(
             functools.partial(outer_body, sub, count), (count * sub,),
             [spec] + [whole(arg.shape) for arg in tables] + [whole(block_head.shape)] * count + [ANY] * len(field),
-            [spec], [full_field], count * (head_flops + mix_flops), count * (2 * field_bytes + head_bytes),
+            [spec], [full_field],
             (*grads, *tables, *middle[first : first + count], *field), order, [held],
             {3 + count: 0} if field else {},
         )
 
     def small(body, outs, *args, after=()):
         shapes = [jax.ShapeDtypeStruct(out, bf16) for out in outs]
-        size = sum(arg.size for arg in args)
         return call(
-            body, (1,), [whole(arg.shape) for arg in args], [whole(out) for out in outs], shapes, 1024 * size, 4 * size, args,
-            after=after,
+            body, (1,), [whole(arg.shape) for arg in args], [whole(out) for out in outs], shapes, args, after=after
         )
 
     span = q_local * time_modes
@@ -340,48 +341,63 @@
         pieces = pieces.reshape((x_devices * y_devices,) + packed[2:])
         return lax.all_to_all(pieces, ("gx",) + YZ, 0, 0, tiled=True).reshape(shape)
 
-    def swap(pieces, count, shape):
-        if paired:
-            pairs = [[(d, d ^ k) for d in range(y_devices)] for k in range(y_devices)]
-            pieces = [lax.ppermute(piece, YZ, pairs[k]) if k else piece for k, piece in enumerate(pieces)]
-        else:
+    def send(k, piece):
+        if not (paired and k):
+            return piece
+        return lax.ppermute(piece, YZ, [(d, d ^ k) for d in range(y_devices)])
+
+    def settle(pieces, count, shape):
+        if not paired:
             pieces = jnp.stack(pieces).reshape(y_devices, -1, lanes)
             pieces = lax.all_to_all(pieces, YZ, 0, 0, tiled=True).reshape((count,) + shape)
         return [pieces[k].reshape(shape) for k in range(count)]
 
-    def spectral(back, heads, weight, after=()):
-        cells = (x_piece, c_piece, y_local, lanes)
-        (part,) = small(y_down_body, [packed], y_mat, *swap(heads, y_devices, cells), after=after)
+    cells = (x_piece, c_piece, y_local, lanes)
+
+    def analyze(back, heads, weight, after):
+        (part,) = small(y_down_body, [packed], y_mat, *settle(heads, y_devices, cells), after=after)
         part = exchange(part).reshape((x_devices, x_pieces, c_pieces) + packed[2:])
         kept, part = small(
             functools.partial(spectral_body, back), [(channels, span, j_local * modes), part.shape], part, x_mat, weight
         )
-        part = exchange(part).reshape(packed)
-        pieces = small(y_up_body, [cells] * y_devices, part, y_mat_t)
-        return swap(pieces, blocks, block_head.shape), kept
-
-    weight = jnp.transpose(spectral_weight, (2, 3, 1, 4, 0, 5)).reshape(channels, channels, span, j_local * modes)
+        return kept, exchange(part).reshape(packed)
+
+    def synthesize(part, after):
+        pieces = small(y_up_body, [cells] * y_devices, part, y_mat_t, after=after)
+        pieces = [send(k, piece) for k, piece in enumerate(pieces)]
+        return settle(pieces, blocks, block_head.shape)
+
+    weight = call(
+        weight_body, (q_local,),
+        [pl.BlockSpec((j_local, 1, channels, channels, time_modes, modes), lambda q: (0, q, 0, 0, 0, 0))],
+        pl.BlockSpec((1, channels, channels, time_modes, j_local * modes), lambda q: (q, 0, 0, 0, 0)),
+        jax.ShapeDtypeStruct((q_local, channels, channels, time_modes, j_local * modes), bf16), (spectral_weight,),
+    )
 
     heads, after = [None] * blocks, ()
-    half = -(-blocks // 2)
-    for first, count in ((half, blocks - half), (0, half)):
-        if count:
-            heads[first : first + count] = head_call(first, count, after)
-            after = (heads[first],)
-    middle, modes_in = spectral(False, heads, weight, (weight, mix_up, mix_back))
-    grads = ()
+    for first, count in ((6, 2), (2, 4), (0, 2)) if blocks == 8 else ((0, blocks),):
+        done = head_call(first, count, after)
+        heads[first : first + count] = [send(first + e, piece) for e, piece in enumerate(done)]
+        after = (done[0],) if first == 6 else tuple(heads[6:])
+    modes_in, part = analyze(False, heads, weight, (weight, mix_up, mix_back, y_mat_t))
+    middle = synthesize(part, ())
+
+    grads, sent = (), [(), ()]
     for first, count in groups:
-        grads, heads[first : first + count] = inner_call(first, count, middle, grads)
-    middle, grad_modes = spectral(True, heads, weight)
+        grads, done = inner_call(first, count, middle, grads, sent[-2])
+        heads[first : first + count] = [send(first + e, piece) for e, piece in enumerate(done)]
+        sent.append(tuple(heads[max(first, 1) : first + count]) if paired else ())
+    grad_modes, part = analyze(True, heads, weight, ())
     spec = whole(modes_in.shape)
     grad_spectral = call(
         outer_product_body, (j_local,), [spec, spec],
         pl.BlockSpec((1,) + spectral_weight.shape[1:], lambda j: (j, 0, 0, 0, 0, 0)),
         jax.ShapeDtypeStruct(spectral_weight.shape, jnp.float32),
-        spectral_weight.size, 16 * spectral_weight.size, (modes_in, grad_modes),
-    )
+        (modes_in, grad_modes),
+    )
+    middle = synthesize(part, (grad_spectral,))
     field = ()
-    for first, count in sorted(groups):
+    for first, count in pairs:
         field = outer_call(first, count, middle, grads, field)
     return field[0], grad_spectral
 

time: 257 us -> 221 us (0.86)
  local copies, waits for them, and re-layouts: 29.5 us -> 8.07 us
  Pallas kernels: 111 us -> 104 us
  waiting for transfers between devices: 30.4 us -> 26.6 us
  starting transfers between devices: 31.6 us -> 28 us
    transpose x1 -> x0, local copies, waits for them, and re-layouts: 10.6 us -> none  [shards(): jnp.transpose(spectral_weight, (2, 3, 1, 4, 0, 5))]
    pallas_call x19 -> x20, Pallas kernels: 111 us -> 104 us  [call(): pl.pallas_call(placed, grid_spec=spec, out_shape=out_shape, input_output_...]
    reshape x1 -> x0, local copies, waits for them, and re-layouts: 6.44 us -> none  [shards(): jnp.transpose(spectral_weight, (2, 3, 1, 4, 0, 5))]
    unnamed x86 -> x14, local copies, waits for them, and re-layouts: 6.69 us -> 2.72 us
    ppermute x28, starting transfers between devices: 29 us -> 25.4 us  [send(): return lax.ppermute(piece, YZ, [(d, d ^ k) for d in range(y_devices)])]
    all_to_all x1, waiting for transfers between devices: 11.6 us -> 8.56 us  [exchange(): return lax.all_to_all(pieces, ('gx',) + YZ, 0, 0, tiled=True).reshape(shape)]
  transfers between devices with their start and end apart: 29 -> 29, of which waited for: 6 -> 6; matrix products, arithmetic and copies ran while one was open for 9% -> 3% of each run, Pallas kernels for 26% -> 35%
where the time goes in v5:
time: 221 us; the launch traced here: 218 us
  Pallas kernels  104 us (47%)
  blocking collectives  49.4 us (22%)
  starting transfers between devices  28 us (13%)
  waiting for transfers between devices  26.6 us (12%)
  local copies, waits for them, and re-layouts  8.07 us (4%)
    pallas_call x20, Pallas kernels, call(): pl.pallas_call(placed, grid_spec=spec, out_shape=out_shape, input_output_...  104 us
    all_to_all x3, blocking collectives, exchange(): return lax.all_to_all(pieces, ('gx',) + YZ, 0, 0, tiled=True).reshape(shape)  49.4 us
    ppermute x28, starting transfers between devices, send(): return lax.ppermute(piece, YZ, [(d, d ^ k) for d in range(y_devices)])  25.4 us
    ppermute x28, waiting for transfers between devices, send(): return lax.ppermute(piece, YZ, [(d, d ^ k) for d in range(y_devices)])  18 us
    all_to_all x1, waiting for transfers between devices, exchange(): return lax.all_to_all(pieces, ('gx',) + YZ, 0, 0, tiled=True).reshape(shape)  8.56 us
  transfers between devices with their start and end apart: 29, of which 6 were waited for; matrix products, arithmetic and copies ran while one was open for 3% of the time, Pallas kernels for 35%

profile of v5, /device:TPU:0, one launch (start us, length us, event | category | flops | bytes accessed | tf_op | source)
XLA Modules:
  0.0 218.5 jit_solution(14444444774801872868)
XLA Ops:
  0.7 0.9 copy-done.2
  1.6 3.2 %shard_map.104 = (bf16[4,192,128]{2,1,0:T(8,128)(2,1)S(1)}, bf16[4,192,128]{2,1,0:T(8,128)(2,1)S(1)}) custom-call(s32[8]{0:T(128)S(1)} %iota_xor_fusion.refs_0_, bf16[8,12,32,16,128]{4,3,2,1,0:T(8,128)(2,1)} %refs_1_.17, bf16[1024,128]{1,0:T(8,128)(2,1)S(1)} %copy-done.2), custom_call_target="tpu_custom_call" | custom-call | tf_op jit(solution)/shard_map/pallas_call | solution.py:68
  4.8 3.4 %collective-permute-start.1 = (bf16[4,192,128]{2,1,0:T(8,128)(2,1)S(1)}, bf16[4,192,128]{2,1,0:T(8,128)(2,1)S(1)}, u32[]{:S(2)}, u32[]{:S(2)}) collective-permute-start(bf16[4,192,128]{2,1,0:T(8,128)(2,1)S(1)} %get-tuple-element.44), channel_id=1, source_target_pairs={{0,7},{1,6},{2,5},{3,4},{4,3},{5,2},{6,1},{7,0},{8,15},{9,14},{10,... | collective-permute-start | bytes 589832 | tf_op jit(solution)/shard_map/ppermute | solution.py:347
  8.2 0.6 collective-permute-start
  8.8 5.3 %shard_map.106 = (bf16[4,192,128]{2,1,0:T(8,128)(2,1)S(1)}, bf16[4,192,128]{2,1,0:T(8,128)(2,1)S(1)}, bf16[4,192,128]{2,1,0:T(8,128)(2,1)S(1)}, bf16[4,192,128]{2,1,0:T(8,128)(2,1)S(1)}) custom-call(s32[8]{0:T(128)S(1)} %iota_xor_fusion.refs_0_, bf16[8,12,32,16,128]{4,3,2,1,0:T(8,128)(2,1)} %refs_1_.17, bf16[1024,128]{1,0:T(8,128)(2,1)S(1)} %copy-done.2, ...), custom_call_target="tpu_custom_call" | custom-call | tf_op jit(solution)/shard_map/pallas_call | solution.py:68
  14.2 1.4 collective-permute-start.3
  15.6 1.7 collective-permute-start.5
  17.4 0.1 copy.19
  17.5 7.1 %shard_map.107.refs_9_.refs_2_ = bf16[8,12,12,4,128]{4,3,2,1,0:T(4,128)(2,1)S(1)} custom-call(bf16[4,8,12,12,4,32]{5,4,3,2,1,0:T(4,128)(2,1)} %refs_0_.1), custom_call_target="tpu_custom_call" | custom-call | tf_op jit(solution)/shard_map/pallas_call | solution.py:68
  24.6 1.0 copy-done.1
  25.6 1.3 broadcast_multiply_fusion
  27.0 1.7 mul.51.refs_11_.refs_2_
  28.7 1.7 mul.48.refs_10_.refs_3_
  30.4 0.4 collective-permute-start.6
  30.8 3.2 %shard_map.105 = (bf16[4,192,128]{2,1,0:T(8,128)(2,1)S(1)}, bf16[4,192,128]{2,1,0:T(8,128)(2,1)S(1)}) custom-call(s32[8]{0:T(128)S(1)} %iota_xor_fusion.refs_0_, bf16[8,12,32,16,128]{4,3,2,1,0:T(8,128)(2,1)} %refs_1_.17, bf16[1024,128]{1,0:T(8,128)(2,1)S(1)} %copy-done.3, bf16[4,192,128]{2,1,0:T(8,128)(2,1)S(1)} %collective-permute-done.refs_3_, ...), custom_call_target="tpu_custom_call" | custom-call | tf_op jit(solution)/shard_map/pallas_call | solution.py:68
  34.0 0.1 collective-permute-start.2
  34.1 0.9 dynamic-slice_bitcast_fusion.refs_12_.refs_1_
  35.0 0.9 dynamic-slice_bitcast_fusion.1.refs_0_
  36.0 1.4 collective-permute-done.6
  37.4 1.4 shard_map.108
  38.8 17.9 %all_to_all.20 = bf16[32,3,16,128]{3,2,1,0:T(8,128)(2,1)S(1)} all-to-all(bf16[32,3,16,128]{3,2,1,0:T(8,128)(2,1)} %bitcast.83), channel_id=1, replica_groups=mesh['parts'=1,'gx'=4,'gy'=4,'gz'=2] {'gx','gy','gz'}, dimensions={0} | all-to-all | bytes 786432 | tf_op jit(solution)/shard_map/all_to_all | solution.py:342
  56.7 2.2 %shard_map.109 = (bf16[12,32,128]{2,1,0:T(8,128)(2,1)S(1)}, bf16[4,8,1,3,16,128]{5,4,3,2,1,0:T(8,128)(2,1)S(1)}) custom-call(bf16[4,8,1,3,16,128]{5,4,3,2,1,0:T(8,128)(2,1)S(1)} %bitcast.46, bf16[512,128]{1,0:T(8,128)(2,1)S(1)} %copy-done.4, bf16[8,12,12,4,128]{4,3,2,1,0:T(4,128)(2,1)} %copy-done.1), custom_call_target="tpu_custom_call" | custom-call | tf_op jit(solution)/shard_map/pallas_call | solution.py:68
  58.9 15.7 %all_to_all.21 = bf16[32,3,16,128]{3,2,1,0:T(8,128)(2,1)} all-to-all(bf16[32,3,16,128]{3,2,1,0:T(8,128)(2,1)S(1)} %bitcast.53), channel_id=1, replica_groups=mesh['parts'=1,'gx'=4,'gy'=4,'gz'=2] {'gx','gy','gz'}, dimensions={0} | all-to-all | bytes 786432 | tf_op jit(solution)/shard_map/all_to_all | solution.py:342
  74.7 1.7 shard_map.110
  76.3 0.6 collective-permute-start.12
  76.9 0.3 collective-permute-start.13
  77.2 1.1 collective-permute-start.10
  78.4 1.5 collective-permute-start.11
  79.9 1.4 collective-permute-start.8
  81.3 2.9 %collective-permute-done.12 = bf16[4,12,16,128]{3,2,1,0:T(8,128)(2,1)S(1)} collective-permute-done((bf16[4,12,16,128]{3,2,1,0:T(8,128)(2,1)S(1)}, bf16[4,12,16,128]{3,2,1,0:T(8,128)(2,1)S(1)}, u32[]{:S(2)}, u32[]{:S(2)}) %collective-permute-start.12) | collective-permute-done | bytes 196640 | tf_op jit(solution)/shard_map/ppermute | solution.py:347
  84.2 6.8 %shard_map.111 = (bf16[8,12,32,16,128]{4,3,2,1,0:T(8,128)(2,1)}, bf16[4,192,128]{2,1,0:T(8,128)(2,1)S(1)}) custom-call(s32[8]{0:T(128)S(1)} %iota_xor_fusion.refs_0_, bf16[8,12,32,16,128]{4,3,2,1,0:T(8,128)(2,1)} %refs_1_.17, bf16[8,12,32,16,128]{4,3,2,1,0:T(8,128)(2,1)} %refs_2_.12, bf16[192,192]{1,0:T(8,128)(2,1)S(1)} %mul.48.refs_10_.refs_3_, ...), custom_call_target="tpu_custom_call" | custom-call | tf_op jit(solution)/shard_map/pallas_call | solution.py:68
  91.1 1.5 collective-permute-start.7
  92.6 10.8 %shard_map.112 = (bf16[8,12,32,16,128]{4,3,2,1,0:T(8,128)(2,1)}, bf16[4,192,128]{2,1,0:T(8,128)(2,1)S(1)}, bf16[4,192,128]{2,1,0:T(8,128)(2,1)S(1)}) custom-call(s32[8]{0:T(128)S(1)} %iota_xor_fusion.refs_0_, bf16[8,12,32,16,128]{4,3,2,1,0:T(8,128)(2,1)} %refs_1_.17, bf16[8,12,32,16,128]{4,3,2,1,0:T(8,128)(2,1)} %refs_2_.12, ...), custom_call_target="tpu_custom_call", output_to_operand_aliasing={{0}: (8, {})} | custom-call | tf_op jit(solution)/shard_map/pallas_call | solution.py:68
  103.4 1.1 collective-permute-start.14
  104.5 0.3 collective-permute-start.15
  104.8 10.9 %shard_map.113 = (bf16[8,12,32,16,128]{4,3,2,1,0:T(8,128)(2,1)}, bf16[4,192,128]{2,1,0:T(8,128)(2,1)S(1)}, bf16[4,192,128]{2,1,0:T(8,128)(2,1)S(1)}) custom-call(s32[8]{0:T(128)S(1)} %iota_xor_fusion.refs_0_, bf16[8,12,32,16,128]{4,3,2,1,0:T(8,128)(2,1)} %refs_1_.17, bf16[8,12,32,16,128]{4,3,2,1,0:T(8,128)(2,1)} %refs_2_.12, ...), custom_call_target="tpu_custom_call", output_to_operand_aliasing={{0}: (8, {})} | custom-call | tf_op jit(solution)/shard_map/pallas_call | solution.py:68
  115.7 0.8 collective-permute-start.16
  116.5 1.3 collective-permute-start.17
  117.8 10.9 %shard_map.114 = (bf16[8,12,32,16,128]{4,3,2,1,0:T(8,128)(2,1)}, bf16[4,192,128]{2,1,0:T(8,128)(2,1)S(1)}, bf16[4,192,128]{2,1,0:T(8,128)(2,1)S(1)}) custom-call(s32[8]{0:T(128)S(1)} %iota_xor_fusion.refs_0_, bf16[8,12,32,16,128]{4,3,2,1,0:T(8,128)(2,1)} %refs_1_.17, bf16[8,12,32,16,128]{4,3,2,1,0:T(8,128)(2,1)} %refs_2_.12, ...), custom_call_target="tpu_custom_call", output_to_operand_aliasing={{0}: (8, {})} | custom-call | tf_op jit(solution)/shard_map/pallas_call | solution.py:68
  128.6 6.8 %shard_map.115 = (bf16[8,12,32,16,128]{4,3,2,1,0:T(8,128)(2,1)}, bf16[4,192,128]{2,1,0:T(8,128)(2,1)S(1)}) custom-call(s32[8]{0:T(128)S(1)} %iota_xor_fusion.refs_0_, bf16[8,12,32,16,128]{4,3,2,1,0:T(8,128)(2,1)} %refs_1_.17, bf16[8,12,32,16,128]{4,3,2,1,0:T(8,128)(2,1)} %refs_2_.12, ...), custom_call_target="tpu_custom_call", output_to_operand_aliasing={{0}: (7, {})} | custom-call | tf_op jit(solution)/shard_map/pallas_call | solution.py:68
  135.5 0.0 collective-permute-start.18
  135.5 1.5 collective-permute-start.19
  137.1 1.2 collective-permute-start.20
  138.3 5.9 %collective-permute-done.19 = bf16[4,192,128]{2,1,0:T(8,128)(2,1)S(1)} collective-permute-done((bf16[4,192,128]{2,1,0:T(8,128)(2,1)S(1)}, bf16[4,192,128]{2,1,0:T(8,128)(2,1)S(1)}, u32[]{:S(2)}, u32[]{:S(2)}) %collective-permute-start.19) | collective-permute-done | bytes 196640 | tf_op jit(solution)/shard_map/ppermute | solution.py:347
  144.1 3.3 %collective-permute-done.20 = bf16[4,192,128]{2,1,0:T(8,128)(2,1)S(1)} collective-permute-done((bf16[4,192,128]{2,1,0:T(8,128)(2,1)S(1)}, bf16[4,192,128]{2,1,0:T(8,128)(2,1)S(1)}, u32[]{:S(2)}, u32[]{:S(2)}) %collective-permute-start.20) | collective-permute-done | bytes 196640 | tf_op jit(solution)/shard_map/ppermute | solution.py:347
  147.5 1.4 shard_map.116
  148.9 15.8 %all_to_all.22 = bf16[32,3,16,128]{3,2,1,0:T(8,128)(2,1)S(1)} all-to-all(bf16[32,3,16,128]{3,2,1,0:T(8,128)(2,1)} %bitcast.82), channel_id=1, replica_groups=mesh['parts'=1,'gx'=4,'gy'=4,'gz'=2] {'gx','gy','gz'}, dimensions={0} | all-to-all | bytes 786432 | tf_op jit(solution)/shard_map/all_to_all | solution.py:342
  164.6 2.9 %shard_map.117 = (bf16[12,32,128]{2,1,0:T(8,128)(2,1)S(1)}, bf16[4,8,1,3,16,128]{5,4,3,2,1,0:T(8,128)(2,1)}) custom-call(bf16[4,8,1,3,16,128]{5,4,3,2,1,0:T(8,128)(2,1)S(1)} %bitcast.45, bf16[512,128]{1,0:T(8,128)(2,1)S(1)} %copy-done.4, bf16[8,12,12,4,128]{4,3,2,1,0:T(4,128)(2,1)} %copy-done.1), custom_call_target="tpu_custom_call" | custom-call | tf_op jit(solution)/shard_map/pallas_call | solution.py:68
  167.6 2.6 %all-to-all-start.3 = ((bf16[32,3,16,128]{3,2,1,0:T(8,128)(2,1)}), bf16[32,3,16,128]{3,2,1,0:T(8,128)(2,1)S(1)}, u32[]{:S(2)}, u32[]{:S(2)}) async-start(bf16[32,3,16,128]{3,2,1,0:T(8,128)(2,1)} %bitcast.33), calls=%async_computation.3 | async-start | bytes 786432 | tf_op jit(solution)/shard_map/all_to_all | solution.py:342
  170.2 4.6 %shard_map.118.refs_2_ = f32[4,8,12,12,4,32]{5,4,3,2,1,0:T(4,128)} custom-call(bf16[12,32,128]{2,1,0:T(8,128)(2,1)S(1)} %get-tuple-element.74.refs_0_, bf16[12,32,128]{2,1,0:T(8,128)(2,1)S(1)} %get-tuple-element.75.refs_1_), custom_call_target="tpu_custom_call" | custom-call | tf_op jit(solution)/shard_map/pallas_call | solution.py:68
  174.8 8.6 %all-to-all-done.3 = bf16[32,3,16,128]{3,2,1,0:T(8,128)(2,1)S(1)} async-done(((bf16[32,3,16,128]{3,2,1,0:T(8,128)(2,1)}), bf16[32,3,16,128]{3,2,1,0:T(8,128)(2,1)S(1)}, u32[]{:S(2)}, u32[]{:S(2)}) %all-to-all-start.3) | async-done | bytes 393248 | tf_op jit(solution)/shard_map/all_to_all | solution.py:342
  183.4 0.7 copy-done.5
  184.1 1.7 shard_map.119
  185.8 0.5 collective-permute-start.25
  186.3 0.2 collective-permute-start.27
  186.5 1.5 collective-permute-start.26
  188.0 1.0 collective-permute-start.23
  189.0 0.4 collective-permute-start.24
  189.3 4.3 %collective-permute-done.25 = bf16[4,12,16,128]{3,2,1,0:T(8,128)(2,1)S(1)} collective-permute-done((bf16[4,12,16,128]{3,2,1,0:T(8,128)(2,1)S(1)}, bf16[4,12,16,128]{3,2,1,0:T(8,128)(2,1)S(1)}, u32[]{:S(2)}, u32[]{:S(2)}) %collective-permute-start.25) | collective-permute-done | bytes 196640 | tf_op jit(solution)/shard_map/ppermute | solution.py:347
  193.7 1.4 collective-permute-start.21
  195.1 5.8 %shard_map.120.refs_6_ = bf16[8,12,32,16,128]{4,3,2,1,0:T(8,128)(2,1)} custom-call(s32[8]{0:T(128)S(1)} %iota_xor_fusion.refs_0_, bf16[8,12,32,16,128]{4,3,2,1,0:T(8,128)(2,1)} %get-tuple-element.68.refs_1_, bf16[192,192]{1,0:T(8,128)(2,1)S(1)} %mul.51.refs_11_.refs_2_, bf16[128,1024]{1,0:T(8,128)(2,1)S(1)} %copy-done, bf16[4,192,128]{2,1,0:T(8,128)(2,1)S(1)} %bitcast.59, ...), custom_call_target="tpu_custom_call" | custom-call | tf_op jit(solution)/shard_map/pallas_call | solution.py:68
  200.9 5.9 %shard_map.121.refs_6_ = bf16[8,12,32,16,128]{4,3,2,1,0:T(8,128)(2,1)} custom-call(s32[8]{0:T(128)S(1)} %iota_xor_fusion.refs_0_, bf16[8,12,32,16,128]{4,3,2,1,0:T(8,128)(2,1)} %get-tuple-element.68.refs_1_, bf16[192,192]{1,0:T(8,128)(2,1)S(1)} %mul.51.refs_11_.refs_2_, bf16[128,1024]{1,0:T(8,128)(2,1)S(1)} %copy-done, ...), custom_call_target="tpu_custom_call", output_to_operand_aliasing={{}: (6, {})} | custom-call | tf_op jit(solution)/shard_map/pallas_call | solution.py:68
  206.8 5.8 %shard_map.122.refs_6_ = bf16[8,12,32,16,128]{4,3,2,1,0:T(8,128)(2,1)} custom-call(s32[8]{0:T(128)S(1)} %iota_xor_fusion.refs_0_, bf16[8,12,32,16,128]{4,3,2,1,0:T(8,128)(2,1)} %get-tuple-element.68.refs_1_, bf16[192,192]{1,0:T(8,128)(2,1)S(1)} %mul.51.refs_11_.refs_2_, bf16[128,1024]{1,0:T(8,128)(2,1)S(1)} %copy-done, ...), custom_call_target="tpu_custom_call", output_to_operand_aliasing={{}: (6, {})} | custom-call | tf_op jit(solution)/shard_map/pallas_call | solution.py:68
  212.6 5.8 %shard_map.123 = bf16[8,12,32,16,128]{4,3,2,1,0:T(8,128)(2,1)} custom-call(s32[8]{0:T(128)S(1)} %iota_xor_fusion.refs_0_, bf16[8,12,32,16,128]{4,3,2,1,0:T(8,128)(2,1)} %get-tuple-element.68.refs_1_, bf16[192,192]{1,0:T(8,128)(2,1)S(1)} %mul.51.refs_11_.refs_2_, bf16[128,1024]{1,0:T(8,128)(2,1)S(1)} %copy-done, ...), custom_call_target="tpu_custom_call", output_to_operand_aliasing={{}: (6, {})} | custom-call | tf_op jit(solution)/shard_map/pallas_call | solution.py:68
  (39 shorter events, 0.1 us)
Async XLA Ops:
  0.6 1.0 copy-start.2
  1.6 15.8 %copy-start.6 = (bf16[12,12]{1,0:T(8,128)(2,1)S(1)}, bf16[12,12]{1,0:T(8,128)(2,1)}, u32[]{:S(2)}) copy-start(bf16[12,12]{1,0:T(8,128)(2,1)} %param.12) | copy-start | bytes 868
  4.8 26.0 %copy-start.3 = (bf16[1024,128]{1,0:T(8,128)(2,1)S(1)}, bf16[1024,128]{1,0:T(8,128)(2,1)}, u32[]{:S(2)}) copy-start(bf16[1024,128]{1,0:T(8,128)(2,1)} %constant.31.clone.refs_2_.refs_5_) | copy-start | bytes 786436
  4.8 25.6 %collective-permute-start.1 = (bf16[4,192,128]{2,1,0:T(8,128)(2,1)S(1)}, bf16[4,192,128]{2,1,0:T(8,128)(2,1)S(1)}, u32[]{:S(2)}, u32[]{:S(2)}) collective-permute-start(bf16[4,192,128]{2,1,0:T(8,128)(2,1)S(1)} %get-tuple-element.44), channel_id=1, source_target_pairs={{0,7},{1,6},{2,5},{3,4},{4,3},{5,2},{6,1},{7,0},{8,15},{9,14},{10,... | collective-permute-start | bytes 589832 | tf_op jit(solution)/shard_map/ppermute | solution.py:347
  8.2 22.6 %collective-permute-start = (bf16[4,192,128]{2,1,0:T(8,128)(2,1)S(1)}, bf16[4,192,128]{2,1,0:T(8,128)(2,1)S(1)}, u32[]{:S(2)}, u32[]{:S(2)}) collective-permute-start(bf16[4,192,128]{2,1,0:T(8,128)(2,1)S(1)} %get-tuple-element.43.refs_3_), channel_id=1, source_target_pairs={{0,6},{1,7},{2,4},{3,5},{4,2},{5,3},{6,0},{7,1},{8,14},{9,15},{10,... | collective-permute-start | bytes 589832 | tf_op jit(solution)/shard_map/ppermute | solution.py:347
  14.2 21.8 %collective-permute-start.3 = (bf16[4,192,128]{2,1,0:T(8,128)(2,1)S(1)}, bf16[4,192,128]{2,1,0:T(8,128)(2,1)S(1)}, u32[]{:S(2)}, u32[]{:S(2)}) collective-permute-start(bf16[4,192,128]{2,1,0:T(8,128)(2,1)S(1)} %get-tuple-element.47), channel_id=1, source_target_pairs={{0,2},{1,3},{2,0},{3,1},{4,6},{5,7},{6,4},{7,5},{8,10},{9,11},{10,... | collective-permute-start | bytes 589832 | tf_op jit(solution)/shard_map/ppermute | solution.py:347
  15.6 20.4 %collective-permute-start.4 = (bf16[4,192,128]{2,1,0:T(8,128)(2,1)S(1)}, bf16[4,192,128]{2,1,0:T(8,128)(2,1)S(1)}, u32[]{:S(2)}, u32[]{:S(2)}) collective-permute-start(bf16[4,192,128]{2,1,0:T(8,128)(2,1)S(1)} %get-tuple-element.48), channel_id=1, source_target_pairs={{0,3},{1,2},{2,1},{3,0},{4,7},{5,6},{6,5},{7,4},{8,11},{9,10},{10,... | collective-permute-start | bytes 589832 | tf_op jit(solution)/shard_map/ppermute | solution.py:347
  15.6 20.3 %collective-permute-start.5 = (bf16[4,192,128]{2,1,0:T(8,128)(2,1)S(1)}, bf16[4,192,128]{2,1,0:T(8,128)(2,1)S(1)}, u32[]{:S(2)}, u32[]{:S(2)}) collective-permute-start(bf16[4,192,128]{2,1,0:T(8,128)(2,1)S(1)} %get-tuple-element.49), channel_id=1, source_target_pairs={{0,4},{1,5},{2,6},{3,7},{4,0},{5,1},{6,2},{7,3},{8,12},{9,13},{10,... | collective-permute-start | bytes 589832 | tf_op jit(solution)/shard_map/ppermute | solution.py:347
  17.5 39.3 %copy-start.4 = (bf16[512,128]{1,0:T(8,128)(2,1)S(1)}, bf16[512,128]{1,0:T(8,128)(2,1)}, u32[]{:S(2)}) copy-start(bf16[512,128]{1,0:T(8,128)(2,1)} %constant.32.clone.refs_1_) | copy-start | bytes 393220
  24.6 1.0 copy-start.1
  25.6 58.6 %copy-start = (bf16[128,1024]{1,0:T(8,128)(2,1)S(1)}, bf16[128,1024]{1,0:T(8,128)(2,1)}, u32[]{:S(2)}) copy-start(bf16[128,1024]{1,0:T(8,128)(2,1)} %constant.30.clone.refs_4_.refs_3_) | copy-start | bytes 786436
  30.4 7.0 %collective-permute-start.6 = (bf16[4,192,128]{2,1,0:T(8,128)(2,1)S(1)}, bf16[4,192,128]{2,1,0:T(8,128)(2,1)S(1)}, u32[]{:S(2)}, u32[]{:S(2)}) collective-permute-start(bf16[4,192,128]{2,1,0:T(8,128)(2,1)S(1)} %get-tuple-element.50), channel_id=1, source_target_pairs={{0,5},{1,4},{2,7},{3,6},{4,1},{5,0},{6,3},{7,2},{8,13},{9,12},{10,... | collective-permute-start | bytes 589832 | tf_op jit(solution)/shard_map/ppermute | solution.py:347
  34.0 3.4 %collective-permute-start.2 = (bf16[4,192,128]{2,1,0:T(8,128)(2,1)S(1)}, bf16[4,192,128]{2,1,0:T(8,128)(2,1)S(1)}, u32[]{:S(2)}, u32[]{:S(2)}) collective-permute-start(bf16[4,192,128]{2,1,0:T(8,128)(2,1)S(1)} %get-tuple-element.46), channel_id=1, source_target_pairs={{0,1},{1,0},{2,3},{3,2},{4,5},{5,4},{6,7},{7,6},{8,9},{9,8},{10,11... | collective-permute-start | bytes 589832 | tf_op jit(solution)/shard_map/ppermute | solution.py:347
  76.3 7.9 %collective-permute-start.12 = (bf16[4,12,16,128]{3,2,1,0:T(8,128)(2,1)S(1)}, bf16[4,12,16,128]{3,2,1,0:T(8,128)(2,1)S(1)}, u32[]{:S(2)}, u32[]{:S(2)}) collective-permute-start(bf16[4,12,16,128]{3,2,1,0:T(8,128)(2,1)S(1)} %get-tuple-element.57), channel_id=1, source_target_pairs={{0,2},{1,3},{2,0},{3,1},{4,6},{5,7},{6,4},{7,5},{8,10},{9,11},{10,... | collective-permute-start | bytes 589832 | tf_op jit(solution)/shard_map/ppermute | solution.py:347
  76.9 14.2 %collective-permute-start.13 = (bf16[4,12,16,128]{3,2,1,0:T(8,128)(2,1)S(1)}, bf16[4,12,16,128]{3,2,1,0:T(8,128)(2,1)S(1)}, u32[]{:S(2)}, u32[]{:S(2)}) collective-permute-start(bf16[4,12,16,128]{3,2,1,0:T(8,128)(2,1)S(1)} %get-tuple-element.58), channel_id=1, source_target_pairs={{0,3},{1,2},{2,1},{3,0},{4,7},{5,6},{6,5},{7,4},{8,11},{9,10},{10,... | collective-permute-start | bytes 589832 | tf_op jit(solution)/shard_map/ppermute | solution.py:347
  77.2 26.2 %collective-permute-start.10 = (bf16[4,12,16,128]{3,2,1,0:T(8,128)(2,1)S(1)}, bf16[4,12,16,128]{3,2,1,0:T(8,128)(2,1)S(1)}, u32[]{:S(2)}, u32[]{:S(2)}) collective-permute-start(bf16[4,12,16,128]{3,2,1,0:T(8,128)(2,1)S(1)} %get-tuple-element.55), channel_id=1, source_target_pairs={{0,4},{1,5},{2,6},{3,7},{4,0},{5,1},{6,2},{7,3},{8,12},{9,13},{10,... | collective-permute-start | bytes 589832 | tf_op jit(solution)/shard_map/ppermute | solution.py:347
  78.4 26.1 %collective-permute-start.11 = (bf16[4,12,16,128]{3,2,1,0:T(8,128)(2,1)S(1)}, bf16[4,12,16,128]{3,2,1,0:T(8,128)(2,1)S(1)}, u32[]{:S(2)}, u32[]{:S(2)}) collective-permute-start(bf16[4,12,16,128]{3,2,1,0:T(8,128)(2,1)S(1)} %get-tuple-element.56), channel_id=1, source_target_pairs={{0,5},{1,4},{2,7},{3,6},{4,1},{5,0},{6,3},{7,2},{8,13},{9,12},{10,... | collective-permute-start | bytes 589832 | tf_op jit(solution)/shard_map/ppermute | solution.py:347
  79.9 35.8 %collective-permute-start.8 = (bf16[4,12,16,128]{3,2,1,0:T(8,128)(2,1)S(1)}, bf16[4,12,16,128]{3,2,1,0:T(8,128)(2,1)S(1)}, u32[]{:S(2)}, u32[]{:S(2)}) collective-permute-start(bf16[4,12,16,128]{3,2,1,0:T(8,128)(2,1)S(1)} %get-tuple-element.53), channel_id=1, source_target_pairs={{0,6},{1,7},{2,4},{3,5},{4,2},{5,3},{6,0},{7,1},{8,14},{9,15},{10,... | collective-permute-start | bytes 589832 | tf_op jit(solution)/shard_map/ppermute | solution.py:347
  84.2 32.2 %collective-permute-start.9 = (bf16[4,12,16,128]{3,2,1,0:T(8,128)(2,1)S(1)}, bf16[4,12,16,128]{3,2,1,0:T(8,128)(2,1)S(1)}, u32[]{:S(2)}, u32[]{:S(2)}) collective-permute-start(bf16[4,12,16,128]{3,2,1,0:T(8,128)(2,1)S(1)} %get-tuple-element.54), channel_id=1, source_target_pairs={{0,7},{1,6},{2,5},{3,4},{4,3},{5,2},{6,1},{7,0},{8,15},{9,14},{10,... | collective-permute-start | bytes 589832 | tf_op jit(solution)/shard_map/ppermute | solution.py:347
  91.1 37.6 %collective-permute-start.7 = (bf16[4,12,16,128]{3,2,1,0:T(8,128)(2,1)S(1)}, bf16[4,12,16,128]{3,2,1,0:T(8,128)(2,1)S(1)}, u32[]{:S(2)}, u32[]{:S(2)}) collective-permute-start(bf16[4,12,16,128]{3,2,1,0:T(8,128)(2,1)S(1)} %get-tuple-element.52), channel_id=1, source_target_pairs={{0,1},{1,0},{2,3},{3,2},{4,5},{5,4},{6,7},{7,6},{8,9},{9,8},{10,11... | collective-permute-start | bytes 589832 | tf_op jit(solution)/shard_map/ppermute | solution.py:347
  103.4 14.3 %collective-permute-start.14 = (bf16[4,192,128]{2,1,0:T(8,128)(2,1)S(1)}, bf16[4,192,128]{2,1,0:T(8,128)(2,1)S(1)}, u32[]{:S(2)}, u32[]{:S(2)}) collective-permute-start(bf16[4,192,128]{2,1,0:T(8,128)(2,1)S(1)} %get-tuple-element.63), channel_id=1, source_target_pairs={{0,2},{1,3},{2,0},{3,1},{4,6},{5,7},{6,4},{7,5},{8,10},{9,11},{10,... | collective-permute-start | bytes 589832 | tf_op jit(solution)/shard_map/ppermute | solution.py:347
  104.5 13.3 %collective-permute-start.15 = (bf16[4,192,128]{2,1,0:T(8,128)(2,1)S(1)}, bf16[4,192,128]{2,1,0:T(8,128)(2,1)S(1)}, u32[]{:S(2)}, u32[]{:S(2)}) collective-permute-start(bf16[4,192,128]{2,1,0:T(8,128)(2,1)S(1)} %get-tuple-element.64), channel_id=1, source_target_pairs={{0,3},{1,2},{2,1},{3,0},{4,7},{5,6},{6,5},{7,4},{8,11},{9,10},{10,... | collective-permute-start | bytes 589832 | tf_op jit(solution)/shard_map/ppermute | solution.py:347
  115.7 12.9 %collective-permute-start.16 = (bf16[4,192,128]{2,1,0:T(8,128)(2,1)S(1)}, bf16[4,192,128]{2,1,0:T(8,128)(2,1)S(1)}, u32[]{:S(2)}, u32[]{:S(2)}) collective-permute-start(bf16[4,192,128]{2,1,0:T(8,128)(2,1)S(1)} %get-tuple-element.66), channel_id=1, source_target_pairs={{0,4},{1,5},{2,6},{3,7},{4,0},{5,1},{6,2},{7,3},{8,12},{9,13},{10,... | collective-permute-start | bytes 589832 | tf_op jit(solution)/shard_map/ppermute | solution.py:347
  116.5 12.2 %collective-permute-start.17 = (bf16[4,192,128]{2,1,0:T(8,128)(2,1)S(1)}, bf16[4,192,128]{2,1,0:T(8,128)(2,1)S(1)}, u32[]{:S(2)}, u32[]{:S(2)}) collective-permute-start(bf16[4,192,128]{2,1,0:T(8,128)(2,1)S(1)} %get-tuple-element.67), channel_id=1, source_target_pairs={{0,5},{1,4},{2,7},{3,6},{4,1},{5,0},{6,3},{7,2},{8,13},{9,12},{10,... | collective-permute-start | bytes 589832 | tf_op jit(solution)/shard_map/ppermute | solution.py:347
  135.5 2.8 %collective-permute-start.18 = (bf16[4,192,128]{2,1,0:T(8,128)(2,1)S(1)}, bf16[4,192,128]{2,1,0:T(8,128)(2,1)S(1)}, u32[]{:S(2)}, u32[]{:S(2)}) collective-permute-start(bf16[4,192,128]{2,1,0:T(8,128)(2,1)S(1)} %get-tuple-element.70), channel_id=1, source_target_pairs={{0,1},{1,0},{2,3},{3,2},{4,5},{5,4},{6,7},{7,6},{8,9},{9,8},{10,11... | collective-permute-start | bytes 589832 | tf_op jit(solution)/shard_map/ppermute | solution.py:347
  135.5 8.6 %collective-permute-start.19 = (bf16[4,192,128]{2,1,0:T(8,128)(2,1)S(1)}, bf16[4,192,128]{2,1,0:T(8,128)(2,1)S(1)}, u32[]{:S(2)}, u32[]{:S(2)}) collective-permute-start(bf16[4,192,128]{2,1,0:T(8,128)(2,1)S(1)} %get-tuple-element.71), channel_id=1, source_target_pairs={{0,6},{1,7},{2,4},{3,5},{4,2},{5,3},{6,0},{7,1},{8,14},{9,15},{10,... | collective-permute-start | bytes 589832 | tf_op jit(solution)/shard_map/ppermute | solution.py:347
  137.1 10.4 %collective-permute-start.20 = (bf16[4,192,128]{2,1,0:T(8,128)(2,1)S(1)}, bf16[4,192,128]{2,1,0:T(8,128)(2,1)S(1)}, u32[]{:S(2)}, u32[]{:S(2)}) collective-permute-start(bf16[4,192,128]{2,1,0:T(8,128)(2,1)S(1)} %get-tuple-element.72), channel_id=1, source_target_pairs={{0,7},{1,6},{2,5},{3,4},{4,3},{5,2},{6,1},{7,0},{8,15},{9,14},{10,... | collective-permute-start | bytes 589832 | tf_op jit(solution)/shard_map/ppermute | solution.py:347
  167.6 15.8 %all-to-all-start.3 = ((bf16[32,3,16,128]{3,2,1,0:T(8,128)(2,1)}), bf16[32,3,16,128]{3,2,1,0:T(8,128)(2,1)S(1)}, u32[]{:S(2)}, u32[]{:S(2)}) async-start(bf16[32,3,16,128]{3,2,1,0:T(8,128)(2,1)} %bitcast.33), calls=%async_computation.3 | async-start | bytes 786432 | tf_op jit(solution)/shard_map/all_to_all | solution.py:342
  183.4 0.7 copy-start.5
  185.8 7.9 %collective-permute-start.25 = (bf16[4,12,16,128]{3,2,1,0:T(8,128)(2,1)S(1)}, bf16[4,12,16,128]{3,2,1,0:T(8,128)(2,1)S(1)}, u32[]{:S(2)}, u32[]{:S(2)}) collective-permute-start(bf16[4,12,16,128]{3,2,1,0:T(8,128)(2,1)S(1)} %get-tuple-element.80), channel_id=1, source_target_pairs={{0,2},{1,3},{2,0},{3,1},{4,6},{5,7},{6,4},{7,5},{8,10},{9,11},{10,... | collective-permute-start | bytes 589832 | tf_op jit(solution)/shard_map/ppermute | solution.py:347
  186.3 8.8 %collective-permute-start.27 = (bf16[4,12,16,128]{3,2,1,0:T(8,128)(2,1)S(1)}, bf16[4,12,16,128]{3,2,1,0:T(8,128)(2,1)S(1)}, u32[]{:S(2)}, u32[]{:S(2)}) collective-permute-start(bf16[4,12,16,128]{3,2,1,0:T(8,128)(2,1)S(1)} %get-tuple-element.83), channel_id=1, source_target_pairs={{0,1},{1,0},{2,3},{3,2},{4,5},{5,4},{6,7},{7,6},{8,9},{9,8},{10,11... | collective-permute-start | bytes 589832 | tf_op jit(solution)/shard_map/ppermute | solution.py:347
  186.5 14.4 %collective-permute-start.26 = (bf16[4,12,16,128]{3,2,1,0:T(8,128)(2,1)S(1)}, bf16[4,12,16,128]{3,2,1,0:T(8,128)(2,1)S(1)}, u32[]{:S(2)}, u32[]{:S(2)}) collective-permute-start(bf16[4,12,16,128]{3,2,1,0:T(8,128)(2,1)S(1)} %get-tuple-element.81), channel_id=1, source_target_pairs={{0,3},{1,2},{2,1},{3,0},{4,7},{5,6},{6,5},{7,4},{8,11},{9,10},{10,... | collective-permute-start | bytes 589832 | tf_op jit(solution)/shard_map/ppermute | solution.py:347
  188.0 18.8 %collective-permute-start.23 = (bf16[4,12,16,128]{3,2,1,0:T(8,128)(2,1)S(1)}, bf16[4,12,16,128]{3,2,1,0:T(8,128)(2,1)S(1)}, u32[]{:S(2)}, u32[]{:S(2)}) collective-permute-start(bf16[4,12,16,128]{3,2,1,0:T(8,128)(2,1)S(1)} %get-tuple-element.78), channel_id=1, source_target_pairs={{0,4},{1,5},{2,6},{3,7},{4,0},{5,1},{6,2},{7,3},{8,12},{9,13},{10,... | collective-permute-start | bytes 589832 | tf_op jit(solution)/shard_map/ppermute | solution.py:347
  189.0 17.8 %collective-permute-start.24 = (bf16[4,12,16,128]{3,2,1,0:T(8,128)(2,1)S(1)}, bf16[4,12,16,128]{3,2,1,0:T(8,128)(2,1)S(1)}, u32[]{:S(2)}, u32[]{:S(2)}) collective-permute-start(bf16[4,12,16,128]{3,2,1,0:T(8,128)(2,1)S(1)} %get-tuple-element.79), channel_id=1, source_target_pairs={{0,5},{1,4},{2,7},{3,6},{4,1},{5,0},{6,3},{7,2},{8,13},{9,12},{10,... | collective-permute-start | bytes 589832 | tf_op jit(solution)/shard_map/ppermute | solution.py:347
  193.7 18.9 %collective-permute-start.21 = (bf16[4,12,16,128]{3,2,1,0:T(8,128)(2,1)S(1)}, bf16[4,12,16,128]{3,2,1,0:T(8,128)(2,1)S(1)}, u32[]{:S(2)}, u32[]{:S(2)}) collective-permute-start(bf16[4,12,16,128]{3,2,1,0:T(8,128)(2,1)S(1)} %get-tuple-element.76), channel_id=1, source_target_pairs={{0,6},{1,7},{2,4},{3,5},{4,2},{5,3},{6,0},{7,1},{8,14},{9,15},{10,... | collective-permute-start | bytes 589832 | tf_op jit(solution)/shard_map/ppermute | solution.py:347
  195.1 17.6 %collective-permute-start.22 = (bf16[4,12,16,128]{3,2,1,0:T(8,128)(2,1)S(1)}, bf16[4,12,16,128]{3,2,1,0:T(8,128)(2,1)S(1)}, u32[]{:S(2)}, u32[]{:S(2)}) collective-permute-start(bf16[4,12,16,128]{3,2,1,0:T(8,128)(2,1)S(1)} %get-tuple-element.77), channel_id=1, source_target_pairs={{0,7},{1,6},{2,5},{3,4},{4,3},{5,2},{6,1},{7,0},{8,15},{9,14},{10,... | collective-permute-start | bytes 589832 | tf_op jit(solution)/shard_map/ppermute | solution.py:347

commit v6 on v5

--- a/solution.py
+++ b/solution.py
@@ -51,28 +51,31 @@
 ANY = pl.BlockSpec(memory_space=pl.ANY)
 
 
-def call(body, grid, in_specs, out_specs, out_shape, args, order=None, scratch=(), aliases={}, after=()):
+def call(body, grid, in_specs, out_specs, out_shape, args, order=None, scratch=(), aliases={}, after=(), carry=()):
     lead = 0 if order is None else 1
-    count = lead + len(args)
+    count, outs = lead + len(args), len(out_shape)
+    idle = len(after) + len(carry)
 
     def placed(*refs):
-        body(*refs[:count], *refs[count + len(after) :])
+        ends = count + idle, count + idle + outs, count + idle + outs + len(carry)
+        body(*refs[:count], *refs[ends[0] : ends[1]], *refs[ends[2] :])
 
     spec = pltpu.PrefetchScalarGridSpec(
         num_scalar_prefetch=lead,
         grid=grid,
-        in_specs=list(in_specs) + [ANY] * len(after),
-        out_specs=out_specs,
+        in_specs=list(in_specs) + [ANY] * idle,
+        out_specs=list(out_specs) + [ANY] * len(carry),
         scratch_shapes=scratch,
     )
+    kept = {count + len(after) + e: outs + e for e in range(len(carry))}
     return pl.pallas_call(
         placed,
         grid_spec=spec,
-        out_shape=out_shape,
-        input_output_aliases={lead + operand: out for operand, out in aliases.items()},
-        compiler_params=pltpu.CompilerParams(vmem_limit_bytes=52 * 1024 * 1024),
+        out_shape=list(out_shape) + [jax.ShapeDtypeStruct(x.shape, x.dtype) for x in carry],
+        input_output_aliases={lead + operand: out for operand, out in aliases.items()} | kept,
+        compiler_params=pltpu.CompilerParams(vmem_limit_bytes=50 * 1024 * 1024),
         cost_estimate=pl.CostEstimate(flops=0, bytes_accessed=0, transcendentals=0),
-    )(*(() if order is None else (order,)), *args, *after)
+    )(*(() if order is None else (order,)), *args, *after, *carry)
 
 
 def whole(shape):
@@ -84,79 +87,87 @@
     return jnp.concatenate([ref[t, :, cell].reshape(channels * y_local, depth) for t in times], axis=1)
 
 
-def admit(held, pieces, sub):
+def pieces_of(order_ref, first, unit, pieces, held):
+    cells = held.shape[0] // unit
     for e, piece in enumerate(pieces):
-
-        @pl.when(pl.program_id(0) == e * sub)
-        def _(piece=piece):
-            held[...] = piece[...]
-
-
-def release(held, pieces, sub):
-    for e, piece in enumerate(pieces):
-
-        @pl.when(pl.program_id(0) == e * sub + sub - 1)
-        def _(piece=piece):
-            piece[...] = held[...]
-
-
-def own_cells(sub, cells):
-    return pl.ds(lax.rem(pl.program_id(0), sub) * cells, cells)
-
-
-def head_body(sub, order_ref, field_ref, table_ref, *refs):
+        start = lax.rem(order_ref[first + e], unit) * cells
+        yield e // unit, pl.ds(start, cells), piece
+
+
+def admit(order_ref, first, unit, pieces, held):
+    for which, cells, piece in pieces_of(order_ref, first, unit, pieces, held):
+
+        @pl.when((pl.program_id(0) == which) & (pl.program_id(1) == 0))
+        def _(cells=cells, piece=piece):
+            held[cells] = piece[...]
+
+
+def release(order_ref, first, unit, pieces, held):
+    for which, cells, piece in pieces_of(order_ref, first, unit, pieces, held):
+
+        @pl.when((pl.program_id(0) == which) & (pl.program_id(1) == pl.num_programs(1) - 1))
+        def _(cells=cells, piece=piece):
+            piece[...] = held[cells].astype(piece.dtype)
+
+
+def add_time(held, cells, part):
+    before = jnp.where(pl.program_id(1) == 0, 0.0, held[cells])
+    held[cells] = before + part.reshape(before.shape)
+
+
+def bunches(cells, most):
+    size = math.gcd(cells, most)
+    return [slice(c, c + size) for c in range(0, cells, size)]
+
+
+def head_body(first, unit, order_ref, field_ref, table_ref, *refs):
     heads, held = refs[:-1], refs[-1]
-    steps, _, cells, _, depth = field_ref.shape
-    first = lax.rem(pl.program_id(0), sub) * cells
-    for cell in range(cells):
-        total = 0.0
-        for t in range(0, steps, 2):
-            total += dot(wide(field_ref, cell, (t, t + 1)), table_ref[t * depth : (t + 2) * depth, :])
-        held[first + cell] = total.astype(jnp.bfloat16)
-    release(held, heads, sub)
-
-
-def inner_body(sub, count, order_ref, field_ref, cot_ref, mix_ref, syn_ref, table_ref, *refs):
+    times = range(field_ref.shape[0])
+    for cells in bunches(field_ref.shape[2], 4):
+        values = jnp.concatenate([wide(field_ref, cell, times) for cell in range(cells.start, cells.stop)], axis=0)
+        add_time(held, cells, dot(values, table_ref[...]))
+    release(order_ref, first, unit, heads, held)
+
+
+def inner_body(first, unit, count, order_ref, field_ref, cot_ref, mix_ref, syn_ref, table_ref, *refs):
     mids, (grad_ref, *heads), (mid_held, head_held) = refs[:count], refs[-count - 3 : -2], refs[-2:]
-    steps, channels, cells, y_local, depth = field_ref.shape
+    span, channels, _, y_local, depth = field_ref.shape
     rows = channels * y_local
     band = math.gcd(rows, 32)
-    admit(mid_held, mids, sub)
-    middle = mid_held[own_cells(sub, cells)].reshape(cells * rows, -1)
-    total = 0.0
-    for t in range(0, steps, 2):
-        lanes = slice(t * depth, (t + 2) * depth)
-        spread = dot(middle, syn_ref[:, lanes])
-        bands = []
-        for cell in range(cells):
-            preact = spread[cell * rows : (cell + 1) * rows] + dot(mix_ref[...], wide(field_ref, cell, (t, t + 1)))
-            cot = wide(cot_ref, cell, (t, t + 1))
+    admit(order_ref, first, unit, mids, mid_held)
+    for cells in bunches(field_ref.shape[2], 2):
+        middle = mid_held[cells]
+        spread = dot(middle.reshape(-1, middle.shape[2]), syn_ref[...])
+        grads = []
+        for k, cell in enumerate(range(cells.start, cells.stop)):
+            values = wide(field_ref, cell, range(span))
+            preact = spread[k * rows : (k + 1) * rows] + dot(mix_ref[...], values)
+            cot = wide(cot_ref, cell, range(span))
+            bands = []
             for r in range(0, rows, band):
                 slope = gelu_slope(preact[r : r + band])
                 bands.append((cot[r : r + band].astype(jnp.float32) * slope).astype(jnp.bfloat16))
-        grad = jnp.concatenate(bands, axis=0)
-        for cell in range(cells):
-            for k in range(2):
-                part = grad[cell * rows : (cell + 1) * rows, k * depth : (k + 1) * depth]
-                grad_ref[t + k, :, cell] = part.reshape(channels, y_local, depth)
-        total += dot(grad, table_ref[lanes, :])
-    head_held[own_cells(sub, cells)] = total.astype(jnp.bfloat16).reshape((cells,) + head_held.shape[1:])
-    release(head_held, heads, sub)
-
-
-def outer_body(sub, count, order_ref, grad_ref, mix_ref, syn_ref, *refs):
+            grads.append(jnp.concatenate(bands, axis=0))
+            for t in range(span):
+                part = grads[-1][:, t * depth : (t + 1) * depth]
+                grad_ref[t, :, cell] = part.reshape(channels, y_local, depth)
+        add_time(head_held, cells, dot(jnp.concatenate(grads, axis=0), table_ref[...]))
+    release(order_ref, first, unit, heads, head_held)
+
+
+def outer_body(first, unit, count, order_ref, grad_ref, mix_ref, syn_ref, *refs):
     mids, out_ref, mid_held = refs[:count], refs[-2], refs[-1]
-    steps, channels, cells, y_local, depth = grad_ref.shape
+    span, channels, _, y_local, depth = grad_ref.shape
     rows = channels * y_local
-    admit(mid_held, mids, sub)
-    middle = mid_held[own_cells(sub, cells)].reshape(cells * rows, -1)
-    for t in range(0, steps, 2):
-        spread = dot(middle, syn_ref[:, t * depth : (t + 2) * depth])
-        for cell in range(cells):
-            total = spread[cell * rows : (cell + 1) * rows] + dot(mix_ref[...], wide(grad_ref, cell, (t, t + 1)))
+    admit(order_ref, first, unit, mids, mid_held)
+    for cells in bunches(grad_ref.shape[2], 2):
+        middle = mid_held[cells]
+        spread = dot(middle.reshape(-1, middle.shape[2]), syn_ref[...])
+        for k, cell in enumerate(range(cells.start, cells.stop)):
+            total = spread[k * rows : (k + 1) * rows] + dot(mix_ref[...], wide(grad_ref, cell, range(span)))
             total = total.astype(jnp.bfloat16)
-            for k in range(2):
-                out_ref[t + k, :, cell] = total[:, k * depth : (k + 1) * depth].reshape(channels, y_local, depth)
+            for t in range(span):
+                out_ref[t, :, cell] = total[:, t * depth : (t + 1) * depth].reshape(channels, y_local, depth)
 
 
 def y_down_body(table_ref, *refs):
@@ -208,8 +219,6 @@
             first = (h * groups + k) * members
             done = dot(stacked, table_ref[...], 0, 0).astype(jnp.bfloat16)
             modes_ref[first : first + members] = done.reshape(members, span, lanes)
-    held = weight_ref.shape[:1] + weight_ref.shape[3:]
-    modes = [modes_ref[c].astype(jnp.float32).reshape(held) for c in range(channels)]
     for h in range(c_pieces):
         for k in range(groups):
             mixed = []
@@ -217,9 +226,9 @@
                 to = (h * groups + k) * members + m
                 total = 0.0
                 for of in range(channels):
-                    weight = weight_ref[:, to, of] if back else weight_ref[:, of, to]
-                    total += weight.astype(jnp.float32) * modes[of]
-                mixed.append(total.reshape(span, lanes).astype(jnp.bfloat16))
+                    weight = weight_ref[to, of] if back else weight_ref[of, to]
+                    total += weight.astype(jnp.float32) * modes_ref[of].astype(jnp.float32)
+                mixed.append(total.astype(jnp.bfloat16))
             done = dot(table_ref[...], jnp.concatenate(mixed, axis=0), 1, 1).astype(jnp.bfloat16)
             for g in range(planes):
                 for x in range(x_pieces):
@@ -228,7 +237,13 @@
 
 
 def weight_body(weight_ref, out_ref):
-    out_ref[0] = jnp.concatenate([weight_ref[j, 0] for j in range(weight_ref.shape[0])], axis=-1)
+    j_local, q_local, _, channels = weight_ref.shape[:4]
+    for o in range(channels):
+        rows = [
+            jnp.concatenate([weight_ref[j, q, 0, o].astype(jnp.float32) for j in range(j_local)], axis=1)
+            for q in range(q_local)
+        ]
+        out_ref[0, o] = jnp.concatenate(rows, axis=0).astype(out_ref.dtype)
 
 
 def outer_product_body(left_ref, right_ref, out_ref):
@@ -282,49 +297,47 @@
 
     block_head = jax.ShapeDtypeStruct((x_piece, rows, lanes), bf16)
     full_field = jax.ShapeDtypeStruct(state_field.shape, bf16)
-    held = pltpu.VMEM(block_head.shape, bf16)
-    head_step, step = math.gcd(x_piece, 4), math.gcd(x_piece, 2)
-
-    def grouped(first, step):
-        sub = x_piece // step
-        where = lambda g, order: (0, 0, order[first + g // sub] * sub + g % sub, 0, 0)
-        return pl.BlockSpec((steps, channels, step, y_local, depth), where)
+    span_t = math.gcd(steps, 2)
+
+    def plan(first, unit, count):
+        where = lambda n, t, order: (t, 0, lax.div(order[first + n * unit], unit), 0, 0)
+        field = pl.BlockSpec((span_t, channels, unit * x_piece, y_local, depth), where)
+        syn_spec = pl.BlockSpec((lanes, span_t * depth), lambda n, t, order: (0, t))
+        ana_spec = pl.BlockSpec((span_t * depth, lanes), lambda n, t, order: (t, 0))
+        held = (unit * x_piece, rows, lanes)
+        return (count // unit, steps // span_t), field, syn_spec, ana_spec, held
 
     pairs = [(k, min(2, blocks - k)) for k in range(0, blocks, 2)]
-    groups = [(0, 1)] + pairs[1:] + [(1, 1)] if blocks > 1 else pairs
-
-    def head_call(first, count, after):
-        sub = x_piece // head_step
+    groups = [(1, 1)] + pairs[1:] + [(0, 1)] if blocks > 1 else pairs
+
+    def head_call(first, unit, count, after):
+        grid, field, _, ana_spec, held = plan(first, unit, count)
         return call(
-            functools.partial(head_body, sub), (count * sub,), [grouped(first, head_step), whole(ana.shape)],
-            [whole(block_head.shape)] * count, [block_head] * count,
-            (state_field, ana), order, [held], after=after,
-        )
-
-    def inner_call(first, count, middle, grads, after):
-        sub = x_piece // step
-        tables = (mix_up, syn, ana)
-        spec = grouped(first, step)
+            functools.partial(head_body, first, unit), grid, [field, ana_spec],
+            [whole(block_head.shape)] * count, [block_head] * count, (state_field, ana), order,
+            [pltpu.VMEM(held, jnp.float32)], after=after,
+        )
+
+    def inner_call(first, count, middle, grads, after, carry):
+        grid, field, syn_spec, ana_spec, held = plan(first, count, count)
         done = call(
-            functools.partial(inner_body, sub, count), (count * sub,),
-            [spec] * 2 + [whole(arg.shape) for arg in tables] + [whole(block_head.shape)] * count + [ANY] * len(grads),
-            [spec] + [whole(block_head.shape)] * count, [full_field] + [block_head] * count,
-            (state_field, cotangent, *tables, *middle[first : first + count], *grads), order, [held, held],
-            {5 + count: 0} if grads else {}, after,
+            functools.partial(inner_body, first, count, count), grid,
+            [field] * 2 + [whole(mix_up.shape), syn_spec, ana_spec] + [whole(block_head.shape)] * count + [ANY] * len(grads),
+            [field] + [whole(block_head.shape)] * count, [full_field] + [block_head] * count,
+            (state_field, cotangent, mix_up, syn, ana, *middle[first : first + count], *grads), order,
+            [pltpu.VMEM(held, bf16), pltpu.VMEM(held, jnp.float32)], {5 + count: 0} if grads else {}, after, carry,
+        )
+        return done[:1], done[1 : 1 + count], done[1 + count :]
+
+    def outer_call(first, count, middle, grads, field, carry):
+        grid, spec, syn_spec, _, held = plan(first, count, count)
+        done = call(
+            functools.partial(outer_body, first, count, count), grid,
+            [spec, whole(mix_back.shape), syn_spec] + [whole(block_head.shape)] * count + [ANY] * len(field),
+            [spec], [full_field], (*grads, mix_back, syn, *middle[first : first + count], *field), order,
+            [pltpu.VMEM(held, bf16)], {3 + count: 0} if field else {}, (), carry,
         )
         return done[:1], done[1:]
-
-    def outer_call(first, count, middle, grads, field):
-        sub = x_piece // step
-        tables = (mix_back, syn)
-        spec = grouped(first, step)
-        return call(
-            functools.partial(outer_body, sub, count), (count * sub,),
-            [spec] + [whole(arg.shape) for arg in tables] + [whole(block_head.shape)] * count + [ANY] * len(field),
-            [spec], [full_field],
-            (*grads, *tables, *middle[first : first + count], *field), order, [held],
-            {3 + count: 0} if field else {},
-        )
 
     def small(body, outs, *args, after=()):
         shapes = [jax.ShapeDtypeStruct(out, bf16) for out in outs]
@@ -354,51 +367,68 @@
 
     cells = (x_piece, c_piece, y_local, lanes)
 
-    def analyze(back, heads, weight, after):
-        (part,) = small(y_down_body, [packed], y_mat, *settle(heads, y_devices, cells), after=after)
+    def analyze(heads):
+        return small(y_down_body, [packed], y_mat, *settle(heads, y_devices, cells))[0]
+
+    def mix(back, part, weight, after):
         part = exchange(part).reshape((x_devices, x_pieces, c_pieces) + packed[2:])
         kept, part = small(
-            functools.partial(spectral_body, back), [(channels, span, j_local * modes), part.shape], part, x_mat, weight
+            functools.partial(spectral_body, back), [(channels, span, j_local * modes), part.shape],
+            part, x_mat, weight, after=after,
         )
         return kept, exchange(part).reshape(packed)
 
     def synthesize(part, after):
         pieces = small(y_up_body, [cells] * y_devices, part, y_mat_t, after=after)
-        pieces = [send(k, piece) for k, piece in enumerate(pieces)]
+        if paired:
+            pieces = [piece.reshape(block_head.shape) for piece in pieces]
+        late = pieces[6:] if paired else []
+        return [send(k, piece) for k, piece in enumerate(pieces[: len(pieces) - len(late)])], late
+
+    def rest(pieces, late):
+        pieces = pieces + [send(len(pieces) + e, piece) for e, piece in enumerate(late)]
         return settle(pieces, blocks, block_head.shape)
-
-    weight = call(
-        weight_body, (q_local,),
-        [pl.BlockSpec((j_local, 1, channels, channels, time_modes, modes), lambda q: (0, q, 0, 0, 0, 0))],
-        pl.BlockSpec((1, channels, channels, time_modes, j_local * modes), lambda q: (q, 0, 0, 0, 0)),
-        jax.ShapeDtypeStruct((q_local, channels, channels, time_modes, j_local * modes), bf16), (spectral_weight,),
-    )
 
     heads, after = [None] * blocks, ()
     for first, count in ((6, 2), (2, 4), (0, 2)) if blocks == 8 else ((0, blocks),):
-        done = head_call(first, count, after)
+        done = head_call(first, math.gcd(count, 2), count, after)
         heads[first : first + count] = [send(first + e, piece) for e, piece in enumerate(done)]
         after = (done[0],) if first == 6 else tuple(heads[6:])
-    modes_in, part = analyze(False, heads, weight, (weight, mix_up, mix_back, y_mat_t))
-    middle = synthesize(part, ())
-
-    grads, sent = (), [(), ()]
+    part = analyze(heads)
+    (weight,) = call(
+        weight_body, (channels,),
+        [pl.BlockSpec((j_local, q_local, 1, channels, time_modes, modes), lambda c: (0, 0, c, 0, 0, 0))],
+        [pl.BlockSpec((1, channels, span, j_local * modes), lambda c: (c, 0, 0, 0))],
+        [jax.ShapeDtypeStruct((channels, channels, span, j_local * modes), bf16)], (spectral_weight,), after=(part,),
+    )
+    modes_in, part = mix(False, part, weight, (mix_up, mix_back, y_mat_t))
+
+    middle, late = synthesize(part, ())
+    sent, grads = [(), ()], ()
+    if not paired:
+        middle = rest(middle, late)
     for first, count in groups:
-        grads, done = inner_call(first, count, middle, grads, sent[-2])
+        grads, done, late = inner_call(first, count, middle, grads, sent[-2], late)
+        if late:
+            middle, late = rest(middle, late), []
         heads[first : first + count] = [send(first + e, piece) for e, piece in enumerate(done)]
         sent.append(tuple(heads[max(first, 1) : first + count]) if paired else ())
-    grad_modes, part = analyze(True, heads, weight, ())
+    part = analyze(heads)
+    grad_modes, part = mix(True, part, weight, ())
     spec = whole(modes_in.shape)
-    grad_spectral = call(
+    (grad_spectral,) = call(
         outer_product_body, (j_local,), [spec, spec],
-        pl.BlockSpec((1,) + spectral_weight.shape[1:], lambda j: (j, 0, 0, 0, 0, 0)),
-        jax.ShapeDtypeStruct(spectral_weight.shape, jnp.float32),
-        (modes_in, grad_modes),
-    )
-    middle = synthesize(part, (grad_spectral,))
+        [pl.BlockSpec((1,) + spectral_weight.shape[1:], lambda j: (j, 0, 0, 0, 0, 0))],
+        [jax.ShapeDtypeStruct(spectral_weight.shape, jnp.float32)], (modes_in, grad_modes),
+    )
+    middle, late = synthesize(part, (grad_spectral,))
+    if not paired:
+        middle = rest(middle, late)
     field = ()
     for first, count in pairs:
-        field = outer_call(first, count, middle, grads, field)
+        field, late = outer_call(first, count, middle, grads, field, late)
+        if late:
+            middle, late = rest(middle, late), []
     return field[0], grad_spectral
 
 

time: 221 us -> 204 us (0.923)
  blocking collectives: 49.4 us -> 33.8 us
  waiting for transfers between devices: 26.6 us -> 14 us
  Pallas kernels: 104 us -> 113 us
  starting transfers between devices: 28 us -> 34.4 us
  local copies, waits for them, and re-layouts: 8.07 us -> 5.26 us
    all_to_all x3 -> x2, blocking collectives: 49.4 us -> 33.8 us  [exchange(): return lax.all_to_all(pieces, ('gx',) + YZ, 0, 0, tiled=True).reshape(shape)]
    ppermute x28, waiting for transfers between devices: 18 us -> 4.56 us  [send(): return lax.ppermute(piece, YZ, [(d, d ^ k) for d in range(y_devices)])]
    pallas_call x20, Pallas kernels: 104 us -> 113 us  [call(): pl.pallas_call(placed, grid_spec=spec, out_shape=list(out_shape) + [jax.S...]
    all_to_all x1 -> x2, starting transfers between devices: 2.6 us -> 8.1 us  [exchange(): return lax.all_to_all(pieces, ('gx',) + YZ, 0, 0, tiled=True).reshape(shape)]
    all_to_all x1 -> x2, waiting for transfers between devices: 8.56 us -> 9.44 us  [exchange(): return lax.all_to_all(pieces, ('gx',) + YZ, 0, 0, tiled=True).reshape(shape)]
  transfers between devices with their start and end apart: 29 -> 30, of which waited for: 6 -> 5; matrix products, arithmetic and copies ran while one was open for 3% -> 3% of each run, Pallas kernels for 35% -> 48%
where the time goes in v6:
time: 204 us; the launch traced here: 203 us
  Pallas kernels  113 us (55%)
  starting transfers between devices  34.4 us (17%)
  blocking collectives  33.8 us (17%)
  waiting for transfers between devices  14 us (7%)
  local copies, waits for them, and re-layouts  5.26 us (3%)
    pallas_call x20, Pallas kernels, call(): pl.pallas_call(placed, grid_spec=spec, out_shape=list(out_shape) + [jax.S...  113 us
    all_to_all x2, blocking collectives, exchange(): return lax.all_to_all(pieces, ('gx',) + YZ, 0, 0, tiled=True).reshape(shape)  33.8 us
    ppermute x28, starting transfers between devices, send(): return lax.ppermute(piece, YZ, [(d, d ^ k) for d in range(y_devices)])  26.3 us
    all_to_all x2, waiting for transfers between devices, exchange(): return lax.all_to_all(pieces, ('gx',) + YZ, 0, 0, tiled=True).reshape(shape)  9.44 us
    all_to_all x2, starting transfers between devices, exchange(): return lax.all_to_all(pieces, ('gx',) + YZ, 0, 0, tiled=True).reshape(shape)  8.1 us
    ppermute x28, waiting for transfers between devices, send(): return lax.ppermute(piece, YZ, [(d, d ^ k) for d in range(y_devices)])  4.56 us
  transfers between devices with their start and end apart: 30, of which 5 were waited for; matrix products, arithmetic and copies ran while one was open for 3% of the time, Pallas kernels for 48%

profile of v6, /device:TPU:0, one launch (start us, length us, event | category | flops | bytes accessed | tf_op | source)
XLA Modules:
  0.0 202.8 jit_solution(7838339690122482883)
XLA Ops:
  0.7 0.9 copy-done.1
  1.6 4.1 %shard_map.104 = (bf16[4,192,128]{2,1,0:T(8,128)(2,1)S(1)}, bf16[4,192,128]{2,1,0:T(8,128)(2,1)S(1)}) custom-call(s32[8]{0:T(128)S(1)} %iota_xor_fusion.refs_0_, bf16[8,12,32,16,128]{4,3,2,1,0:T(8,128)(2,1)} %refs_1_.17, bf16[1024,128]{1,0:T(8,128)(2,1)S(1)} %copy-done.1), custom_call_target="tpu_custom_call" | custom-call | tf_op jit(solution)/shard_map/pallas_call | solution.py:71
  5.7 3.4 %collective-permute-start.1 = (bf16[4,192,128]{2,1,0:T(8,128)(2,1)S(1)}, bf16[4,192,128]{2,1,0:T(8,128)(2,1)S(1)}, u32[]{:S(2)}, u32[]{:S(2)}) collective-permute-start(bf16[4,192,128]{2,1,0:T(8,128)(2,1)S(1)} %get-tuple-element.49), channel_id=1, source_target_pairs={{0,7},{1,6},{2,5},{3,4},{4,3},{5,2},{6,1},{7,0},{8,15},{9,14},{10,... | collective-permute-start | bytes 589832 | tf_op jit(solution)/shard_map/ppermute | solution.py:360
  9.1 0.6 collective-permute-start
  9.8 7.4 %shard_map.106 = (bf16[4,192,128]{2,1,0:T(8,128)(2,1)S(1)}, bf16[4,192,128]{2,1,0:T(8,128)(2,1)S(1)}, bf16[4,192,128]{2,1,0:T(8,128)(2,1)S(1)}, bf16[4,192,128]{2,1,0:T(8,128)(2,1)S(1)}) custom-call(s32[8]{0:T(128)S(1)} %iota_xor_fusion.refs_0_, bf16[8,12,32,16,128]{4,3,2,1,0:T(8,128)(2,1)} %refs_1_.17, bf16[1024,128]{1,0:T(8,128)(2,1)S(1)} %copy-done.1, ...), custom_call_target="tpu_custom_call" | custom-call | tf_op jit(solution)/shard_map/pallas_call | solution.py:71
  17.2 1.4 collective-permute-start.3
  18.6 0.1 collective-permute-start.4
  18.7 1.7 collective-permute-start.5
  20.4 0.5 collective-permute-start.6
  20.8 4.8 %shard_map.105 = (bf16[4,192,128]{2,1,0:T(8,128)(2,1)S(1)}, bf16[4,192,128]{2,1,0:T(8,128)(2,1)}) custom-call(s32[8]{0:T(128)S(1)} %iota_xor_fusion.refs_0_, bf16[8,12,32,16,128]{4,3,2,1,0:T(8,128)(2,1)} %refs_1_.17, bf16[1024,128]{1,0:T(8,128)(2,1)S(1)} %copy-done.1, bf16[4,192,128]{2,1,0:T(8,128)(2,1)S(1)} %collective-permute-done.refs_3_, ...), custom_call_target="tpu_custom_call" | custom-call | tf_op jit(solution)/shard_map/pallas_call | solution.py:71
  25.6 0.1 collective-permute-start.2
  25.7 0.9 dynamic-slice_bitcast_fusion.1.refs_0_
  26.6 1.0 collective-permute-done.4
  27.6 2.7 %collective-permute-done.6 = bf16[4,192,128]{2,1,0:T(8,128)(2,1)S(1)} collective-permute-done((bf16[4,192,128]{2,1,0:T(8,128)(2,1)S(1)}, bf16[4,192,128]{2,1,0:T(8,128)(2,1)S(1)}, u32[]{:S(2)}, u32[]{:S(2)}) %collective-permute-start.6) | collective-permute-done | bytes 196640 | tf_op jit(solution)/shard_map/ppermute | solution.py:360
  30.2 1.4 shard_map.107.refs_1_
  31.6 5.5 %all-to-all-start = ((bf16[32,3,16,128]{3,2,1,0:T(8,128)(2,1)}), bf16[32,3,16,128]{3,2,1,0:T(8,128)(2,1)S(1)}, u32[]{:S(2)}, u32[]{:S(2)}) async-start(bf16[32,3,16,128]{3,2,1,0:T(8,128)(2,1)} %bitcast.10), calls=%async_computation | async-start | bytes 786432 | tf_op jit(solution)/shard_map/all_to_all | solution.py:355
  37.1 0.1 copy.23
  37.2 1.1 broadcast_multiply_fusion
  38.2 1.7 mul.51.refs_4_.refs_2_
  40.0 0.7 mul.48.refs_3_
  40.6 0.9 dynamic-slice_bitcast_fusion.refs_5_.refs_1_
  41.5 7.8 %shard_map.108.refs_2_ = bf16[12,12,32,128]{3,2,1,0:T(8,128)(2,1)S(1)} custom-call(bf16[4,8,12,12,4,32]{5,4,3,2,1,0:T(4,128)(2,1)} %refs_0_.1, bf16[4,8,3,16,128]{4,3,2,1,0:T(8,128)(2,1)} %shard_map.107.refs_1_), custom_call_target="tpu_custom_call" | custom-call | tf_op jit(solution)/shard_map/pallas_call | solution.py:71
  49.4 0.9 all-to-all-done
  50.2 0.6 shard_map.109
  50.9 18.0 %all_to_all.20 = bf16[32,3,16,128]{3,2,1,0:T(8,128)(2,1)S(1)} all-to-all(bf16[32,3,16,128]{3,2,1,0:T(8,128)(2,1)S(1)} %bitcast.57), channel_id=1, replica_groups=mesh['parts'=1,'gx'=4,'gy'=4,'gz'=2] {'gx','gy','gz'}, dimensions={0} | all-to-all | bytes 786432 | tf_op jit(solution)/shard_map/all_to_all | solution.py:355
  68.8 0.7 shard_map.110
  69.5 0.1 collective-permute-start.7
  69.6 1.0 collective-permute-start.12
  70.5 0.9 collective-permute-start.13
  71.4 1.0 collective-permute-start.10
  72.4 0.7 collective-permute-start.11
  73.1 8.0 %shard_map.111 = (bf16[8,12,32,16,128]{4,3,2,1,0:T(8,128)(2,1)}, bf16[4,192,128]{2,1,0:T(8,128)(2,1)S(1)}, bf16[4,192,128]{2,1,0:T(8,128)(2,1)S(1)}, bf16[4,192,128]{2,1,0:T(8,128)(2,1)S(1)}) custom-call(s32[8]{0:T(128)S(1)} %iota_xor_fusion.refs_0_, bf16[8,12,32,16,128]{4,3,2,1,0:T(8,128)(2,1)} %refs_1_.17, ...), custom_call_target="tpu_custom_call", output_to_operand_aliasing={{2}: (7, {}), {3}: (8, {})} | custom-call | tf_op jit(solution)/shard_map/pallas_call | solution.py:71
  81.2 1.4 collective-permute-start.8
  82.6 0.2 collective-permute-start.14
  82.8 1.4 collective-permute-start.9
  84.2 13.3 %shard_map.112 = (bf16[8,12,32,16,128]{4,3,2,1,0:T(8,128)(2,1)}, bf16[4,192,128]{2,1,0:T(8,128)(2,1)S(1)}, bf16[4,192,128]{2,1,0:T(8,128)(2,1)S(1)}) custom-call(s32[8]{0:T(128)S(1)} %iota_xor_fusion.refs_0_, bf16[8,12,32,16,128]{4,3,2,1,0:T(8,128)(2,1)} %refs_1_.17, bf16[8,12,32,16,128]{4,3,2,1,0:T(8,128)(2,1)} %refs_2_.12, ...), custom_call_target="tpu_custom_call", output_to_operand_aliasing={{0}: (8, {})} | custom-call | tf_op jit(solution)/shard_map/pallas_call | solution.py:71
  97.5 0.9 collective-permute-start.15
  98.5 0.6 collective-permute-start.16
  99.1 13.4 %shard_map.113 = (bf16[8,12,32,16,128]{4,3,2,1,0:T(8,128)(2,1)}, bf16[4,192,128]{2,1,0:T(8,128)(2,1)S(1)}, bf16[4,192,128]{2,1,0:T(8,128)(2,1)S(1)}) custom-call(s32[8]{0:T(128)S(1)} %iota_xor_fusion.refs_0_, bf16[8,12,32,16,128]{4,3,2,1,0:T(8,128)(2,1)} %refs_1_.17, bf16[8,12,32,16,128]{4,3,2,1,0:T(8,128)(2,1)} %refs_2_.12, ...), custom_call_target="tpu_custom_call", output_to_operand_aliasing={{0}: (8, {})} | custom-call | tf_op jit(solution)/shard_map/pallas_call | solution.py:71
  112.5 1.0 collective-permute-start.17
  113.5 1.0 collective-permute-start.18
  114.5 13.4 %shard_map.114 = (bf16[8,12,32,16,128]{4,3,2,1,0:T(8,128)(2,1)}, bf16[4,192,128]{2,1,0:T(8,128)(2,1)S(1)}, bf16[4,192,128]{2,1,0:T(8,128)(2,1)S(1)}) custom-call(s32[8]{0:T(128)S(1)} %iota_xor_fusion.refs_0_, bf16[8,12,32,16,128]{4,3,2,1,0:T(8,128)(2,1)} %refs_1_.17, bf16[8,12,32,16,128]{4,3,2,1,0:T(8,128)(2,1)} %refs_2_.12, ...), custom_call_target="tpu_custom_call", output_to_operand_aliasing={{0}: (8, {})} | custom-call | tf_op jit(solution)/shard_map/pallas_call | solution.py:71
  127.9 1.3 collective-permute-start.19
  129.2 1.1 collective-permute-start.20
  130.3 8.0 %shard_map.115 = (bf16[8,12,32,16,128]{4,3,2,1,0:T(8,128)(2,1)}, bf16[4,192,128]{2,1,0:T(8,128)(2,1)S(1)}) custom-call(s32[8]{0:T(128)S(1)} %iota_xor_fusion.refs_0_, bf16[8,12,32,16,128]{4,3,2,1,0:T(8,128)(2,1)} %refs_1_.17, bf16[8,12,32,16,128]{4,3,2,1,0:T(8,128)(2,1)} %refs_2_.12, ...), custom_call_target="tpu_custom_call", output_to_operand_aliasing={{0}: (7, {})} | custom-call | tf_op jit(solution)/shard_map/pallas_call | solution.py:71
  138.3 0.9 collective-permute-done.20
  139.2 0.6 shard_map.116
  139.8 15.8 %all_to_all.21 = bf16[32,3,16,128]{3,2,1,0:T(8,128)(2,1)S(1)} all-to-all(bf16[32,3,16,128]{3,2,1,0:T(8,128)(2,1)S(1)} %bitcast.47), channel_id=1, replica_groups=mesh['parts'=1,'gx'=4,'gy'=4,'gz'=2] {'gx','gy','gz'}, dimensions={0} | all-to-all | bytes 786432 | tf_op jit(solution)/shard_map/all_to_all | solution.py:355
  155.6 1.3 shard_map.117
  157.0 2.6 %all-to-all-start.3 = ((bf16[32,3,16,128]{3,2,1,0:T(8,128)(2,1)}), bf16[32,3,16,128]{3,2,1,0:T(8,128)(2,1)S(1)}, u32[]{:S(2)}, u32[]{:S(2)}) async-start(bf16[32,3,16,128]{3,2,1,0:T(8,128)(2,1)} %bitcast.33), calls=%async_computation.3 | async-start | bytes 786432 | tf_op jit(solution)/shard_map/all_to_all | solution.py:355
  159.6 4.6 %shard_map.118.refs_2_ = f32[4,8,12,12,4,32]{5,4,3,2,1,0:T(4,128)} custom-call(bf16[12,32,128]{2,1,0:T(8,128)(2,1)S(1)} %get-tuple-element.81.refs_0_, bf16[12,32,128]{2,1,0:T(8,128)(2,1)S(1)} %get-tuple-element.82.refs_1_), custom_call_target="tpu_custom_call" | custom-call | tf_op jit(solution)/shard_map/pallas_call | solution.py:71
  164.2 8.6 %all-to-all-done.3 = bf16[32,3,16,128]{3,2,1,0:T(8,128)(2,1)S(1)} async-done(((bf16[32,3,16,128]{3,2,1,0:T(8,128)(2,1)}), bf16[32,3,16,128]{3,2,1,0:T(8,128)(2,1)S(1)}, u32[]{:S(2)}, u32[]{:S(2)}) %all-to-all-start.3) | async-done | bytes 393248 | tf_op jit(solution)/shard_map/all_to_all | solution.py:355
  172.8 0.7 shard_map.119
  173.5 0.1 collective-permute-start.21
  173.5 1.0 collective-permute-start.26
  174.5 1.1 collective-permute-start.24
  175.6 0.1 collective-permute-start.25
  175.6 1.7 collective-permute-start.27
  177.4 5.8 %shard_map.120 = (bf16[8,12,32,16,128]{4,3,2,1,0:T(8,128)(2,1)}, bf16[4,192,128]{2,1,0:T(8,128)(2,1)S(1)}, bf16[4,192,128]{2,1,0:T(8,128)(2,1)S(1)}) custom-call(s32[8]{0:T(128)S(1)} %iota_xor_fusion.refs_0_, bf16[8,12,32,16,128]{4,3,2,1,0:T(8,128)(2,1)} %get-tuple-element.76.refs_1_, ...), custom_call_target="tpu_custom_call", output_to_operand_aliasing={{1}: (6, {}), {2}: (7, {})} | custom-call | tf_op jit(solution)/shard_map/pallas_call | solution.py:71
  183.2 1.4 collective-permute-start.22
  184.6 0.7 collective-permute-start.23
  185.4 5.8 %shard_map.121.refs_6_ = bf16[8,12,32,16,128]{4,3,2,1,0:T(8,128)(2,1)} custom-call(s32[8]{0:T(128)S(1)} %iota_xor_fusion.refs_0_, bf16[8,12,32,16,128]{4,3,2,1,0:T(8,128)(2,1)} %get-tuple-element.76.refs_1_, bf16[192,192]{1,0:T(8,128)(2,1)S(1)} %mul.51.refs_4_.refs_2_, bf16[128,1024]{1,0:T(8,128)(2,1)S(1)} %copy-done, ...), custom_call_target="tpu_custom_call", output_to_operand_aliasing={{}: (6, {})} | custom-call | tf_op jit(solution)/shard_map/pallas_call | solution.py:71
  191.2 5.8 %shard_map.122.refs_6_ = bf16[8,12,32,16,128]{4,3,2,1,0:T(8,128)(2,1)} custom-call(s32[8]{0:T(128)S(1)} %iota_xor_fusion.refs_0_, bf16[8,12,32,16,128]{4,3,2,1,0:T(8,128)(2,1)} %get-tuple-element.76.refs_1_, bf16[192,192]{1,0:T(8,128)(2,1)S(1)} %mul.51.refs_4_.refs_2_, bf16[128,1024]{1,0:T(8,128)(2,1)S(1)} %copy-done, ...), custom_call_target="tpu_custom_call", output_to_operand_aliasing={{}: (6, {})} | custom-call | tf_op jit(solution)/shard_map/pallas_call | solution.py:71
  197.0 5.8 %shard_map.123 = bf16[8,12,32,16,128]{4,3,2,1,0:T(8,128)(2,1)} custom-call(s32[8]{0:T(128)S(1)} %iota_xor_fusion.refs_0_, bf16[8,12,32,16,128]{4,3,2,1,0:T(8,128)(2,1)} %get-tuple-element.76.refs_1_, bf16[192,192]{1,0:T(8,128)(2,1)S(1)} %mul.51.refs_4_.refs_2_, bf16[128,1024]{1,0:T(8,128)(2,1)S(1)} %copy-done, ...), custom_call_target="tpu_custom_call", output_to_operand_aliasing={{}: (6, {})} | custom-call | tf_op jit(solution)/shard_map/pallas_call | solution.py:71
  (36 shorter events, 0.1 us)
Async XLA Ops:
  0.6 1.0 copy-start.1
  5.7 14.6 %collective-permute-start.1 = (bf16[4,192,128]{2,1,0:T(8,128)(2,1)S(1)}, bf16[4,192,128]{2,1,0:T(8,128)(2,1)S(1)}, u32[]{:S(2)}, u32[]{:S(2)}) collective-permute-start(bf16[4,192,128]{2,1,0:T(8,128)(2,1)S(1)} %get-tuple-element.49), channel_id=1, source_target_pairs={{0,7},{1,6},{2,5},{3,4},{4,3},{5,2},{6,1},{7,0},{8,15},{9,14},{10,... | collective-permute-start | bytes 589832 | tf_op jit(solution)/shard_map/ppermute | solution.py:360
  9.1 28.0 %copy-start.4 = (bf16[12,12]{1,0:T(8,128)(2,1)S(1)}, bf16[12,12]{1,0:T(8,128)(2,1)}, u32[]{:S(2)}) copy-start(bf16[12,12]{1,0:T(8,128)(2,1)} %param.12) | copy-start | bytes 868
  9.1 11.7 %collective-permute-start = (bf16[4,192,128]{2,1,0:T(8,128)(2,1)S(1)}, bf16[4,192,128]{2,1,0:T(8,128)(2,1)S(1)}, u32[]{:S(2)}, u32[]{:S(2)}) collective-permute-start(bf16[4,192,128]{2,1,0:T(8,128)(2,1)S(1)} %get-tuple-element.48.refs_3_), channel_id=1, source_target_pairs={{0,6},{1,7},{2,4},{3,5},{4,2},{5,3},{6,0},{7,1},{8,14},{9,15},{10,... | collective-permute-start | bytes 589832 | tf_op jit(solution)/shard_map/ppermute | solution.py:360
  17.2 9.4 %collective-permute-start.3 = (bf16[4,192,128]{2,1,0:T(8,128)(2,1)S(1)}, bf16[4,192,128]{2,1,0:T(8,128)(2,1)S(1)}, u32[]{:S(2)}, u32[]{:S(2)}) collective-permute-start(bf16[4,192,128]{2,1,0:T(8,128)(2,1)S(1)} %get-tuple-element.52), channel_id=1, source_target_pairs={{0,2},{1,3},{2,0},{3,1},{4,6},{5,7},{6,4},{7,5},{8,10},{9,11},{10,... | collective-permute-start | bytes 589832 | tf_op jit(solution)/shard_map/ppermute | solution.py:360
  18.6 9.0 %collective-permute-start.4 = (bf16[4,192,128]{2,1,0:T(8,128)(2,1)S(1)}, bf16[4,192,128]{2,1,0:T(8,128)(2,1)S(1)}, u32[]{:S(2)}, u32[]{:S(2)}) collective-permute-start(bf16[4,192,128]{2,1,0:T(8,128)(2,1)S(1)} %get-tuple-element.53), channel_id=1, source_target_pairs={{0,3},{1,2},{2,1},{3,0},{4,7},{5,6},{6,5},{7,4},{8,11},{9,10},{10,... | collective-permute-start | bytes 589832 | tf_op jit(solution)/shard_map/ppermute | solution.py:360
  18.7 8.9 %collective-permute-start.5 = (bf16[4,192,128]{2,1,0:T(8,128)(2,1)S(1)}, bf16[4,192,128]{2,1,0:T(8,128)(2,1)S(1)}, u32[]{:S(2)}, u32[]{:S(2)}) collective-permute-start(bf16[4,192,128]{2,1,0:T(8,128)(2,1)S(1)} %get-tuple-element.54), channel_id=1, source_target_pairs={{0,4},{1,5},{2,6},{3,7},{4,0},{5,1},{6,2},{7,3},{8,12},{9,13},{10,... | collective-permute-start | bytes 589832 | tf_op jit(solution)/shard_map/ppermute | solution.py:360
  20.4 29.9 %copy-start.3 = (bf16[512,128]{1,0:T(8,128)(2,1)S(1)}, bf16[512,128]{1,0:T(8,128)(2,1)}, u32[]{:S(2)}) copy-start(bf16[512,128]{1,0:T(8,128)(2,1)} %constant.32.clone.refs_1_) | copy-start | bytes 393220
  20.4 52.8 %copy-start = (bf16[128,1024]{1,0:T(8,128)(2,1)S(1)}, bf16[128,1024]{1,0:T(8,128)(2,1)}, u32[]{:S(2)}) copy-start(bf16[128,1024]{1,0:T(8,128)(2,1)} %constant.30.clone.refs_4_.refs_3_) | copy-start | bytes 786436
  20.4 52.8 %copy-start.2 = (bf16[1024,128]{1,0:T(8,128)(2,1)S(1)}, bf16[1024,128]{1,0:T(8,128)(2,1)}, u32[]{:S(2)}) copy-start(bf16[1024,128]{1,0:T(8,128)(2,1)} %constant.31.clone.refs_2_.refs_5_) | copy-start | bytes 786436
  20.4 9.8 %collective-permute-start.6 = (bf16[4,192,128]{2,1,0:T(8,128)(2,1)S(1)}, bf16[4,192,128]{2,1,0:T(8,128)(2,1)S(1)}, u32[]{:S(2)}, u32[]{:S(2)}) collective-permute-start(bf16[4,192,128]{2,1,0:T(8,128)(2,1)S(1)} %get-tuple-element.55), channel_id=1, source_target_pairs={{0,5},{1,4},{2,7},{3,6},{4,1},{5,0},{6,3},{7,2},{8,13},{9,12},{10,... | collective-permute-start | bytes 589832 | tf_op jit(solution)/shard_map/ppermute | solution.py:360
  25.6 4.6 %collective-permute-start.2 = (bf16[4,192,128]{2,1,0:T(8,128)(2,1)}, bf16[4,192,128]{2,1,0:T(8,128)(2,1)S(1)}, u32[]{:S(2)}, u32[]{:S(2)}) collective-permute-start(bf16[4,192,128]{2,1,0:T(8,128)(2,1)} %get-tuple-element.51), channel_id=1, source_target_pairs={{0,1},{1,0},{2,3},{3,2},{4,5},{5,4},{6,7},{7,6},{8,9},{9,8},{10,11... | collective-permute-start | bytes 589832 | tf_op jit(solution)/shard_map/ppermute | solution.py:360
  31.6 18.7 %all-to-all-start = ((bf16[32,3,16,128]{3,2,1,0:T(8,128)(2,1)}), bf16[32,3,16,128]{3,2,1,0:T(8,128)(2,1)S(1)}, u32[]{:S(2)}, u32[]{:S(2)}) async-start(bf16[32,3,16,128]{3,2,1,0:T(8,128)(2,1)} %bitcast.10), calls=%async_computation | async-start | bytes 786432 | tf_op jit(solution)/shard_map/all_to_all | solution.py:355
  69.5 3.6 %collective-permute-start.7 = (bf16[4,192,128]{2,1,0:T(8,128)(2,1)S(1)}, bf16[4,192,128]{2,1,0:T(8,128)(2,1)S(1)}, u32[]{:S(2)}, u32[]{:S(2)}) collective-permute-start(bf16[4,192,128]{2,1,0:T(8,128)(2,1)S(1)} %bitcast.82), channel_id=1, source_target_pairs={{0,1},{1,0},{2,3},{3,2},{4,5},{5,4},{6,7},{7,6},{8,9},{9,8},{10,11... | collective-permute-start | bytes 589832 | tf_op jit(solution)/shard_map/ppermute | solution.py:360
  69.6 13.0 %collective-permute-start.12 = (bf16[4,192,128]{2,1,0:T(8,128)(2,1)S(1)}, bf16[4,192,128]{2,1,0:T(8,128)(2,1)S(1)}, u32[]{:S(2)}, u32[]{:S(2)}) collective-permute-start(bf16[4,192,128]{2,1,0:T(8,128)(2,1)S(1)} %bitcast.80), channel_id=1, source_target_pairs={{0,2},{1,3},{2,0},{3,1},{4,6},{5,7},{6,4},{7,5},{8,10},{9,11},{10,... | collective-permute-start | bytes 589832 | tf_op jit(solution)/shard_map/ppermute | solution.py:360
  70.5 12.3 %collective-permute-start.13 = (bf16[4,192,128]{2,1,0:T(8,128)(2,1)S(1)}, bf16[4,192,128]{2,1,0:T(8,128)(2,1)S(1)}, u32[]{:S(2)}, u32[]{:S(2)}) collective-permute-start(bf16[4,192,128]{2,1,0:T(8,128)(2,1)S(1)} %bitcast.78), channel_id=1, source_target_pairs={{0,3},{1,2},{2,1},{3,0},{4,7},{5,6},{6,5},{7,4},{8,11},{9,10},{10,... | collective-permute-start | bytes 589832 | tf_op jit(solution)/shard_map/ppermute | solution.py:360
  71.4 26.1 %collective-permute-start.10 = (bf16[4,192,128]{2,1,0:T(8,128)(2,1)S(1)}, bf16[4,192,128]{2,1,0:T(8,128)(2,1)S(1)}, u32[]{:S(2)}, u32[]{:S(2)}) collective-permute-start(bf16[4,192,128]{2,1,0:T(8,128)(2,1)S(1)} %bitcast.74), channel_id=1, source_target_pairs={{0,4},{1,5},{2,6},{3,7},{4,0},{5,1},{6,2},{7,3},{8,12},{9,13},{10,... | collective-permute-start | bytes 589832 | tf_op jit(solution)/shard_map/ppermute | solution.py:360
  72.4 26.1 %collective-permute-start.11 = (bf16[4,192,128]{2,1,0:T(8,128)(2,1)S(1)}, bf16[4,192,128]{2,1,0:T(8,128)(2,1)S(1)}, u32[]{:S(2)}, u32[]{:S(2)}) collective-permute-start(bf16[4,192,128]{2,1,0:T(8,128)(2,1)S(1)} %bitcast.73), channel_id=1, source_target_pairs={{0,5},{1,4},{2,7},{3,6},{4,1},{5,0},{6,3},{7,2},{8,13},{9,12},{10,... | collective-permute-start | bytes 589832 | tf_op jit(solution)/shard_map/ppermute | solution.py:360
  81.2 32.3 %collective-permute-start.8 = (bf16[4,192,128]{2,1,0:T(8,128)(2,1)S(1)}, bf16[4,192,128]{2,1,0:T(8,128)(2,1)S(1)}, u32[]{:S(2)}, u32[]{:S(2)}) collective-permute-start(bf16[4,192,128]{2,1,0:T(8,128)(2,1)S(1)} %get-tuple-element.61), channel_id=1, source_target_pairs={{0,6},{1,7},{2,4},{3,5},{4,2},{5,3},{6,0},{7,1},{8,14},{9,15},{10,... | collective-permute-start | bytes 589832 | tf_op jit(solution)/shard_map/ppermute | solution.py:360
  82.6 16.5 %collective-permute-start.14 = (bf16[4,192,128]{2,1,0:T(8,128)(2,1)S(1)}, bf16[4,192,128]{2,1,0:T(8,128)(2,1)S(1)}, u32[]{:S(2)}, u32[]{:S(2)}) collective-permute-start(bf16[4,192,128]{2,1,0:T(8,128)(2,1)S(1)} %get-tuple-element.69), channel_id=1, source_target_pairs={{0,1},{1,0},{2,3},{3,2},{4,5},{5,4},{6,7},{7,6},{8,9},{9,8},{10,11... | collective-permute-start | bytes 589832 | tf_op jit(solution)/shard_map/ppermute | solution.py:360
  82.8 31.7 %collective-permute-start.9 = (bf16[4,192,128]{2,1,0:T(8,128)(2,1)S(1)}, bf16[4,192,128]{2,1,0:T(8,128)(2,1)S(1)}, u32[]{:S(2)}, u32[]{:S(2)}) collective-permute-start(bf16[4,192,128]{2,1,0:T(8,128)(2,1)S(1)} %get-tuple-element.62), channel_id=1, source_target_pairs={{0,7},{1,6},{2,5},{3,4},{4,3},{5,2},{6,1},{7,0},{8,15},{9,14},{10,... | collective-permute-start | bytes 589832 | tf_op jit(solution)/shard_map/ppermute | solution.py:360
  97.5 16.9 %collective-permute-start.15 = (bf16[4,192,128]{2,1,0:T(8,128)(2,1)S(1)}, bf16[4,192,128]{2,1,0:T(8,128)(2,1)S(1)}, u32[]{:S(2)}, u32[]{:S(2)}) collective-permute-start(bf16[4,192,128]{2,1,0:T(8,128)(2,1)S(1)} %get-tuple-element.71), channel_id=1, source_target_pairs={{0,2},{1,3},{2,0},{3,1},{4,6},{5,7},{6,4},{7,5},{8,10},{9,11},{10,... | collective-permute-start | bytes 589832 | tf_op jit(solution)/shard_map/ppermute | solution.py:360
  98.5 16.0 %collective-permute-start.16 = (bf16[4,192,128]{2,1,0:T(8,128)(2,1)S(1)}, bf16[4,192,128]{2,1,0:T(8,128)(2,1)S(1)}, u32[]{:S(2)}, u32[]{:S(2)}) collective-permute-start(bf16[4,192,128]{2,1,0:T(8,128)(2,1)S(1)} %get-tuple-element.72), channel_id=1, source_target_pairs={{0,3},{1,2},{2,1},{3,0},{4,7},{5,6},{6,5},{7,4},{8,11},{9,10},{10,... | collective-permute-start | bytes 589832 | tf_op jit(solution)/shard_map/ppermute | solution.py:360
  112.5 17.8 %collective-permute-start.17 = (bf16[4,192,128]{2,1,0:T(8,128)(2,1)S(1)}, bf16[4,192,128]{2,1,0:T(8,128)(2,1)S(1)}, u32[]{:S(2)}, u32[]{:S(2)}) collective-permute-start(bf16[4,192,128]{2,1,0:T(8,128)(2,1)S(1)} %get-tuple-element.74), channel_id=1, source_target_pairs={{0,4},{1,5},{2,6},{3,7},{4,0},{5,1},{6,2},{7,3},{8,12},{9,13},{10,... | collective-permute-start | bytes 589832 | tf_op jit(solution)/shard_map/ppermute | solution.py:360
  113.5 16.8 %collective-permute-start.18 = (bf16[4,192,128]{2,1,0:T(8,128)(2,1)S(1)}, bf16[4,192,128]{2,1,0:T(8,128)(2,1)S(1)}, u32[]{:S(2)}, u32[]{:S(2)}) collective-permute-start(bf16[4,192,128]{2,1,0:T(8,128)(2,1)S(1)} %get-tuple-element.75), channel_id=1, source_target_pairs={{0,5},{1,4},{2,7},{3,6},{4,1},{5,0},{6,3},{7,2},{8,13},{9,12},{10,... | collective-permute-start | bytes 589832 | tf_op jit(solution)/shard_map/ppermute | solution.py:360
  127.9 10.4 %collective-permute-start.19 = (bf16[4,192,128]{2,1,0:T(8,128)(2,1)S(1)}, bf16[4,192,128]{2,1,0:T(8,128)(2,1)S(1)}, u32[]{:S(2)}, u32[]{:S(2)}) collective-permute-start(bf16[4,192,128]{2,1,0:T(8,128)(2,1)S(1)} %get-tuple-element.78), channel_id=1, source_target_pairs={{0,6},{1,7},{2,4},{3,5},{4,2},{5,3},{6,0},{7,1},{8,14},{9,15},{10,... | collective-permute-start | bytes 589832 | tf_op jit(solution)/shard_map/ppermute | solution.py:360
  129.2 10.0 %collective-permute-start.20 = (bf16[4,192,128]{2,1,0:T(8,128)(2,1)S(1)}, bf16[4,192,128]{2,1,0:T(8,128)(2,1)S(1)}, u32[]{:S(2)}, u32[]{:S(2)}) collective-permute-start(bf16[4,192,128]{2,1,0:T(8,128)(2,1)S(1)} %get-tuple-element.79), channel_id=1, source_target_pairs={{0,7},{1,6},{2,5},{3,4},{4,3},{5,2},{6,1},{7,0},{8,15},{9,14},{10,... | collective-permute-start | bytes 589832 | tf_op jit(solution)/shard_map/ppermute | solution.py:360
  157.0 15.8 %all-to-all-start.3 = ((bf16[32,3,16,128]{3,2,1,0:T(8,128)(2,1)}), bf16[32,3,16,128]{3,2,1,0:T(8,128)(2,1)S(1)}, u32[]{:S(2)}, u32[]{:S(2)}) async-start(bf16[32,3,16,128]{3,2,1,0:T(8,128)(2,1)} %bitcast.33), calls=%async_computation.3 | async-start | bytes 786432 | tf_op jit(solution)/shard_map/all_to_all | solution.py:355
  173.5 3.9 %collective-permute-start.21 = (bf16[4,192,128]{2,1,0:T(8,128)(2,1)S(1)}, bf16[4,192,128]{2,1,0:T(8,128)(2,1)S(1)}, u32[]{:S(2)}, u32[]{:S(2)}) collective-permute-start(bf16[4,192,128]{2,1,0:T(8,128)(2,1)S(1)} %bitcast.81), channel_id=1, source_target_pairs={{0,1},{1,0},{2,3},{3,2},{4,5},{5,4},{6,7},{7,6},{8,9},{9,8},{10,11... | collective-permute-start | bytes 589832 | tf_op jit(solution)/shard_map/ppermute | solution.py:360
  173.5 11.1 %collective-permute-start.26 = (bf16[4,192,128]{2,1,0:T(8,128)(2,1)S(1)}, bf16[4,192,128]{2,1,0:T(8,128)(2,1)S(1)}, u32[]{:S(2)}, u32[]{:S(2)}) collective-permute-start(bf16[4,192,128]{2,1,0:T(8,128)(2,1)S(1)} %bitcast.79), channel_id=1, source_target_pairs={{0,2},{1,3},{2,0},{3,1},{4,6},{5,7},{6,4},{7,5},{8,10},{9,11},{10,... | collective-permute-start | bytes 589832 | tf_op jit(solution)/shard_map/ppermute | solution.py:360
  174.5 16.7 %collective-permute-start.24 = (bf16[4,192,128]{2,1,0:T(8,128)(2,1)S(1)}, bf16[4,192,128]{2,1,0:T(8,128)(2,1)S(1)}, u32[]{:S(2)}, u32[]{:S(2)}) collective-permute-start(bf16[4,192,128]{2,1,0:T(8,128)(2,1)S(1)} %bitcast.76), channel_id=1, source_target_pairs={{0,4},{1,5},{2,6},{3,7},{4,0},{5,1},{6,2},{7,3},{8,12},{9,13},{10,... | collective-permute-start | bytes 589832 | tf_op jit(solution)/shard_map/ppermute | solution.py:360
  175.6 15.6 %collective-permute-start.25 = (bf16[4,192,128]{2,1,0:T(8,128)(2,1)S(1)}, bf16[4,192,128]{2,1,0:T(8,128)(2,1)S(1)}, u32[]{:S(2)}, u32[]{:S(2)}) collective-permute-start(bf16[4,192,128]{2,1,0:T(8,128)(2,1)S(1)} %bitcast.75), channel_id=1, source_target_pairs={{0,5},{1,4},{2,7},{3,6},{4,1},{5,0},{6,3},{7,2},{8,13},{9,12},{10,... | collective-permute-start | bytes 589832 | tf_op jit(solution)/shard_map/ppermute | solution.py:360
  175.6 9.7 %collective-permute-start.27 = (bf16[4,192,128]{2,1,0:T(8,128)(2,1)S(1)}, bf16[4,192,128]{2,1,0:T(8,128)(2,1)S(1)}, u32[]{:S(2)}, u32[]{:S(2)}) collective-permute-start(bf16[4,192,128]{2,1,0:T(8,128)(2,1)S(1)} %bitcast.77), channel_id=1, source_target_pairs={{0,3},{1,2},{2,1},{3,0},{4,7},{5,6},{6,5},{7,4},{8,11},{9,10},{10,... | collective-permute-start | bytes 589832 | tf_op jit(solution)/shard_map/ppermute | solution.py:360
  183.2 13.8 %collective-permute-start.22 = (bf16[4,192,128]{2,1,0:T(8,128)(2,1)S(1)}, bf16[4,192,128]{2,1,0:T(8,128)(2,1)S(1)}, u32[]{:S(2)}, u32[]{:S(2)}) collective-permute-start(bf16[4,192,128]{2,1,0:T(8,128)(2,1)S(1)} %get-tuple-element.87), channel_id=1, source_target_pairs={{0,6},{1,7},{2,4},{3,5},{4,2},{5,3},{6,0},{7,1},{8,14},{9,15},{10,... | collective-permute-start | bytes 589832 | tf_op jit(solution)/shard_map/ppermute | solution.py:360
  184.6 12.4 %collective-permute-start.23 = (bf16[4,192,128]{2,1,0:T(8,128)(2,1)S(1)}, bf16[4,192,128]{2,1,0:T(8,128)(2,1)S(1)}, u32[]{:S(2)}, u32[]{:S(2)}) collective-permute-start(bf16[4,192,128]{2,1,0:T(8,128)(2,1)S(1)} %get-tuple-element.88), channel_id=1, source_target_pairs={{0,7},{1,6},{2,5},{3,4},{4,3},{5,2},{6,1},{7,0},{8,15},{9,14},{10,... | collective-permute-start | bytes 589832 | tf_op jit(solution)/shard_map/ppermute | solution.py:360

commit v7 on v5

--- a/solution.py
+++ b/solution.py
@@ -51,28 +51,31 @@
 ANY = pl.BlockSpec(memory_space=pl.ANY)
 
 
-def call(body, grid, in_specs, out_specs, out_shape, args, order=None, scratch=(), aliases={}, after=()):
+def call(body, grid, in_specs, out_specs, out_shape, args, order=None, scratch=(), aliases={}, after=(), carry=()):
     lead = 0 if order is None else 1
-    count = lead + len(args)
+    count, outs = lead + len(args), len(out_shape)
+    idle = len(after) + len(carry)
 
     def placed(*refs):
-        body(*refs[:count], *refs[count + len(after) :])
+        ends = count + idle, count + idle + outs, count + idle + outs + len(carry)
+        body(*refs[:count], *refs[ends[0] : ends[1]], *refs[ends[2] :])
 
     spec = pltpu.PrefetchScalarGridSpec(
         num_scalar_prefetch=lead,
         grid=grid,
-        in_specs=list(in_specs) + [ANY] * len(after),
-        out_specs=out_specs,
+        in_specs=list(in_specs) + [ANY] * idle,
+        out_specs=list(out_specs) + [ANY] * len(carry),
         scratch_shapes=scratch,
     )
+    kept = {count + len(after) + e: outs + e for e in range(len(carry))}
     return pl.pallas_call(
         placed,
         grid_spec=spec,
-        out_shape=out_shape,
-        input_output_aliases={lead + operand: out for operand, out in aliases.items()},
-        compiler_params=pltpu.CompilerParams(vmem_limit_bytes=52 * 1024 * 1024),
+        out_shape=list(out_shape) + [jax.ShapeDtypeStruct(x.shape, x.dtype) for x in carry],
+        input_output_aliases={lead + operand: out for operand, out in aliases.items()} | kept,
+        compiler_params=pltpu.CompilerParams(vmem_limit_bytes=50 * 1024 * 1024),
         cost_estimate=pl.CostEstimate(flops=0, bytes_accessed=0, transcendentals=0),
-    )(*(() if order is None else (order,)), *args, *after)
+    )(*(() if order is None else (order,)), *args, *after, *carry)
 
 
 def whole(shape):
@@ -208,8 +211,6 @@
             first = (h * groups + k) * members
             done = dot(stacked, table_ref[...], 0, 0).astype(jnp.bfloat16)
             modes_ref[first : first + members] = done.reshape(members, span, lanes)
-    held = weight_ref.shape[:1] + weight_ref.shape[3:]
-    modes = [modes_ref[c].astype(jnp.float32).reshape(held) for c in range(channels)]
     for h in range(c_pieces):
         for k in range(groups):
             mixed = []
@@ -217,9 +218,9 @@
                 to = (h * groups + k) * members + m
                 total = 0.0
                 for of in range(channels):
-                    weight = weight_ref[:, to, of] if back else weight_ref[:, of, to]
-                    total += weight.astype(jnp.float32) * modes[of]
-                mixed.append(total.reshape(span, lanes).astype(jnp.bfloat16))
+                    weight = weight_ref[to, of] if back else weight_ref[of, to]
+                    total += weight.astype(jnp.float32) * modes_ref[of].astype(jnp.float32)
+                mixed.append(total.astype(jnp.bfloat16))
             done = dot(table_ref[...], jnp.concatenate(mixed, axis=0), 1, 1).astype(jnp.bfloat16)
             for g in range(planes):
                 for x in range(x_pieces):
@@ -228,7 +229,13 @@
 
 
 def weight_body(weight_ref, out_ref):
-    out_ref[0] = jnp.concatenate([weight_ref[j, 0] for j in range(weight_ref.shape[0])], axis=-1)
+    j_local, q_local, _, channels = weight_ref.shape[:4]
+    for o in range(channels):
+        rows = [
+            jnp.concatenate([weight_ref[j, q, 0, o].astype(jnp.float32) for j in range(j_local)], axis=1)
+            for q in range(q_local)
+        ]
+        out_ref[0, o] = jnp.concatenate(rows, axis=0).astype(out_ref.dtype)
 
 
 def outer_product_body(left_ref, right_ref, out_ref):
@@ -283,48 +290,45 @@
     block_head = jax.ShapeDtypeStruct((x_piece, rows, lanes), bf16)
     full_field = jax.ShapeDtypeStruct(state_field.shape, bf16)
     held = pltpu.VMEM(block_head.shape, bf16)
-    head_step, step = math.gcd(x_piece, 4), math.gcd(x_piece, 2)
-
-    def grouped(first, step):
+    long, short = math.gcd(x_piece, 4), math.gcd(x_piece, 2)
+
+    def plan(first, count, step):
         sub = x_piece // step
         where = lambda g, order: (0, 0, order[first + g // sub] * sub + g % sub, 0, 0)
-        return pl.BlockSpec((steps, channels, step, y_local, depth), where)
+        return sub, (count * sub,), pl.BlockSpec((steps, channels, step, y_local, depth), where)
 
     pairs = [(k, min(2, blocks - k)) for k in range(0, blocks, 2)]
-    groups = [(0, 1)] + pairs[1:] + [(1, 1)] if blocks > 1 else pairs
+    groups = [(1, 1)] + pairs[1:] + [(0, 1)] if blocks > 1 else pairs
 
     def head_call(first, count, after):
-        sub = x_piece // head_step
+        sub, grid, field = plan(first, count, long)
         return call(
-            functools.partial(head_body, sub), (count * sub,), [grouped(first, head_step), whole(ana.shape)],
-            [whole(block_head.shape)] * count, [block_head] * count,
-            (state_field, ana), order, [held], after=after,
-        )
-
-    def inner_call(first, count, middle, grads, after):
-        sub = x_piece // step
+            functools.partial(head_body, sub), grid, [field, whole(ana.shape)],
+            [whole(block_head.shape)] * count, [block_head] * count, (state_field, ana), order, [held], after=after,
+        )
+
+    def inner_call(first, count, middle, grads, after, carry):
+        sub, grid, field = plan(first, count, short)
         tables = (mix_up, syn, ana)
-        spec = grouped(first, step)
         done = call(
-            functools.partial(inner_body, sub, count), (count * sub,),
-            [spec] * 2 + [whole(arg.shape) for arg in tables] + [whole(block_head.shape)] * count + [ANY] * len(grads),
-            [spec] + [whole(block_head.shape)] * count, [full_field] + [block_head] * count,
-            (state_field, cotangent, *tables, *middle[first : first + count], *grads), order, [held, held],
-            {5 + count: 0} if grads else {}, after,
+            functools.partial(inner_body, sub, count), grid,
+            [field] * 2 + [whole(arg.shape) for arg in tables] + [whole(block_head.shape)] * count + [ANY] * len(grads),
+            [field] + [whole(block_head.shape)] * count, [full_field] + [block_head] * count,
+            (state_field, cotangent, *tables, *middle[first : first + count], *grads), order,
+            [held, held], {5 + count: 0} if grads else {}, after, carry,
+        )
+        return done[:1], done[1 : 1 + count], done[1 + count :]
+
+    def outer_call(first, count, middle, grads, field, carry):
+        sub, grid, spec = plan(first, count, long)
+        tables = (mix_back, syn)
+        done = call(
+            functools.partial(outer_body, sub, count), grid,
+            [spec] + [whole(arg.shape) for arg in tables] + [whole(block_head.shape)] * count + [ANY] * len(field),
+            [spec], [full_field], (*grads, *tables, *middle[first : first + count], *field), order,
+            [held], {3 + count: 0} if field else {}, (), carry,
         )
         return done[:1], done[1:]
-
-    def outer_call(first, count, middle, grads, field):
-        sub = x_piece // step
-        tables = (mix_back, syn)
-        spec = grouped(first, step)
-        return call(
-            functools.partial(outer_body, sub, count), (count * sub,),
-            [spec] + [whole(arg.shape) for arg in tables] + [whole(block_head.shape)] * count + [ANY] * len(field),
-            [spec], [full_field],
-            (*grads, *tables, *middle[first : first + count], *field), order, [held],
-            {3 + count: 0} if field else {},
-        )
 
     def small(body, outs, *args, after=()):
         shapes = [jax.ShapeDtypeStruct(out, bf16) for out in outs]
@@ -354,51 +358,68 @@
 
     cells = (x_piece, c_piece, y_local, lanes)
 
-    def analyze(back, heads, weight, after):
-        (part,) = small(y_down_body, [packed], y_mat, *settle(heads, y_devices, cells), after=after)
+    def analyze(heads):
+        return small(y_down_body, [packed], y_mat, *settle(heads, y_devices, cells))[0]
+
+    def mix(back, part, weight, after):
         part = exchange(part).reshape((x_devices, x_pieces, c_pieces) + packed[2:])
         kept, part = small(
-            functools.partial(spectral_body, back), [(channels, span, j_local * modes), part.shape], part, x_mat, weight
+            functools.partial(spectral_body, back), [(channels, span, j_local * modes), part.shape],
+            part, x_mat, weight, after=after,
         )
         return kept, exchange(part).reshape(packed)
 
     def synthesize(part, after):
         pieces = small(y_up_body, [cells] * y_devices, part, y_mat_t, after=after)
-        pieces = [send(k, piece) for k, piece in enumerate(pieces)]
+        if paired:
+            pieces = [piece.reshape(block_head.shape) for piece in pieces]
+        late = pieces[6:] if paired else []
+        return [send(k, piece) for k, piece in enumerate(pieces[: len(pieces) - len(late)])], late
+
+    def rest(pieces, late):
+        pieces = pieces + [send(len(pieces) + e, piece) for e, piece in enumerate(late)]
         return settle(pieces, blocks, block_head.shape)
-
-    weight = call(
-        weight_body, (q_local,),
-        [pl.BlockSpec((j_local, 1, channels, channels, time_modes, modes), lambda q: (0, q, 0, 0, 0, 0))],
-        pl.BlockSpec((1, channels, channels, time_modes, j_local * modes), lambda q: (q, 0, 0, 0, 0)),
-        jax.ShapeDtypeStruct((q_local, channels, channels, time_modes, j_local * modes), bf16), (spectral_weight,),
-    )
 
     heads, after = [None] * blocks, ()
     for first, count in ((6, 2), (2, 4), (0, 2)) if blocks == 8 else ((0, blocks),):
         done = head_call(first, count, after)
         heads[first : first + count] = [send(first + e, piece) for e, piece in enumerate(done)]
         after = (done[0],) if first == 6 else tuple(heads[6:])
-    modes_in, part = analyze(False, heads, weight, (weight, mix_up, mix_back, y_mat_t))
-    middle = synthesize(part, ())
-
-    grads, sent = (), [(), ()]
+    part = analyze(heads)
+    (weight,) = call(
+        weight_body, (channels,),
+        [pl.BlockSpec((j_local, q_local, 1, channels, time_modes, modes), lambda c: (0, 0, c, 0, 0, 0))],
+        [pl.BlockSpec((1, channels, span, j_local * modes), lambda c: (c, 0, 0, 0))],
+        [jax.ShapeDtypeStruct((channels, channels, span, j_local * modes), bf16)], (spectral_weight,), after=(part,),
+    )
+    modes_in, part = mix(False, part, weight, (mix_up, mix_back, y_mat_t))
+
+    middle, late = synthesize(part, ())
+    sent, grads = [(), ()], ()
+    if not paired:
+        middle = rest(middle, late)
     for first, count in groups:
-        grads, done = inner_call(first, count, middle, grads, sent[-2])
+        grads, done, late = inner_call(first, count, middle, grads, sent[-2], late)
+        if late:
+            middle, late = rest(middle, late), []
         heads[first : first + count] = [send(first + e, piece) for e, piece in enumerate(done)]
         sent.append(tuple(heads[max(first, 1) : first + count]) if paired else ())
-    grad_modes, part = analyze(True, heads, weight, ())
+    part = analyze(heads)
+    grad_modes, part = mix(True, part, weight, ())
     spec = whole(modes_in.shape)
-    grad_spectral = call(
+    (grad_spectral,) = call(
         outer_product_body, (j_local,), [spec, spec],
-        pl.BlockSpec((1,) + spectral_weight.shape[1:], lambda j: (j, 0, 0, 0, 0, 0)),
-        jax.ShapeDtypeStruct(spectral_weight.shape, jnp.float32),
-        (modes_in, grad_modes),
-    )
-    middle = synthesize(part, (grad_spectral,))
+        [pl.BlockSpec((1,) + spectral_weight.shape[1:], lambda j: (j, 0, 0, 0, 0, 0))],
+        [jax.ShapeDtypeStruct(spectral_weight.shape, jnp.float32)], (modes_in, grad_modes),
+    )
+    middle, late = synthesize(part, (grad_spectral,))
+    if not paired:
+        middle = rest(middle, late)
     field = ()
     for first, count in pairs:
-        field = outer_call(first, count, middle, grads, field)
+        field, late = outer_call(first, count, middle, grads, field, late)
+        if late:
+            middle, late = rest(middle, late), []
     return field[0], grad_spectral
 
 

time: 221 us -> 191 us (0.86)
  blocking collectives: 49.4 us -> 33.8 us
  waiting for transfers between devices: 26.6 us -> 16.1 us
  Pallas kernels: 104 us -> 96.7 us
  starting transfers between devices: 28 us -> 34.5 us
  local copies, waits for them, and re-layouts: 8.07 us -> 5.26 us
    all_to_all x3 -> x2, blocking collectives: 49.4 us -> 33.8 us  [exchange(): return lax.all_to_all(pieces, ('gx',) + YZ, 0, 0, tiled=True).reshape(shape)]
    ppermute x28, waiting for transfers between devices: 18 us -> 6.71 us  [send(): return lax.ppermute(piece, YZ, [(d, d ^ k) for d in range(y_devices)])]
    pallas_call x20, Pallas kernels: 104 us -> 96.7 us  [call(): pl.pallas_call(placed, grid_spec=spec, out_shape=list(out_shape) + [jax.S...]
    all_to_all x1 -> x2, starting transfers between devices: 2.6 us -> 8.12 us  [exchange(): return lax.all_to_all(pieces, ('gx',) + YZ, 0, 0, tiled=True).reshape(shape)]
    all_to_all x1 -> x2, waiting for transfers between devices: 8.56 us -> 9.44 us  [exchange(): return lax.all_to_all(pieces, ('gx',) + YZ, 0, 0, tiled=True).reshape(shape)]
  transfers between devices with their start and end apart: 29 -> 30, of which waited for: 6 -> 6; matrix products, arithmetic and copies ran while one was open for 3% -> 3% of each run, Pallas kernels for 35% -> 44%
where the time goes in v7:
time: 191 us; the launch traced here: 188 us
  Pallas kernels  96.7 us (51%)
  starting transfers between devices  34.5 us (18%)
  blocking collectives  33.8 us (18%)
  waiting for transfers between devices  16.1 us (8%)
  local copies, waits for them, and re-layouts  5.26 us (3%)
    pallas_call x20, Pallas kernels, call(): pl.pallas_call(placed, grid_spec=spec, out_shape=list(out_shape) + [jax.S...  96.7 us
    all_to_all x2, blocking collectives, exchange(): return lax.all_to_all(pieces, ('gx',) + YZ, 0, 0, tiled=True).reshape(shape)  33.8 us
    ppermute x28, starting transfers between devices, send(): return lax.ppermute(piece, YZ, [(d, d ^ k) for d in range(y_devices)])  26.3 us
    all_to_all x2, waiting for transfers between devices, exchange(): return lax.all_to_all(pieces, ('gx',) + YZ, 0, 0, tiled=True).reshape(shape)  9.44 us
    all_to_all x2, starting transfers between devices, exchange(): return lax.all_to_all(pieces, ('gx',) + YZ, 0, 0, tiled=True).reshape(shape)  8.12 us
    ppermute x28, waiting for transfers between devices, send(): return lax.ppermute(piece, YZ, [(d, d ^ k) for d in range(y_devices)])  6.71 us
  transfers between devices with their start and end apart: 30, of which 6 were waited for; matrix products, arithmetic and copies ran while one was open for 3% of the time, Pallas kernels for 44%

profile of v7, /device:TPU:0, one launch (start us, length us, event | category | flops | bytes accessed | tf_op | source)
XLA Modules:
  0.0 188.3 jit_solution(11194413734048401599)
XLA Ops:
  0.7 0.9 copy-done.1
  1.6 3.2 %shard_map.104 = (bf16[4,192,128]{2,1,0:T(8,128)(2,1)S(1)}, bf16[4,192,128]{2,1,0:T(8,128)(2,1)S(1)}) custom-call(s32[8]{0:T(128)S(1)} %iota_xor_fusion.refs_0_, bf16[8,12,32,16,128]{4,3,2,1,0:T(8,128)(2,1)} %refs_1_.17, bf16[1024,128]{1,0:T(8,128)(2,1)S(1)} %copy-done.1), custom_call_target="tpu_custom_call" | custom-call | tf_op jit(solution)/shard_map/pallas_call | solution.py:71
  4.8 3.4 %collective-permute-start.1 = (bf16[4,192,128]{2,1,0:T(8,128)(2,1)S(1)}, bf16[4,192,128]{2,1,0:T(8,128)(2,1)S(1)}, u32[]{:S(2)}, u32[]{:S(2)}) collective-permute-start(bf16[4,192,128]{2,1,0:T(8,128)(2,1)S(1)} %get-tuple-element.49), channel_id=1, source_target_pairs={{0,7},{1,6},{2,5},{3,4},{4,3},{5,2},{6,1},{7,0},{8,15},{9,14},{10,... | collective-permute-start | bytes 589832 | tf_op jit(solution)/shard_map/ppermute | solution.py:351
  8.2 0.6 collective-permute-start
  8.8 5.3 %shard_map.106 = (bf16[4,192,128]{2,1,0:T(8,128)(2,1)S(1)}, bf16[4,192,128]{2,1,0:T(8,128)(2,1)S(1)}, bf16[4,192,128]{2,1,0:T(8,128)(2,1)S(1)}, bf16[4,192,128]{2,1,0:T(8,128)(2,1)S(1)}) custom-call(s32[8]{0:T(128)S(1)} %iota_xor_fusion.refs_0_, bf16[8,12,32,16,128]{4,3,2,1,0:T(8,128)(2,1)} %refs_1_.17, bf16[1024,128]{1,0:T(8,128)(2,1)S(1)} %copy-done.1, ...), custom_call_target="tpu_custom_call" | custom-call | tf_op jit(solution)/shard_map/pallas_call | solution.py:71
  14.2 1.4 collective-permute-start.3
  15.6 0.0 collective-permute-start.4
  15.6 1.7 collective-permute-start.5
  17.3 0.5 collective-permute-start.6
  17.8 3.8 %shard_map.105 = (bf16[4,192,128]{2,1,0:T(8,128)(2,1)S(1)}, bf16[4,192,128]{2,1,0:T(8,128)(2,1)}) custom-call(s32[8]{0:T(128)S(1)} %iota_xor_fusion.refs_0_, bf16[8,12,32,16,128]{4,3,2,1,0:T(8,128)(2,1)} %refs_1_.17, bf16[1024,128]{1,0:T(8,128)(2,1)S(1)} %copy-done.1, bf16[4,192,128]{2,1,0:T(8,128)(2,1)S(1)} %collective-permute-done.refs_3_, ...), custom_call_target="tpu_custom_call" | custom-call | tf_op jit(solution)/shard_map/pallas_call | solution.py:71
  21.7 0.9 dynamic-slice_bitcast_fusion.1.refs_0_
  22.6 0.3 collective-permute-done.3
  22.9 4.2 %collective-permute-done.4 = bf16[4,192,128]{2,1,0:T(8,128)(2,1)S(1)} collective-permute-done((bf16[4,192,128]{2,1,0:T(8,128)(2,1)S(1)}, bf16[4,192,128]{2,1,0:T(8,128)(2,1)S(1)}, u32[]{:S(2)}, u32[]{:S(2)}) %collective-permute-start.4) | collective-permute-done | bytes 196640 | tf_op jit(solution)/shard_map/ppermute | solution.py:351
  27.1 0.1 collective-permute-done.6
  27.2 1.4 shard_map.107.refs_1_
  28.6 5.5 %all-to-all-start = ((bf16[32,3,16,128]{3,2,1,0:T(8,128)(2,1)}), bf16[32,3,16,128]{3,2,1,0:T(8,128)(2,1)S(1)}, u32[]{:S(2)}, u32[]{:S(2)}) async-start(bf16[32,3,16,128]{3,2,1,0:T(8,128)(2,1)} %bitcast.10), calls=%async_computation | async-start | bytes 786432 | tf_op jit(solution)/shard_map/all_to_all | solution.py:346
  34.1 0.1 copy.23
  34.2 1.1 broadcast_multiply_fusion
  35.2 1.7 mul.51.refs_4_.refs_2_
  36.9 0.7 mul.48.refs_3_
  37.6 0.9 dynamic-slice_bitcast_fusion.refs_5_.refs_1_
  38.5 7.8 %shard_map.108.refs_2_ = bf16[12,12,32,128]{3,2,1,0:T(8,128)(2,1)S(1)} custom-call(bf16[4,8,12,12,4,32]{5,4,3,2,1,0:T(4,128)(2,1)} %refs_0_.1, bf16[4,8,3,16,128]{4,3,2,1,0:T(8,128)(2,1)} %shard_map.107.refs_1_), custom_call_target="tpu_custom_call" | custom-call | tf_op jit(solution)/shard_map/pallas_call | solution.py:71
  46.3 0.9 all-to-all-done
  47.2 0.6 shard_map.109
  47.8 18.0 %all_to_all.20 = bf16[32,3,16,128]{3,2,1,0:T(8,128)(2,1)S(1)} all-to-all(bf16[32,3,16,128]{3,2,1,0:T(8,128)(2,1)S(1)} %bitcast.57), channel_id=1, replica_groups=mesh['parts'=1,'gx'=4,'gy'=4,'gz'=2] {'gx','gy','gz'}, dimensions={0} | all-to-all | bytes 786432 | tf_op jit(solution)/shard_map/all_to_all | solution.py:346
  65.8 0.7 shard_map.110
  66.5 0.1 collective-permute-start.7
  66.5 1.0 collective-permute-start.12
  67.5 0.9 collective-permute-start.13
  68.4 1.0 collective-permute-start.10
  69.4 0.7 collective-permute-start.11
  70.1 6.8 %shard_map.111 = (bf16[8,12,32,16,128]{4,3,2,1,0:T(8,128)(2,1)}, bf16[4,192,128]{2,1,0:T(8,128)(2,1)S(1)}, bf16[4,192,128]{2,1,0:T(8,128)(2,1)S(1)}, bf16[4,192,128]{2,1,0:T(8,128)(2,1)S(1)}) custom-call(s32[8]{0:T(128)S(1)} %iota_xor_fusion.refs_0_, bf16[8,12,32,16,128]{4,3,2,1,0:T(8,128)(2,1)} %refs_1_.17, ...), custom_call_target="tpu_custom_call", output_to_operand_aliasing={{2}: (7, {}), {3}: (8, {})} | custom-call | tf_op jit(solution)/shard_map/pallas_call | solution.py:71
  76.9 1.4 collective-permute-start.8
  78.3 0.2 collective-permute-start.14
  78.5 1.4 collective-permute-start.9
  80.0 10.8 %shard_map.112 = (bf16[8,12,32,16,128]{4,3,2,1,0:T(8,128)(2,1)}, bf16[4,192,128]{2,1,0:T(8,128)(2,1)S(1)}, bf16[4,192,128]{2,1,0:T(8,128)(2,1)S(1)}) custom-call(s32[8]{0:T(128)S(1)} %iota_xor_fusion.refs_0_, bf16[8,12,32,16,128]{4,3,2,1,0:T(8,128)(2,1)} %refs_1_.17, bf16[8,12,32,16,128]{4,3,2,1,0:T(8,128)(2,1)} %refs_2_.12, ...), custom_call_target="tpu_custom_call", output_to_operand_aliasing={{0}: (8, {})} | custom-call | tf_op jit(solution)/shard_map/pallas_call | solution.py:71
  90.8 0.9 collective-permute-start.15
  91.7 0.6 collective-permute-start.16
  92.4 10.9 %shard_map.113 = (bf16[8,12,32,16,128]{4,3,2,1,0:T(8,128)(2,1)}, bf16[4,192,128]{2,1,0:T(8,128)(2,1)S(1)}, bf16[4,192,128]{2,1,0:T(8,128)(2,1)S(1)}) custom-call(s32[8]{0:T(128)S(1)} %iota_xor_fusion.refs_0_, bf16[8,12,32,16,128]{4,3,2,1,0:T(8,128)(2,1)} %refs_1_.17, bf16[8,12,32,16,128]{4,3,2,1,0:T(8,128)(2,1)} %refs_2_.12, ...), custom_call_target="tpu_custom_call", output_to_operand_aliasing={{0}: (8, {})} | custom-call | tf_op jit(solution)/shard_map/pallas_call | solution.py:71
  103.2 1.0 collective-permute-start.17
  104.2 1.0 collective-permute-start.18
  105.2 10.9 %shard_map.114 = (bf16[8,12,32,16,128]{4,3,2,1,0:T(8,128)(2,1)}, bf16[4,192,128]{2,1,0:T(8,128)(2,1)S(1)}, bf16[4,192,128]{2,1,0:T(8,128)(2,1)S(1)}) custom-call(s32[8]{0:T(128)S(1)} %iota_xor_fusion.refs_0_, bf16[8,12,32,16,128]{4,3,2,1,0:T(8,128)(2,1)} %refs_1_.17, bf16[8,12,32,16,128]{4,3,2,1,0:T(8,128)(2,1)} %refs_2_.12, ...), custom_call_target="tpu_custom_call", output_to_operand_aliasing={{0}: (8, {})} | custom-call | tf_op jit(solution)/shard_map/pallas_call | solution.py:71
  116.1 1.4 collective-permute-start.19
  117.5 1.1 collective-permute-start.20
  118.5 6.8 %shard_map.115 = (bf16[8,12,32,16,128]{4,3,2,1,0:T(8,128)(2,1)}, bf16[4,192,128]{2,1,0:T(8,128)(2,1)S(1)}) custom-call(s32[8]{0:T(128)S(1)} %iota_xor_fusion.refs_0_, bf16[8,12,32,16,128]{4,3,2,1,0:T(8,128)(2,1)} %refs_1_.17, bf16[8,12,32,16,128]{4,3,2,1,0:T(8,128)(2,1)} %refs_2_.12, ...), custom_call_target="tpu_custom_call", output_to_operand_aliasing={{0}: (7, {})} | custom-call | tf_op jit(solution)/shard_map/pallas_call | solution.py:71
  125.4 2.1 %collective-permute-done.20 = bf16[4,192,128]{2,1,0:T(8,128)(2,1)S(1)} collective-permute-done((bf16[4,192,128]{2,1,0:T(8,128)(2,1)S(1)}, bf16[4,192,128]{2,1,0:T(8,128)(2,1)S(1)}, u32[]{:S(2)}, u32[]{:S(2)}) %collective-permute-start.20) | collective-permute-done | bytes 196640 | tf_op jit(solution)/shard_map/ppermute | solution.py:351
  127.4 0.6 shard_map.116
  128.1 15.8 %all_to_all.21 = bf16[32,3,16,128]{3,2,1,0:T(8,128)(2,1)S(1)} all-to-all(bf16[32,3,16,128]{3,2,1,0:T(8,128)(2,1)S(1)} %bitcast.47), channel_id=1, replica_groups=mesh['parts'=1,'gx'=4,'gy'=4,'gz'=2] {'gx','gy','gz'}, dimensions={0} | all-to-all | bytes 786432 | tf_op jit(solution)/shard_map/all_to_all | solution.py:346
  143.9 1.3 shard_map.117
  145.3 2.6 %all-to-all-start.3 = ((bf16[32,3,16,128]{3,2,1,0:T(8,128)(2,1)}), bf16[32,3,16,128]{3,2,1,0:T(8,128)(2,1)S(1)}, u32[]{:S(2)}, u32[]{:S(2)}) async-start(bf16[32,3,16,128]{3,2,1,0:T(8,128)(2,1)} %bitcast.33), calls=%async_computation.3 | async-start | bytes 786432 | tf_op jit(solution)/shard_map/all_to_all | solution.py:346
  147.9 4.6 %shard_map.118.refs_2_ = f32[4,8,12,12,4,32]{5,4,3,2,1,0:T(4,128)} custom-call(bf16[12,32,128]{2,1,0:T(8,128)(2,1)S(1)} %get-tuple-element.81.refs_0_, bf16[12,32,128]{2,1,0:T(8,128)(2,1)S(1)} %get-tuple-element.82.refs_1_), custom_call_target="tpu_custom_call" | custom-call | tf_op jit(solution)/shard_map/pallas_call | solution.py:71
  152.5 8.6 %all-to-all-done.3 = bf16[32,3,16,128]{3,2,1,0:T(8,128)(2,1)S(1)} async-done(((bf16[32,3,16,128]{3,2,1,0:T(8,128)(2,1)}), bf16[32,3,16,128]{3,2,1,0:T(8,128)(2,1)S(1)}, u32[]{:S(2)}, u32[]{:S(2)}) %all-to-all-start.3) | async-done | bytes 393248 | tf_op jit(solution)/shard_map/all_to_all | solution.py:346
  161.1 0.7 shard_map.119
  161.7 0.1 collective-permute-start.21
  161.8 0.9 collective-permute-start.26
  162.8 1.1 collective-permute-start.24
  163.9 0.1 collective-permute-start.25
  163.9 1.7 collective-permute-start.27
  165.7 5.1 %shard_map.120 = (bf16[8,12,32,16,128]{4,3,2,1,0:T(8,128)(2,1)}, bf16[4,192,128]{2,1,0:T(8,128)(2,1)S(1)}, bf16[4,192,128]{2,1,0:T(8,128)(2,1)S(1)}) custom-call(s32[8]{0:T(128)S(1)} %iota_xor_fusion.refs_0_, bf16[8,12,32,16,128]{4,3,2,1,0:T(8,128)(2,1)} %get-tuple-element.76.refs_1_, ...), custom_call_target="tpu_custom_call", output_to_operand_aliasing={{1}: (6, {}), {2}: (7, {})} | custom-call | tf_op jit(solution)/shard_map/pallas_call | solution.py:71
  170.8 1.4 collective-permute-start.22
  172.2 0.7 collective-permute-start.23
  172.9 5.1 %shard_map.121.refs_6_ = bf16[8,12,32,16,128]{4,3,2,1,0:T(8,128)(2,1)} custom-call(s32[8]{0:T(128)S(1)} %iota_xor_fusion.refs_0_, bf16[8,12,32,16,128]{4,3,2,1,0:T(8,128)(2,1)} %get-tuple-element.76.refs_1_, bf16[192,192]{1,0:T(8,128)(2,1)S(1)} %mul.51.refs_4_.refs_2_, bf16[128,1024]{1,0:T(8,128)(2,1)S(1)} %copy-done, ...), custom_call_target="tpu_custom_call", output_to_operand_aliasing={{}: (6, {})} | custom-call | tf_op jit(solution)/shard_map/pallas_call | solution.py:71
  178.0 5.1 %shard_map.122.refs_6_ = bf16[8,12,32,16,128]{4,3,2,1,0:T(8,128)(2,1)} custom-call(s32[8]{0:T(128)S(1)} %iota_xor_fusion.refs_0_, bf16[8,12,32,16,128]{4,3,2,1,0:T(8,128)(2,1)} %get-tuple-element.76.refs_1_, bf16[192,192]{1,0:T(8,128)(2,1)S(1)} %mul.51.refs_4_.refs_2_, bf16[128,1024]{1,0:T(8,128)(2,1)S(1)} %copy-done, ...), custom_call_target="tpu_custom_call", output_to_operand_aliasing={{}: (6, {})} | custom-call | tf_op jit(solution)/shard_map/pallas_call | solution.py:71
  183.2 5.1 %shard_map.123 = bf16[8,12,32,16,128]{4,3,2,1,0:T(8,128)(2,1)} custom-call(s32[8]{0:T(128)S(1)} %iota_xor_fusion.refs_0_, bf16[8,12,32,16,128]{4,3,2,1,0:T(8,128)(2,1)} %get-tuple-element.76.refs_1_, bf16[192,192]{1,0:T(8,128)(2,1)S(1)} %mul.51.refs_4_.refs_2_, bf16[128,1024]{1,0:T(8,128)(2,1)S(1)} %copy-done, ...), custom_call_target="tpu_custom_call", output_to_operand_aliasing={{}: (6, {})} | custom-call | tf_op jit(solution)/shard_map/pallas_call | solution.py:71
  (36 shorter events, 0.1 us)
Async XLA Ops:
  0.6 1.0 copy-start.1
  4.8 12.6 %collective-permute-start.1 = (bf16[4,192,128]{2,1,0:T(8,128)(2,1)S(1)}, bf16[4,192,128]{2,1,0:T(8,128)(2,1)S(1)}, u32[]{:S(2)}, u32[]{:S(2)}) collective-permute-start(bf16[4,192,128]{2,1,0:T(8,128)(2,1)S(1)} %get-tuple-element.49), channel_id=1, source_target_pairs={{0,7},{1,6},{2,5},{3,4},{4,3},{5,2},{6,1},{7,0},{8,15},{9,14},{10,... | collective-permute-start | bytes 589832 | tf_op jit(solution)/shard_map/ppermute | solution.py:351
  8.2 25.9 %copy-start.4 = (bf16[12,12]{1,0:T(8,128)(2,1)S(1)}, bf16[12,12]{1,0:T(8,128)(2,1)}, u32[]{:S(2)}) copy-start(bf16[12,12]{1,0:T(8,128)(2,1)} %param.12) | copy-start | bytes 868
  8.2 9.7 %collective-permute-start = (bf16[4,192,128]{2,1,0:T(8,128)(2,1)S(1)}, bf16[4,192,128]{2,1,0:T(8,128)(2,1)S(1)}, u32[]{:S(2)}, u32[]{:S(2)}) collective-permute-start(bf16[4,192,128]{2,1,0:T(8,128)(2,1)S(1)} %get-tuple-element.48.refs_3_), channel_id=1, source_target_pairs={{0,6},{1,7},{2,4},{3,5},{4,2},{5,3},{6,0},{7,1},{8,14},{9,15},{10,... | collective-permute-start | bytes 589832 | tf_op jit(solution)/shard_map/ppermute | solution.py:351
  14.2 8.7 %collective-permute-start.3 = (bf16[4,192,128]{2,1,0:T(8,128)(2,1)S(1)}, bf16[4,192,128]{2,1,0:T(8,128)(2,1)S(1)}, u32[]{:S(2)}, u32[]{:S(2)}) collective-permute-start(bf16[4,192,128]{2,1,0:T(8,128)(2,1)S(1)} %get-tuple-element.52), channel_id=1, source_target_pairs={{0,2},{1,3},{2,0},{3,1},{4,6},{5,7},{6,4},{7,5},{8,10},{9,11},{10,... | collective-permute-start | bytes 589832 | tf_op jit(solution)/shard_map/ppermute | solution.py:351
  15.6 11.5 %collective-permute-start.4 = (bf16[4,192,128]{2,1,0:T(8,128)(2,1)S(1)}, bf16[4,192,128]{2,1,0:T(8,128)(2,1)S(1)}, u32[]{:S(2)}, u32[]{:S(2)}) collective-permute-start(bf16[4,192,128]{2,1,0:T(8,128)(2,1)S(1)} %get-tuple-element.53), channel_id=1, source_target_pairs={{0,3},{1,2},{2,1},{3,0},{4,7},{5,6},{6,5},{7,4},{8,11},{9,10},{10,... | collective-permute-start | bytes 589832 | tf_op jit(solution)/shard_map/ppermute | solution.py:351
  15.6 11.4 %collective-permute-start.5 = (bf16[4,192,128]{2,1,0:T(8,128)(2,1)S(1)}, bf16[4,192,128]{2,1,0:T(8,128)(2,1)S(1)}, u32[]{:S(2)}, u32[]{:S(2)}) collective-permute-start(bf16[4,192,128]{2,1,0:T(8,128)(2,1)S(1)} %get-tuple-element.54), channel_id=1, source_target_pairs={{0,4},{1,5},{2,6},{3,7},{4,0},{5,1},{6,2},{7,3},{8,12},{9,13},{10,... | collective-permute-start | bytes 589832 | tf_op jit(solution)/shard_map/ppermute | solution.py:351
  17.3 29.9 %copy-start.3 = (bf16[512,128]{1,0:T(8,128)(2,1)S(1)}, bf16[512,128]{1,0:T(8,128)(2,1)}, u32[]{:S(2)}) copy-start(bf16[512,128]{1,0:T(8,128)(2,1)} %constant.32.clone.refs_1_) | copy-start | bytes 393220
  17.3 52.8 %copy-start = (bf16[128,1024]{1,0:T(8,128)(2,1)S(1)}, bf16[128,1024]{1,0:T(8,128)(2,1)}, u32[]{:S(2)}) copy-start(bf16[128,1024]{1,0:T(8,128)(2,1)} %constant.30.clone.refs_4_.refs_3_) | copy-start | bytes 786436
  17.3 52.8 %copy-start.2 = (bf16[1024,128]{1,0:T(8,128)(2,1)S(1)}, bf16[1024,128]{1,0:T(8,128)(2,1)}, u32[]{:S(2)}) copy-start(bf16[1024,128]{1,0:T(8,128)(2,1)} %constant.31.clone.refs_2_.refs_5_) | copy-start | bytes 786436
  17.3 9.8 %collective-permute-start.6 = (bf16[4,192,128]{2,1,0:T(8,128)(2,1)S(1)}, bf16[4,192,128]{2,1,0:T(8,128)(2,1)S(1)}, u32[]{:S(2)}, u32[]{:S(2)}) collective-permute-start(bf16[4,192,128]{2,1,0:T(8,128)(2,1)S(1)} %get-tuple-element.55), channel_id=1, source_target_pairs={{0,5},{1,4},{2,7},{3,6},{4,1},{5,0},{6,3},{7,2},{8,13},{9,12},{10,... | collective-permute-start | bytes 589832 | tf_op jit(solution)/shard_map/ppermute | solution.py:351
  21.7 5.5 %collective-permute-start.2 = (bf16[4,192,128]{2,1,0:T(8,128)(2,1)}, bf16[4,192,128]{2,1,0:T(8,128)(2,1)S(1)}, u32[]{:S(2)}, u32[]{:S(2)}) collective-permute-start(bf16[4,192,128]{2,1,0:T(8,128)(2,1)} %get-tuple-element.51), channel_id=1, source_target_pairs={{0,1},{1,0},{2,3},{3,2},{4,5},{5,4},{6,7},{7,6},{8,9},{9,8},{10,11... | collective-permute-start | bytes 589832 | tf_op jit(solution)/shard_map/ppermute | solution.py:351
  28.6 18.7 %all-to-all-start = ((bf16[32,3,16,128]{3,2,1,0:T(8,128)(2,1)}), bf16[32,3,16,128]{3,2,1,0:T(8,128)(2,1)S(1)}, u32[]{:S(2)}, u32[]{:S(2)}) async-start(bf16[32,3,16,128]{3,2,1,0:T(8,128)(2,1)} %bitcast.10), calls=%async_computation | async-start | bytes 786432 | tf_op jit(solution)/shard_map/all_to_all | solution.py:346
  66.5 3.6 %collective-permute-start.7 = (bf16[4,192,128]{2,1,0:T(8,128)(2,1)S(1)}, bf16[4,192,128]{2,1,0:T(8,128)(2,1)S(1)}, u32[]{:S(2)}, u32[]{:S(2)}) collective-permute-start(bf16[4,192,128]{2,1,0:T(8,128)(2,1)S(1)} %bitcast.82), channel_id=1, source_target_pairs={{0,1},{1,0},{2,3},{3,2},{4,5},{5,4},{6,7},{7,6},{8,9},{9,8},{10,11... | collective-permute-start | bytes 589832 | tf_op jit(solution)/shard_map/ppermute | solution.py:351
  66.5 11.8 %collective-permute-start.12 = (bf16[4,192,128]{2,1,0:T(8,128)(2,1)S(1)}, bf16[4,192,128]{2,1,0:T(8,128)(2,1)S(1)}, u32[]{:S(2)}, u32[]{:S(2)}) collective-permute-start(bf16[4,192,128]{2,1,0:T(8,128)(2,1)S(1)} %bitcast.80), channel_id=1, source_target_pairs={{0,2},{1,3},{2,0},{3,1},{4,6},{5,7},{6,4},{7,5},{8,10},{9,11},{10,... | collective-permute-start | bytes 589832 | tf_op jit(solution)/shard_map/ppermute | solution.py:351
  67.5 11.0 %collective-permute-start.13 = (bf16[4,192,128]{2,1,0:T(8,128)(2,1)S(1)}, bf16[4,192,128]{2,1,0:T(8,128)(2,1)S(1)}, u32[]{:S(2)}, u32[]{:S(2)}) collective-permute-start(bf16[4,192,128]{2,1,0:T(8,128)(2,1)S(1)} %bitcast.78), channel_id=1, source_target_pairs={{0,3},{1,2},{2,1},{3,0},{4,7},{5,6},{6,5},{7,4},{8,11},{9,10},{10,... | collective-permute-start | bytes 589832 | tf_op jit(solution)/shard_map/ppermute | solution.py:351
  68.4 22.4 %collective-permute-start.10 = (bf16[4,192,128]{2,1,0:T(8,128)(2,1)S(1)}, bf16[4,192,128]{2,1,0:T(8,128)(2,1)S(1)}, u32[]{:S(2)}, u32[]{:S(2)}) collective-permute-start(bf16[4,192,128]{2,1,0:T(8,128)(2,1)S(1)} %bitcast.74), channel_id=1, source_target_pairs={{0,4},{1,5},{2,6},{3,7},{4,0},{5,1},{6,2},{7,3},{8,12},{9,13},{10,... | collective-permute-start | bytes 589832 | tf_op jit(solution)/shard_map/ppermute | solution.py:351
  69.4 22.3 %collective-permute-start.11 = (bf16[4,192,128]{2,1,0:T(8,128)(2,1)S(1)}, bf16[4,192,128]{2,1,0:T(8,128)(2,1)S(1)}, u32[]{:S(2)}, u32[]{:S(2)}) collective-permute-start(bf16[4,192,128]{2,1,0:T(8,128)(2,1)S(1)} %bitcast.73), channel_id=1, source_target_pairs={{0,5},{1,4},{2,7},{3,6},{4,1},{5,0},{6,3},{7,2},{8,13},{9,12},{10,... | collective-permute-start | bytes 589832 | tf_op jit(solution)/shard_map/ppermute | solution.py:351
  76.9 27.3 %collective-permute-start.8 = (bf16[4,192,128]{2,1,0:T(8,128)(2,1)S(1)}, bf16[4,192,128]{2,1,0:T(8,128)(2,1)S(1)}, u32[]{:S(2)}, u32[]{:S(2)}) collective-permute-start(bf16[4,192,128]{2,1,0:T(8,128)(2,1)S(1)} %get-tuple-element.61), channel_id=1, source_target_pairs={{0,6},{1,7},{2,4},{3,5},{4,2},{5,3},{6,0},{7,1},{8,14},{9,15},{10,... | collective-permute-start | bytes 589832 | tf_op jit(solution)/shard_map/ppermute | solution.py:351
  78.3 14.0 %collective-permute-start.14 = (bf16[4,192,128]{2,1,0:T(8,128)(2,1)S(1)}, bf16[4,192,128]{2,1,0:T(8,128)(2,1)S(1)}, u32[]{:S(2)}, u32[]{:S(2)}) collective-permute-start(bf16[4,192,128]{2,1,0:T(8,128)(2,1)S(1)} %get-tuple-element.69), channel_id=1, source_target_pairs={{0,1},{1,0},{2,3},{3,2},{4,5},{5,4},{6,7},{7,6},{8,9},{9,8},{10,11... | collective-permute-start | bytes 589832 | tf_op jit(solution)/shard_map/ppermute | solution.py:351
  78.5 26.7 %collective-permute-start.9 = (bf16[4,192,128]{2,1,0:T(8,128)(2,1)S(1)}, bf16[4,192,128]{2,1,0:T(8,128)(2,1)S(1)}, u32[]{:S(2)}, u32[]{:S(2)}) collective-permute-start(bf16[4,192,128]{2,1,0:T(8,128)(2,1)S(1)} %get-tuple-element.62), channel_id=1, source_target_pairs={{0,7},{1,6},{2,5},{3,4},{4,3},{5,2},{6,1},{7,0},{8,15},{9,14},{10,... | collective-permute-start | bytes 589832 | tf_op jit(solution)/shard_map/ppermute | solution.py:351
  90.8 14.4 %collective-permute-start.15 = (bf16[4,192,128]{2,1,0:T(8,128)(2,1)S(1)}, bf16[4,192,128]{2,1,0:T(8,128)(2,1)S(1)}, u32[]{:S(2)}, u32[]{:S(2)}) collective-permute-start(bf16[4,192,128]{2,1,0:T(8,128)(2,1)S(1)} %get-tuple-element.71), channel_id=1, source_target_pairs={{0,2},{1,3},{2,0},{3,1},{4,6},{5,7},{6,4},{7,5},{8,10},{9,11},{10,... | collective-permute-start | bytes 589832 | tf_op jit(solution)/shard_map/ppermute | solution.py:351
  91.7 13.5 %collective-permute-start.16 = (bf16[4,192,128]{2,1,0:T(8,128)(2,1)S(1)}, bf16[4,192,128]{2,1,0:T(8,128)(2,1)S(1)}, u32[]{:S(2)}, u32[]{:S(2)}) collective-permute-start(bf16[4,192,128]{2,1,0:T(8,128)(2,1)S(1)} %get-tuple-element.72), channel_id=1, source_target_pairs={{0,3},{1,2},{2,1},{3,0},{4,7},{5,6},{6,5},{7,4},{8,11},{9,10},{10,... | collective-permute-start | bytes 589832 | tf_op jit(solution)/shard_map/ppermute | solution.py:351
  103.2 15.3 %collective-permute-start.17 = (bf16[4,192,128]{2,1,0:T(8,128)(2,1)S(1)}, bf16[4,192,128]{2,1,0:T(8,128)(2,1)S(1)}, u32[]{:S(2)}, u32[]{:S(2)}) collective-permute-start(bf16[4,192,128]{2,1,0:T(8,128)(2,1)S(1)} %get-tuple-element.74), channel_id=1, source_target_pairs={{0,4},{1,5},{2,6},{3,7},{4,0},{5,1},{6,2},{7,3},{8,12},{9,13},{10,... | collective-permute-start | bytes 589832 | tf_op jit(solution)/shard_map/ppermute | solution.py:351
  104.2 14.3 %collective-permute-start.18 = (bf16[4,192,128]{2,1,0:T(8,128)(2,1)S(1)}, bf16[4,192,128]{2,1,0:T(8,128)(2,1)S(1)}, u32[]{:S(2)}, u32[]{:S(2)}) collective-permute-start(bf16[4,192,128]{2,1,0:T(8,128)(2,1)S(1)} %get-tuple-element.75), channel_id=1, source_target_pairs={{0,5},{1,4},{2,7},{3,6},{4,1},{5,0},{6,3},{7,2},{8,13},{9,12},{10,... | collective-permute-start | bytes 589832 | tf_op jit(solution)/shard_map/ppermute | solution.py:351
  116.1 9.3 %collective-permute-start.19 = (bf16[4,192,128]{2,1,0:T(8,128)(2,1)S(1)}, bf16[4,192,128]{2,1,0:T(8,128)(2,1)S(1)}, u32[]{:S(2)}, u32[]{:S(2)}) collective-permute-start(bf16[4,192,128]{2,1,0:T(8,128)(2,1)S(1)} %get-tuple-element.78), channel_id=1, source_target_pairs={{0,6},{1,7},{2,4},{3,5},{4,2},{5,3},{6,0},{7,1},{8,14},{9,15},{10,... | collective-permute-start | bytes 589832 | tf_op jit(solution)/shard_map/ppermute | solution.py:351
  117.5 10.0 %collective-permute-start.20 = (bf16[4,192,128]{2,1,0:T(8,128)(2,1)S(1)}, bf16[4,192,128]{2,1,0:T(8,128)(2,1)S(1)}, u32[]{:S(2)}, u32[]{:S(2)}) collective-permute-start(bf16[4,192,128]{2,1,0:T(8,128)(2,1)S(1)} %get-tuple-element.79), channel_id=1, source_target_pairs={{0,7},{1,6},{2,5},{3,4},{4,3},{5,2},{6,1},{7,0},{8,15},{9,14},{10,... | collective-permute-start | bytes 589832 | tf_op jit(solution)/shard_map/ppermute | solution.py:351
  145.3 15.8 %all-to-all-start.3 = ((bf16[32,3,16,128]{3,2,1,0:T(8,128)(2,1)}), bf16[32,3,16,128]{3,2,1,0:T(8,128)(2,1)S(1)}, u32[]{:S(2)}, u32[]{:S(2)}) async-start(bf16[32,3,16,128]{3,2,1,0:T(8,128)(2,1)} %bitcast.33), calls=%async_computation.3 | async-start | bytes 786432 | tf_op jit(solution)/shard_map/all_to_all | solution.py:346
  161.7 3.9 %collective-permute-start.21 = (bf16[4,192,128]{2,1,0:T(8,128)(2,1)S(1)}, bf16[4,192,128]{2,1,0:T(8,128)(2,1)S(1)}, u32[]{:S(2)}, u32[]{:S(2)}) collective-permute-start(bf16[4,192,128]{2,1,0:T(8,128)(2,1)S(1)} %bitcast.81), channel_id=1, source_target_pairs={{0,1},{1,0},{2,3},{3,2},{4,5},{5,4},{6,7},{7,6},{8,9},{9,8},{10,11... | collective-permute-start | bytes 589832 | tf_op jit(solution)/shard_map/ppermute | solution.py:351
  161.8 10.4 %collective-permute-start.26 = (bf16[4,192,128]{2,1,0:T(8,128)(2,1)S(1)}, bf16[4,192,128]{2,1,0:T(8,128)(2,1)S(1)}, u32[]{:S(2)}, u32[]{:S(2)}) collective-permute-start(bf16[4,192,128]{2,1,0:T(8,128)(2,1)S(1)} %bitcast.79), channel_id=1, source_target_pairs={{0,2},{1,3},{2,0},{3,1},{4,6},{5,7},{6,4},{7,5},{8,10},{9,11},{10,... | collective-permute-start | bytes 589832 | tf_op jit(solution)/shard_map/ppermute | solution.py:351
  162.8 15.3 %collective-permute-start.24 = (bf16[4,192,128]{2,1,0:T(8,128)(2,1)S(1)}, bf16[4,192,128]{2,1,0:T(8,128)(2,1)S(1)}, u32[]{:S(2)}, u32[]{:S(2)}) collective-permute-start(bf16[4,192,128]{2,1,0:T(8,128)(2,1)S(1)} %bitcast.76), channel_id=1, source_target_pairs={{0,4},{1,5},{2,6},{3,7},{4,0},{5,1},{6,2},{7,3},{8,12},{9,13},{10,... | collective-permute-start | bytes 589832 | tf_op jit(solution)/shard_map/ppermute | solution.py:351
  163.9 14.2 %collective-permute-start.25 = (bf16[4,192,128]{2,1,0:T(8,128)(2,1)S(1)}, bf16[4,192,128]{2,1,0:T(8,128)(2,1)S(1)}, u32[]{:S(2)}, u32[]{:S(2)}) collective-permute-start(bf16[4,192,128]{2,1,0:T(8,128)(2,1)S(1)} %bitcast.75), channel_id=1, source_target_pairs={{0,5},{1,4},{2,7},{3,6},{4,1},{5,0},{6,3},{7,2},{8,13},{9,12},{10,... | collective-permute-start | bytes 589832 | tf_op jit(solution)/shard_map/ppermute | solution.py:351
  163.9 9.0 %collective-permute-start.27 = (bf16[4,192,128]{2,1,0:T(8,128)(2,1)S(1)}, bf16[4,192,128]{2,1,0:T(8,128)(2,1)S(1)}, u32[]{:S(2)}, u32[]{:S(2)}) collective-permute-start(bf16[4,192,128]{2,1,0:T(8,128)(2,1)S(1)} %bitcast.77), channel_id=1, source_target_pairs={{0,3},{1,2},{2,1},{3,0},{4,7},{5,6},{6,5},{7,4},{8,11},{9,10},{10,... | collective-permute-start | bytes 589832 | tf_op jit(solution)/shard_map/ppermute | solution.py:351
  170.8 12.4 %collective-permute-start.22 = (bf16[4,192,128]{2,1,0:T(8,128)(2,1)S(1)}, bf16[4,192,128]{2,1,0:T(8,128)(2,1)S(1)}, u32[]{:S(2)}, u32[]{:S(2)}) collective-permute-start(bf16[4,192,128]{2,1,0:T(8,128)(2,1)S(1)} %get-tuple-element.87), channel_id=1, source_target_pairs={{0,6},{1,7},{2,4},{3,5},{4,2},{5,3},{6,0},{7,1},{8,14},{9,15},{10,... | collective-permute-start | bytes 589832 | tf_op jit(solution)/shard_map/ppermute | solution.py:351
  172.2 11.0 %collective-permute-start.23 = (bf16[4,192,128]{2,1,0:T(8,128)(2,1)S(1)}, bf16[4,192,128]{2,1,0:T(8,128)(2,1)S(1)}, u32[]{:S(2)}, u32[]{:S(2)}) collective-permute-start(bf16[4,192,128]{2,1,0:T(8,128)(2,1)S(1)} %get-tuple-element.88), channel_id=1, source_target_pairs={{0,7},{1,6},{2,5},{3,4},{4,3},{5,2},{6,1},{7,0},{8,15},{9,14},{10,... | collective-permute-start | bytes 589832 | tf_op jit(solution)/shard_map/ppermute | solution.py:351

commit v8 on v7

--- a/solution.py
+++ b/solution.py
@@ -136,7 +136,7 @@
             cot = wide(cot_ref, cell, (t, t + 1))
             for r in range(0, rows, band):
                 slope = gelu_slope(preact[r : r + band])
-                bands.append((cot[r : r + band].astype(jnp.float32) * slope).astype(jnp.bfloat16))
+                bands.append(cot[r : r + band] * slope.astype(jnp.bfloat16))
         grad = jnp.concatenate(bands, axis=0)
         for cell in range(cells):
             for k in range(2):
@@ -358,14 +358,14 @@
 
     cells = (x_piece, c_piece, y_local, lanes)
 
-    def analyze(heads):
-        return small(y_down_body, [packed], y_mat, *settle(heads, y_devices, cells))[0]
-
-    def mix(back, part, weight, after):
+    def analyze(heads, after=()):
+        return small(y_down_body, [packed], y_mat, *settle(heads, y_devices, cells), after=after)[0]
+
+    def mix(back, part, weight):
         part = exchange(part).reshape((x_devices, x_pieces, c_pieces) + packed[2:])
         kept, part = small(
             functools.partial(spectral_body, back), [(channels, span, j_local * modes), part.shape],
-            part, x_mat, weight, after=after,
+            part, x_mat, weight,
         )
         return kept, exchange(part).reshape(packed)
 
@@ -385,14 +385,14 @@
         done = head_call(first, count, after)
         heads[first : first + count] = [send(first + e, piece) for e, piece in enumerate(done)]
         after = (done[0],) if first == 6 else tuple(heads[6:])
-    part = analyze(heads)
+    part = analyze(heads, (mix_up, mix_back, y_mat_t))
     (weight,) = call(
         weight_body, (channels,),
         [pl.BlockSpec((j_local, q_local, 1, channels, time_modes, modes), lambda c: (0, 0, c, 0, 0, 0))],
         [pl.BlockSpec((1, channels, span, j_local * modes), lambda c: (c, 0, 0, 0))],
         [jax.ShapeDtypeStruct((channels, channels, span, j_local * modes), bf16)], (spectral_weight,), after=(part,),
     )
-    modes_in, part = mix(False, part, weight, (mix_up, mix_back, y_mat_t))
+    modes_in, part = mix(False, part, weight)
 
     middle, late = synthesize(part, ())
     sent, grads = [(), ()], ()
@@ -405,7 +405,7 @@
         heads[first : first + count] = [send(first + e, piece) for e, piece in enumerate(done)]
         sent.append(tuple(heads[max(first, 1) : first + count]) if paired else ())
     part = analyze(heads)
-    grad_modes, part = mix(True, part, weight, ())
+    grad_modes, part = mix(True, part, weight)
     spec = whole(modes_in.shape)
     (grad_spectral,) = call(
         outer_product_body, (j_local,), [spec, spec],
@@ -416,7 +416,7 @@
     if not paired:
         middle = rest(middle, late)
     field = ()
-    for first, count in pairs:
+    for first, count in pairs[:2] + [(4, blocks - 4)] if blocks > 4 else pairs:
         field, late = outer_call(first, count, middle, grads, field, late)
         if late:
             middle, late = rest(middle, late), []

time: 191 us -> 190 us (level); the launches traced: 188 us -> 190 us
  waiting for transfers between devices: 16.1 us -> 21.4 us
  Pallas kernels: 96.7 us -> 93.9 us
  blocking collectives: 33.8 us -> 31.5 us
    all_to_all x2, waiting for transfers between devices: 9.44 us -> 13.9 us  [exchange(): return lax.all_to_all(pieces, ('gx',) + YZ, 0, 0, tiled=True).reshape(shape)]
    pallas_call x20 -> x19, Pallas kernels: 96.7 us -> 93.9 us  [call(): pl.pallas_call(placed, grid_spec=spec, out_shape=list(out_shape) + [jax.S...]
    all_to_all x2, blocking collectives: 33.8 us -> 31.5 us  [exchange(): return lax.all_to_all(pieces, ('gx',) + YZ, 0, 0, tiled=True).reshape(shape)]
  transfers between devices with their start and end apart: 30 -> 30, of which waited for: 6 -> 6; matrix products, arithmetic and copies ran while one was open for 3% -> 4% of each run, Pallas kernels for 44% -> 41%
where the time goes in v8:
time: 190 us
  Pallas kernels  93.9 us (49%)
  starting transfers between devices  34.2 us (18%)
  blocking collectives  31.5 us (17%)
  waiting for transfers between devices  21.4 us (11%)
  local copies, waits for them, and re-layouts  6.35 us (3%)
    pallas_call x19, Pallas kernels, call(): pl.pallas_call(placed, grid_spec=spec, out_shape=list(out_shape) + [jax.S...  93.9 us
    all_to_all x2, blocking collectives, exchange(): return lax.all_to_all(pieces, ('gx',) + YZ, 0, 0, tiled=True).reshape(shape)  31.5 us
    ppermute x28, starting transfers between devices, send(): return lax.ppermute(piece, YZ, [(d, d ^ k) for d in range(y_devices)])  26.7 us
    all_to_all x2, waiting for transfers between devices, exchange(): return lax.all_to_all(pieces, ('gx',) + YZ, 0, 0, tiled=True).reshape(shape)  13.9 us
    all_to_all x2, starting transfers between devices, exchange(): return lax.all_to_all(pieces, ('gx',) + YZ, 0, 0, tiled=True).reshape(shape)  7.53 us
    ppermute x28, waiting for transfers between devices, send(): return lax.ppermute(piece, YZ, [(d, d ^ k) for d in range(y_devices)])  7.51 us
  transfers between devices with their start and end apart: 30, of which 6 were waited for; matrix products, arithmetic and copies ran while one was open for 4% of the time, Pallas kernels for 41%

profile of v8, /device:TPU:0, one launch (start us, length us, event | category | flops | bytes accessed | tf_op | source)
XLA Modules:
  0.0 189.6 jit_solution(6741743866115051151)
XLA Ops:
  0.7 0.9 copy-done.1
  1.6 3.2 %shard_map.104 = (bf16[4,192,128]{2,1,0:T(8,128)(2,1)S(1)}, bf16[4,192,128]{2,1,0:T(8,128)(2,1)S(1)}) custom-call(s32[8]{0:T(128)S(1)} %iota_xor_fusion.refs_0_, bf16[8,12,32,16,128]{4,3,2,1,0:T(8,128)(2,1)} %refs_1_.17, bf16[1024,128]{1,0:T(8,128)(2,1)S(1)} %copy-done.1), custom_call_target="tpu_custom_call" | custom-call | tf_op jit(solution)/shard_map/pallas_call | solution.py:71
  4.8 3.4 %collective-permute-start.1 = (bf16[4,192,128]{2,1,0:T(8,128)(2,1)S(1)}, bf16[4,192,128]{2,1,0:T(8,128)(2,1)S(1)}, u32[]{:S(2)}, u32[]{:S(2)}) collective-permute-start(bf16[4,192,128]{2,1,0:T(8,128)(2,1)S(1)} %get-tuple-element.49), channel_id=1, source_target_pairs={{0,7},{1,6},{2,5},{3,4},{4,3},{5,2},{6,1},{7,0},{8,15},{9,14},{10,... | collective-permute-start | bytes 589832 | tf_op jit(solution)/shard_map/ppermute | solution.py:351
  8.2 0.6 collective-permute-start
  8.8 5.3 %shard_map.106 = (bf16[4,192,128]{2,1,0:T(8,128)(2,1)S(1)}, bf16[4,192,128]{2,1,0:T(8,128)(2,1)S(1)}, bf16[4,192,128]{2,1,0:T(8,128)(2,1)S(1)}, bf16[4,192,128]{2,1,0:T(8,128)(2,1)S(1)}) custom-call(s32[8]{0:T(128)S(1)} %iota_xor_fusion.refs_0_, bf16[8,12,32,16,128]{4,3,2,1,0:T(8,128)(2,1)} %refs_1_.17, bf16[1024,128]{1,0:T(8,128)(2,1)S(1)} %copy-done.1, ...), custom_call_target="tpu_custom_call" | custom-call | tf_op jit(solution)/shard_map/pallas_call | solution.py:71
  14.2 1.4 collective-permute-start.3
  15.5 0.1 collective-permute-start.4
  15.6 1.7 collective-permute-start.5
  17.3 0.1 copy.22
  17.4 1.3 broadcast_multiply_fusion
  18.8 1.7 mul.51.refs_10_.refs_2_
  20.5 1.7 mul.48.refs_9_.refs_3_
  22.3 0.5 collective-permute-start.6
  22.7 3.2 %shard_map.105 = (bf16[4,192,128]{2,1,0:T(8,128)(2,1)S(1)}, bf16[4,192,128]{2,1,0:T(8,128)(2,1)S(1)}) custom-call(s32[8]{0:T(128)S(1)} %iota_xor_fusion.refs_0_, bf16[8,12,32,16,128]{4,3,2,1,0:T(8,128)(2,1)} %refs_1_.17, bf16[1024,128]{1,0:T(8,128)(2,1)S(1)} %copy-done.2, bf16[4,192,128]{2,1,0:T(8,128)(2,1)S(1)} %collective-permute-done.refs_3_, ...), custom_call_target="tpu_custom_call" | custom-call | tf_op jit(solution)/shard_map/pallas_call | solution.py:71
  25.9 0.1 collective-permute-start.2
  26.0 0.9 dynamic-slice_bitcast_fusion.refs_11_.refs_1_
  26.9 0.9 dynamic-slice_bitcast_fusion.1.refs_0_
  27.9 1.3 collective-permute-done.6
  29.2 1.4 shard_map.107.refs_1_
  30.6 4.9 %all-to-all-start = ((bf16[32,3,16,128]{3,2,1,0:T(8,128)(2,1)}), bf16[32,3,16,128]{3,2,1,0:T(8,128)(2,1)S(1)}, u32[]{:S(2)}, u32[]{:S(2)}) async-start(bf16[32,3,16,128]{3,2,1,0:T(8,128)(2,1)} %bitcast.11), calls=%async_computation | async-start | bytes 786432 | tf_op jit(solution)/shard_map/all_to_all | solution.py:346
  35.5 7.8 %shard_map.108.refs_2_ = bf16[12,12,32,128]{3,2,1,0:T(8,128)(2,1)S(1)} custom-call(bf16[4,8,12,12,4,32]{5,4,3,2,1,0:T(4,128)(2,1)} %refs_0_.1, bf16[4,8,3,16,128]{4,3,2,1,0:T(8,128)(2,1)} %shard_map.107.refs_1_), custom_call_target="tpu_custom_call" | custom-call | tf_op jit(solution)/shard_map/pallas_call | solution.py:71
  43.3 5.4 %all-to-all-done = bf16[32,3,16,128]{3,2,1,0:T(8,128)(2,1)S(1)} async-done(((bf16[32,3,16,128]{3,2,1,0:T(8,128)(2,1)}), bf16[32,3,16,128]{3,2,1,0:T(8,128)(2,1)S(1)}, u32[]{:S(2)}, u32[]{:S(2)}) %all-to-all-start) | async-done | bytes 393248 | tf_op jit(solution)/shard_map/all_to_all | solution.py:346
  48.6 0.6 shard_map.109
  49.3 15.6 %all_to_all.20 = bf16[32,3,16,128]{3,2,1,0:T(8,128)(2,1)S(1)} all-to-all(bf16[32,3,16,128]{3,2,1,0:T(8,128)(2,1)S(1)} %bitcast.57), channel_id=1, replica_groups=mesh['parts'=1,'gx'=4,'gy'=4,'gz'=2] {'gx','gy','gz'}, dimensions={0} | all-to-all | bytes 786432 | tf_op jit(solution)/shard_map/all_to_all | solution.py:346
  64.9 0.7 shard_map.110
  65.5 0.1 collective-permute-start.7
  65.6 0.9 collective-permute-start.12
  66.6 0.9 collective-permute-start.13
  67.5 1.0 collective-permute-start.10
  68.5 0.7 collective-permute-start.11
  69.2 6.8 %shard_map.111 = (bf16[8,12,32,16,128]{4,3,2,1,0:T(8,128)(2,1)}, bf16[4,192,128]{2,1,0:T(8,128)(2,1)S(1)}, bf16[4,192,128]{2,1,0:T(8,128)(2,1)S(1)}, bf16[4,192,128]{2,1,0:T(8,128)(2,1)S(1)}) custom-call(s32[8]{0:T(128)S(1)} %iota_xor_fusion.refs_0_, bf16[8,12,32,16,128]{4,3,2,1,0:T(8,128)(2,1)} %refs_1_.17, ...), custom_call_target="tpu_custom_call", output_to_operand_aliasing={{2}: (7, {}), {3}: (8, {})} | custom-call | tf_op jit(solution)/shard_map/pallas_call | solution.py:71
  76.0 1.4 collective-permute-start.8
  77.4 0.2 collective-permute-start.14
  77.6 1.4 collective-permute-start.9
  79.0 10.8 %shard_map.112 = (bf16[8,12,32,16,128]{4,3,2,1,0:T(8,128)(2,1)}, bf16[4,192,128]{2,1,0:T(8,128)(2,1)S(1)}, bf16[4,192,128]{2,1,0:T(8,128)(2,1)S(1)}) custom-call(s32[8]{0:T(128)S(1)} %iota_xor_fusion.refs_0_, bf16[8,12,32,16,128]{4,3,2,1,0:T(8,128)(2,1)} %refs_1_.17, bf16[8,12,32,16,128]{4,3,2,1,0:T(8,128)(2,1)} %refs_2_.12, ...), custom_call_target="tpu_custom_call", output_to_operand_aliasing={{0}: (8, {})} | custom-call | tf_op jit(solution)/shard_map/pallas_call | solution.py:71
  89.8 0.9 collective-permute-start.15
  90.7 0.7 collective-permute-start.16
  91.4 10.8 %shard_map.113 = (bf16[8,12,32,16,128]{4,3,2,1,0:T(8,128)(2,1)}, bf16[4,192,128]{2,1,0:T(8,128)(2,1)S(1)}, bf16[4,192,128]{2,1,0:T(8,128)(2,1)S(1)}) custom-call(s32[8]{0:T(128)S(1)} %iota_xor_fusion.refs_0_, bf16[8,12,32,16,128]{4,3,2,1,0:T(8,128)(2,1)} %refs_1_.17, bf16[8,12,32,16,128]{4,3,2,1,0:T(8,128)(2,1)} %refs_2_.12, ...), custom_call_target="tpu_custom_call", output_to_operand_aliasing={{0}: (8, {})} | custom-call | tf_op jit(solution)/shard_map/pallas_call | solution.py:71
  102.2 1.0 collective-permute-start.17
  103.2 1.0 collective-permute-start.18
  104.2 10.8 %shard_map.114 = (bf16[8,12,32,16,128]{4,3,2,1,0:T(8,128)(2,1)}, bf16[4,192,128]{2,1,0:T(8,128)(2,1)S(1)}, bf16[4,192,128]{2,1,0:T(8,128)(2,1)S(1)}) custom-call(s32[8]{0:T(128)S(1)} %iota_xor_fusion.refs_0_, bf16[8,12,32,16,128]{4,3,2,1,0:T(8,128)(2,1)} %refs_1_.17, bf16[8,12,32,16,128]{4,3,2,1,0:T(8,128)(2,1)} %refs_2_.12, ...), custom_call_target="tpu_custom_call", output_to_operand_aliasing={{0}: (8, {})} | custom-call | tf_op jit(solution)/shard_map/pallas_call | solution.py:71
  115.0 1.4 collective-permute-start.19
  116.4 1.0 collective-permute-start.20
  117.4 6.8 %shard_map.115 = (bf16[8,12,32,16,128]{4,3,2,1,0:T(8,128)(2,1)}, bf16[4,192,128]{2,1,0:T(8,128)(2,1)S(1)}) custom-call(s32[8]{0:T(128)S(1)} %iota_xor_fusion.refs_0_, bf16[8,12,32,16,128]{4,3,2,1,0:T(8,128)(2,1)} %refs_1_.17, bf16[8,12,32,16,128]{4,3,2,1,0:T(8,128)(2,1)} %refs_2_.12, ...), custom_call_target="tpu_custom_call", output_to_operand_aliasing={{0}: (7, {})} | custom-call | tf_op jit(solution)/shard_map/pallas_call | solution.py:71
  124.2 2.1 %collective-permute-done.20 = bf16[4,192,128]{2,1,0:T(8,128)(2,1)S(1)} collective-permute-done((bf16[4,192,128]{2,1,0:T(8,128)(2,1)S(1)}, bf16[4,192,128]{2,1,0:T(8,128)(2,1)S(1)}, u32[]{:S(2)}, u32[]{:S(2)}) %collective-permute-start.20) | collective-permute-done | bytes 196640 | tf_op jit(solution)/shard_map/ppermute | solution.py:351
  126.3 0.6 shard_map.116
  126.9 15.9 %all_to_all.21 = bf16[32,3,16,128]{3,2,1,0:T(8,128)(2,1)S(1)} all-to-all(bf16[32,3,16,128]{3,2,1,0:T(8,128)(2,1)S(1)} %bitcast.47), channel_id=1, replica_groups=mesh['parts'=1,'gx'=4,'gy'=4,'gz'=2] {'gx','gy','gz'}, dimensions={0} | all-to-all | bytes 786432 | tf_op jit(solution)/shard_map/all_to_all | solution.py:346
  142.8 1.3 shard_map.117
  144.2 2.6 %all-to-all-start.3 = ((bf16[32,3,16,128]{3,2,1,0:T(8,128)(2,1)}), bf16[32,3,16,128]{3,2,1,0:T(8,128)(2,1)S(1)}, u32[]{:S(2)}, u32[]{:S(2)}) async-start(bf16[32,3,16,128]{3,2,1,0:T(8,128)(2,1)} %bitcast.33), calls=%async_computation.3 | async-start | bytes 786432 | tf_op jit(solution)/shard_map/all_to_all | solution.py:346
  146.8 4.6 %shard_map.118.refs_2_ = f32[4,8,12,12,4,32]{5,4,3,2,1,0:T(4,128)} custom-call(bf16[12,32,128]{2,1,0:T(8,128)(2,1)S(1)} %get-tuple-element.81.refs_0_, bf16[12,32,128]{2,1,0:T(8,128)(2,1)S(1)} %get-tuple-element.82.refs_1_), custom_call_target="tpu_custom_call" | custom-call | tf_op jit(solution)/shard_map/pallas_call | solution.py:71
  151.4 8.6 %all-to-all-done.3 = bf16[32,3,16,128]{3,2,1,0:T(8,128)(2,1)S(1)} async-done(((bf16[32,3,16,128]{3,2,1,0:T(8,128)(2,1)}), bf16[32,3,16,128]{3,2,1,0:T(8,128)(2,1)S(1)}, u32[]{:S(2)}, u32[]{:S(2)}) %all-to-all-start.3) | async-done | bytes 393248 | tf_op jit(solution)/shard_map/all_to_all | solution.py:346
  160.0 0.7 shard_map.119
  160.7 0.1 collective-permute-start.23
  160.7 1.0 collective-permute-start.26
  161.7 0.9 collective-permute-start.22
  162.5 0.6 collective-permute-start.21
  163.1 1.2 collective-permute-start.27
  164.3 5.1 %shard_map.120 = (bf16[8,12,32,16,128]{4,3,2,1,0:T(8,128)(2,1)}, bf16[4,192,128]{2,1,0:T(8,128)(2,1)S(1)}, bf16[4,192,128]{2,1,0:T(8,128)(2,1)S(1)}) custom-call(s32[8]{0:T(128)S(1)} %iota_xor_fusion.refs_0_, bf16[8,12,32,16,128]{4,3,2,1,0:T(8,128)(2,1)} %get-tuple-element.76.refs_1_, ...), custom_call_target="tpu_custom_call", output_to_operand_aliasing={{1}: (6, {}), {2}: (7, {})} | custom-call | tf_op jit(solution)/shard_map/pallas_call | solution.py:71
  169.4 1.4 collective-permute-start.24
  170.8 1.3 collective-permute-start.25
  172.1 5.1 %shard_map.121.refs_8_ = bf16[8,12,32,16,128]{4,3,2,1,0:T(8,128)(2,1)} custom-call(s32[8]{0:T(128)S(1)} %iota_xor_fusion.refs_0_, bf16[8,12,32,16,128]{4,3,2,1,0:T(8,128)(2,1)} %get-tuple-element.76.refs_1_, bf16[192,192]{1,0:T(8,128)(2,1)S(1)} %mul.51.refs_10_.refs_2_, bf16[128,1024]{1,0:T(8,128)(2,1)S(1)} %copy-done, ...), custom_call_target="tpu_custom_call", output_to_operand_aliasing={{}: (6, {})} | custom-call | tf_op jit(solution)/shard_map/pallas_call | solution.py:71
  177.2 0.8 collective-permute-done.24.refs_6_
  178.0 3.3 %collective-permute-done.25.refs_7_ = bf16[4,192,128]{2,1,0:T(8,128)(2,1)S(1)} collective-permute-done((bf16[4,192,128]{2,1,0:T(8,128)(2,1)S(1)}, bf16[4,192,128]{2,1,0:T(8,128)(2,1)S(1)}, u32[]{:S(2)}, u32[]{:S(2)}) %collective-permute-start.25) | collective-permute-done | bytes 196640 | tf_op jit(solution)/shard_map/ppermute | solution.py:351
  181.3 8.3 %shard_map.122 = bf16[8,12,32,16,128]{4,3,2,1,0:T(8,128)(2,1)} custom-call(s32[8]{0:T(128)S(1)} %iota_xor_fusion.refs_0_, bf16[8,12,32,16,128]{4,3,2,1,0:T(8,128)(2,1)} %get-tuple-element.76.refs_1_, bf16[192,192]{1,0:T(8,128)(2,1)S(1)} %mul.51.refs_10_.refs_2_, bf16[128,1024]{1,0:T(8,128)(2,1)S(1)} %copy-done, ...), custom_call_target="tpu_custom_call", output_to_operand_aliasing={{}: (8, {})} | custom-call | tf_op jit(solution)/shard_map/pallas_call | solution.py:71
  (35 shorter events, 0.1 us)
Async XLA Ops:
  0.6 1.0 copy-start.1
  1.6 15.7 %copy-start.4 = (bf16[12,12]{1,0:T(8,128)(2,1)S(1)}, bf16[12,12]{1,0:T(8,128)(2,1)}, u32[]{:S(2)}) copy-start(bf16[12,12]{1,0:T(8,128)(2,1)} %param.12) | copy-start | bytes 868
  1.6 21.1 %copy-start.2 = (bf16[1024,128]{1,0:T(8,128)(2,1)S(1)}, bf16[1024,128]{1,0:T(8,128)(2,1)}, u32[]{:S(2)}) copy-start(bf16[1024,128]{1,0:T(8,128)(2,1)} %constant.31.clone.refs_2_.refs_5_) | copy-start | bytes 786436
  4.8 17.5 %collective-permute-start.1 = (bf16[4,192,128]{2,1,0:T(8,128)(2,1)S(1)}, bf16[4,192,128]{2,1,0:T(8,128)(2,1)S(1)}, u32[]{:S(2)}, u32[]{:S(2)}) collective-permute-start(bf16[4,192,128]{2,1,0:T(8,128)(2,1)S(1)} %get-tuple-element.49), channel_id=1, source_target_pairs={{0,7},{1,6},{2,5},{3,4},{4,3},{5,2},{6,1},{7,0},{8,15},{9,14},{10,... | collective-permute-start | bytes 589832 | tf_op jit(solution)/shard_map/ppermute | solution.py:351
  8.2 14.5 %collective-permute-start = (bf16[4,192,128]{2,1,0:T(8,128)(2,1)S(1)}, bf16[4,192,128]{2,1,0:T(8,128)(2,1)S(1)}, u32[]{:S(2)}, u32[]{:S(2)}) collective-permute-start(bf16[4,192,128]{2,1,0:T(8,128)(2,1)S(1)} %get-tuple-element.48.refs_3_), channel_id=1, source_target_pairs={{0,6},{1,7},{2,4},{3,5},{4,2},{5,3},{6,0},{7,1},{8,14},{9,15},{10,... | collective-permute-start | bytes 589832 | tf_op jit(solution)/shard_map/ppermute | solution.py:351
  14.2 13.7 %collective-permute-start.3 = (bf16[4,192,128]{2,1,0:T(8,128)(2,1)S(1)}, bf16[4,192,128]{2,1,0:T(8,128)(2,1)S(1)}, u32[]{:S(2)}, u32[]{:S(2)}) collective-permute-start(bf16[4,192,128]{2,1,0:T(8,128)(2,1)S(1)} %get-tuple-element.52), channel_id=1, source_target_pairs={{0,2},{1,3},{2,0},{3,1},{4,6},{5,7},{6,4},{7,5},{8,10},{9,11},{10,... | collective-permute-start | bytes 589832 | tf_op jit(solution)/shard_map/ppermute | solution.py:351
  15.5 12.3 %collective-permute-start.4 = (bf16[4,192,128]{2,1,0:T(8,128)(2,1)S(1)}, bf16[4,192,128]{2,1,0:T(8,128)(2,1)S(1)}, u32[]{:S(2)}, u32[]{:S(2)}) collective-permute-start(bf16[4,192,128]{2,1,0:T(8,128)(2,1)S(1)} %get-tuple-element.53), channel_id=1, source_target_pairs={{0,3},{1,2},{2,1},{3,0},{4,7},{5,6},{6,5},{7,4},{8,11},{9,10},{10,... | collective-permute-start | bytes 589832 | tf_op jit(solution)/shard_map/ppermute | solution.py:351
  15.6 12.2 %collective-permute-start.5 = (bf16[4,192,128]{2,1,0:T(8,128)(2,1)S(1)}, bf16[4,192,128]{2,1,0:T(8,128)(2,1)S(1)}, u32[]{:S(2)}, u32[]{:S(2)}) collective-permute-start(bf16[4,192,128]{2,1,0:T(8,128)(2,1)S(1)} %get-tuple-element.54), channel_id=1, source_target_pairs={{0,4},{1,5},{2,6},{3,7},{4,0},{5,1},{6,2},{7,3},{8,12},{9,13},{10,... | collective-permute-start | bytes 589832 | tf_op jit(solution)/shard_map/ppermute | solution.py:351
  18.8 29.9 %copy-start.3 = (bf16[512,128]{1,0:T(8,128)(2,1)S(1)}, bf16[512,128]{1,0:T(8,128)(2,1)}, u32[]{:S(2)}) copy-start(bf16[512,128]{1,0:T(8,128)(2,1)} %constant.32.clone.refs_1_) | copy-start | bytes 393220
  22.2 46.9 %copy-start = (bf16[128,1024]{1,0:T(8,128)(2,1)S(1)}, bf16[128,1024]{1,0:T(8,128)(2,1)}, u32[]{:S(2)}) copy-start(bf16[128,1024]{1,0:T(8,128)(2,1)} %constant.30.clone.refs_4_.refs_3_) | copy-start | bytes 786436
  22.3 6.9 %collective-permute-start.6 = (bf16[4,192,128]{2,1,0:T(8,128)(2,1)S(1)}, bf16[4,192,128]{2,1,0:T(8,128)(2,1)S(1)}, u32[]{:S(2)}, u32[]{:S(2)}) collective-permute-start(bf16[4,192,128]{2,1,0:T(8,128)(2,1)S(1)} %get-tuple-element.55), channel_id=1, source_target_pairs={{0,5},{1,4},{2,7},{3,6},{4,1},{5,0},{6,3},{7,2},{8,13},{9,12},{10,... | collective-permute-start | bytes 589832 | tf_op jit(solution)/shard_map/ppermute | solution.py:351
  25.9 3.3 %collective-permute-start.2 = (bf16[4,192,128]{2,1,0:T(8,128)(2,1)S(1)}, bf16[4,192,128]{2,1,0:T(8,128)(2,1)S(1)}, u32[]{:S(2)}, u32[]{:S(2)}) collective-permute-start(bf16[4,192,128]{2,1,0:T(8,128)(2,1)S(1)} %get-tuple-element.51), channel_id=1, source_target_pairs={{0,1},{1,0},{2,3},{3,2},{4,5},{5,4},{6,7},{7,6},{8,9},{9,8},{10,11... | collective-permute-start | bytes 589832 | tf_op jit(solution)/shard_map/ppermute | solution.py:351
  30.6 18.1 %all-to-all-start = ((bf16[32,3,16,128]{3,2,1,0:T(8,128)(2,1)}), bf16[32,3,16,128]{3,2,1,0:T(8,128)(2,1)S(1)}, u32[]{:S(2)}, u32[]{:S(2)}) async-start(bf16[32,3,16,128]{3,2,1,0:T(8,128)(2,1)} %bitcast.11), calls=%async_computation | async-start | bytes 786432 | tf_op jit(solution)/shard_map/all_to_all | solution.py:346
  65.5 3.6 %collective-permute-start.7 = (bf16[4,192,128]{2,1,0:T(8,128)(2,1)S(1)}, bf16[4,192,128]{2,1,0:T(8,128)(2,1)S(1)}, u32[]{:S(2)}, u32[]{:S(2)}) collective-permute-start(bf16[4,192,128]{2,1,0:T(8,128)(2,1)S(1)} %bitcast.82), channel_id=1, source_target_pairs={{0,1},{1,0},{2,3},{3,2},{4,5},{5,4},{6,7},{7,6},{8,9},{9,8},{10,11... | collective-permute-start | bytes 589832 | tf_op jit(solution)/shard_map/ppermute | solution.py:351
  65.6 11.8 %collective-permute-start.12 = (bf16[4,192,128]{2,1,0:T(8,128)(2,1)S(1)}, bf16[4,192,128]{2,1,0:T(8,128)(2,1)S(1)}, u32[]{:S(2)}, u32[]{:S(2)}) collective-permute-start(bf16[4,192,128]{2,1,0:T(8,128)(2,1)S(1)} %bitcast.80), channel_id=1, source_target_pairs={{0,2},{1,3},{2,0},{3,1},{4,6},{5,7},{6,4},{7,5},{8,10},{9,11},{10,... | collective-permute-start | bytes 589832 | tf_op jit(solution)/shard_map/ppermute | solution.py:351
  66.6 11.0 %collective-permute-start.13 = (bf16[4,192,128]{2,1,0:T(8,128)(2,1)S(1)}, bf16[4,192,128]{2,1,0:T(8,128)(2,1)S(1)}, u32[]{:S(2)}, u32[]{:S(2)}) collective-permute-start(bf16[4,192,128]{2,1,0:T(8,128)(2,1)S(1)} %bitcast.78), channel_id=1, source_target_pairs={{0,3},{1,2},{2,1},{3,0},{4,7},{5,6},{6,5},{7,4},{8,11},{9,10},{10,... | collective-permute-start | bytes 589832 | tf_op jit(solution)/shard_map/ppermute | solution.py:351
  67.5 22.3 %collective-permute-start.10 = (bf16[4,192,128]{2,1,0:T(8,128)(2,1)S(1)}, bf16[4,192,128]{2,1,0:T(8,128)(2,1)S(1)}, u32[]{:S(2)}, u32[]{:S(2)}) collective-permute-start(bf16[4,192,128]{2,1,0:T(8,128)(2,1)S(1)} %bitcast.74), channel_id=1, source_target_pairs={{0,4},{1,5},{2,6},{3,7},{4,0},{5,1},{6,2},{7,3},{8,12},{9,13},{10,... | collective-permute-start | bytes 589832 | tf_op jit(solution)/shard_map/ppermute | solution.py:351
  68.5 22.2 %collective-permute-start.11 = (bf16[4,192,128]{2,1,0:T(8,128)(2,1)S(1)}, bf16[4,192,128]{2,1,0:T(8,128)(2,1)S(1)}, u32[]{:S(2)}, u32[]{:S(2)}) collective-permute-start(bf16[4,192,128]{2,1,0:T(8,128)(2,1)S(1)} %bitcast.73), channel_id=1, source_target_pairs={{0,5},{1,4},{2,7},{3,6},{4,1},{5,0},{6,3},{7,2},{8,13},{9,12},{10,... | collective-permute-start | bytes 589832 | tf_op jit(solution)/shard_map/ppermute | solution.py:351
  76.0 27.2 %collective-permute-start.8 = (bf16[4,192,128]{2,1,0:T(8,128)(2,1)S(1)}, bf16[4,192,128]{2,1,0:T(8,128)(2,1)S(1)}, u32[]{:S(2)}, u32[]{:S(2)}) collective-permute-start(bf16[4,192,128]{2,1,0:T(8,128)(2,1)S(1)} %get-tuple-element.61), channel_id=1, source_target_pairs={{0,6},{1,7},{2,4},{3,5},{4,2},{5,3},{6,0},{7,1},{8,14},{9,15},{10,... | collective-permute-start | bytes 589832 | tf_op jit(solution)/shard_map/ppermute | solution.py:351
  77.4 14.0 %collective-permute-start.14 = (bf16[4,192,128]{2,1,0:T(8,128)(2,1)S(1)}, bf16[4,192,128]{2,1,0:T(8,128)(2,1)S(1)}, u32[]{:S(2)}, u32[]{:S(2)}) collective-permute-start(bf16[4,192,128]{2,1,0:T(8,128)(2,1)S(1)} %get-tuple-element.69), channel_id=1, source_target_pairs={{0,1},{1,0},{2,3},{3,2},{4,5},{5,4},{6,7},{7,6},{8,9},{9,8},{10,11... | collective-permute-start | bytes 589832 | tf_op jit(solution)/shard_map/ppermute | solution.py:351
  77.6 26.6 %collective-permute-start.9 = (bf16[4,192,128]{2,1,0:T(8,128)(2,1)S(1)}, bf16[4,192,128]{2,1,0:T(8,128)(2,1)S(1)}, u32[]{:S(2)}, u32[]{:S(2)}) collective-permute-start(bf16[4,192,128]{2,1,0:T(8,128)(2,1)S(1)} %get-tuple-element.62), channel_id=1, source_target_pairs={{0,7},{1,6},{2,5},{3,4},{4,3},{5,2},{6,1},{7,0},{8,15},{9,14},{10,... | collective-permute-start | bytes 589832 | tf_op jit(solution)/shard_map/ppermute | solution.py:351
  89.8 14.4 %collective-permute-start.15 = (bf16[4,192,128]{2,1,0:T(8,128)(2,1)S(1)}, bf16[4,192,128]{2,1,0:T(8,128)(2,1)S(1)}, u32[]{:S(2)}, u32[]{:S(2)}) collective-permute-start(bf16[4,192,128]{2,1,0:T(8,128)(2,1)S(1)} %get-tuple-element.71), channel_id=1, source_target_pairs={{0,2},{1,3},{2,0},{3,1},{4,6},{5,7},{6,4},{7,5},{8,10},{9,11},{10,... | collective-permute-start | bytes 589832 | tf_op jit(solution)/shard_map/ppermute | solution.py:351
  90.7 13.5 %collective-permute-start.16 = (bf16[4,192,128]{2,1,0:T(8,128)(2,1)S(1)}, bf16[4,192,128]{2,1,0:T(8,128)(2,1)S(1)}, u32[]{:S(2)}, u32[]{:S(2)}) collective-permute-start(bf16[4,192,128]{2,1,0:T(8,128)(2,1)S(1)} %get-tuple-element.72), channel_id=1, source_target_pairs={{0,3},{1,2},{2,1},{3,0},{4,7},{5,6},{6,5},{7,4},{8,11},{9,10},{10,... | collective-permute-start | bytes 589832 | tf_op jit(solution)/shard_map/ppermute | solution.py:351
  102.2 15.2 %collective-permute-start.17 = (bf16[4,192,128]{2,1,0:T(8,128)(2,1)S(1)}, bf16[4,192,128]{2,1,0:T(8,128)(2,1)S(1)}, u32[]{:S(2)}, u32[]{:S(2)}) collective-permute-start(bf16[4,192,128]{2,1,0:T(8,128)(2,1)S(1)} %get-tuple-element.74), channel_id=1, source_target_pairs={{0,4},{1,5},{2,6},{3,7},{4,0},{5,1},{6,2},{7,3},{8,12},{9,13},{10,... | collective-permute-start | bytes 589832 | tf_op jit(solution)/shard_map/ppermute | solution.py:351
  103.2 14.2 %collective-permute-start.18 = (bf16[4,192,128]{2,1,0:T(8,128)(2,1)S(1)}, bf16[4,192,128]{2,1,0:T(8,128)(2,1)S(1)}, u32[]{:S(2)}, u32[]{:S(2)}) collective-permute-start(bf16[4,192,128]{2,1,0:T(8,128)(2,1)S(1)} %get-tuple-element.75), channel_id=1, source_target_pairs={{0,5},{1,4},{2,7},{3,6},{4,1},{5,0},{6,3},{7,2},{8,13},{9,12},{10,... | collective-permute-start | bytes 589832 | tf_op jit(solution)/shard_map/ppermute | solution.py:351
  115.0 9.2 %collective-permute-start.19 = (bf16[4,192,128]{2,1,0:T(8,128)(2,1)S(1)}, bf16[4,192,128]{2,1,0:T(8,128)(2,1)S(1)}, u32[]{:S(2)}, u32[]{:S(2)}) collective-permute-start(bf16[4,192,128]{2,1,0:T(8,128)(2,1)S(1)} %get-tuple-element.78), channel_id=1, source_target_pairs={{0,6},{1,7},{2,4},{3,5},{4,2},{5,3},{6,0},{7,1},{8,14},{9,15},{10,... | collective-permute-start | bytes 589832 | tf_op jit(solution)/shard_map/ppermute | solution.py:351
  116.4 9.9 %collective-permute-start.20 = (bf16[4,192,128]{2,1,0:T(8,128)(2,1)S(1)}, bf16[4,192,128]{2,1,0:T(8,128)(2,1)S(1)}, u32[]{:S(2)}, u32[]{:S(2)}) collective-permute-start(bf16[4,192,128]{2,1,0:T(8,128)(2,1)S(1)} %get-tuple-element.79), channel_id=1, source_target_pairs={{0,7},{1,6},{2,5},{3,4},{4,3},{5,2},{6,1},{7,0},{8,15},{9,14},{10,... | collective-permute-start | bytes 589832 | tf_op jit(solution)/shard_map/ppermute | solution.py:351
  144.2 15.8 %all-to-all-start.3 = ((bf16[32,3,16,128]{3,2,1,0:T(8,128)(2,1)}), bf16[32,3,16,128]{3,2,1,0:T(8,128)(2,1)S(1)}, u32[]{:S(2)}, u32[]{:S(2)}) async-start(bf16[32,3,16,128]{3,2,1,0:T(8,128)(2,1)} %bitcast.33), calls=%async_computation.3 | async-start | bytes 786432 | tf_op jit(solution)/shard_map/all_to_all | solution.py:346
  160.7 3.6 %collective-permute-start.23 = (bf16[4,192,128]{2,1,0:T(8,128)(2,1)S(1)}, bf16[4,192,128]{2,1,0:T(8,128)(2,1)S(1)}, u32[]{:S(2)}, u32[]{:S(2)}) collective-permute-start(bf16[4,192,128]{2,1,0:T(8,128)(2,1)S(1)} %bitcast.81), channel_id=1, source_target_pairs={{0,1},{1,0},{2,3},{3,2},{4,5},{5,4},{6,7},{7,6},{8,9},{9,8},{10,11... | collective-permute-start | bytes 589832 | tf_op jit(solution)/shard_map/ppermute | solution.py:351
  160.7 10.1 %collective-permute-start.26 = (bf16[4,192,128]{2,1,0:T(8,128)(2,1)S(1)}, bf16[4,192,128]{2,1,0:T(8,128)(2,1)S(1)}, u32[]{:S(2)}, u32[]{:S(2)}) collective-permute-start(bf16[4,192,128]{2,1,0:T(8,128)(2,1)S(1)} %bitcast.79), channel_id=1, source_target_pairs={{0,2},{1,3},{2,0},{3,1},{4,6},{5,7},{6,4},{7,5},{8,10},{9,11},{10,... | collective-permute-start | bytes 589832 | tf_op jit(solution)/shard_map/ppermute | solution.py:351
  161.7 15.5 %collective-permute-start.22 = (bf16[4,192,128]{2,1,0:T(8,128)(2,1)S(1)}, bf16[4,192,128]{2,1,0:T(8,128)(2,1)S(1)}, u32[]{:S(2)}, u32[]{:S(2)}) collective-permute-start(bf16[4,192,128]{2,1,0:T(8,128)(2,1)S(1)} %bitcast.76), channel_id=1, source_target_pairs={{0,5},{1,4},{2,7},{3,6},{4,1},{5,0},{6,3},{7,2},{8,13},{9,12},{10,... | collective-permute-start | bytes 589832 | tf_op jit(solution)/shard_map/ppermute | solution.py:351
  162.5 14.7 %collective-permute-start.21 = (bf16[4,192,128]{2,1,0:T(8,128)(2,1)S(1)}, bf16[4,192,128]{2,1,0:T(8,128)(2,1)S(1)}, u32[]{:S(2)}, u32[]{:S(2)}) collective-permute-start(bf16[4,192,128]{2,1,0:T(8,128)(2,1)S(1)} %bitcast.75), channel_id=1, source_target_pairs={{0,4},{1,5},{2,6},{3,7},{4,0},{5,1},{6,2},{7,3},{8,12},{9,13},{10,... | collective-permute-start | bytes 589832 | tf_op jit(solution)/shard_map/ppermute | solution.py:351
  163.1 9.0 %collective-permute-start.27 = (bf16[4,192,128]{2,1,0:T(8,128)(2,1)S(1)}, bf16[4,192,128]{2,1,0:T(8,128)(2,1)S(1)}, u32[]{:S(2)}, u32[]{:S(2)}) collective-permute-start(bf16[4,192,128]{2,1,0:T(8,128)(2,1)S(1)} %bitcast.77), channel_id=1, source_target_pairs={{0,3},{1,2},{2,1},{3,0},{4,7},{5,6},{6,5},{7,4},{8,11},{9,10},{10,... | collective-permute-start | bytes 589832 | tf_op jit(solution)/shard_map/ppermute | solution.py:351
  169.4 8.6 %collective-permute-start.24 = (bf16[4,192,128]{2,1,0:T(8,128)(2,1)S(1)}, bf16[4,192,128]{2,1,0:T(8,128)(2,1)S(1)}, u32[]{:S(2)}, u32[]{:S(2)}) collective-permute-start(bf16[4,192,128]{2,1,0:T(8,128)(2,1)S(1)} %get-tuple-element.89), channel_id=1, source_target_pairs={{0,6},{1,7},{2,4},{3,5},{4,2},{5,3},{6,0},{7,1},{8,14},{9,15},{10,... | collective-permute-start | bytes 589832 | tf_op jit(solution)/shard_map/ppermute | solution.py:351
  170.8 10.5 %collective-permute-start.25 = (bf16[4,192,128]{2,1,0:T(8,128)(2,1)S(1)}, bf16[4,192,128]{2,1,0:T(8,128)(2,1)S(1)}, u32[]{:S(2)}, u32[]{:S(2)}) collective-permute-start(bf16[4,192,128]{2,1,0:T(8,128)(2,1)S(1)} %get-tuple-element.90), channel_id=1, source_target_pairs={{0,7},{1,6},{2,5},{3,4},{4,3},{5,2},{6,1},{7,0},{8,15},{9,14},{10,... | collective-permute-start | bytes 589832 | tf_op jit(solution)/shard_map/ppermute | solution.py:351
